TPU v7x, 768 devices: a whole 4x8x12 slice. The times are simulated.
768 devices in a mesh: gx: 96 (over z, y), gy: 8 (over x, core).
Axes of the slice: x: 4, y: 8, z: 12, core: 2. Of those that a mesh axis runs over, the one named last changes fastest.
Arguments:
- populations: float32 [19, 768, 128, 128], P(None, 'gx', 'gy'), may hold values from 0.03 to 0.08
- concentration: float32 [2, 768, 128, 128], P(None, 'gx', 'gy'), may hold values from 0.5 to 1.5
- potential: float32 [768, 128, 128], P('gx', 'gy'), may hold values from -3 to 3
- permittivity: float32 [768, 128, 128], P('gx', 'gy'), may hold values from 1 to 10
- fluid_mask: int32 [768, 128, 128], P('gx', 'gy'), may hold values 0 or 1
- owners: int32 [96, 8], P('gx', 'gy'), may hold values from 0 to 7, each once within a row
Outputs:
- final_populations: float32 [19, 768, 128, 128], P(None, 'gx', 'gy')
- final_potential: float32 [768, 128, 128], P('gx', 'gy')
- migrated: float32 [2, 768, 128, 128], P(None, 'gx', 'gy')
Inputs may be any that keep to these rules, and one draw needn't show every extreme that they name: Each row of owners is a permutation of the slab indices across the flow.
All inputs are finite; a program needn't handle non-finite values. No bound on the sum of `fluid_mask` on one device may be relied on, other than what follows from the above.
Results may differ from a plain program's by a relative error of at most 0.00012.
Values sent between devices are 32-bit elements; how exact they have to be, the bound alone decides.
No kernel may reach another device: no remote copies, remote signals or barrier semaphores. Data moves between devices by JAX's collectives and lax.ppermute only.
A program may use at most 32 MiB of HBM per device.

v0:
```python
import jax
import jax.numpy as jnp
from jax import lax
from jax.sharding import PartitionSpec as P

STEPS = 2
SWEEPS = 4


LATTICE_VELOCITY = (
    (0, 0, 0),
    (1, 0, 0),
    (-1, 0, 0),
    (0, 1, 0),
    (0, -1, 0),
    (0, 0, 1),
    (0, 0, -1),
    (1, 1, 0),
    (-1, -1, 0),
    (1, -1, 0),
    (-1, 1, 0),
    (1, 0, 1),
    (-1, 0, -1),
    (1, 0, -1),
    (-1, 0, 1),
    (0, 1, 1),
    (0, -1, -1),
    (0, 1, -1),
    (0, -1, 1),
)
LATTICE_WEIGHT = (1.0 / 3.0,) + (1.0 / 18.0,) * 6 + (1.0 / 36.0,) * 12
OPPOSITE = (0, 2, 1, 4, 3, 6, 5, 8, 7, 10, 9, 12, 11, 14, 13, 16, 15, 18, 17)
RELAX_TIME = 0.8
COUPLING = 0.05
DRIVE_FORCE = 0.001
DIFFUSIVITY = (0.1, 0.15)
VALENCE = (1.0, -1.0)


def extended(cells, sides, width):
    for axis, dim in sides:
        count = lax.axis_size(axis)
        head = lax.slice_in_dim(cells, 0, width, axis=dim)
        tail = lax.slice_in_dim(cells, cells.shape[dim] - width, cells.shape[dim], axis=dim)
        cells = jnp.concatenate(
            [
                lax.ppermute(tail, axis, [(i, (i + 1) % count) for i in range(count)]),
                cells,
                lax.ppermute(head, axis, [((i + 1) % count, i) for i in range(count)]),
            ],
            axis=dim,
        )
    return cells


def collide_cells(popul, fluid, force):
    lattice = jnp.array(LATTICE_VELOCITY, jnp.float32)
    weight = jnp.array(LATTICE_WEIGHT, jnp.float32).reshape(19, 1, 1, 1)
    density = jnp.sum(popul, axis=0)
    moment = jnp.einsum("ic,ixyz->cxyz", lattice, popul, precision=lax.Precision.HIGHEST)
    velocity = fluid * (moment + 0.5 * force) / density
    shifted = (moment + RELAX_TIME * force) / density
    projected = jnp.einsum("ic,cxyz->ixyz", lattice, shifted, precision=lax.Precision.HIGHEST)
    square = jnp.sum(shifted * shifted, axis=0)
    equilibrium = (
        weight * density * (1.0 + 3.0 * projected + 4.5 * projected * projected - 1.5 * square)
    )
    relaxed = popul - (popul - equilibrium) / RELAX_TIME
    return (fluid * relaxed, relaxed, velocity)


def face_flux(conc_a, conc_b, pot_a, pot_b, vel_a, vel_b, fluid_a, fluid_b):
    diffus = jnp.array(DIFFUSIVITY, jnp.float32).reshape(2, 1, 1, 1)
    valence = jnp.array(VALENCE, jnp.float32).reshape(2, 1, 1, 1)
    drift = valence * 0.5 * (conc_a + conc_b) * (pot_b - pot_a)
    return (
        fluid_a
        * fluid_b
        * (-diffus * (conc_b - conc_a + drift) + 0.25 * (vel_a + vel_b) * (conc_a + conc_b))
    )


def jacobi_padded(pot_pad, perm_pad, charge_mid):
    pot_mid = pot_pad[1:-1, 1:-1]
    perm_mid = perm_pad[1:-1, 1:-1]
    others = [
        (pot_pad[2:, 1:-1], perm_pad[2:, 1:-1]),
        (pot_pad[:-2, 1:-1], perm_pad[:-2, 1:-1]),
        (pot_pad[1:-1, 2:], perm_pad[1:-1, 2:]),
        (pot_pad[1:-1, :-2], perm_pad[1:-1, :-2]),
        (jnp.roll(pot_mid, -1, 2), jnp.roll(perm_mid, -1, 2)),
        (jnp.roll(pot_mid, 1, 2), jnp.roll(perm_mid, 1, 2)),
    ]
    numer = jnp.zeros_like(pot_mid)
    denom = jnp.zeros_like(pot_mid)
    for other_pot, other_perm in others:
        face = 0.5 * (perm_mid + other_perm)
        numer = numer + face * other_pot
        denom = denom + face
    return (numer + charge_mid) / denom


def move_ions(side, pot_pad, fluid_pad, conc, velocity):
    conc_pad = side[:2]
    vel_pad = side[2:]
    outflow = face_flux(
        conc_pad[:, :-1, 1:-1],
        conc_pad[:, 1:, 1:-1],
        pot_pad[:-1, 1:-1],
        pot_pad[1:, 1:-1],
        vel_pad[0, :-1, 1:-1],
        vel_pad[0, 1:, 1:-1],
        fluid_pad[:-1, 1:-1],
        fluid_pad[1:, 1:-1],
    )
    total = outflow[:, 1:] - outflow[:, :-1]
    outflow = face_flux(
        conc_pad[:, 1:-1, :-1],
        conc_pad[:, 1:-1, 1:],
        pot_pad[1:-1, :-1],
        pot_pad[1:-1, 1:],
        vel_pad[1, 1:-1, :-1],
        vel_pad[1, 1:-1, 1:],
        fluid_pad[1:-1, :-1],
        fluid_pad[1:-1, 1:],
    )
    total = total + outflow[:, :, 1:] - outflow[:, :, :-1]
    pot_mid = pot_pad[1:-1, 1:-1]
    fluid_mid = fluid_pad[1:-1, 1:-1]
    outflow = face_flux(
        conc,
        jnp.roll(conc, -1, 3),
        pot_mid,
        jnp.roll(pot_mid, -1, 2),
        velocity[2],
        jnp.roll(velocity[2], -1, 2),
        fluid_mid,
        jnp.roll(fluid_mid, -1, 2),
    )
    total = total + outflow - jnp.roll(outflow, 1, 3)
    return conc - total


def body(populations, concentration, potential, permittivity, fluid_mask, owners):
    depth_x, depth_y, depth_z = potential.shape
    fluid = fluid_mask.astype(jnp.float32)
    width = 1
    static = extended(jnp.stack([permittivity, fluid]), (("gx", 1), ("gy", 2)), width)
    perm_wide = static[0]
    fluid_one = static[1]
    along = jnp.array([1.0, 0.0, 0.0], jnp.float32).reshape(3, 1, 1, 1)
    popul, conc, poten = (populations, concentration, potential)
    for step_index in range(STEPS):
        charge = VALENCE[0] * conc[0] + VALENCE[1] * conc[1]
        for sweep_index in range(SWEEPS + 1):
            pot_pad = extended(poten, (("gx", 0), ("gy", 1)), 1)
            if sweep_index < SWEEPS:
                poten = jacobi_padded(pot_pad, perm_wide, charge)
        poten = pot_pad[1:-1, 1:-1]
        field = jnp.stack(
            [
                -0.5 * (pot_pad[2:, 1:-1] - pot_pad[:-2, 1:-1]),
                -0.5 * (pot_pad[1:-1, 2:] - pot_pad[1:-1, :-2]),
                -0.5 * (jnp.roll(poten, -1, 2) - jnp.roll(poten, 1, 2)),
            ]
        )
        fluid_mid = fluid_one[1:-1, 1:-1]
        force = fluid_mid * (COUPLING * charge * field + DRIVE_FORCE * along)
        leaving, relaxed, velocity = collide_cells(popul, fluid_mid, force)
        padded = extended(jnp.concatenate([leaving, conc, velocity]), (("gx", 1), ("gy", 2)), 1)
        side = padded[19:]
        rows = []
        for index in range(19):
            step_x, step_y, step_z = LATTICE_VELOCITY[index]
            rows.append(
                padded[index, 1 - step_x : 1 - step_x + depth_x, 1 - step_y : 1 - step_y + depth_y]
            )
        read = []
        for index in range(19):
            step_x, step_y, step_z = LATTICE_VELOCITY[index]
            incoming = jnp.roll(rows[index], step_z, 2)
            source = jnp.roll(
                fluid_one[1 - step_x : 1 - step_x + depth_x, 1 - step_y : 1 - step_y + depth_y],
                step_z,
                2,
            )
            read.append(
                fluid_mid * (incoming + (1.0 - source) * relaxed[OPPOSITE[index]])
                + (1.0 - fluid_mid) * popul[index]
            )
        conc = move_ions(side, pot_pad, fluid_one, conc, velocity)
        popul = jnp.stack(read)
    owner_row = owners[0, 0]
    piece = lax.all_gather(conc, "gy", axis=2, tiled=True)
    length = piece.shape[2]
    wanted = owner_row * depth_y + jnp.arange(depth_y, dtype=jnp.int32)
    offered = jnp.arange(length, dtype=jnp.int32)
    select = (wanted[:, None] == offered[None, :]).astype(jnp.float32)
    migrated = jnp.einsum("jr,cxrz->cxjz", select, piece, precision=lax.Precision.HIGHEST)
    return (popul, poten, migrated)


def solution(mesh):
    in_specs = (
        P(None, "gx", "gy", None),
        P(None, "gx", "gy", None),
        P("gx", "gy", None),
        P("gx", "gy", None),
        P("gx", "gy", None),
        P("gx", "gy"),
    )
    out_specs = (P(None, "gx", "gy", None), P("gx", "gy", None), P(None, "gx", "gy", None))
    return jax.shard_map(body, mesh=mesh, in_specs=in_specs, out_specs=out_specs, check_vma=False)
```

profile of v0, /device:TPU:1, one launch (start us, length us, event | category | flops | bytes accessed | tf_op | source)
XLA Modules:
  0.0 265.2 jit_solution(16906114256433407450)
XLA Ops:
  8.8 18.0 %collective-permute-start.1 = (f32[2,1,16,128]{3,2,1,0:T(8,128)S(1)}, f32[2,1,16,128]{3,2,1,0:T(8,128)S(1)}, u32[]{:S(2)}, u32[]{:S(2)}) collective-permute-start(f32[2,1,16,128]{3,2,1,0:T(8,128)S(1)} %get-tuple-element.84), channel_id=1, source_target_pairs={{8,0},{16,8},{24,16},{32,24},{40,32},{48,40},{56,48},{64,56},{72,6... | collective-permute-start | bytes 49160 | tf_op jit(solution)/shard_map/ppermute | solution.py:49
  26.8 1.9 collective-permute-start
  29.5 1.9 collective-permute-start.5
  31.4 6.7 %collective-permute-start.4 = (f32[1,16,128]{2,1,0:T(8,128)S(1)}, f32[1,16,128]{2,1,0:T(8,128)S(1)}, u32[]{:S(2)}, u32[]{:S(2)}) collective-permute-start(f32[1,16,128]{2,1,0:T(8,128)S(1)} %get-tuple-element.195), channel_id=1, source_target_pairs={{8,0},{16,8},{24,16},{32,24},{40,32},{48,40},{56,48},{64,56},{72,6... | collective-permute-start | bytes 24584 | tf_op jit(solution)/shard_map/ppermute | solution.py:49
  43.0 2.9 %fusion.2 = f32[3,8,16,128]{3,0,2,1:T(4,128)S(1)} fusion(f32[19,3,1,1]{0,1,3,2:T(4,128)} %constant.60, f32[19,8,16,128]{3,2,1,0:T(8,128)} %param.23), kind=kOutput, calls=%fused_computation.4 | convolution fusion | flops 11206656 | bytes 1442020 | tf_op jit(solution)/shard_map/ic,ixyz->cxyz/dot_general | solution.py:60
  51.4 1.9 collective-permute-done.6
  53.7 3.6 %collective-permute-start.8 = (f32[1,16,128]{2,1,0:T(8,128)S(1)}, f32[1,16,128]{2,1,0:T(8,128)S(1)}, u32[]{:S(2)}, u32[]{:S(2)}) collective-permute-start(f32[1,16,128]{2,1,0:T(8,128)S(1)} %get-tuple-element.190), channel_id=1, source_target_pairs={{8,0},{16,8},{24,16},{32,24},{40,32},{48,40},{56,48},{64,56},{72,6... | collective-permute-start | bytes 24584 | tf_op jit(solution)/shard_map/ppermute | solution.py:49
  57.4 1.9 collective-permute-start.9
  59.4 5.7 %collective-permute-done.9 = f32[1,16,128]{2,1,0:T(8,128)S(1)} collective-permute-done((f32[1,16,128]{2,1,0:T(8,128)S(1)}, f32[1,16,128]{2,1,0:T(8,128)S(1)}, u32[]{:S(2)}, u32[]{:S(2)}) %collective-permute-start.9) | collective-permute-done | bytes 8224 | tf_op jit(solution)/shard_map/ppermute | solution.py:47
  65.1 1.8 collective-permute-start.11
  70.1 1.9 collective-permute-start.12
  72.0 3.4 %collective-permute-start.13 = (f32[1,16,128]{2,1,0:T(8,128)S(1)}, f32[1,16,128]{2,1,0:T(8,128)S(1)}, u32[]{:S(2)}, u32[]{:S(2)}) collective-permute-start(f32[1,16,128]{2,1,0:T(8,128)S(1)} %get-tuple-element.183), channel_id=1, source_target_pairs={{0,8},{8,16},{16,24},{24,32},{32,40},{40,48},{48,56},{56,64},{64,7... | collective-permute-start | bytes 24584 | tf_op jit(solution)/shard_map/ppermute | solution.py:47
  75.5 4.3 %collective-permute-done.13 = f32[1,16,128]{2,1,0:T(8,128)S(1)} collective-permute-done((f32[1,16,128]{2,1,0:T(8,128)S(1)}, f32[1,16,128]{2,1,0:T(8,128)S(1)}, u32[]{:S(2)}, u32[]{:S(2)}) %collective-permute-start.13) | collective-permute-done | bytes 8224 | tf_op jit(solution)/shard_map/ppermute | solution.py:47
  81.0 2.4 collective-permute-start.14
  84.3 1.9 collective-permute-start.16
  86.2 3.4 %collective-permute-start.17 = (f32[1,16,128]{2,1,0:T(8,128)S(1)}, f32[1,16,128]{2,1,0:T(8,128)S(1)}, u32[]{:S(2)}, u32[]{:S(2)}) collective-permute-start(f32[1,16,128]{2,1,0:T(8,128)S(1)} %get-tuple-element.177), channel_id=1, source_target_pairs={{0,8},{8,16},{16,24},{24,32},{32,40},{40,48},{48,56},{56,64},{64,7... | collective-permute-start | bytes 24584 | tf_op jit(solution)/shard_map/ppermute | solution.py:47
  89.7 4.3 %collective-permute-done.17 = f32[1,16,128]{2,1,0:T(8,128)S(1)} collective-permute-done((f32[1,16,128]{2,1,0:T(8,128)S(1)}, f32[1,16,128]{2,1,0:T(8,128)S(1)}, u32[]{:S(2)}, u32[]{:S(2)}) %collective-permute-start.17) | collective-permute-done | bytes 8224 | tf_op jit(solution)/shard_map/ppermute | solution.py:47
  95.0 3.6 %collective-permute-start.18 = (f32[10,1,128]{2,1,0:T(1,128)S(1)}, f32[10,1,128]{2,1,0:T(1,128)S(1)}, u32[]{:S(2)}, u32[]{:S(2)}) collective-permute-start(f32[10,1,128]{2,1,0:T(1,128)S(1)} %get-tuple-element.125), channel_id=1, source_target_pairs={{1,0},{2,1},{3,2},{4,3},{5,4},{6,5},{7,6},{0,7},{9,8},{10,9},{11,1... | collective-permute-start | bytes 15368 | tf_op jit(solution)/shard_map/ppermute | solution.py:49
  99.7 1.9 collective-permute-start.20
  101.7 3.4 %collective-permute-start.21 = (f32[1,16,128]{2,1,0:T(8,128)S(1)}, f32[1,16,128]{2,1,0:T(8,128)S(1)}, u32[]{:S(2)}, u32[]{:S(2)}) collective-permute-start(f32[1,16,128]{2,1,0:T(8,128)S(1)} %get-tuple-element.171), channel_id=1, source_target_pairs={{0,8},{8,16},{16,24},{24,32},{32,40},{40,48},{48,56},{56,64},{64,7... | collective-permute-start | bytes 24584 | tf_op jit(solution)/shard_map/ppermute | solution.py:47
  105.2 4.2 %collective-permute-done.21 = f32[1,16,128]{2,1,0:T(8,128)S(1)} collective-permute-done((f32[1,16,128]{2,1,0:T(8,128)S(1)}, f32[1,16,128]{2,1,0:T(8,128)S(1)}, u32[]{:S(2)}, u32[]{:S(2)}) %collective-permute-start.21) | collective-permute-done | bytes 8224 | tf_op jit(solution)/shard_map/ppermute | solution.py:47
  109.4 4.6 %collective-permute-start.22 = (f32[10,1,128]{2,1,0:T(1,128)S(1)}, f32[10,1,128]{2,1,0:T(1,128)S(1)}, u32[]{:S(2)}, u32[]{:S(2)}) collective-permute-start(f32[10,1,128]{2,1,0:T(1,128)S(1)} %get-tuple-element.123), channel_id=1, source_target_pairs={{1,0},{2,1},{3,2},{4,3},{5,4},{6,5},{7,6},{0,7},{9,8},{10,9},{11,1... | collective-permute-start | bytes 15368 | tf_op jit(solution)/shard_map/ppermute | solution.py:49
  118.8 1.9 collective-permute-start.25
  120.7 3.4 %collective-permute-start.24 = (f32[24,1,16,128]{3,2,1,0:T(8,128)S(1)}, f32[24,1,16,128]{3,2,1,0:T(8,128)S(1)}, u32[]{:S(2)}, u32[]{:S(2)}) collective-permute-start(f32[24,1,16,128]{3,2,1,0:T(8,128)S(1)} %get-tuple-element.65), channel_id=1, source_target_pairs={{0,8},{8,16},{16,24},{24,32},{32,40},{40,48},{48,56},{56,64},{64,7... | collective-permute-start | bytes 589832 | tf_op jit(solution)/shard_map/ppermute | solution.py:47
  125.2 5.2 %collective-permute-done.24 = f32[24,1,16,128]{3,2,1,0:T(8,128)S(1)} collective-permute-done((f32[24,1,16,128]{3,2,1,0:T(8,128)S(1)}, f32[24,1,16,128]{3,2,1,0:T(8,128)S(1)}, u32[]{:S(2)}, u32[]{:S(2)}) %collective-permute-start.24) | collective-permute-done | bytes 196640 | tf_op jit(solution)/shard_map/ppermute | solution.py:47
  130.6 4.8 %collective-permute-start.27 = (f32[24,10,1,128]{3,2,1,0:T(1,128)S(1)}, f32[24,10,1,128]{3,2,1,0:T(1,128)S(1)}, u32[]{:S(2)}, u32[]{:S(2)}) collective-permute-start(f32[24,10,1,128]{3,2,1,0:T(1,128)S(1)} %get-tuple-element.53), channel_id=1, source_target_pairs={{1,0},{2,1},{3,2},{4,3},{5,4},{6,5},{7,6},{0,7},{9,8},{10,9},{11,1... | collective-permute-start | bytes 368648 | tf_op jit(solution)/shard_map/ppermute | solution.py:49
  138.8 1.9 collective-permute-start.28
  140.8 3.4 %collective-permute-start.29 = (f32[1,16,128]{2,1,0:T(8,128)S(1)}, f32[1,16,128]{2,1,0:T(8,128)S(1)}, u32[]{:S(2)}, u32[]{:S(2)}) collective-permute-start(f32[1,16,128]{2,1,0:T(8,128)S(1)} %get-tuple-element.159), channel_id=1, source_target_pairs={{0,8},{8,16},{16,24},{24,32},{32,40},{40,48},{48,56},{56,64},{64,7... | collective-permute-start | bytes 24584 | tf_op jit(solution)/shard_map/ppermute | solution.py:47
  148.5 3.6 %collective-permute-start.31 = (f32[10,1,128]{2,1,0:T(1,128)S(1)}, f32[10,1,128]{2,1,0:T(1,128)S(1)}, u32[]{:S(2)}, u32[]{:S(2)}) collective-permute-start(f32[10,1,128]{2,1,0:T(1,128)S(1)} %get-tuple-element.120), channel_id=1, source_target_pairs={{0,1},{1,2},{2,3},{3,4},{4,5},{5,6},{6,7},{7,0},{8,9},{9,10},{10,1... | collective-permute-start | bytes 15368 | tf_op jit(solution)/shard_map/ppermute | solution.py:47
  155.3 2.8 %collective-permute-start.32 = (f32[1,16,128]{2,1,0:T(8,128)S(1)}, f32[1,16,128]{2,1,0:T(8,128)S(1)}, u32[]{:S(2)}, u32[]{:S(2)}) collective-permute-start(f32[1,16,128]{2,1,0:T(8,128)S(1)} %get-tuple-element.154), channel_id=1, source_target_pairs={{8,0},{16,8},{24,16},{32,24},{40,32},{48,40},{56,48},{64,56},{72,6... | collective-permute-start | bytes 24584 | tf_op jit(solution)/shard_map/ppermute | solution.py:49
  158.0 2.5 collective-permute-start.33
  160.7 5.1 %collective-permute-done.33 = f32[1,16,128]{2,1,0:T(8,128)S(1)} collective-permute-done((f32[1,16,128]{2,1,0:T(8,128)S(1)}, f32[1,16,128]{2,1,0:T(8,128)S(1)}, u32[]{:S(2)}, u32[]{:S(2)}) %collective-permute-start.33) | collective-permute-done | bytes 8224 | tf_op jit(solution)/shard_map/ppermute | solution.py:47
  167.3 2.5 collective-permute-start.34
  170.7 1.9 collective-permute-start.36
  172.6 3.5 %collective-permute-start.37 = (f32[1,16,128]{2,1,0:T(8,128)S(1)}, f32[1,16,128]{2,1,0:T(8,128)S(1)}, u32[]{:S(2)}, u32[]{:S(2)}) collective-permute-start(f32[1,16,128]{2,1,0:T(8,128)S(1)} %get-tuple-element.147), channel_id=1, source_target_pairs={{0,8},{8,16},{16,24},{24,32},{32,40},{40,48},{48,56},{56,64},{64,7... | collective-permute-start | bytes 24584 | tf_op jit(solution)/shard_map/ppermute | solution.py:47
  176.2 4.1 %collective-permute-done.37 = f32[1,16,128]{2,1,0:T(8,128)S(1)} collective-permute-done((f32[1,16,128]{2,1,0:T(8,128)S(1)}, f32[1,16,128]{2,1,0:T(8,128)S(1)}, u32[]{:S(2)}, u32[]{:S(2)}) %collective-permute-start.37) | collective-permute-done | bytes 8224 | tf_op jit(solution)/shard_map/ppermute | solution.py:47
  181.3 3.7 %collective-permute-start.38 = (f32[10,1,128]{2,1,0:T(1,128)S(1)}, f32[10,1,128]{2,1,0:T(1,128)S(1)}, u32[]{:S(2)}, u32[]{:S(2)}) collective-permute-start(f32[10,1,128]{2,1,0:T(1,128)S(1)} %get-tuple-element.115), channel_id=1, source_target_pairs={{1,0},{2,1},{3,2},{4,3},{5,4},{6,5},{7,6},{0,7},{9,8},{10,9},{11,1... | collective-permute-start | bytes 15368 | tf_op jit(solution)/shard_map/ppermute | solution.py:49
  186.1 1.9 collective-permute-start.40
  188.0 3.4 %collective-permute-start.41 = (f32[1,16,128]{2,1,0:T(8,128)S(1)}, f32[1,16,128]{2,1,0:T(8,128)S(1)}, u32[]{:S(2)}, u32[]{:S(2)}) collective-permute-start(f32[1,16,128]{2,1,0:T(8,128)S(1)} %get-tuple-element.141), channel_id=1, source_target_pairs={{0,8},{8,16},{16,24},{24,32},{32,40},{40,48},{48,56},{56,64},{64,7... | collective-permute-start | bytes 24584 | tf_op jit(solution)/shard_map/ppermute | solution.py:47
  191.5 4.2 %collective-permute-done.41 = f32[1,16,128]{2,1,0:T(8,128)S(1)} collective-permute-done((f32[1,16,128]{2,1,0:T(8,128)S(1)}, f32[1,16,128]{2,1,0:T(8,128)S(1)}, u32[]{:S(2)}, u32[]{:S(2)}) %collective-permute-start.41) | collective-permute-done | bytes 8224 | tf_op jit(solution)/shard_map/ppermute | solution.py:47
  195.7 4.6 %collective-permute-start.42 = (f32[10,1,128]{2,1,0:T(1,128)S(1)}, f32[10,1,128]{2,1,0:T(1,128)S(1)}, u32[]{:S(2)}, u32[]{:S(2)}) collective-permute-start(f32[10,1,128]{2,1,0:T(1,128)S(1)} %get-tuple-element.113), channel_id=1, source_target_pairs={{1,0},{2,1},{3,2},{4,3},{5,4},{6,5},{7,6},{0,7},{9,8},{10,9},{11,1... | collective-permute-start | bytes 15368 | tf_op jit(solution)/shard_map/ppermute | solution.py:49
  205.1 1.9 collective-permute-start.45
  207.0 3.4 %collective-permute-start.44 = (f32[24,1,16,128]{3,2,1,0:T(8,128)S(1)}, f32[24,1,16,128]{3,2,1,0:T(8,128)S(1)}, u32[]{:S(2)}, u32[]{:S(2)}) collective-permute-start(f32[24,1,16,128]{3,2,1,0:T(8,128)S(1)} %get-tuple-element.62), channel_id=1, source_target_pairs={{0,8},{8,16},{16,24},{24,32},{32,40},{40,48},{48,56},{56,64},{64,7... | collective-permute-start | bytes 589832 | tf_op jit(solution)/shard_map/ppermute | solution.py:47
  211.5 5.3 %collective-permute-done.44 = f32[24,1,16,128]{3,2,1,0:T(8,128)S(1)} collective-permute-done((f32[24,1,16,128]{3,2,1,0:T(8,128)S(1)}, f32[24,1,16,128]{3,2,1,0:T(8,128)S(1)}, u32[]{:S(2)}, u32[]{:S(2)}) %collective-permute-start.44) | collective-permute-done | bytes 196640 | tf_op jit(solution)/shard_map/ppermute | solution.py:47
  216.9 1.8 collective-permute-start.46
  218.7 3.0 %collective-permute-start.47 = (f32[24,10,1,128]{3,2,1,0:T(1,128)S(1)}, f32[24,10,1,128]{3,2,1,0:T(1,128)S(1)}, u32[]{:S(2)}, u32[]{:S(2)}) collective-permute-start(f32[24,10,1,128]{3,2,1,0:T(1,128)S(1)} %get-tuple-element.50), channel_id=1, source_target_pairs={{1,0},{2,1},{3,2},{4,3},{5,4},{6,5},{7,6},{0,7},{9,8},{10,9},{11,1... | collective-permute-start | bytes 368648 | tf_op jit(solution)/shard_map/ppermute | solution.py:49
  241.3 14.8 %all-gather.2.cloned.1.call-done = f32[2,8,128,128]{3,2,1,0:T(8,128)} async-done(((f32[2,8,16,128]{3,2,1,0:T(8,128)}), f32[2,8,128,128]{3,2,1,0:T(8,128)}) %all-gather.2.cloned.1.call-update) | async-done | bytes 1048592 | tf_op jit(solution)/shard_map/all_gather | solution.py:194
  256.0 2.3 convolution_bitcast_fusion
  (265 shorter events, 66.8 us)
Async XLA Ops:
  7.2 248.9 %all-gather.2.cloned.1.call-start = ((), (), s32[]{:S(2)}) async-start(), calls=%async_computation | async-start | bytes 1179648 | tf_op jit(solution)/shard_map/all_gather | solution.py:194
  8.8 38.0 %collective-permute-start.1 = (f32[2,1,16,128]{3,2,1,0:T(8,128)S(1)}, f32[2,1,16,128]{3,2,1,0:T(8,128)S(1)}, u32[]{:S(2)}, u32[]{:S(2)}) collective-permute-start(f32[2,1,16,128]{3,2,1,0:T(8,128)S(1)} %get-tuple-element.84), channel_id=1, source_target_pairs={{8,0},{16,8},{24,16},{32,24},{40,32},{48,40},{56,48},{64,56},{72,6... | collective-permute-start | bytes 49160 | tf_op jit(solution)/shard_map/ppermute | solution.py:49
  26.8 20.0 %collective-permute-start = (f32[2,1,16,128]{3,2,1,0:T(8,128)S(1)}, f32[2,1,16,128]{3,2,1,0:T(8,128)S(1)}, u32[]{:S(2)}, u32[]{:S(2)}) collective-permute-start(f32[2,1,16,128]{3,2,1,0:T(8,128)S(1)} %get-tuple-element.83), channel_id=1, source_target_pairs={{0,8},{8,16},{16,24},{24,32},{32,40},{40,48},{48,56},{56,64},{64,7... | collective-permute-start | bytes 49160 | tf_op jit(solution)/shard_map/ppermute | solution.py:47
  29.5 16.7 %collective-permute-start.5 = (f32[1,16,128]{2,1,0:T(8,128)S(1)}, f32[1,16,128]{2,1,0:T(8,128)S(1)}, u32[]{:S(2)}, u32[]{:S(2)}) collective-permute-start(f32[1,16,128]{2,1,0:T(8,128)S(1)} %get-tuple-element.196), channel_id=1, source_target_pairs={{0,8},{8,16},{16,24},{24,32},{32,40},{40,48},{48,56},{56,64},{64,7... | collective-permute-start | bytes 24584 | tf_op jit(solution)/shard_map/ppermute | solution.py:47
  31.4 15.4 %collective-permute-start.4 = (f32[1,16,128]{2,1,0:T(8,128)S(1)}, f32[1,16,128]{2,1,0:T(8,128)S(1)}, u32[]{:S(2)}, u32[]{:S(2)}) collective-permute-start(f32[1,16,128]{2,1,0:T(8,128)S(1)} %get-tuple-element.195), channel_id=1, source_target_pairs={{8,0},{16,8},{24,16},{32,24},{40,32},{48,40},{56,48},{64,56},{72,6... | collective-permute-start | bytes 24584 | tf_op jit(solution)/shard_map/ppermute | solution.py:49
  46.8 4.0 %collective-permute-start.3 = (f32[2,10,1,128]{3,2,1,0:T(1,128)S(1)}, f32[2,10,1,128]{3,2,1,0:T(1,128)S(1)}, u32[]{:S(2)}, u32[]{:S(2)}) collective-permute-start(f32[2,10,1,128]{3,2,1,0:T(1,128)S(1)} %get-tuple-element.82), channel_id=1, source_target_pairs={{1,0},{2,1},{3,2},{4,3},{5,4},{6,5},{7,6},{0,7},{9,8},{10,9},{11,1... | collective-permute-start | bytes 30728 | tf_op jit(solution)/shard_map/ppermute | solution.py:49
  48.3 2.5 collective-permute-start.2
  49.5 1.9 collective-permute-start.7
  50.0 3.3 %collective-permute-start.6 = (f32[10,1,128]{2,1,0:T(1,128)S(1)}, f32[10,1,128]{2,1,0:T(1,128)S(1)}, u32[]{:S(2)}, u32[]{:S(2)}) collective-permute-start(f32[10,1,128]{2,1,0:T(1,128)S(1)} %get-tuple-element.131), channel_id=1, source_target_pairs={{1,0},{2,1},{3,2},{4,3},{5,4},{6,5},{7,6},{0,7},{9,8},{10,9},{11,1... | collective-permute-start | bytes 15368 | tf_op jit(solution)/shard_map/ppermute | solution.py:49
  53.7 5.7 %collective-permute-start.8 = (f32[1,16,128]{2,1,0:T(8,128)S(1)}, f32[1,16,128]{2,1,0:T(8,128)S(1)}, u32[]{:S(2)}, u32[]{:S(2)}) collective-permute-start(f32[1,16,128]{2,1,0:T(8,128)S(1)} %get-tuple-element.190), channel_id=1, source_target_pairs={{8,0},{16,8},{24,16},{32,24},{40,32},{48,40},{56,48},{64,56},{72,6... | collective-permute-start | bytes 24584 | tf_op jit(solution)/shard_map/ppermute | solution.py:49
  57.4 7.7 %collective-permute-start.9 = (f32[1,16,128]{2,1,0:T(8,128)S(1)}, f32[1,16,128]{2,1,0:T(8,128)S(1)}, u32[]{:S(2)}, u32[]{:S(2)}) collective-permute-start(f32[1,16,128]{2,1,0:T(8,128)S(1)} %get-tuple-element.189), channel_id=1, source_target_pairs={{0,8},{8,16},{16,24},{24,32},{32,40},{40,48},{48,56},{56,64},{64,7... | collective-permute-start | bytes 24584 | tf_op jit(solution)/shard_map/ppermute | solution.py:47
  65.1 3.7 %collective-permute-start.11 = (f32[10,1,128]{2,1,0:T(1,128)S(1)}, f32[10,1,128]{2,1,0:T(1,128)S(1)}, u32[]{:S(2)}, u32[]{:S(2)}) collective-permute-start(f32[10,1,128]{2,1,0:T(1,128)S(1)} %get-tuple-element.130), channel_id=1, source_target_pairs={{0,1},{1,2},{2,3},{3,4},{4,5},{5,6},{6,7},{7,0},{8,9},{9,10},{10,1... | collective-permute-start | bytes 15368 | tf_op jit(solution)/shard_map/ppermute | solution.py:47
  66.9 3.0 %collective-permute-start.10 = (f32[10,1,128]{2,1,0:T(1,128)S(1)}, f32[10,1,128]{2,1,0:T(1,128)S(1)}, u32[]{:S(2)}, u32[]{:S(2)}) collective-permute-start(f32[10,1,128]{2,1,0:T(1,128)S(1)} %get-tuple-element.129), channel_id=1, source_target_pairs={{1,0},{2,1},{3,2},{4,3},{5,4},{6,5},{7,6},{0,7},{9,8},{10,9},{11,1... | collective-permute-start | bytes 15368 | tf_op jit(solution)/shard_map/ppermute | solution.py:49
  70.1 5.4 %collective-permute-start.12 = (f32[1,16,128]{2,1,0:T(8,128)S(1)}, f32[1,16,128]{2,1,0:T(8,128)S(1)}, u32[]{:S(2)}, u32[]{:S(2)}) collective-permute-start(f32[1,16,128]{2,1,0:T(8,128)S(1)} %get-tuple-element.184), channel_id=1, source_target_pairs={{8,0},{16,8},{24,16},{32,24},{40,32},{48,40},{56,48},{64,56},{72,6... | collective-permute-start | bytes 24584 | tf_op jit(solution)/shard_map/ppermute | solution.py:49
  72.0 7.7 %collective-permute-start.13 = (f32[1,16,128]{2,1,0:T(8,128)S(1)}, f32[1,16,128]{2,1,0:T(8,128)S(1)}, u32[]{:S(2)}, u32[]{:S(2)}) collective-permute-start(f32[1,16,128]{2,1,0:T(8,128)S(1)} %get-tuple-element.183), channel_id=1, source_target_pairs={{0,8},{8,16},{16,24},{24,32},{32,40},{40,48},{48,56},{56,64},{64,7... | collective-permute-start | bytes 24584 | tf_op jit(solution)/shard_map/ppermute | solution.py:47
  79.8 4.2 %collective-permute-start.15 = (f32[10,1,128]{2,1,0:T(1,128)S(1)}, f32[10,1,128]{2,1,0:T(1,128)S(1)}, u32[]{:S(2)}, u32[]{:S(2)}) collective-permute-start(f32[10,1,128]{2,1,0:T(1,128)S(1)} %get-tuple-element.128), channel_id=1, source_target_pairs={{0,1},{1,2},{2,3},{3,4},{4,5},{5,6},{6,7},{7,0},{8,9},{9,10},{10,1... | collective-permute-start | bytes 15368 | tf_op jit(solution)/shard_map/ppermute | solution.py:47
  81.0 3.2 %collective-permute-start.14 = (f32[10,1,128]{2,1,0:T(1,128)S(1)}, f32[10,1,128]{2,1,0:T(1,128)S(1)}, u32[]{:S(2)}, u32[]{:S(2)}) collective-permute-start(f32[10,1,128]{2,1,0:T(1,128)S(1)} %get-tuple-element.127), channel_id=1, source_target_pairs={{1,0},{2,1},{3,2},{4,3},{5,4},{6,5},{7,6},{0,7},{9,8},{10,9},{11,1... | collective-permute-start | bytes 15368 | tf_op jit(solution)/shard_map/ppermute | solution.py:49
  84.3 5.4 %collective-permute-start.16 = (f32[1,16,128]{2,1,0:T(8,128)S(1)}, f32[1,16,128]{2,1,0:T(8,128)S(1)}, u32[]{:S(2)}, u32[]{:S(2)}) collective-permute-start(f32[1,16,128]{2,1,0:T(8,128)S(1)} %get-tuple-element.178), channel_id=1, source_target_pairs={{8,0},{16,8},{24,16},{32,24},{40,32},{48,40},{56,48},{64,56},{72,6... | collective-permute-start | bytes 24584 | tf_op jit(solution)/shard_map/ppermute | solution.py:49
  86.2 7.7 %collective-permute-start.17 = (f32[1,16,128]{2,1,0:T(8,128)S(1)}, f32[1,16,128]{2,1,0:T(8,128)S(1)}, u32[]{:S(2)}, u32[]{:S(2)}) collective-permute-start(f32[1,16,128]{2,1,0:T(8,128)S(1)} %get-tuple-element.177), channel_id=1, source_target_pairs={{0,8},{8,16},{16,24},{24,32},{32,40},{40,48},{48,56},{56,64},{64,7... | collective-permute-start | bytes 24584 | tf_op jit(solution)/shard_map/ppermute | solution.py:47
  94.0 5.3 %collective-permute-start.19 = (f32[10,1,128]{2,1,0:T(1,128)S(1)}, f32[10,1,128]{2,1,0:T(1,128)S(1)}, u32[]{:S(2)}, u32[]{:S(2)}) collective-permute-start(f32[10,1,128]{2,1,0:T(1,128)S(1)} %get-tuple-element.126), channel_id=1, source_target_pairs={{0,1},{1,2},{2,3},{3,4},{4,5},{5,6},{6,7},{7,0},{8,9},{9,10},{10,1... | collective-permute-start | bytes 15368 | tf_op jit(solution)/shard_map/ppermute | solution.py:47
  95.0 4.4 %collective-permute-start.18 = (f32[10,1,128]{2,1,0:T(1,128)S(1)}, f32[10,1,128]{2,1,0:T(1,128)S(1)}, u32[]{:S(2)}, u32[]{:S(2)}) collective-permute-start(f32[10,1,128]{2,1,0:T(1,128)S(1)} %get-tuple-element.125), channel_id=1, source_target_pairs={{1,0},{2,1},{3,2},{4,3},{5,4},{6,5},{7,6},{0,7},{9,8},{10,9},{11,1... | collective-permute-start | bytes 15368 | tf_op jit(solution)/shard_map/ppermute | solution.py:49
  99.7 5.4 %collective-permute-start.20 = (f32[1,16,128]{2,1,0:T(8,128)S(1)}, f32[1,16,128]{2,1,0:T(8,128)S(1)}, u32[]{:S(2)}, u32[]{:S(2)}) collective-permute-start(f32[1,16,128]{2,1,0:T(8,128)S(1)} %get-tuple-element.172), channel_id=1, source_target_pairs={{8,0},{16,8},{24,16},{32,24},{40,32},{48,40},{56,48},{64,56},{72,6... | collective-permute-start | bytes 24584 | tf_op jit(solution)/shard_map/ppermute | solution.py:49
  101.7 7.7 %collective-permute-start.21 = (f32[1,16,128]{2,1,0:T(8,128)S(1)}, f32[1,16,128]{2,1,0:T(8,128)S(1)}, u32[]{:S(2)}, u32[]{:S(2)}) collective-permute-start(f32[1,16,128]{2,1,0:T(8,128)S(1)} %get-tuple-element.171), channel_id=1, source_target_pairs={{0,8},{8,16},{16,24},{24,32},{32,40},{40,48},{48,56},{56,64},{64,7... | collective-permute-start | bytes 24584 | tf_op jit(solution)/shard_map/ppermute | solution.py:47
  109.4 5.4 %collective-permute-start.22 = (f32[10,1,128]{2,1,0:T(1,128)S(1)}, f32[10,1,128]{2,1,0:T(1,128)S(1)}, u32[]{:S(2)}, u32[]{:S(2)}) collective-permute-start(f32[10,1,128]{2,1,0:T(1,128)S(1)} %get-tuple-element.123), channel_id=1, source_target_pairs={{1,0},{2,1},{3,2},{4,3},{5,4},{6,5},{7,6},{0,7},{9,8},{10,9},{11,1... | collective-permute-start | bytes 15368 | tf_op jit(solution)/shard_map/ppermute | solution.py:49
  114.0 2.4 collective-permute-start.23
  118.8 6.4 %collective-permute-start.25 = (f32[24,1,16,128]{3,2,1,0:T(8,128)S(1)}, f32[24,1,16,128]{3,2,1,0:T(8,128)S(1)}, u32[]{:S(2)}, u32[]{:S(2)}) collective-permute-start(f32[24,1,16,128]{3,2,1,0:T(8,128)S(1)} %get-tuple-element.66), channel_id=1, source_target_pairs={{8,0},{16,8},{24,16},{32,24},{40,32},{48,40},{56,48},{64,56},{72,6... | collective-permute-start | bytes 589832 | tf_op jit(solution)/shard_map/ppermute | solution.py:49
  120.7 9.7 %collective-permute-start.24 = (f32[24,1,16,128]{3,2,1,0:T(8,128)S(1)}, f32[24,1,16,128]{3,2,1,0:T(8,128)S(1)}, u32[]{:S(2)}, u32[]{:S(2)}) collective-permute-start(f32[24,1,16,128]{3,2,1,0:T(8,128)S(1)} %get-tuple-element.65), channel_id=1, source_target_pairs={{0,8},{8,16},{16,24},{24,32},{32,40},{40,48},{48,56},{56,64},{64,7... | collective-permute-start | bytes 589832 | tf_op jit(solution)/shard_map/ppermute | solution.py:47
  130.6 6.8 %collective-permute-start.27 = (f32[24,10,1,128]{3,2,1,0:T(1,128)S(1)}, f32[24,10,1,128]{3,2,1,0:T(1,128)S(1)}, u32[]{:S(2)}, u32[]{:S(2)}) collective-permute-start(f32[24,10,1,128]{3,2,1,0:T(1,128)S(1)} %get-tuple-element.53), channel_id=1, source_target_pairs={{1,0},{2,1},{3,2},{4,3},{5,4},{6,5},{7,6},{0,7},{9,8},{10,9},{11,1... | collective-permute-start | bytes 368648 | tf_op jit(solution)/shard_map/ppermute | solution.py:49
  138.8 8.0 %collective-permute-start.28 = (f32[1,16,128]{2,1,0:T(8,128)S(1)}, f32[1,16,128]{2,1,0:T(8,128)S(1)}, u32[]{:S(2)}, u32[]{:S(2)}) collective-permute-start(f32[1,16,128]{2,1,0:T(8,128)S(1)} %get-tuple-element.160), channel_id=1, source_target_pairs={{8,0},{16,8},{24,16},{32,24},{40,32},{48,40},{56,48},{64,56},{72,6... | collective-permute-start | bytes 24584 | tf_op jit(solution)/shard_map/ppermute | solution.py:49
  140.8 7.7 %collective-permute-start.29 = (f32[1,16,128]{2,1,0:T(8,128)S(1)}, f32[1,16,128]{2,1,0:T(8,128)S(1)}, u32[]{:S(2)}, u32[]{:S(2)}) collective-permute-start(f32[1,16,128]{2,1,0:T(8,128)S(1)} %get-tuple-element.159), channel_id=1, source_target_pairs={{0,8},{8,16},{16,24},{24,32},{32,40},{40,48},{48,56},{56,64},{64,7... | collective-permute-start | bytes 24584 | tf_op jit(solution)/shard_map/ppermute | solution.py:47
  148.5 5.5 %collective-permute-start.31 = (f32[10,1,128]{2,1,0:T(1,128)S(1)}, f32[10,1,128]{2,1,0:T(1,128)S(1)}, u32[]{:S(2)}, u32[]{:S(2)}) collective-permute-start(f32[10,1,128]{2,1,0:T(1,128)S(1)} %get-tuple-element.120), channel_id=1, source_target_pairs={{0,1},{1,2},{2,3},{3,4},{4,5},{5,6},{6,7},{7,0},{8,9},{9,10},{10,1... | collective-permute-start | bytes 15368 | tf_op jit(solution)/shard_map/ppermute | solution.py:47
  152.1 3.0 %collective-permute-start.30 = (f32[10,1,128]{2,1,0:T(1,128)S(1)}, f32[10,1,128]{2,1,0:T(1,128)S(1)}, u32[]{:S(2)}, u32[]{:S(2)}) collective-permute-start(f32[10,1,128]{2,1,0:T(1,128)S(1)} %get-tuple-element.119), channel_id=1, source_target_pairs={{1,0},{2,1},{3,2},{4,3},{5,4},{6,5},{7,6},{0,7},{9,8},{10,9},{11,1... | collective-permute-start | bytes 15368 | tf_op jit(solution)/shard_map/ppermute | solution.py:49
  155.3 5.4 %collective-permute-start.32 = (f32[1,16,128]{2,1,0:T(8,128)S(1)}, f32[1,16,128]{2,1,0:T(8,128)S(1)}, u32[]{:S(2)}, u32[]{:S(2)}) collective-permute-start(f32[1,16,128]{2,1,0:T(8,128)S(1)} %get-tuple-element.154), channel_id=1, source_target_pairs={{8,0},{16,8},{24,16},{32,24},{40,32},{48,40},{56,48},{64,56},{72,6... | collective-permute-start | bytes 24584 | tf_op jit(solution)/shard_map/ppermute | solution.py:49
  158.0 7.7 %collective-permute-start.33 = (f32[1,16,128]{2,1,0:T(8,128)S(1)}, f32[1,16,128]{2,1,0:T(8,128)S(1)}, u32[]{:S(2)}, u32[]{:S(2)}) collective-permute-start(f32[1,16,128]{2,1,0:T(8,128)S(1)} %get-tuple-element.153), channel_id=1, source_target_pairs={{0,8},{8,16},{16,24},{24,32},{32,40},{40,48},{48,56},{56,64},{64,7... | collective-permute-start | bytes 24584 | tf_op jit(solution)/shard_map/ppermute | solution.py:47
  165.8 4.6 %collective-permute-start.35 = (f32[10,1,128]{2,1,0:T(1,128)S(1)}, f32[10,1,128]{2,1,0:T(1,128)S(1)}, u32[]{:S(2)}, u32[]{:S(2)}) collective-permute-start(f32[10,1,128]{2,1,0:T(1,128)S(1)} %get-tuple-element.118), channel_id=1, source_target_pairs={{0,1},{1,2},{2,3},{3,4},{4,5},{5,6},{6,7},{7,0},{8,9},{9,10},{10,1... | collective-permute-start | bytes 15368 | tf_op jit(solution)/shard_map/ppermute | solution.py:47
  167.3 3.3 %collective-permute-start.34 = (f32[10,1,128]{2,1,0:T(1,128)S(1)}, f32[10,1,128]{2,1,0:T(1,128)S(1)}, u32[]{:S(2)}, u32[]{:S(2)}) collective-permute-start(f32[10,1,128]{2,1,0:T(1,128)S(1)} %get-tuple-element.117), channel_id=1, source_target_pairs={{1,0},{2,1},{3,2},{4,3},{5,4},{6,5},{7,6},{0,7},{9,8},{10,9},{11,1... | collective-permute-start | bytes 15368 | tf_op jit(solution)/shard_map/ppermute | solution.py:49
  170.7 5.6 %collective-permute-start.36 = (f32[1,16,128]{2,1,0:T(8,128)S(1)}, f32[1,16,128]{2,1,0:T(8,128)S(1)}, u32[]{:S(2)}, u32[]{:S(2)}) collective-permute-start(f32[1,16,128]{2,1,0:T(8,128)S(1)} %get-tuple-element.148), channel_id=1, source_target_pairs={{8,0},{16,8},{24,16},{32,24},{40,32},{48,40},{56,48},{64,56},{72,6... | collective-permute-start | bytes 24584 | tf_op jit(solution)/shard_map/ppermute | solution.py:49
  172.6 7.7 %collective-permute-start.37 = (f32[1,16,128]{2,1,0:T(8,128)S(1)}, f32[1,16,128]{2,1,0:T(8,128)S(1)}, u32[]{:S(2)}, u32[]{:S(2)}) collective-permute-start(f32[1,16,128]{2,1,0:T(8,128)S(1)} %get-tuple-element.147), channel_id=1, source_target_pairs={{0,8},{8,16},{16,24},{24,32},{32,40},{40,48},{48,56},{56,64},{64,7... | collective-permute-start | bytes 24584 | tf_op jit(solution)/shard_map/ppermute | solution.py:47
  180.3 5.3 %collective-permute-start.39 = (f32[10,1,128]{2,1,0:T(1,128)S(1)}, f32[10,1,128]{2,1,0:T(1,128)S(1)}, u32[]{:S(2)}, u32[]{:S(2)}) collective-permute-start(f32[10,1,128]{2,1,0:T(1,128)S(1)} %get-tuple-element.116), channel_id=1, source_target_pairs={{0,1},{1,2},{2,3},{3,4},{4,5},{5,6},{6,7},{7,0},{8,9},{9,10},{10,1... | collective-permute-start | bytes 15368 | tf_op jit(solution)/shard_map/ppermute | solution.py:47
  181.3 4.5 %collective-permute-start.38 = (f32[10,1,128]{2,1,0:T(1,128)S(1)}, f32[10,1,128]{2,1,0:T(1,128)S(1)}, u32[]{:S(2)}, u32[]{:S(2)}) collective-permute-start(f32[10,1,128]{2,1,0:T(1,128)S(1)} %get-tuple-element.115), channel_id=1, source_target_pairs={{1,0},{2,1},{3,2},{4,3},{5,4},{6,5},{7,6},{0,7},{9,8},{10,9},{11,1... | collective-permute-start | bytes 15368 | tf_op jit(solution)/shard_map/ppermute | solution.py:49
  186.1 5.4 %collective-permute-start.40 = (f32[1,16,128]{2,1,0:T(8,128)S(1)}, f32[1,16,128]{2,1,0:T(8,128)S(1)}, u32[]{:S(2)}, u32[]{:S(2)}) collective-permute-start(f32[1,16,128]{2,1,0:T(8,128)S(1)} %get-tuple-element.142), channel_id=1, source_target_pairs={{8,0},{16,8},{24,16},{32,24},{40,32},{48,40},{56,48},{64,56},{72,6... | collective-permute-start | bytes 24584 | tf_op jit(solution)/shard_map/ppermute | solution.py:49
  188.0 7.7 %collective-permute-start.41 = (f32[1,16,128]{2,1,0:T(8,128)S(1)}, f32[1,16,128]{2,1,0:T(8,128)S(1)}, u32[]{:S(2)}, u32[]{:S(2)}) collective-permute-start(f32[1,16,128]{2,1,0:T(8,128)S(1)} %get-tuple-element.141), channel_id=1, source_target_pairs={{0,8},{8,16},{16,24},{24,32},{32,40},{40,48},{48,56},{56,64},{64,7... | collective-permute-start | bytes 24584 | tf_op jit(solution)/shard_map/ppermute | solution.py:47
  195.7 5.4 %collective-permute-start.42 = (f32[10,1,128]{2,1,0:T(1,128)S(1)}, f32[10,1,128]{2,1,0:T(1,128)S(1)}, u32[]{:S(2)}, u32[]{:S(2)}) collective-permute-start(f32[10,1,128]{2,1,0:T(1,128)S(1)} %get-tuple-element.113), channel_id=1, source_target_pairs={{1,0},{2,1},{3,2},{4,3},{5,4},{6,5},{7,6},{0,7},{9,8},{10,9},{11,1... | collective-permute-start | bytes 15368 | tf_op jit(solution)/shard_map/ppermute | solution.py:49
  200.4 2.4 collective-permute-start.43
  205.1 6.4 %collective-permute-start.45 = (f32[24,1,16,128]{3,2,1,0:T(8,128)S(1)}, f32[24,1,16,128]{3,2,1,0:T(8,128)S(1)}, u32[]{:S(2)}, u32[]{:S(2)}) collective-permute-start(f32[24,1,16,128]{3,2,1,0:T(8,128)S(1)} %get-tuple-element.61), channel_id=1, source_target_pairs={{8,0},{16,8},{24,16},{32,24},{40,32},{48,40},{56,48},{64,56},{72,6... | collective-permute-start | bytes 589832 | tf_op jit(solution)/shard_map/ppermute | solution.py:49
  207.0 9.7 %collective-permute-start.44 = (f32[24,1,16,128]{3,2,1,0:T(8,128)S(1)}, f32[24,1,16,128]{3,2,1,0:T(8,128)S(1)}, u32[]{:S(2)}, u32[]{:S(2)}) collective-permute-start(f32[24,1,16,128]{3,2,1,0:T(8,128)S(1)} %get-tuple-element.62), channel_id=1, source_target_pairs={{0,8},{8,16},{16,24},{24,32},{32,40},{40,48},{48,56},{56,64},{64,7... | collective-permute-start | bytes 589832 | tf_op jit(solution)/shard_map/ppermute | solution.py:47
  216.9 6.3 %collective-permute-start.46 = (f32[24,10,1,128]{3,2,1,0:T(1,128)S(1)}, f32[24,10,1,128]{3,2,1,0:T(1,128)S(1)}, u32[]{:S(2)}, u32[]{:S(2)}) collective-permute-start(f32[24,10,1,128]{3,2,1,0:T(1,128)S(1)} %get-tuple-element.51), channel_id=1, source_target_pairs={{0,1},{1,2},{2,3},{3,4},{4,5},{5,6},{6,7},{7,0},{8,9},{9,10},{10,1... | collective-permute-start | bytes 368648 | tf_op jit(solution)/shard_map/ppermute | solution.py:47
  218.7 4.3 %collective-permute-start.47 = (f32[24,10,1,128]{3,2,1,0:T(1,128)S(1)}, f32[24,10,1,128]{3,2,1,0:T(1,128)S(1)}, u32[]{:S(2)}, u32[]{:S(2)}) collective-permute-start(f32[24,10,1,128]{3,2,1,0:T(1,128)S(1)} %get-tuple-element.50), channel_id=1, source_target_pairs={{1,0},{2,1},{3,2},{4,3},{5,4},{6,5},{7,6},{0,7},{9,8},{10,9},{11,1... | collective-permute-start | bytes 368648 | tf_op jit(solution)/shard_map/ppermute | solution.py:49
  (21 other events, 106.4 us)
Sparse Core Ops, SparseCore 0:
  231.1 24.8 all-gather.1
where the time goes:
time: 267 us; the launch traced here: 265 us
  starting transfers between devices  129 us (48%)
  waiting for transfers between devices  76.9 us (29%)
  other arithmetic  19.7 us (7%)
  between operations  15.9 us (6%)
  local copies, waits for them, and re-layouts  14.4 us (5%)
  matrix products  9.81 us (4%)
    ppermute x24, starting transfers between devices, extended(): lax.ppermute(head, axis, [((i + 1) % count, i) for i in range(count)])  79.7 us
    ppermute x24, waiting for transfers between devices, extended(): lax.ppermute(tail, axis, [(i, (i + 1) % count) for i in range(count)])  51.6 us
    ppermute x24, starting transfers between devices, extended(): lax.ppermute(tail, axis, [(i, (i + 1) % count) for i in range(count)])  48.8 us
    all_gather x1, waiting for transfers between devices, body(): piece = lax.all_gather(conc, 'gy', axis=2, tiled=True)  14.8 us
    ppermute x24, waiting for transfers between devices, extended(): lax.ppermute(head, axis, [((i + 1) % count, i) for i in range(count)])  10.5 us
    unnamed x15, other arithmetic  9.93 us
    slice x20, local copies, waits for them, and re-layouts, body(): incoming = jnp.roll(rows[index], step_z, 2)  6.8 us
  transfers between devices with their start and end apart: 49, of which 33 were waited for; matrix products, arithmetic and copies ran while one was open for 9% of the time, Pallas kernels for 0%

commit v1 on v0

v1 whole, which is shorter than its diff:
```python
import jax
import jax.numpy as jnp
from jax import lax
from jax.experimental import pallas as pl
from jax.experimental.pallas import tpu as pltpu
from jax.sharding import PartitionSpec as P

STEPS = 2
SWEEPS = 4
VEL = (
    (0, 0, 0), (1, 0, 0), (-1, 0, 0), (0, 1, 0), (0, -1, 0), (0, 0, 1), (0, 0, -1),
    (1, 1, 0), (-1, -1, 0), (1, -1, 0), (-1, 1, 0), (1, 0, 1), (-1, 0, -1), (1, 0, -1),
    (-1, 0, 1), (0, 1, 1), (0, -1, -1), (0, 1, -1), (0, -1, 1),
)
WEIGHT = (1.0 / 3.0,) + (1.0 / 18.0,) * 6 + (1.0 / 36.0,) * 12
OPP = (0, 2, 1, 4, 3, 6, 5, 8, 7, 10, 9, 12, 11, 14, 13, 16, 15, 18, 17)
TAU = 0.8
COUPLING = 0.05
DRIVE = 0.001
DIFF = (0.1, 0.15)
VALENCE = (1.0, -1.0)

CX, CY, NZ = 8, 16, 128
EX, EY = 20, 32
F32 = jnp.float32

X_IN_LO = tuple(i for i in range(19) if VEL[i][0] == 1)
X_IN_HI = tuple(i for i in range(19) if VEL[i][0] == -1)
Y_IN_LO = tuple(i for i in range(19) if VEL[i][1] == 1)
Y_IN_HI = tuple(i for i in range(19) if VEL[i][1] == -1)
LO_LO, HI_LO = VEL.index((1, 1, 0)), VEL.index((-1, 1, 0))
LO_HI, HI_HI = VEL.index((1, -1, 0)), VEL.index((-1, -1, 0))


def shape(*dims):
    return jax.ShapeDtypeStruct(dims, F32)


def turn(v, by, axis):
    return pltpu.roll(v, by % v.shape[axis], axis)


class Plan:
    def __init__(self, first):
        self.first = first
        self.x_perm = 6 if first else None
        at = 12 if first else 6
        self.x_charge = at
        self.x_conc = at + 5
        at += 7
        if first:
            self.x_fluid = at
            at += 1
        self.x_pop = at
        self.x_dm = at + 5
        self.x_planes = at + 9
        self.y_perm = 8 if first else None
        at = 16 if first else 8
        self.y_charge = at
        self.y_misc = at + 8
        self.y_rows = at + 24
        self.c_charge = 12 if first else 6
        self.c_misc = self.c_charge + 5
        self.c_tiles = self.c_charge + 6


ONE, TWO = Plan(True), Plan(False)


def pack_x(plan, out, low, phi, charge, conc, pop, dm, perm=None, fluid=None):
    deep = slice(0, 6) if low else slice(2, 8)
    out[0:6] = phi[deep]
    if plan.first:
        out[6:12] = perm[deep]
        out[plan.x_fluid] = fluid[0 if low else 7]
    out[plan.x_charge : plan.x_charge + 5] = charge[0:5] if low else charge[3:8]
    edge = 0 if low else 7
    out[plan.x_conc] = conc[0, edge]
    out[plan.x_conc + 1] = conc[1, edge]
    for k, i in enumerate(X_IN_HI if low else X_IN_LO):
        out[plan.x_pop + k] = pop[i, edge]
    for k in range(4):
        out[plan.x_dm + k] = dm[k, edge]


def pack_y(plan, out, low, phi, charge, conc, pop, dm, perm=None, fluid=None):
    tile = slice(0, 8) if low else slice(8, 16)
    row = slice(0, 1) if low else slice(15, 16)
    out[:, 0:8] = phi[:, tile]
    if plan.first:
        out[:, 8:16] = perm[:, tile]
    out[:, plan.y_charge : plan.y_charge + 8] = charge[:, tile]
    rows = [conc[0, :, row], conc[1, :, row]]
    rows.append(fluid[:, row] if plan.first else conc[0, :, row])
    rows += [pop[i, :, row] for i in (Y_IN_HI if low else Y_IN_LO)]
    rows += [dm[k, :, row] for k in range(4)]
    for k, values in enumerate(rows):
        out[:, plan.y_misc + k : plan.y_misc + k + 1] = values


def moments(load):
    dens = load(0)
    mom = [None, None, None]
    for i in range(1, 19):
        v = load(i)
        dens = dens + v
        for c in range(3):
            if VEL[i][c]:
                t = v if VEL[i][c] > 0 else -v
                mom[c] = t if mom[c] is None else mom[c] + t
    return [dens] + mom


def first_kernel(pop, conc, phi, perm, mask, x_hi, x_lo, y_hi, y_lo, dm, charge, fluid):
    charge[...] = conc[0] - conc[1]
    fluid[...] = mask[...].astype(F32)

    def plane(x, _):
        for k, v in enumerate(moments(lambda i: pop[i, x])):
            dm[k, x] = v
        return 0

    lax.fori_loop(0, CX, plane, 0)
    for low, xo, yo in ((False, x_hi, y_hi), (True, x_lo, y_lo)):
        pack_x(ONE, xo, low, phi, charge, conc, pop, dm, perm, fluid)
        pack_y(ONE, yo, low, phi, charge, conc, pop, dm, perm, fluid)


def corner_kernel(plan, xl, xh, c_hi, c_lo):
    for out, tile, row, picks in (
        (c_hi, slice(8, 16), slice(15, 16), (LO_LO, HI_LO)),
        (c_lo, slice(0, 8), slice(0, 1), (LO_HI, HI_HI)),
    ):
        for side, x, names in ((0, xl, X_IN_LO), (1, xh, X_IN_HI)):
            out[side, 0 : plan.c_misc] = x[0 : plan.c_misc, tile]
            pop_at = plan.x_pop + names.index(picks[side])
            rows = [x[plan.x_fluid if plan.first else pop_at, row], x[pop_at, row]]
            rows += [x[plan.x_dm + k, row] for k in range(4)]
            for k, v in enumerate(rows):
                out[side, plan.c_misc, k : k + 1] = v


def lay(ext, own, xl, xh, yl, yh, cl, ch, lo, depth):
    a = 6 - depth
    ext[6:14, 8:24] = own
    ext[a:6, 8:24] = xl
    ext[14 : 14 + depth, 8:24] = xh
    ext[6:14, 0:8] = yl
    ext[6:14, 24:32] = yh
    for part, rows in ((cl, slice(0, 8)), (ch, slice(24, 32))):
        ext[a:6, rows] = part[0, lo : lo + depth]
        ext[14 : 14 + depth, rows] = part[1, lo : lo + depth]


def step(plan, own, msgs, state, work, outs, next_msgs):
    phi, conc, pop, dm, charge_own = own
    xl, xh, yl, yh, cl, ch = msgs
    coef, inv, fl = state
    pa, pb, ce, dn, mm, cc, ypl, yph, vel, lv = work
    pop_out, phi_out, conc_out = outs
    lay(pa, phi[...], xl[0:6], xh[0:6], yl[:, 0:8], yh[:, 0:8], cl, ch, 0, 6)
    q, w = plan.x_charge, plan.y_charge
    lay(ce, charge_own, xl[q : q + 5], xh[q : q + 5], yl[:, w : w + 8], yh[:, w : w + 8],
        cl, ch, plan.c_charge, 5)
    ym = plan.y_misc
    for s in range(2):
        cc[s, 1:9, 8:24] = conc[s]
        cc[s, 0, 8:24] = xl[plan.x_conc + s]
        cc[s, 9, 8:24] = xh[plan.x_conc + s]
        cc[s, 1:9, 7:8] = yl[:, ym + s : ym + s + 1]
        cc[s, 1:9, 24:25] = yh[:, ym + s : ym + s + 1]
    for k, ext in enumerate((dn, mm.at[0], mm.at[1], mm.at[2])):
        ext[1:9, 8:24] = dm[k]
        ext[0, 8:24] = xl[plan.x_dm + k]
        ext[9, 8:24] = xh[plan.x_dm + k]
        for y, c, r in ((yl, cl, 7), (yh, ch, 24)):
            ext[1:9, r : r + 1] = y[:, ym + 8 + k : ym + 9 + k]
            for side, p in ((0, 0), (1, 9)):
                ext[p, r : r + 1] = c[side, plan.c_misc, 2 + k : 3 + k]
    for k in range(5):
        ypl[k, :, 7:8] = yl[:, ym + 3 + k : ym + 4 + k]
        yph[k, :, 0:1] = yh[:, ym + 3 + k : ym + 4 + k]

    src, dst = pa, pb
    for sweep in range(SWEEPS):

        def relax(x, _, src=src, dst=dst):
            mid = src[x]
            acc = ce[x] * inv[x]
            acc += coef[0, x] * src[x - 1] + coef[1, x] * src[x + 1]
            acc += coef[2, x] * turn(mid, 1, 0) + coef[3, x] * turn(mid, -1, 0)
            acc += coef[4, x] * turn(mid, 1, 1) + coef[5, x] * turn(mid, -1, 1)
            dst[x] = acc
            return 0

        lax.fori_loop(1 + sweep, 19 - sweep, relax, 0, unroll=2)
        src, dst = dst, src
    fin = src
    phi_out[...] = fin[6:14, 8:24]

    bad = float("nan")

    def shared(p):
        mid = fin[p + 5]
        grad = [
            -0.5 * (fin[p + 6] - fin[p + 4]),
            -0.5 * (turn(mid, -1, 0) - turn(mid, 1, 0)),
            -0.5 * (turn(mid, -1, 1) - turn(mid, 1, 1)),
        ]
        f = fl[p]
        scale = COUPLING * ce[p + 5]
        force = [f * (scale * g + d) if d else f * (scale * g) for g, d in zip(grad, (DRIVE, 0, 0))]
        dens = dn[p]
        over = 1.0 / dens
        mom = [mm[c, p] for c in range(3)]
        for c in range(3):
            vel[c, p] = f * (mom[c] + 0.5 * force[c]) * over
        sh = [(mom[c] + TAU * force[c]) * over for c in range(3)]
        base = 1.0 - 1.5 * (sh[0] * sh[0] + sh[1] * sh[1] + sh[2] * sh[2])
        return f != 0.0, dens * (1.0 / TAU), sh, base

    def relaxed_of(i, pop_i, part, rows):
        _, dens, sh, base = part
        pr = None
        for c in range(3):
            if VEL[i][c]:
                t = sh[c][rows] if VEL[i][c] > 0 else -sh[c][rows]
                pr = t if pr is None else pr + t
        poly = base[rows]
        if pr is not None:
            poly = poly + pr * (3.0 + 4.5 * pr)
        return (1.0 - 1.0 / TAU) * pop_i + (WEIGHT[i] * dens[rows]) * poly

    lo_t, mid_t, hi_t = slice(0, 8), slice(8, 24), slice(24, 32)

    def emit(i, p, pop_i, part, rows):
        value = relaxed_of(i, pop_i, part, rows)
        lv[i, p, rows] = jnp.where(part[0][rows], value, bad)
        return value

    def collide(p, _):
        part = shared(p)
        is_fluid = part[0][mid_t]
        x = p - 1
        for i in range(19):
            if i > OPP[i]:
                continue
            j = OPP[i]
            pi = pop[i, x]
            ri = relaxed_of(i, pi, part, mid_t)
            if i == j:
                pop_out[i, x] = jnp.where(is_fluid, ri, pi)
                continue
            pj = pop[j, x]
            rj = relaxed_of(j, pj, part, mid_t)
            lv[i, p, mid_t] = jnp.where(is_fluid, ri, bad)
            lv[j, p, mid_t] = jnp.where(is_fluid, rj, bad)
            pop_out[i, x] = jnp.where(is_fluid, rj, pi)
            pop_out[j, x] = jnp.where(is_fluid, ri, pj)
        for k, i in enumerate(Y_IN_LO):
            emit(i, p, ypl[k, x], part, lo_t)
        for k, i in enumerate(Y_IN_HI):
            emit(i, p, yph[k, x], part, hi_t)
        return 0

    lax.fori_loop(1, 9, collide, 0)
    for p, side, x, names, low_pop, high_pop in (
        (0, 0, xl, X_IN_LO, LO_LO, LO_HI),
        (9, 1, xh, X_IN_HI, HI_LO, HI_HI),
    ):
        part = shared(p)
        for k, i in enumerate(names):
            emit(i, p, x[plan.x_pop + k], part, mid_t)
        for c, r, i in ((cl, 7, low_pop), (ch, 24, high_pop)):
            one = [part[0][r : r + 1], part[1][r : r + 1], [s[r : r + 1] for s in part[2]], part[3][r : r + 1]]
            value = relaxed_of(i, c[side, plan.c_misc, 1:2], one, slice(None))
            lv[i, p, r : r + 1] = jnp.where(one[0], value, bad)

    def flux(s, ca, cb, pot_a, pot_b, ua, ub, wall):
        total = ca + cb
        speed = 0.25 * (ua + ub) - (0.5 * DIFF[s] * VALENCE[s]) * (pot_b - pot_a)
        return wall * (total * speed - DIFF[s] * (cb - ca))

    def x_face(s, p):
        wall = fl[p, mid_t] * fl[p + 1, mid_t]
        return flux(s, cc[s, p, mid_t], cc[s, p + 1, mid_t], fin[p + 5, mid_t], fin[p + 6, mid_t],
                    vel[0, p, mid_t], vel[0, p + 1, mid_t], wall)

    def ions(p, before):
        after = []
        f, pot, vy = fl[p], fin[p + 5], vel[1, p]
        for s in range(2):
            face = x_face(s, p)
            total = face - before[s]
            after.append(face)
            c = cc[s, p]
            face = flux(s, c, turn(c, -1, 0), pot, turn(pot, -1, 0), vy, turn(vy, -1, 0), f * turn(f, -1, 0))
            total = total + (face - turn(face, 1, 0))[mid_t]
            fm, cm, pm, vz = f[mid_t], c[mid_t], pot[mid_t], vel[2, p, mid_t]
            face = flux(s, cm, turn(cm, -1, 1), pm, turn(pm, -1, 1), vz, turn(vz, -1, 1), fm * turn(fm, -1, 1))
            total = total + face - turn(face, 1, 1)
            conc_out[s, p - 1] = cm - total
        return tuple(after)

    lax.fori_loop(1, 9, ions, (x_face(0, 0), x_face(1, 0)))

    def stream(x, _):
        f = fl[x + 1, mid_t] != 0.0
        for i in range(1, 19):
            ex, ey, ez = VEL[i]
            came = lv[i, x + 1 - ex, 8 - ey : 24 - ey]
            if ez:
                came = turn(came, ez, 1)
            pop_out[i, x] = jnp.where(f & (came == came), came, pop_out[i, x])
        if next_msgs is not None:
            for k, v in enumerate(moments(lambda i: pop_out[i, x])):
                next_msgs[4][k, x] = v
        return 0

    lax.fori_loop(0, CX, stream, 0)
    if next_msgs is not None:
        x_hi, x_lo, y_hi, y_lo, dm_out, charge_out = next_msgs
        charge_out[...] = conc_out[0] - conc_out[1]
        for low, xo, yo in ((False, x_hi, y_hi), (True, x_lo, y_lo)):
            pack_x(TWO, xo, low, phi_out, charge_out, conc_out, pop_out, dm_out)
            pack_y(TWO, yo, low, phi_out, charge_out, conc_out, pop_out, dm_out)


def step_one_kernel(pop, conc, phi, perm, dm, fluid, xl, xh, yl, yh, cl, ch,
                    pop_out, phi_out, conc_out, x_hi, x_lo, y_hi, y_lo, dm_out, coef, inv, fl,
                    pe, charge_out, *work):
    lay(pe, perm[...], xl[6:12], xh[6:12], yl[:, 8:16], yh[:, 8:16], cl, ch, 6, 6)

    def coefs(x, _):
        mid = pe[x]
        faces = [0.5 * (mid + other) for other in (
            pe[x - 1], pe[x + 1], turn(mid, 1, 0), turn(mid, -1, 0), turn(mid, 1, 1), turn(mid, -1, 1))]
        over = 1.0 / (faces[0] + faces[1] + faces[2] + faces[3] + faces[4] + faces[5])
        inv[x] = over
        for k in range(6):
            coef[k, x] = faces[k] * over
        return 0

    lax.fori_loop(1, 19, coefs, 0)
    fl[1:9, 8:24] = fluid[...]
    fl[0, 8:24] = xl[ONE.x_fluid]
    fl[9, 8:24] = xh[ONE.x_fluid]
    for y, c, r in ((yl, cl, 7), (yh, ch, 24)):
        fl[1:9, r : r + 1] = y[:, ONE.y_misc + 2 : ONE.y_misc + 3]
        for side, p in ((0, 0), (1, 9)):
            fl[p, r : r + 1] = c[side, ONE.c_misc, 0:1]
    step(ONE, (phi, conc, pop, dm, conc[0] - conc[1]), (xl, xh, yl, yh, cl, ch), (coef, inv, fl), work,
         (pop_out, phi_out, conc_out), (x_hi, x_lo, y_hi, y_lo, dm_out, charge_out))


def step_two_kernel(pop, conc, phi, dm, coef, inv, fl, xl, xh, yl, yh, cl, ch,
                    pop_out, phi_out, conc_out, *work):
    step(TWO, (phi, conc, pop, dm, conc[0] - conc[1]), (xl, xh, yl, yh, cl, ch), (coef, inv, fl), work,
         (pop_out, phi_out, conc_out), None)


def call(kernel, outs, args, scratch=()):
    return pl.pallas_call(
        kernel,
        out_shape=outs,
        in_specs=[pl.BlockSpec(memory_space=pltpu.VMEM)] * len(args),
        out_specs=[pl.BlockSpec(memory_space=pltpu.VMEM)] * len(outs),
        scratch_shapes=[pltpu.VMEM(s, F32) for s in scratch],
        compiler_params=pltpu.CompilerParams(vmem_limit_bytes=48 * 1024 * 1024),
    )(*args)


WORK = (
    (EX, EY, NZ), (EX, EY, NZ), (EX, EY, NZ),
    (10, EY, NZ), (3, 10, EY, NZ), (2, 10, EY, NZ),
    (5, CX, 8, NZ), (5, CX, 8, NZ),
    (3, 10, EY, NZ), (19, 10, EY, NZ),
)


def shift(values, axis, by):
    n = lax.axis_size(axis)
    return lax.ppermute(values, axis, [(i, (i + by) % n) for i in range(n)])


def exchange(plan, x_hi, x_lo, y_hi, y_lo):
    yl, yh = shift(y_hi, "gy", 1), shift(y_lo, "gy", -1)
    xl, xh = shift(x_hi, "gx", 1), shift(x_lo, "gx", -1)
    tiles = shape(2, plan.c_tiles, 8, NZ)
    c_hi, c_lo = call(lambda *r: corner_kernel(plan, *r), (tiles, tiles), (xl, xh))
    cl, ch = shift(c_hi, "gy", 1), shift(c_lo, "gy", -1)
    return xl, xh, yl, yh, cl, ch


def messages(plan):
    x, y = shape(plan.x_planes, CY, NZ), shape(CX, plan.y_rows, NZ)
    return (x, x, y, y)


def migrate(conc, owners):
    row = lax.all_gather(owners.reshape(1), "gy", axis=0, tiled=True)
    me = lax.axis_index("gy")
    mate = lax.ppermute(conc, "gy", [(i, i ^ 1) for i in range(8)])
    odd = (me % 2) == 1
    even_block = jnp.where(odd, mate, conc)
    odd_block = jnp.where(odd, conc, mate)

    def block_for(dest):
        return jnp.where(row[dest] % 2 == 1, odd_block, even_block)

    result = block_for(me)
    distance = ((me // 2) - (row[me] // 2)) % 4
    for d in (1, 2, 3):
        got = shift(block_for((me + 2 * d) % 8), "gy", 2 * d)
        result = jnp.where(distance == d, got, result)
    return result


def body(populations, concentration, potential, permittivity, fluid_mask, owners):
    block = shape(CX, CY, NZ)
    pops, ions, four = shape(19, CX, CY, NZ), shape(2, CX, CY, NZ), shape(4, CX, CY, NZ)
    *sent, dm, _, fluid = call(
        first_kernel, messages(ONE) + (four, block, block),
        (populations, concentration, potential, permittivity, fluid_mask))
    got = exchange(ONE, *sent)
    pop, phi, conc, *rest = call(
        step_one_kernel,
        (pops, block, ions) + messages(TWO) + (four, shape(6, EX, EY, NZ), shape(EX, EY, NZ), shape(10, EY, NZ)),
        (populations, concentration, potential, permittivity, dm, fluid) + got,
        ((EX, EY, NZ), (CX, CY, NZ)) + WORK)
    sent, (dm, coef, inv, fl) = rest[:4], rest[4:]
    got = exchange(TWO, *sent)
    pop, phi, conc = call(
        step_two_kernel, (pops, block, ions), (pop, conc, phi, dm, coef, inv, fl) + got, WORK)
    return (pop, phi, migrate(conc, owners))


def solution(mesh):
    in_specs = (
        P(None, "gx", "gy", None),
        P(None, "gx", "gy", None),
        P("gx", "gy", None),
        P("gx", "gy", None),
        P("gx", "gy", None),
        P("gx", "gy"),
    )
    out_specs = (P(None, "gx", "gy", None), P("gx", "gy", None), P(None, "gx", "gy", None))
    return jax.shard_map(body, mesh=mesh, in_specs=in_specs, out_specs=out_specs, check_vma=False)
```

time: 267 us -> 108 us (0.40)
  starting transfers between devices: 129 us -> 45.6 us
  waiting for transfers between devices: 76.9 us -> 17.7 us
  other arithmetic: 19.7 us -> 0.75 us
  Pallas kernels: 0 us -> 17 us
  matrix products: 9.81 us -> 0 us
  blocking collectives: 0 us -> 7.61 us
  between operations: 15.9 us -> 9.92 us
  local copies, waits for them, and re-layouts: 14.4 us -> 8.87 us
    ppermute x48 -> x16, starting transfers between devices: 128 us -> 45.6 us  [the longest x15 42.7 us: shift(): return lax.ppermute(values, axis, [(i, (i + by) % n) for i in range(n)])]
    ppermute x48 -> x16, waiting for transfers between devices: 62.1 us -> 17.7 us  [the longest x15 17.7 us: shift(): return lax.ppermute(values, axis, [(i, (i + by) % n) for i in range(n)])]
    pallas_call x0 -> x5, Pallas kernels: none -> 17 us  [call(): pl.pallas_call(kernel, out_shape=outs, in_specs=[pl.BlockSpec(memory_spac...]
    all_gather x1 -> x0, waiting for transfers between devices: 14.8 us -> none  [body(): piece = lax.all_gather(conc, 'gy', axis=2, tiled=True)]
    slice x56 -> x0, local copies, waits for them, and re-layouts: 13 us -> none  [the longest x20 6.8 us: body(): incoming = jnp.roll(rows[index], step_z, 2)]
    unnamed x15 -> x0, other arithmetic: 9.93 us -> none
    dot_general x5 -> x0, matrix products: 9.81 us -> none  [the longest x2 4.53 us: collide_cells(): jnp.einsum('ic,ixyz->cxyz', lattice, popul, precision=lax.Precision.HIGHEST)]
    unnamed x0 -> x1, blocking collectives: none -> 7.61 us
  transfers between devices with their start and end apart: 49 -> 16, of which waited for: 33 -> 10; matrix products, arithmetic and copies ran while one was open for 9% -> 2% of each run, Pallas kernels for 0% -> 0%
where the time goes in v1:
time: 108 us
  starting transfers between devices  45.6 us (42%)
  waiting for transfers between devices  17.7 us (16%)
  Pallas kernels  17 us (16%)
  between operations  9.92 us (9%)
  local copies, waits for them, and re-layouts  8.87 us (8%)
  blocking collectives  7.61 us (7%)
    ppermute x15, starting transfers between devices, shift(): return lax.ppermute(values, axis, [(i, (i + by) % n) for i in range(n)])  42.7 us
    ppermute x15, waiting for transfers between devices, shift(): return lax.ppermute(values, axis, [(i, (i + by) % n) for i in range(n)])  17.7 us
    pallas_call x5, Pallas kernels, call(): pl.pallas_call(kernel, out_shape=outs, in_specs=[pl.BlockSpec(memory_spac...  17 us
    unnamed x18, local copies, waits for them, and re-layouts  8.87 us
    unnamed x1, blocking collectives  7.61 us
    ppermute x1, starting transfers between devices, migrate(): mate = lax.ppermute(conc, 'gy', [(i, i ^ 1) for i in range(8)])  2.93 us
  transfers between devices with their start and end apart: 16, of which 10 were waited for; matrix products, arithmetic and copies ran while one was open for 2% of the time, Pallas kernels for 0%

profile of v1, /device:TPU:1, one launch (start us, length us, event | category | flops | bytes accessed | tf_op | source)
XLA Modules:
  0.0 107.5 jit_solution(4731391098197979696)
XLA Ops:
  0.6 0.0 copy-start
  0.6 1.3 %copy-done = f32[19,8,16,128]{3,2,1,0:T(8,128)S(1)} copy-done((f32[19,8,16,128]{3,2,1,0:T(8,128)S(1)}, f32[19,8,16,128]{3,2,1,0:T(8,128)}, u32[]{:S(2)}) %copy-start) | copy-done | bytes 1245208
  1.9 0.9 copy-done.3
  2.8 0.8 copy-done.4
  3.7 0.8 copy-done.5
  4.5 0.8 copy-done.6
  5.4 0.9 shard_map.85
  6.2 4.0 %collective-permute-start = (f32[29,16,128]{2,1,0:T(8,128)S(1)}, f32[29,16,128]{2,1,0:T(8,128)S(1)}, u32[]{:S(2)}, u32[]{:S(2)}) collective-permute-start(f32[29,16,128]{2,1,0:T(8,128)S(1)} %get-tuple-element.29), channel_id=1, source_target_pairs={{0,8},{8,16},{16,24},{24,32},{32,40},{40,48},{48,56},{56,64},{64,7... | collective-permute-start | bytes 712712 | tf_op jit(solution)/shard_map/ppermute | solution.py:383
  10.2 15.9 %collective-permute-start.1 = (f32[29,16,128]{2,1,0:T(8,128)S(1)}, f32[29,16,128]{2,1,0:T(8,128)S(1)}, u32[]{:S(2)}, u32[]{:S(2)}) collective-permute-start(f32[29,16,128]{2,1,0:T(8,128)S(1)} %get-tuple-element.30), channel_id=1, source_target_pairs={{0,760},{8,0},{16,8},{24,16},{32,24},{40,32},{48,40},{56,48},{64,5... | collective-permute-start | bytes 712712 | tf_op jit(solution)/shard_map/ppermute | solution.py:383
  26.2 2.1 %collective-permute-start.2 = (f32[8,40,128]{2,1,0:T(8,128)S(1)}, f32[8,40,128]{2,1,0:T(8,128)S(1)}, u32[]{:S(2)}, u32[]{:S(2)}) collective-permute-start(f32[8,40,128]{2,1,0:T(8,128)S(1)} %get-tuple-element.31), channel_id=1, source_target_pairs={{0,1},{1,2},{2,3},{3,4},{4,5},{5,6},{6,7},{7,0},{8,9},{9,10},{10,1... | collective-permute-start | bytes 491528 | tf_op jit(solution)/shard_map/ppermute | solution.py:383
  28.2 0.0 collective-permute-start.3
  28.2 1.5 %collective-permute-done.r_0_.xl = f32[29,16,128]{2,1,0:T(8,128)S(1)} collective-permute-done((f32[29,16,128]{2,1,0:T(8,128)S(1)}, f32[29,16,128]{2,1,0:T(8,128)S(1)}, u32[]{:S(2)}, u32[]{:S(2)}) %collective-permute-start) | collective-permute-done | bytes 237600 | tf_op jit(solution)/shard_map/ppermute | solution.py:383
  29.7 0.9 collective-permute-done.1.r_1_.xh
  30.6 2.7 %collective-permute-start.4 = (f32[2,18,8,128]{3,2,1,0:T(8,128)S(1)}, f32[2,18,8,128]{3,2,1,0:T(8,128)S(1)}, u32[]{:S(2)}, u32[]{:S(2)}) collective-permute-start(f32[2,18,8,128]{3,2,1,0:T(8,128)S(1)} %get-tuple-element.33), channel_id=1, source_target_pairs={{0,1},{1,2},{2,3},{3,4},{4,5},{5,6},{6,7},{7,0},{8,9},{9,10},{10,1... | collective-permute-start | bytes 442376 | tf_op jit(solution)/shard_map/ppermute | solution.py:383
  33.3 0.0 collective-permute-start.5
  33.3 0.0 collective-permute-done.2.yl
  33.3 0.0 collective-permute-done.3.yh
  33.3 2.1 %collective-permute-done.4.cl = f32[2,18,8,128]{3,2,1,0:T(8,128)S(1)} collective-permute-done((f32[2,18,8,128]{3,2,1,0:T(8,128)S(1)}, f32[2,18,8,128]{3,2,1,0:T(8,128)S(1)}, u32[]{:S(2)}, u32[]{:S(2)}) %collective-permute-start.4) | collective-permute-done | bytes 147488 | tf_op jit(solution)/shard_map/ppermute | solution.py:383
  35.4 2.5 %collective-permute-done.5.ch = f32[2,18,8,128]{3,2,1,0:T(8,128)S(1)} collective-permute-done((f32[2,18,8,128]{3,2,1,0:T(8,128)S(1)}, f32[2,18,8,128]{3,2,1,0:T(8,128)S(1)}, u32[]{:S(2)}, u32[]{:S(2)}) %collective-permute-start.5) | collective-permute-done | bytes 147488 | tf_op jit(solution)/shard_map/ppermute | solution.py:383
  37.8 0.0 copy-done.1
  37.9 9.0 %shard_map.87 = (f32[19,8,16,128]{3,2,1,0:T(8,128)S(1)}, f32[8,16,128]{2,1,0:T(8,128)S(1)}, f32[2,8,16,128]{3,2,1,0:T(8,128)S(1)}, f32[22,16,128]{2,1,0:T(8,128)...) custom-call(f32[19,8,16,128]{3,2,1,0:T(8,128)S(1)} %copy-done.1, ...), custom_call_target="tpu_custom_call" | custom-call | tf_op jit(solution)/shard_map/pallas_call | solution.py:363
  46.9 1.9 %collective-permute-start.6 = (f32[22,16,128]{2,1,0:T(8,128)S(1)}, f32[22,16,128]{2,1,0:T(8,128)S(1)}, u32[]{:S(2)}, u32[]{:S(2)}) collective-permute-start(f32[22,16,128]{2,1,0:T(8,128)S(1)} %get-tuple-element.42), channel_id=1, source_target_pairs={{0,8},{8,16},{16,24},{24,32},{32,40},{40,48},{48,56},{56,64},{64,7... | collective-permute-start | bytes 540680 | tf_op jit(solution)/shard_map/ppermute | solution.py:383
  48.8 7.4 %collective-permute-start.7 = (f32[22,16,128]{2,1,0:T(8,128)S(1)}, f32[22,16,128]{2,1,0:T(8,128)S(1)}, u32[]{:S(2)}, u32[]{:S(2)}) collective-permute-start(f32[22,16,128]{2,1,0:T(8,128)S(1)} %get-tuple-element.43), channel_id=1, source_target_pairs={{0,760},{8,0},{16,8},{24,16},{32,24},{40,32},{48,40},{56,48},{64,5... | collective-permute-start | bytes 540680 | tf_op jit(solution)/shard_map/ppermute | solution.py:383
  56.2 0.3 collective-permute-start.8
  56.5 0.2 collective-permute-start.9
  56.8 2.3 %collective-permute-done.6.r_0_.xl = f32[22,16,128]{2,1,0:T(8,128)S(1)} collective-permute-done((f32[22,16,128]{2,1,0:T(8,128)S(1)}, f32[22,16,128]{2,1,0:T(8,128)S(1)}, u32[]{:S(2)}, u32[]{:S(2)}) %collective-permute-start.6) | collective-permute-done | bytes 180256 | tf_op jit(solution)/shard_map/ppermute | solution.py:383
  59.1 0.9 collective-permute-done.7.r_1_.xh
  60.1 0.8 collective-permute-start.10
  60.9 0.1 collective-permute-start.11
  61.0 0.0 collective-permute-done.8.yl
  61.0 0.2 collective-permute-done.9.yh
  61.2 1.3 %collective-permute-done.10.cl = f32[2,12,8,128]{3,2,1,0:T(8,128)S(1)} collective-permute-done((f32[2,12,8,128]{3,2,1,0:T(8,128)S(1)}, f32[2,12,8,128]{3,2,1,0:T(8,128)S(1)}, u32[]{:S(2)}, u32[]{:S(2)}) %collective-permute-start.10) | collective-permute-done | bytes 98336 | tf_op jit(solution)/shard_map/ppermute | solution.py:383
  62.5 2.7 %collective-permute-done.11.ch = f32[2,12,8,128]{3,2,1,0:T(8,128)S(1)} collective-permute-done((f32[2,12,8,128]{3,2,1,0:T(8,128)S(1)}, f32[2,12,8,128]{3,2,1,0:T(8,128)S(1)}, u32[]{:S(2)}, u32[]{:S(2)}) %collective-permute-start.11) | collective-permute-done | bytes 98336 | tf_op jit(solution)/shard_map/ppermute | solution.py:383
  65.2 1.5 %copy-done.2 = f32[6,20,32,128]{3,2,1,0:T(8,128)S(1)} copy-done((f32[6,20,32,128]{3,2,1,0:T(8,128)S(1)}, f32[6,20,32,128]{3,2,1,0:T(8,128)}, u32[]{:S(2)}) %copy-start.2) | copy-done | bytes 1966104
  66.8 7.0 %shard_map.89 = (f32[19,8,16,128]{3,2,1,0:T(8,128)}, f32[8,16,128]{2,1,0:T(8,128)}, f32[2,8,16,128]{3,2,1,0:T(8,128)S(1)}) custom-call(f32[19,8,16,128]{3,2,1,0:T(8,128)S(1)} %get-tuple-element.35.pop, f32[2,8,16,128]{3,2,1,0:T(8,128)S(1)} %get-tuple-element.36.conc, f32[8,16,128]{2,1,0:T(8,128)S(1)} %get-tuple-element.37.phi, ...), custom_call_target="tpu_custom_call" | custom-call | tf_op jit(solution)/shard_map/pallas_call | solution.py:363
  73.8 2.9 %collective-permute-start.12 = (f32[2,8,16,128]{3,2,1,0:T(8,128)S(1)}, f32[2,8,16,128]{3,2,1,0:T(8,128)S(1)}, u32[]{:S(2)}, u32[]{:S(2)}) collective-permute-start(f32[2,8,16,128]{3,2,1,0:T(8,128)S(1)} %get-tuple-element.50), channel_id=1, source_target_pairs={{0,1},{1,0},{2,3},{3,2},{4,5},{5,4},{6,7},{7,6},{8,9},{9,8},{10,11... | collective-permute-start | bytes 393224 | tf_op jit(solution)/shard_map/ppermute | solution.py:403
  77.4 1.3 %dynamic-slice.4 = u32[1]{0:T(128)} dynamic-slice(u32[768]{0:T(1024)} %constant.96, u32[]{:T(128)S(6)} %add.68), dynamic_slice_sizes={1} | dynamic-slice | bytes 12
  78.7 0.7 bitcast_dynamic-update-slice_fusion
  79.4 7.6 %all-reduce = s32[8]{0:T(128)S(1)} all-reduce(s32[8]{0:T(128)S(1)} %bitcast_dynamic-update-slice_fusion), channel_id=2, replica_groups=mesh['gx'=96,'gy'=8] {'gy'}, use_global_device_ids=true, to_apply=%add | all-reduce | flops 8 | bytes 64
  87.0 0.7 fusion
  93.5 0.0 collective-permute-done.12
  93.6 2.0 %collective-permute-start.13 = (f32[2,8,16,128]{3,2,1,0:T(8,128)S(1)}, f32[2,8,16,128]{3,2,1,0:T(8,128)S(1)}, u32[]{:S(2)}, u32[]{:S(2)}) collective-permute-start(f32[2,8,16,128]{3,2,1,0:T(8,128)S(1)} %get-tuple-element.55), channel_id=1, source_target_pairs={{0,6},{1,7},{2,0},{3,1},{4,2},{5,3},{6,4},{7,5},{8,14},{9,15},{10,... | collective-permute-start | bytes 393224 | tf_op jit(solution)/shard_map/ppermute | solution.py:383
  95.6 3.3 %collective-permute-start.14 = (f32[2,8,16,128]{3,2,1,0:T(8,128)S(1)}, f32[2,8,16,128]{3,2,1,0:T(8,128)S(1)}, u32[]{:S(2)}, u32[]{:S(2)}) collective-permute-start(f32[2,8,16,128]{3,2,1,0:T(8,128)S(1)} %get-tuple-element.54), channel_id=1, source_target_pairs={{0,4},{1,5},{2,6},{3,7},{4,0},{5,1},{6,2},{7,3},{8,12},{9,13},{10,... | collective-permute-start | bytes 393224 | tf_op jit(solution)/shard_map/ppermute | solution.py:383
  98.9 1.9 %collective-permute-start.15 = (f32[2,8,16,128]{3,2,1,0:T(8,128)S(1)}, f32[2,8,16,128]{3,2,1,0:T(8,128)S(1)}, u32[]{:S(2)}, u32[]{:S(2)}) collective-permute-start(f32[2,8,16,128]{3,2,1,0:T(8,128)S(1)} %get-tuple-element.51), channel_id=1, source_target_pairs={{0,2},{1,3},{2,4},{3,5},{4,6},{5,7},{6,0},{7,1},{8,10},{9,11},{10,... | collective-permute-start | bytes 393224 | tf_op jit(solution)/shard_map/ppermute | solution.py:383
  103.5 0.0 collective-permute-done.13
  103.5 0.0 collective-permute-done.14
  103.5 3.3 %collective-permute-done.15 = f32[2,8,16,128]{3,2,1,0:T(8,128)S(1)} collective-permute-done((f32[2,8,16,128]{3,2,1,0:T(8,128)S(1)}, f32[2,8,16,128]{3,2,1,0:T(8,128)S(1)}, u32[]{:S(2)}, u32[]{:S(2)}) %collective-permute-start.15) | collective-permute-done | bytes 131104 | tf_op jit(solution)/shard_map/ppermute | solution.py:383
  106.8 0.7 select_select_fusion
  (11 shorter events, 0.1 us)
Async XLA Ops:
  0.6 1.3 %copy-start = (f32[19,8,16,128]{3,2,1,0:T(8,128)S(1)}, f32[19,8,16,128]{3,2,1,0:T(8,128)}, u32[]{:S(2)}) copy-start(f32[19,8,16,128]{3,2,1,0:T(8,128)} %pop.3) | copy-start | bytes 3735556
  1.9 0.9 copy-start.3
  2.8 0.8 copy-start.4
  3.7 0.8 copy-start.5
  4.5 0.8 copy-start.6
  5.4 32.5 %copy-start.1 = (f32[19,8,16,128]{3,2,1,0:T(8,128)S(1)}, f32[19,8,16,128]{3,2,1,0:T(8,128)}, u32[]{:S(2)}) copy-start(f32[19,8,16,128]{3,2,1,0:T(8,128)} %pop.3) | copy-start | bytes 3735556
  6.2 23.5 %collective-permute-start = (f32[29,16,128]{2,1,0:T(8,128)S(1)}, f32[29,16,128]{2,1,0:T(8,128)S(1)}, u32[]{:S(2)}, u32[]{:S(2)}) collective-permute-start(f32[29,16,128]{2,1,0:T(8,128)S(1)} %get-tuple-element.29), channel_id=1, source_target_pairs={{0,8},{8,16},{16,24},{24,32},{32,40},{40,48},{48,56},{56,64},{64,7... | collective-permute-start | bytes 712712 | tf_op jit(solution)/shard_map/ppermute | solution.py:383
  10.2 20.4 %collective-permute-start.1 = (f32[29,16,128]{2,1,0:T(8,128)S(1)}, f32[29,16,128]{2,1,0:T(8,128)S(1)}, u32[]{:S(2)}, u32[]{:S(2)}) collective-permute-start(f32[29,16,128]{2,1,0:T(8,128)S(1)} %get-tuple-element.30), channel_id=1, source_target_pairs={{0,760},{8,0},{16,8},{24,16},{32,24},{40,32},{48,40},{56,48},{64,5... | collective-permute-start | bytes 712712 | tf_op jit(solution)/shard_map/ppermute | solution.py:383
  26.2 7.1 %collective-permute-start.2 = (f32[8,40,128]{2,1,0:T(8,128)S(1)}, f32[8,40,128]{2,1,0:T(8,128)S(1)}, u32[]{:S(2)}, u32[]{:S(2)}) collective-permute-start(f32[8,40,128]{2,1,0:T(8,128)S(1)} %get-tuple-element.31), channel_id=1, source_target_pairs={{0,1},{1,2},{2,3},{3,4},{4,5},{5,6},{6,7},{7,0},{8,9},{9,10},{10,1... | collective-permute-start | bytes 491528 | tf_op jit(solution)/shard_map/ppermute | solution.py:383
  28.2 5.1 %collective-permute-start.3 = (f32[8,40,128]{2,1,0:T(8,128)S(1)}, f32[8,40,128]{2,1,0:T(8,128)S(1)}, u32[]{:S(2)}, u32[]{:S(2)}) collective-permute-start(f32[8,40,128]{2,1,0:T(8,128)S(1)} %get-tuple-element.32), channel_id=1, source_target_pairs={{0,7},{1,0},{2,1},{3,2},{4,3},{5,4},{6,5},{7,6},{8,15},{9,8},{10,9... | collective-permute-start | bytes 491528 | tf_op jit(solution)/shard_map/ppermute | solution.py:383
  30.6 4.8 %collective-permute-start.4 = (f32[2,18,8,128]{3,2,1,0:T(8,128)S(1)}, f32[2,18,8,128]{3,2,1,0:T(8,128)S(1)}, u32[]{:S(2)}, u32[]{:S(2)}) collective-permute-start(f32[2,18,8,128]{3,2,1,0:T(8,128)S(1)} %get-tuple-element.33), channel_id=1, source_target_pairs={{0,1},{1,2},{2,3},{3,4},{4,5},{5,6},{6,7},{7,0},{8,9},{9,10},{10,1... | collective-permute-start | bytes 442376 | tf_op jit(solution)/shard_map/ppermute | solution.py:383
  33.3 4.6 %collective-permute-start.5 = (f32[2,18,8,128]{3,2,1,0:T(8,128)S(1)}, f32[2,18,8,128]{3,2,1,0:T(8,128)S(1)}, u32[]{:S(2)}, u32[]{:S(2)}) collective-permute-start(f32[2,18,8,128]{3,2,1,0:T(8,128)S(1)} %get-tuple-element.34), channel_id=1, source_target_pairs={{0,7},{1,0},{2,1},{3,2},{4,3},{5,4},{6,5},{7,6},{8,15},{9,8},{10,9... | collective-permute-start | bytes 442376 | tf_op jit(solution)/shard_map/ppermute | solution.py:383
  46.9 12.2 %collective-permute-start.6 = (f32[22,16,128]{2,1,0:T(8,128)S(1)}, f32[22,16,128]{2,1,0:T(8,128)S(1)}, u32[]{:S(2)}, u32[]{:S(2)}) collective-permute-start(f32[22,16,128]{2,1,0:T(8,128)S(1)} %get-tuple-element.42), channel_id=1, source_target_pairs={{0,8},{8,16},{16,24},{24,32},{32,40},{40,48},{48,56},{56,64},{64,7... | collective-permute-start | bytes 540680 | tf_op jit(solution)/shard_map/ppermute | solution.py:383
  48.8 11.2 %collective-permute-start.7 = (f32[22,16,128]{2,1,0:T(8,128)S(1)}, f32[22,16,128]{2,1,0:T(8,128)S(1)}, u32[]{:S(2)}, u32[]{:S(2)}) collective-permute-start(f32[22,16,128]{2,1,0:T(8,128)S(1)} %get-tuple-element.43), channel_id=1, source_target_pairs={{0,760},{8,0},{16,8},{24,16},{32,24},{40,32},{48,40},{56,48},{64,5... | collective-permute-start | bytes 540680 | tf_op jit(solution)/shard_map/ppermute | solution.py:383
  56.2 4.8 %collective-permute-start.8 = (f32[8,32,128]{2,1,0:T(8,128)S(1)}, f32[8,32,128]{2,1,0:T(8,128)S(1)}, u32[]{:S(2)}, u32[]{:S(2)}) collective-permute-start(f32[8,32,128]{2,1,0:T(8,128)S(1)} %get-tuple-element.44), channel_id=1, source_target_pairs={{0,1},{1,2},{2,3},{3,4},{4,5},{5,6},{6,7},{7,0},{8,9},{9,10},{10,1... | collective-permute-start | bytes 393224 | tf_op jit(solution)/shard_map/ppermute | solution.py:383
  56.5 4.7 %collective-permute-start.9 = (f32[8,32,128]{2,1,0:T(8,128)S(1)}, f32[8,32,128]{2,1,0:T(8,128)S(1)}, u32[]{:S(2)}, u32[]{:S(2)}) collective-permute-start(f32[8,32,128]{2,1,0:T(8,128)S(1)} %get-tuple-element.45), channel_id=1, source_target_pairs={{0,7},{1,0},{2,1},{3,2},{4,3},{5,4},{6,5},{7,6},{8,15},{9,8},{10,9... | collective-permute-start | bytes 393224 | tf_op jit(solution)/shard_map/ppermute | solution.py:383
  60.1 2.5 %collective-permute-start.10 = (f32[2,12,8,128]{3,2,1,0:T(8,128)S(1)}, f32[2,12,8,128]{3,2,1,0:T(8,128)S(1)}, u32[]{:S(2)}, u32[]{:S(2)}) collective-permute-start(f32[2,12,8,128]{3,2,1,0:T(8,128)S(1)} %get-tuple-element.46), channel_id=1, source_target_pairs={{0,1},{1,2},{2,3},{3,4},{4,5},{5,6},{6,7},{7,0},{8,9},{9,10},{10,1... | collective-permute-start | bytes 294920 | tf_op jit(solution)/shard_map/ppermute | solution.py:383
  60.9 4.3 %collective-permute-start.11 = (f32[2,12,8,128]{3,2,1,0:T(8,128)S(1)}, f32[2,12,8,128]{3,2,1,0:T(8,128)S(1)}, u32[]{:S(2)}, u32[]{:S(2)}) collective-permute-start(f32[2,12,8,128]{3,2,1,0:T(8,128)S(1)} %get-tuple-element.47), channel_id=1, source_target_pairs={{0,7},{1,0},{2,1},{3,2},{4,3},{5,4},{6,5},{7,6},{8,15},{9,8},{10,9... | collective-permute-start | bytes 294920 | tf_op jit(solution)/shard_map/ppermute | solution.py:383
  65.2 1.5 %copy-start.2 = (f32[6,20,32,128]{3,2,1,0:T(8,128)S(1)}, f32[6,20,32,128]{3,2,1,0:T(8,128)}, u32[]{:S(2)}) copy-start(f32[6,20,32,128]{3,2,1,0:T(8,128)} %get-tuple-element.39.coef) | copy-start | bytes 5898244
  73.8 19.7 %collective-permute-start.12 = (f32[2,8,16,128]{3,2,1,0:T(8,128)S(1)}, f32[2,8,16,128]{3,2,1,0:T(8,128)S(1)}, u32[]{:S(2)}, u32[]{:S(2)}) collective-permute-start(f32[2,8,16,128]{3,2,1,0:T(8,128)S(1)} %get-tuple-element.50), channel_id=1, source_target_pairs={{0,1},{1,0},{2,3},{3,2},{4,5},{5,4},{6,7},{7,6},{8,9},{9,8},{10,11... | collective-permute-start | bytes 393224 | tf_op jit(solution)/shard_map/ppermute | solution.py:403
  93.6 9.9 %collective-permute-start.13 = (f32[2,8,16,128]{3,2,1,0:T(8,128)S(1)}, f32[2,8,16,128]{3,2,1,0:T(8,128)S(1)}, u32[]{:S(2)}, u32[]{:S(2)}) collective-permute-start(f32[2,8,16,128]{3,2,1,0:T(8,128)S(1)} %get-tuple-element.55), channel_id=1, source_target_pairs={{0,6},{1,7},{2,0},{3,1},{4,2},{5,3},{6,4},{7,5},{8,14},{9,15},{10,... | collective-permute-start | bytes 393224 | tf_op jit(solution)/shard_map/ppermute | solution.py:383
  95.6 7.9 %collective-permute-start.14 = (f32[2,8,16,128]{3,2,1,0:T(8,128)S(1)}, f32[2,8,16,128]{3,2,1,0:T(8,128)S(1)}, u32[]{:S(2)}, u32[]{:S(2)}) collective-permute-start(f32[2,8,16,128]{3,2,1,0:T(8,128)S(1)} %get-tuple-element.54), channel_id=1, source_target_pairs={{0,4},{1,5},{2,6},{3,7},{4,0},{5,1},{6,2},{7,3},{8,12},{9,13},{10,... | collective-permute-start | bytes 393224 | tf_op jit(solution)/shard_map/ppermute | solution.py:383
  98.9 7.9 %collective-permute-start.15 = (f32[2,8,16,128]{3,2,1,0:T(8,128)S(1)}, f32[2,8,16,128]{3,2,1,0:T(8,128)S(1)}, u32[]{:S(2)}, u32[]{:S(2)}) collective-permute-start(f32[2,8,16,128]{3,2,1,0:T(8,128)S(1)} %get-tuple-element.51), channel_id=1, source_target_pairs={{0,2},{1,3},{2,4},{3,5},{4,6},{5,7},{6,0},{7,1},{8,10},{9,11},{10,... | collective-permute-start | bytes 393224 | tf_op jit(solution)/shard_map/ppermute | solution.py:383

commit v2 on v1

v2 whole, which is shorter than its diff:
```python
import jax
import jax.numpy as jnp
from jax import lax
from jax.experimental import pallas as pl
from jax.experimental.pallas import tpu as pltpu
from jax.sharding import PartitionSpec as P

STEPS = 2
SWEEPS = 4
VEL = (
    (0, 0, 0), (1, 0, 0), (-1, 0, 0), (0, 1, 0), (0, -1, 0), (0, 0, 1), (0, 0, -1),
    (1, 1, 0), (-1, -1, 0), (1, -1, 0), (-1, 1, 0), (1, 0, 1), (-1, 0, -1), (1, 0, -1),
    (-1, 0, 1), (0, 1, 1), (0, -1, -1), (0, 1, -1), (0, -1, 1),
)
WEIGHT = (1.0 / 3.0,) + (1.0 / 18.0,) * 6 + (1.0 / 36.0,) * 12
OPP = (0, 2, 1, 4, 3, 6, 5, 8, 7, 10, 9, 12, 11, 14, 13, 16, 15, 18, 17)
TAU = 0.8
COUPLING = 0.05
DRIVE = 0.001
DIFF = (0.1, 0.15)
VALENCE = (1.0, -1.0)

CX, CY, NZ = 8, 16, 128
EX, EY = 20, 32
F32 = jnp.float32

X_IN_LO = tuple(i for i in range(19) if VEL[i][0] == 1)
X_IN_HI = tuple(i for i in range(19) if VEL[i][0] == -1)
Y_IN_LO = tuple(i for i in range(19) if VEL[i][1] == 1)
Y_IN_HI = tuple(i for i in range(19) if VEL[i][1] == -1)
LO_LO, HI_LO = VEL.index((1, 1, 0)), VEL.index((-1, 1, 0))
LO_HI, HI_HI = VEL.index((1, -1, 0)), VEL.index((-1, -1, 0))


def shape(*dims):
    return jax.ShapeDtypeStruct(dims, F32)


def turn(v, by, axis):
    return pltpu.roll(v, by % v.shape[axis], axis)


class Plan:
    def __init__(self, first):
        self.first = first
        self.x_perm = 6 if first else None
        at = 12 if first else 6
        self.x_charge = at
        self.x_conc = at + 5
        at += 7
        if first:
            self.x_fluid = at
            at += 1
        self.x_pop = at
        self.x_dm = at + 5
        self.x_planes = at + 9
        self.y_perm = 8 if first else None
        at = 16 if first else 8
        self.y_charge = at
        self.y_misc = at + 8
        self.y_rows = at + 24
        self.c_charge = 12 if first else 6
        self.c_misc = self.c_charge + 5
        self.c_tiles = self.c_charge + 6


ONE, TWO = Plan(True), Plan(False)


def pack_x(plan, out, low, phi, charge, conc, pop, dm, perm=None, fluid=None):
    deep = slice(0, 6) if low else slice(2, 8)
    out[0:6] = phi[deep]
    if plan.first:
        out[6:12] = perm[deep]
        out[plan.x_fluid] = fluid[0 if low else 7]
    out[plan.x_charge : plan.x_charge + 5] = charge[0:5] if low else charge[3:8]
    edge = 0 if low else 7
    out[plan.x_conc] = conc[0, edge]
    out[plan.x_conc + 1] = conc[1, edge]
    for k, i in enumerate(X_IN_HI if low else X_IN_LO):
        out[plan.x_pop + k] = pop[i, edge]
    for k in range(4):
        out[plan.x_dm + k] = dm[k, edge]


def pack_y(plan, out, low, owner, phi, charge, conc, pop, dm, perm=None, fluid=None):
    tile = slice(0, 8) if low else slice(8, 16)
    row = slice(0, 1) if low else slice(15, 16)
    out[:, 0:8] = phi[:, tile]
    if plan.first:
        out[:, 8:16] = perm[:, tile]
    out[:, plan.y_charge : plan.y_charge + 8] = charge[:, tile]
    rows = [conc[0, :, row], conc[1, :, row]]
    rows.append(fluid[:, row] if plan.first else conc[0, :, row])
    rows += [pop[i, :, row] for i in (Y_IN_HI if low else Y_IN_LO)]
    rows += [dm[k, :, row] for k in range(4)]
    for k, values in enumerate(rows):
        out[:, plan.y_misc + k : plan.y_misc + k + 1] = values
    out[0, plan.y_misc + 12 : plan.y_misc + 13] = owner


def moments(load):
    dens = load(0)
    mom = [None, None, None]
    for i in range(1, 19):
        v = load(i)
        dens = dens + v
        for c in range(3):
            if VEL[i][c]:
                t = v if VEL[i][c] > 0 else -v
                mom[c] = t if mom[c] is None else mom[c] + t
    return [dens] + mom


def first_kernel(owner, *refs):
    far, near, sems = refs[:5], refs[13:18], refs[18]
    pop, conc, phi, perm, mask = near
    x_hi, x_lo, y_hi, y_lo, dm, charge, fluid, owner_row = refs[5:13]
    copies = [pltpu.make_async_copy(a, b, sems.at[k]) for k, (a, b) in enumerate(zip(far, near))]
    for copy in copies:
        copy.start()
    owner_row[...] = jnp.full((8, NZ), owner[0, 0], jnp.int32).astype(F32)
    for copy in copies:
        copy.wait()
    charge[...] = conc[0] - conc[1]
    fluid[...] = mask[...].astype(F32)

    def plane(x, _):
        for k, v in enumerate(moments(lambda i: pop[i, x])):
            dm[k, x] = v
        return 0

    lax.fori_loop(0, CX, plane, 0)
    for low, xo, yo in ((False, x_hi, y_hi), (True, x_lo, y_lo)):
        pack_x(ONE, xo, low, phi, charge, conc, pop, dm, perm, fluid)
        pack_y(ONE, yo, low, owner_row[0:1], phi, charge, conc, pop, dm, perm, fluid)


def corner_kernel(plan, xl, xh, c_hi, c_lo):
    for out, tile, row, picks in (
        (c_hi, slice(8, 16), slice(15, 16), (LO_LO, HI_LO)),
        (c_lo, slice(0, 8), slice(0, 1), (LO_HI, HI_HI)),
    ):
        for side, x, names in ((0, xl, X_IN_LO), (1, xh, X_IN_HI)):
            out[side, 0 : plan.c_misc] = x[0 : plan.c_misc, tile]
            pop_at = plan.x_pop + names.index(picks[side])
            rows = [x[plan.x_fluid if plan.first else pop_at, row], x[pop_at, row]]
            rows += [x[plan.x_dm + k, row] for k in range(4)]
            for k, v in enumerate(rows):
                out[side, plan.c_misc, k : k + 1] = v


def lay(ext, own, xl, xh, yl, yh, cl, ch, lo, depth):
    a = 6 - depth
    ext[6:14, 8:24] = own
    ext[a:6, 8:24] = xl
    ext[14 : 14 + depth, 8:24] = xh
    ext[6:14, 0:8] = yl
    ext[6:14, 24:32] = yh
    for part, rows in ((cl, slice(0, 8)), (ch, slice(24, 32))):
        ext[a:6, rows] = part[0, lo : lo + depth]
        ext[14 : 14 + depth, rows] = part[1, lo : lo + depth]


def lay_all(plan, phi, conc, dm, charge_own, msgs, pa, ce, dn, mm, cc):
    xl, xh, yl, yh, cl, ch = msgs
    lay(pa, phi[...], xl[0:6], xh[0:6], yl[:, 0:8], yh[:, 0:8], cl, ch, 0, 6)
    q, w = plan.x_charge, plan.y_charge
    lay(ce, charge_own, xl[q : q + 5], xh[q : q + 5], yl[:, w : w + 8], yh[:, w : w + 8],
        cl, ch, plan.c_charge, 5)
    ym = plan.y_misc
    for s in range(2):
        cc[s, 1:9, 8:24] = conc[s]
        cc[s, 0, 8:24] = xl[plan.x_conc + s]
        cc[s, 9, 8:24] = xh[plan.x_conc + s]
        cc[s, 1:9, 7:8] = yl[:, ym + s : ym + s + 1]
        cc[s, 1:9, 24:25] = yh[:, ym + s : ym + s + 1]
    for k, ext in enumerate((dn, mm.at[0], mm.at[1], mm.at[2])):
        ext[1:9, 8:24] = dm[k]
        ext[0, 8:24] = xl[plan.x_dm + k]
        ext[9, 8:24] = xh[plan.x_dm + k]
        for y, c, r in ((yl, cl, 7), (yh, ch, 24)):
            ext[1:9, r : r + 1] = y[:, ym + 8 + k : ym + 9 + k]
            for side, p in ((0, 0), (1, 9)):
                ext[p, r : r + 1] = c[side, plan.c_misc, 2 + k : 3 + k]


LO_T, MID_T, HI_T = slice(0, 8), slice(8, 24), slice(24, 32)


def sweeps(coef, inv, ce, src, dst):
    for sweep in range(SWEEPS):

        def relax(x, _, src=src, dst=dst):
            mid = src[x]
            acc = ce[x] * inv[x]
            acc += coef[0, x] * src[x - 1] + coef[1, x] * src[x + 1]
            acc += coef[2, x] * turn(mid, 1, 0) + coef[3, x] * turn(mid, -1, 0)
            acc += coef[4, x] * turn(mid, 1, 1) + coef[5, x] * turn(mid, -1, 1)
            dst[x] = acc
            return 0

        lax.fori_loop(1 + sweep, 19 - sweep, relax, 0, unroll=6)
        src, dst = dst, src
    return src


def motion(fin, ce, fl, dn, mm, vel, sh):
    def plane(p, _):
        mid = fin[p + 5]
        grad = [
            -0.5 * (fin[p + 6] - fin[p + 4]),
            -0.5 * (turn(mid, -1, 0) - turn(mid, 1, 0)),
            -0.5 * (turn(mid, -1, 1) - turn(mid, 1, 1)),
        ]
        f = fl[p]
        scale = COUPLING * ce[p + 5]
        force = [f * (scale * g + d) if d else f * (scale * g) for g, d in zip(grad, (DRIVE, 0, 0))]
        dens = dn[p]
        over = 1.0 / dens
        mom = [mm[c, p] for c in range(3)]
        for c in range(3):
            vel[c, p] = f * (mom[c] + 0.5 * force[c]) * over
        u = [(mom[c] + TAU * force[c]) * over for c in range(3)]
        for c in range(3):
            sh[c, p] = u[c]
        sh[3, p] = 1.0 - 1.5 * (u[0] * u[0] + u[1] * u[1] + u[2] * u[2])
        sh[4, p] = dens * (1.0 / TAU)
        return 0

    lax.fori_loop(0, 10, plane, 0, unroll=2)


def ions(fin, fl, cc, vel, store):
    def flux(s, ca, cb, pot_a, pot_b, ua, ub, wall):
        total = ca + cb
        speed = 0.25 * (ua + ub) - (0.5 * DIFF[s] * VALENCE[s]) * (pot_b - pot_a)
        return wall * (total * speed - DIFF[s] * (cb - ca))

    def x_face(s, p):
        wall = fl[p, MID_T] * fl[p + 1, MID_T]
        return flux(s, cc[s, p, MID_T], cc[s, p + 1, MID_T], fin[p + 5, MID_T], fin[p + 6, MID_T],
                    vel[0, p, MID_T], vel[0, p + 1, MID_T], wall)

    def plane(p, before):
        after = []
        f, pot, vy = fl[p], fin[p + 5], vel[1, p]
        for s in range(2):
            face = x_face(s, p)
            total = face - before[s]
            after.append(face)
            c = cc[s, p]
            face = flux(s, c, turn(c, -1, 0), pot, turn(pot, -1, 0), vy, turn(vy, -1, 0), f * turn(f, -1, 0))
            total = total + (face - turn(face, 1, 0))[MID_T]
            fm, cm, pm, vz = f[MID_T], c[MID_T], pot[MID_T], vel[2, p, MID_T]
            face = flux(s, cm, turn(cm, -1, 1), pm, turn(pm, -1, 1), vz, turn(vz, -1, 1), fm * turn(fm, -1, 1))
            total = total + face - turn(face, 1, 1)
            store(s, p - 1, cm - total)
        return tuple(after)

    lax.fori_loop(1, 9, plane, (x_face(0, 0), x_face(1, 0)), unroll=4)


def collide_and_stream(plan, pop, fl, sh, msgs, lv, pop_out, dm_out):
    xl, xh, yl, yh, cl, ch = msgs
    ym = plan.y_misc
    bad = float("nan")

    def load(p, rows):
        return [sh[c, p, rows] for c in range(5)] + [fl[p, rows] != 0.0]

    def relaxed_of(i, pop_i, part):
        pr = None
        for c in range(3):
            if VEL[i][c]:
                t = part[c] if VEL[i][c] > 0 else -part[c]
                pr = t if pr is None else pr + t
        poly = part[3]
        if pr is not None:
            poly = poly + pr * (3.0 + 4.5 * pr)
        return (1.0 - 1.0 / TAU) * pop_i + (WEIGHT[i] * part[4]) * poly

    def collide(p, _):
        x = p - 1
        part = load(p, MID_T)
        wet = part[5]
        for i in range(19):
            j = OPP[i]
            if i > j:
                continue
            pi = pop[i, x]
            ri = relaxed_of(i, pi, part)
            if i == j:
                pop_out[i, x] = jnp.where(wet, ri, pi)
                continue
            pj = pop[j, x]
            rj = relaxed_of(j, pj, part)
            lv[i, p, MID_T] = jnp.where(wet, ri, bad)
            lv[j, p, MID_T] = jnp.where(wet, rj, bad)
            pop_out[i, x] = jnp.where(wet, rj, pi)
            pop_out[j, x] = jnp.where(wet, ri, pj)
        for y, names, r in ((yl, Y_IN_LO, 7), (yh, Y_IN_HI, 24)):
            row = slice(r, r + 1)
            part = load(p, row)
            for k, i in enumerate(names):
                value = relaxed_of(i, y[x, ym + 3 + k : ym + 4 + k], part)
                lv[i, p, row] = jnp.where(part[5], value, bad)
        return 0

    lax.fori_loop(1, 9, collide, 0)
    for p, side, x, names, low_pop, high_pop in (
        (0, 0, xl, X_IN_LO, LO_LO, LO_HI),
        (9, 1, xh, X_IN_HI, HI_LO, HI_HI),
    ):
        part = load(p, MID_T)
        for k, i in enumerate(names):
            lv[i, p, MID_T] = jnp.where(part[5], relaxed_of(i, x[plan.x_pop + k], part), bad)
        for c, r, i in ((cl, 7, low_pop), (ch, 24, high_pop)):
            row = slice(r, r + 1)
            part = load(p, row)
            lv[i, p, row] = jnp.where(part[5], relaxed_of(i, c[side, plan.c_misc, 1:2], part), bad)

    def stream(x, _):
        wet = fl[x + 1, MID_T] != 0.0
        for i in range(1, 19):
            ex, ey, ez = VEL[i]
            came = lv[i, x + 1 - ex, 8 - ey : 24 - ey]
            if ez:
                came = turn(came, ez, 1)
            pop_out[i, x] = jnp.where(wet & (came == came), came, pop_out[i, x])
        if dm_out is not None:
            for k, v in enumerate(moments(lambda i: pop_out[i, x])):
                dm_out[k, x] = v
        return 0

    lax.fori_loop(0, CX, stream, 0, unroll=2)


def step_one_kernel(pop, conc, phi, perm, dm, fluid, owner_two, xl, xh, yl, yh, cl, ch,
                    pop_out, phi_out, conc_out, x_hi, x_lo, y_hi, y_lo, dm_out, coef, inv, fl,
                    pe, charge, pa, pb, ce, dn, mm, cc, vel, sh, lv):
    msgs = (xl, xh, yl, yh, cl, ch)
    lay(pe, perm[...], xl[6:12], xh[6:12], yl[:, 8:16], yh[:, 8:16], cl, ch, 6, 6)

    def coefs(x, _):
        mid = pe[x]
        faces = [0.5 * (mid + other) for other in (
            pe[x - 1], pe[x + 1], turn(mid, 1, 0), turn(mid, -1, 0), turn(mid, 1, 1), turn(mid, -1, 1))]
        over = 1.0 / (faces[0] + faces[1] + faces[2] + faces[3] + faces[4] + faces[5])
        inv[x] = over
        for k in range(6):
            coef[k, x] = faces[k] * over
        return 0

    lax.fori_loop(1, 19, coefs, 0, unroll=6)
    fl[1:9, 8:24] = fluid[...]
    fl[0, 8:24] = xl[ONE.x_fluid]
    fl[9, 8:24] = xh[ONE.x_fluid]
    for y, c, r in ((yl, cl, 7), (yh, ch, 24)):
        fl[1:9, r : r + 1] = y[:, ONE.y_misc + 2 : ONE.y_misc + 3]
        for side, p in ((0, 0), (1, 9)):
            fl[p, r : r + 1] = c[side, ONE.c_misc, 0:1]
    lay_all(ONE, phi, conc, dm, conc[0] - conc[1], msgs, pa, ce, dn, mm, cc)
    fin = sweeps(coef, inv, ce, pa, pb)
    phi_out[...] = fin[6:14, MID_T]
    motion(fin, ce, fl, dn, mm, vel, sh)

    def store(s, x, values):
        conc_out[s, x] = values

    ions(fin, fl, cc, vel, store)
    collide_and_stream(ONE, pop, fl, sh, msgs, lv, pop_out, dm_out)
    charge[...] = conc_out[0] - conc_out[1]
    above = yh[0, ONE.y_misc + 12 : ONE.y_misc + 13]
    for low, xo, yo, owner in ((False, x_hi, y_hi, owner_two[0:1]), (True, x_lo, y_lo, above)):
        pack_x(TWO, xo, low, phi_out, charge, conc_out, pop_out, dm_out)
        pack_y(TWO, yo, low, owner, phi_out, charge, conc_out, pop_out, dm_out)


def ions_two_kernel(conc, phi, dm, coef, inv, fl, xl, xh, yl, yh, cl, ch,
                    phi_out, slab, sh, pa, pb, ce, dn, mm, cc, vel):
    lay_all(TWO, phi, conc, dm, conc[0] - conc[1], (xl, xh, yl, yh, cl, ch), pa, ce, dn, mm, cc)
    fin = sweeps(coef, inv, ce, pa, pb)
    phi_out[...] = fin[6:14, MID_T]
    motion(fin, ce, fl, dn, mm, vel, sh)

    def store(s, x, values):
        slab[s * CX + x] = values

    ions(fin, fl, cc, vel, store)
    slab[2 * CX, 0:8] = jnp.broadcast_to(yl[0, TWO.y_misc + 12 : TWO.y_misc + 13], (8, NZ))


def flow_two_kernel(pop, fl, sh, xl, xh, yl, yh, cl, ch, pop_out, lv):
    collide_and_stream(TWO, pop, fl, sh, (xl, xh, yl, yh, cl, ch), lv, pop_out, None)


def owner_kernel(yl, out):
    out[...] = jnp.broadcast_to(yl[0, ONE.y_misc + 12 : ONE.y_misc + 13], (8, NZ))


def route_kernel(mine, other, yh, owner_two, *outs):
    me = jnp.full((1, NZ), lax.axis_index("gy"), jnp.int32).astype(F32)
    wanted = (yh[0, TWO.y_misc + 12 : TWO.y_misc + 13], other[2 * CX, 0:1], owner_two[0:1])
    for want, out in zip(wanted, outs):
        pick = want == me
        for s in range(2):
            for x in range(CX):
                out[s, x] = jnp.where(pick, mine[s * CX + x], other[s * CX + x])


def arrive_kernel(mine, other, one, two, three, owner_row, out):
    me = jnp.full((1, NZ), lax.axis_index("gy"), jnp.int32).astype(F32)
    away = me - owner_row[0:1]
    away = jnp.where(away < 0, away + 8.0, away)
    for s in range(2):
        for x in range(CX):
            v = jnp.where(away < 0.5, mine[s * CX + x], other[s * CX + x])
            v = jnp.where(away > 1.5, one[s, x], v)
            v = jnp.where(away > 3.5, two[s, x], v)
            out[s, x] = jnp.where(away > 5.5, three[s, x], v)


VMEM, FAR, SMEM = (pl.BlockSpec(memory_space=m) for m in (pltpu.VMEM, pltpu.HBM, pltpu.SMEM))


def call(kernel, outs, args, scratch=(), specs=None, flops=0):
    return pl.pallas_call(
        kernel,
        out_shape=outs,
        in_specs=specs or [VMEM] * len(args),
        out_specs=[VMEM] * len(outs),
        scratch_shapes=[pltpu.VMEM(s, F32) if isinstance(s, tuple) else s for s in scratch],
        compiler_params=pltpu.CompilerParams(vmem_limit_bytes=24 * 1024 * 1024),
        cost_estimate=pl.CostEstimate(flops=flops, bytes_accessed=0, transcendentals=0) if flops else None,
    )(*args)


HALO = (EX, EY, NZ)
RIM = (10, EY, NZ)
FIELDS = (HALO, HALO, HALO, RIM, (3,) + RIM, (2,) + RIM, (3,) + RIM)


def shift(values, axis, by):
    n = lax.axis_size(axis)
    return lax.ppermute(values, axis, [(i, (i + by) % n) for i in range(n)])


def exchange(plan, x_hi, x_lo, y_hi, y_lo):
    yl, yh = shift(y_hi, "gy", 1), shift(y_lo, "gy", -1)
    xl, xh = shift(x_hi, "gx", 1), shift(x_lo, "gx", -1)
    tiles = shape(2, plan.c_tiles, 8, NZ)
    c_hi, c_lo = call(lambda *r: corner_kernel(plan, *r), (tiles, tiles), (xl, xh))
    cl, ch = shift(c_hi, "gy", 1), shift(c_lo, "gy", -1)
    return xl, xh, yl, yh, cl, ch


def messages(plan):
    x, y = shape(plan.x_planes, CY, NZ), shape(CX, plan.y_rows, NZ)
    return (x, x, y, y)


def body(populations, concentration, potential, permittivity, fluid_mask, owners):
    block, row = shape(CX, CY, NZ), shape(8, NZ)
    pops, both, four = shape(19, CX, CY, NZ), shape(2, CX, CY, NZ), shape(4, CX, CY, NZ)
    *sent, dm, _, fluid, owner = call(
        first_kernel, messages(ONE) + (four, block, block, row),
        (owners,) + tuple(pltpu.with_memory_space_constraint(v, pltpu.HBM) for v in (
            populations, concentration, potential, permittivity, fluid_mask)),
        (pops.shape, both.shape, block.shape, block.shape, pltpu.VMEM(block.shape, jnp.int32),
         pltpu.SemaphoreType.DMA((5,))),
        [SMEM] + [FAR] * 5)
    got = exchange(ONE, *sent)
    (owner_one,) = call(owner_kernel, (row,), (got[2],))
    owner_two = shift(owner_one, "gy", 1)
    pop, phi, conc, *rest = call(
        step_one_kernel,
        (pops, block, both) + messages(TWO) + (four, shape(6, *HALO), shape(*HALO), shape(*RIM)),
        (populations, concentration, potential, permittivity, dm, fluid, owner_two) + got,
        (HALO, block.shape) + FIELDS + ((5,) + RIM, (19,) + RIM))
    sent, (dm, coef, inv, fl) = rest[:4], rest[4:]
    got = exchange(TWO, *sent)
    phi, mine, sh = call(
        ions_two_kernel, (block, shape(2 * CX + 1, CY, NZ), shape(5, *RIM)),
        (conc, phi, dm, coef, inv, fl) + got, FIELDS)
    other = shift(mine, "gy", 1)
    (pop,) = call(flow_two_kernel, (pops,), (pop, fl, sh) + got, ((19,) + RIM,), flops=40_000_000)
    routed = call(route_kernel, (both, both, both), (mine, other, got[3], owner_two))
    came = [shift(v, "gy", d) for v, d in zip(routed, (2, 4, 6))]
    (migrated,) = call(arrive_kernel, (both,), (mine, other, *came, owner))
    return (pop, phi, migrated)


def solution(mesh):
    in_specs = (
        P(None, "gx", "gy", None),
        P(None, "gx", "gy", None),
        P("gx", "gy", None),
        P("gx", "gy", None),
        P("gx", "gy", None),
        P("gx", "gy"),
    )
    out_specs = (P(None, "gx", "gy", None), P("gx", "gy", None), P(None, "gx", "gy", None))
    return jax.shard_map(body, mesh=mesh, in_specs=in_specs, out_specs=out_specs, check_vma=False)
```

time: 108 us -> 81 us (0.75); the launches traced: 108 us -> 79.4 us
  local copies, waits for them, and re-layouts: 8.87 us -> 0.02 us
  between operations: 9.92 us -> 1.53 us
  blocking collectives: 7.61 us -> 0 us
  starting transfers between devices: 45.6 us -> 50.5 us
  Pallas kernels: 17 us -> 12.7 us
  waiting for transfers between devices: 17.7 us -> 14.7 us
    unnamed x18 -> x8, local copies, waits for them, and re-layouts: 8.87 us -> 0.02 us
    ppermute x15 -> x17, starting transfers between devices: 42.7 us -> 50.5 us  [shift(): return lax.ppermute(values, axis, [(i, (i + by) % n) for i in range(n)])]
    unnamed x1 -> x0, blocking collectives: 7.61 us -> none
    pallas_call x5 -> x9, Pallas kernels: 17 us -> 12.7 us  [call(): pl.pallas_call(kernel, out_shape=outs, in_specs=specs or [VMEM] * len(arg...]
    ppermute x15 -> x17, waiting for transfers between devices: 17.7 us -> 14.7 us  [shift(): return lax.ppermute(values, axis, [(i, (i + by) % n) for i in range(n)])]
    ppermute x1 -> x0, starting transfers between devices: 2.93 us -> none  [migrate(): mate = lax.ppermute(conc, 'gy', [(i, i ^ 1) for i in range(8)])]
  transfers between devices with their start and end apart: 16 -> 17, of which waited for: 10 -> 9; matrix products, arithmetic and copies ran while one was open for 2% -> 0% of each run, Pallas kernels for 0% -> 3%
where the time goes in v2:
time: 81 us; the launch traced here: 79.4 us
  starting transfers between devices  50.5 us (62%)
  waiting for transfers between devices  14.7 us (18%)
  Pallas kernels  12.7 us (16%)
  between operations  1.53 us (2%)
    ppermute x17, starting transfers between devices, shift(): return lax.ppermute(values, axis, [(i, (i + by) % n) for i in range(n)])  50.5 us
    ppermute x17, waiting for transfers between devices, shift(): return lax.ppermute(values, axis, [(i, (i + by) % n) for i in range(n)])  14.7 us
    pallas_call x9, Pallas kernels, call(): pl.pallas_call(kernel, out_shape=outs, in_specs=specs or [VMEM] * len(arg...  12.7 us
  transfers between devices with their start and end apart: 17, of which 9 were waited for; matrix products, arithmetic and copies ran while one was open for 0% of the time, Pallas kernels for 3%

profile of v2, /device:TPU:1, one launch (start us, length us, event | category | flops | bytes accessed | tf_op | source)
XLA Modules:
  0.0 79.4 jit_solution(13991929927362384942)
XLA Ops:
  0.6 0.0 copy-start.3
  0.6 0.0 copy-start.2
  0.7 0.0 copy-start.1
  0.7 0.0 copy-start
  1.4 2.2 %shard_map.85 = (f32[29,16,128]{2,1,0:T(8,128)S(1)}, f32[29,16,128]{2,1,0:T(8,128)S(1)}, f32[8,40,128]{2,1,0:T(8,128)S(1)}, f32[8,40,128]{2,1,0:T(8,128)S(1)}, f...) custom-call(s32[1,1]{1,0:T(1,128)S(6)} %copy.9.owner, ...), custom_call_target="tpu_custom_call" | custom-call | tf_op jit(solution)/shard_map/pallas_call | solution.py:428
  3.6 4.0 %collective-permute-start.2 = (f32[29,16,128]{2,1,0:T(8,128)S(1)}, f32[29,16,128]{2,1,0:T(8,128)S(1)}, u32[]{:S(2)}, u32[]{:S(2)}) collective-permute-start(f32[29,16,128]{2,1,0:T(8,128)S(1)} %get-tuple-element.34), channel_id=1, source_target_pairs={{0,8},{8,16},{16,24},{24,32},{32,40},{40,48},{48,56},{56,64},{64,7... | collective-permute-start | bytes 712712 | tf_op jit(solution)/shard_map/ppermute | solution.py:446
  7.7 15.9 %collective-permute-start.3 = (f32[29,16,128]{2,1,0:T(8,128)S(1)}, f32[29,16,128]{2,1,0:T(8,128)S(1)}, u32[]{:S(2)}, u32[]{:S(2)}) collective-permute-start(f32[29,16,128]{2,1,0:T(8,128)S(1)} %get-tuple-element.35), channel_id=1, source_target_pairs={{0,760},{8,0},{16,8},{24,16},{32,24},{40,32},{48,40},{56,48},{64,5... | collective-permute-start | bytes 712712 | tf_op jit(solution)/shard_map/ppermute | solution.py:446
  23.6 2.1 %collective-permute-start = (f32[8,40,128]{2,1,0:T(8,128)S(1)}, f32[8,40,128]{2,1,0:T(8,128)S(1)}, u32[]{:S(2)}, u32[]{:S(2)}) collective-permute-start(f32[8,40,128]{2,1,0:T(8,128)S(1)} %get-tuple-element.33), channel_id=1, source_target_pairs={{0,1},{1,2},{2,3},{3,4},{4,5},{5,6},{6,7},{7,0},{8,9},{9,10},{10,1... | collective-permute-start | bytes 491528 | tf_op jit(solution)/shard_map/ppermute | solution.py:446
  25.7 0.0 collective-permute-start.4
  25.7 1.5 %collective-permute-done.2.r_0_.xl = f32[29,16,128]{2,1,0:T(8,128)S(1)} collective-permute-done((f32[29,16,128]{2,1,0:T(8,128)S(1)}, f32[29,16,128]{2,1,0:T(8,128)S(1)}, u32[]{:S(2)}, u32[]{:S(2)}) %collective-permute-start.2) | collective-permute-done | bytes 237600 | tf_op jit(solution)/shard_map/ppermute | solution.py:446
  27.1 0.9 %collective-permute-done.3.r_1_.xh = f32[29,16,128]{2,1,0:T(8,128)S(1)} collective-permute-done((f32[29,16,128]{2,1,0:T(8,128)S(1)}, f32[29,16,128]{2,1,0:T(8,128)S(1)}, u32[]{:S(2)}, u32[]{:S(2)}) %collective-permute-start.3) | collective-permute-done | bytes 237600 | tf_op jit(solution)/shard_map/ppermute | solution.py:446
  28.0 2.7 %collective-permute-start.5 = (f32[2,18,8,128]{3,2,1,0:T(8,128)S(1)}, f32[2,18,8,128]{3,2,1,0:T(8,128)S(1)}, u32[]{:S(2)}, u32[]{:S(2)}) collective-permute-start(f32[2,18,8,128]{3,2,1,0:T(8,128)S(1)} %get-tuple-element.37), channel_id=1, source_target_pairs={{0,1},{1,2},{2,3},{3,4},{4,5},{5,6},{6,7},{7,0},{8,9},{9,10},{10,1... | collective-permute-start | bytes 442376 | tf_op jit(solution)/shard_map/ppermute | solution.py:446
  30.7 0.0 collective-permute-start.6
  30.7 0.0 collective-permute-done.yl
  30.7 1.7 %collective-permute-start.1 = (f32[8,128]{1,0:T(8,128)S(1)}, f32[8,128]{1,0:T(8,128)S(1)}, u32[]{:S(2)}, u32[]{:S(2)}) collective-permute-start(f32[8,128]{1,0:T(8,128)S(1)} %shard_map.86), channel_id=1, source_target_pairs={{0,1},{1,2},{2,3},{3,4},{4,5},{5,6},{6,7},{7,0},{8,9},{9,10},{10,1... | collective-permute-start | bytes 12296 | tf_op jit(solution)/shard_map/ppermute | solution.py:446
  32.5 0.0 collective-permute-done.4.yh
  32.5 0.8 collective-permute-done.1.owner_two
  33.2 0.0 collective-permute-done.5.cl
  33.2 2.0 %collective-permute-done.6.ch = f32[2,18,8,128]{3,2,1,0:T(8,128)S(1)} collective-permute-done((f32[2,18,8,128]{3,2,1,0:T(8,128)S(1)}, f32[2,18,8,128]{3,2,1,0:T(8,128)S(1)}, u32[]{:S(2)}, u32[]{:S(2)}) %collective-permute-start.6) | collective-permute-done | bytes 147488 | tf_op jit(solution)/shard_map/ppermute | solution.py:446
  35.3 0.0 copy-done.3
  35.3 0.0 copy-done.2
  35.3 0.0 copy-done.1
  35.3 0.0 copy-done
  35.3 4.3 %shard_map.88 = (f32[19,8,16,128]{3,2,1,0:T(8,128)S(1)}, f32[8,16,128]{2,1,0:T(8,128)S(1)}, f32[2,8,16,128]{3,2,1,0:T(8,128)S(1)}, f32[22,16,128]{2,1,0:T(8,128)...) custom-call(f32[19,8,16,128]{3,2,1,0:T(8,128)S(1)} %copy-done, ...), custom_call_target="tpu_custom_call" | custom-call | tf_op jit(solution)/shard_map/pallas_call | solution.py:428
  39.6 1.9 %collective-permute-start.7 = (f32[22,16,128]{2,1,0:T(8,128)S(1)}, f32[22,16,128]{2,1,0:T(8,128)S(1)}, u32[]{:S(2)}, u32[]{:S(2)}) collective-permute-start(f32[22,16,128]{2,1,0:T(8,128)S(1)} %get-tuple-element.46), channel_id=1, source_target_pairs={{0,8},{8,16},{16,24},{24,32},{32,40},{40,48},{48,56},{56,64},{64,7... | collective-permute-start | bytes 540680 | tf_op jit(solution)/shard_map/ppermute | solution.py:446
  41.6 7.4 %collective-permute-start.8 = (f32[22,16,128]{2,1,0:T(8,128)S(1)}, f32[22,16,128]{2,1,0:T(8,128)S(1)}, u32[]{:S(2)}, u32[]{:S(2)}) collective-permute-start(f32[22,16,128]{2,1,0:T(8,128)S(1)} %get-tuple-element.47), channel_id=1, source_target_pairs={{0,760},{8,0},{16,8},{24,16},{32,24},{40,32},{48,40},{56,48},{64,5... | collective-permute-start | bytes 540680 | tf_op jit(solution)/shard_map/ppermute | solution.py:446
  49.0 0.5 collective-permute-start.9
  49.5 1.3 %collective-permute-start.10 = (f32[8,32,128]{2,1,0:T(8,128)S(1)}, f32[8,32,128]{2,1,0:T(8,128)S(1)}, u32[]{:S(2)}, u32[]{:S(2)}) collective-permute-start(f32[8,32,128]{2,1,0:T(8,128)S(1)} %get-tuple-element.49), channel_id=1, source_target_pairs={{0,7},{1,0},{2,1},{3,2},{4,3},{5,4},{6,5},{7,6},{8,15},{9,8},{10,9... | collective-permute-start | bytes 393224 | tf_op jit(solution)/shard_map/ppermute | solution.py:446
  50.9 0.0 collective-permute-done.7.r_0_.xl
  50.9 0.5 collective-permute-done.8.r_1_.xh
  51.5 2.7 %collective-permute-start.11 = (f32[2,12,8,128]{3,2,1,0:T(8,128)S(1)}, f32[2,12,8,128]{3,2,1,0:T(8,128)S(1)}, u32[]{:S(2)}, u32[]{:S(2)}) collective-permute-start(f32[2,12,8,128]{3,2,1,0:T(8,128)S(1)} %get-tuple-element.50), channel_id=1, source_target_pairs={{0,1},{1,2},{2,3},{3,4},{4,5},{5,6},{6,7},{7,0},{8,9},{9,10},{10,1... | collective-permute-start | bytes 294920 | tf_op jit(solution)/shard_map/ppermute | solution.py:446
  54.2 0.0 collective-permute-start.12
  54.2 0.0 collective-permute-done.9.yl
  54.2 0.0 collective-permute-done.10.yh
  54.2 1.6 %collective-permute-done.11.cl = f32[2,12,8,128]{3,2,1,0:T(8,128)S(1)} collective-permute-done((f32[2,12,8,128]{3,2,1,0:T(8,128)S(1)}, f32[2,12,8,128]{3,2,1,0:T(8,128)S(1)}, u32[]{:S(2)}, u32[]{:S(2)}) %collective-permute-start.11) | collective-permute-done | bytes 98336 | tf_op jit(solution)/shard_map/ppermute | solution.py:446
  55.8 2.7 %collective-permute-done.12.ch = f32[2,12,8,128]{3,2,1,0:T(8,128)S(1)} collective-permute-done((f32[2,12,8,128]{3,2,1,0:T(8,128)S(1)}, f32[2,12,8,128]{3,2,1,0:T(8,128)S(1)}, u32[]{:S(2)}, u32[]{:S(2)}) %collective-permute-start.12) | collective-permute-done | bytes 98336 | tf_op jit(solution)/shard_map/ppermute | solution.py:446
  58.5 3.3 %shard_map.90 = (f32[8,16,128]{2,1,0:T(8,128)}, f32[17,16,128]{2,1,0:T(8,128)S(1)}, f32[5,10,32,128]{3,2,1,0:T(8,128)S(1)}) custom-call(f32[2,8,16,128]{3,2,1,0:T(8,128)S(1)} %get-tuple-element.41.conc, f32[8,16,128]{2,1,0:T(8,128)S(1)} %get-tuple-element.42.phi, f32[4,8,16,128]{3,2,1,0:T(8,128)S(1)} %get-tuple-element.43.dm, ...), custom_call_target="tpu_custom_call" | custom-call | tf_op jit(solution)/shard_map/pallas_call | solution.py:428
  61.8 0.0 collective-permute-start.13
  61.8 2.0 %collective-permute-done.13.other = f32[17,16,128]{2,1,0:T(8,128)S(1)} collective-permute-done((f32[17,16,128]{2,1,0:T(8,128)S(1)}, f32[17,16,128]{2,1,0:T(8,128)S(1)}, u32[]{:S(2)}, u32[]{:S(2)}) %collective-permute-start.13) | collective-permute-done | bytes 139296 | tf_op jit(solution)/shard_map/ppermute | solution.py:446
  63.9 3.0 %collective-permute-start.14 = (f32[2,8,16,128]{3,2,1,0:T(8,128)S(1)}, f32[2,8,16,128]{3,2,1,0:T(8,128)S(1)}, u32[]{:S(2)}, u32[]{:S(2)}) collective-permute-start(f32[2,8,16,128]{3,2,1,0:T(8,128)S(1)} %get-tuple-element.55), channel_id=1, source_target_pairs={{0,2},{1,3},{2,4},{3,5},{4,6},{5,7},{6,0},{7,1},{8,10},{9,11},{10,... | collective-permute-start | bytes 393224 | tf_op jit(solution)/shard_map/ppermute | solution.py:446
  66.9 5.2 %collective-permute-start.15 = (f32[2,8,16,128]{3,2,1,0:T(8,128)S(1)}, f32[2,8,16,128]{3,2,1,0:T(8,128)S(1)}, u32[]{:S(2)}, u32[]{:S(2)}) collective-permute-start(f32[2,8,16,128]{3,2,1,0:T(8,128)S(1)} %get-tuple-element.56), channel_id=1, source_target_pairs={{0,4},{1,5},{2,6},{3,7},{4,0},{5,1},{6,2},{7,3},{8,12},{9,13},{10,... | collective-permute-start | bytes 393224 | tf_op jit(solution)/shard_map/ppermute | solution.py:446
  72.1 1.9 %collective-permute-start.16 = (f32[2,8,16,128]{3,2,1,0:T(8,128)S(1)}, f32[2,8,16,128]{3,2,1,0:T(8,128)S(1)}, u32[]{:S(2)}, u32[]{:S(2)}) collective-permute-start(f32[2,8,16,128]{3,2,1,0:T(8,128)S(1)} %get-tuple-element.57), channel_id=1, source_target_pairs={{0,6},{1,7},{2,0},{3,1},{4,2},{5,3},{6,4},{7,5},{8,14},{9,15},{10,... | collective-permute-start | bytes 393224 | tf_op jit(solution)/shard_map/ppermute | solution.py:446
  74.0 2.1 %shard_map.91 = f32[19,8,16,128]{3,2,1,0:T(8,128)} custom-call(f32[19,8,16,128]{3,2,1,0:T(8,128)S(1)} %get-tuple-element.39.pop, f32[10,32,128]{2,1,0:T(8,128)S(1)} %get-tuple-element.40.fl, f32[5,10,32,128]{3,2,1,0:T(8,128)S(1)} %get-tuple-element.52.sh, f32[22,16,128]{2,1,0:T(8,128)S(1)} %collective-permute-done.7.r_0_.xl, ...), custom_call_target="tpu_custom_call" | custom-call | flops 40000000 | tf_op jit(solution)/shard_map/pallas_call | solution.py:428
  76.1 0.0 collective-permute-done.14.one
  76.1 0.0 collective-permute-done.15.two
  76.1 2.6 %collective-permute-done.16.three = f32[2,8,16,128]{3,2,1,0:T(8,128)S(1)} collective-permute-done((f32[2,8,16,128]{3,2,1,0:T(8,128)S(1)}, f32[2,8,16,128]{3,2,1,0:T(8,128)S(1)}, u32[]{:S(2)}, u32[]{:S(2)}) %collective-permute-start.16) | collective-permute-done | bytes 131104 | tf_op jit(solution)/shard_map/ppermute | solution.py:446
  78.7 0.7 shard_map.93
  (4 shorter events, 0.1 us)
Async XLA Ops:
  0.6 34.6 %copy-start.3 = (f32[8,16,128]{2,1,0:T(8,128)S(1)}, f32[8,16,128]{2,1,0:T(8,128)}, u32[]{:S(2)}) copy-start(f32[8,16,128]{2,1,0:T(8,128)} %perm.1) | copy-start | bytes 196612
  0.6 34.6 %copy-start.2 = (f32[8,16,128]{2,1,0:T(8,128)S(1)}, f32[8,16,128]{2,1,0:T(8,128)}, u32[]{:S(2)}) copy-start(f32[8,16,128]{2,1,0:T(8,128)} %phi.1) | copy-start | bytes 196612
  0.7 34.6 %copy-start.1 = (f32[2,8,16,128]{3,2,1,0:T(8,128)S(1)}, f32[2,8,16,128]{3,2,1,0:T(8,128)}, u32[]{:S(2)}) copy-start(f32[2,8,16,128]{3,2,1,0:T(8,128)} %conc.1) | copy-start | bytes 393220
  0.7 34.6 %copy-start = (f32[19,8,16,128]{3,2,1,0:T(8,128)S(1)}, f32[19,8,16,128]{3,2,1,0:T(8,128)}, u32[]{:S(2)}) copy-start(f32[19,8,16,128]{3,2,1,0:T(8,128)} %pop.1) | copy-start | bytes 3735556
  3.6 23.5 %collective-permute-start.2 = (f32[29,16,128]{2,1,0:T(8,128)S(1)}, f32[29,16,128]{2,1,0:T(8,128)S(1)}, u32[]{:S(2)}, u32[]{:S(2)}) collective-permute-start(f32[29,16,128]{2,1,0:T(8,128)S(1)} %get-tuple-element.34), channel_id=1, source_target_pairs={{0,8},{8,16},{16,24},{24,32},{32,40},{40,48},{48,56},{56,64},{64,7... | collective-permute-start | bytes 712712 | tf_op jit(solution)/shard_map/ppermute | solution.py:446
  7.7 20.4 %collective-permute-start.3 = (f32[29,16,128]{2,1,0:T(8,128)S(1)}, f32[29,16,128]{2,1,0:T(8,128)S(1)}, u32[]{:S(2)}, u32[]{:S(2)}) collective-permute-start(f32[29,16,128]{2,1,0:T(8,128)S(1)} %get-tuple-element.35), channel_id=1, source_target_pairs={{0,760},{8,0},{16,8},{24,16},{32,24},{40,32},{48,40},{56,48},{64,5... | collective-permute-start | bytes 712712 | tf_op jit(solution)/shard_map/ppermute | solution.py:446
  23.6 7.1 %collective-permute-start = (f32[8,40,128]{2,1,0:T(8,128)S(1)}, f32[8,40,128]{2,1,0:T(8,128)S(1)}, u32[]{:S(2)}, u32[]{:S(2)}) collective-permute-start(f32[8,40,128]{2,1,0:T(8,128)S(1)} %get-tuple-element.33), channel_id=1, source_target_pairs={{0,1},{1,2},{2,3},{3,4},{4,5},{5,6},{6,7},{7,0},{8,9},{9,10},{10,1... | collective-permute-start | bytes 491528 | tf_op jit(solution)/shard_map/ppermute | solution.py:446
  25.7 6.8 %collective-permute-start.4 = (f32[8,40,128]{2,1,0:T(8,128)S(1)}, f32[8,40,128]{2,1,0:T(8,128)S(1)}, u32[]{:S(2)}, u32[]{:S(2)}) collective-permute-start(f32[8,40,128]{2,1,0:T(8,128)S(1)} %get-tuple-element.36), channel_id=1, source_target_pairs={{0,7},{1,0},{2,1},{3,2},{4,3},{5,4},{6,5},{7,6},{8,15},{9,8},{10,9... | collective-permute-start | bytes 491528 | tf_op jit(solution)/shard_map/ppermute | solution.py:446
  28.0 5.2 %collective-permute-start.5 = (f32[2,18,8,128]{3,2,1,0:T(8,128)S(1)}, f32[2,18,8,128]{3,2,1,0:T(8,128)S(1)}, u32[]{:S(2)}, u32[]{:S(2)}) collective-permute-start(f32[2,18,8,128]{3,2,1,0:T(8,128)S(1)} %get-tuple-element.37), channel_id=1, source_target_pairs={{0,1},{1,2},{2,3},{3,4},{4,5},{5,6},{6,7},{7,0},{8,9},{9,10},{10,1... | collective-permute-start | bytes 442376 | tf_op jit(solution)/shard_map/ppermute | solution.py:446
  30.7 4.6 %collective-permute-start.6 = (f32[2,18,8,128]{3,2,1,0:T(8,128)S(1)}, f32[2,18,8,128]{3,2,1,0:T(8,128)S(1)}, u32[]{:S(2)}, u32[]{:S(2)}) collective-permute-start(f32[2,18,8,128]{3,2,1,0:T(8,128)S(1)} %get-tuple-element.38), channel_id=1, source_target_pairs={{0,7},{1,0},{2,1},{3,2},{4,3},{5,4},{6,5},{7,6},{8,15},{9,8},{10,9... | collective-permute-start | bytes 442376 | tf_op jit(solution)/shard_map/ppermute | solution.py:446
  30.7 2.5 %collective-permute-start.1 = (f32[8,128]{1,0:T(8,128)S(1)}, f32[8,128]{1,0:T(8,128)S(1)}, u32[]{:S(2)}, u32[]{:S(2)}) collective-permute-start(f32[8,128]{1,0:T(8,128)S(1)} %shard_map.86), channel_id=1, source_target_pairs={{0,1},{1,2},{2,3},{3,4},{4,5},{5,6},{6,7},{7,0},{8,9},{9,10},{10,1... | collective-permute-start | bytes 12296 | tf_op jit(solution)/shard_map/ppermute | solution.py:446
  39.6 11.2 %collective-permute-start.7 = (f32[22,16,128]{2,1,0:T(8,128)S(1)}, f32[22,16,128]{2,1,0:T(8,128)S(1)}, u32[]{:S(2)}, u32[]{:S(2)}) collective-permute-start(f32[22,16,128]{2,1,0:T(8,128)S(1)} %get-tuple-element.46), channel_id=1, source_target_pairs={{0,8},{8,16},{16,24},{24,32},{32,40},{40,48},{48,56},{56,64},{64,7... | collective-permute-start | bytes 540680 | tf_op jit(solution)/shard_map/ppermute | solution.py:446
  41.6 9.9 %collective-permute-start.8 = (f32[22,16,128]{2,1,0:T(8,128)S(1)}, f32[22,16,128]{2,1,0:T(8,128)S(1)}, u32[]{:S(2)}, u32[]{:S(2)}) collective-permute-start(f32[22,16,128]{2,1,0:T(8,128)S(1)} %get-tuple-element.47), channel_id=1, source_target_pairs={{0,760},{8,0},{16,8},{24,16},{32,24},{40,32},{48,40},{56,48},{64,5... | collective-permute-start | bytes 540680 | tf_op jit(solution)/shard_map/ppermute | solution.py:446
  49.0 5.2 %collective-permute-start.9 = (f32[8,32,128]{2,1,0:T(8,128)S(1)}, f32[8,32,128]{2,1,0:T(8,128)S(1)}, u32[]{:S(2)}, u32[]{:S(2)}) collective-permute-start(f32[8,32,128]{2,1,0:T(8,128)S(1)} %get-tuple-element.48), channel_id=1, source_target_pairs={{0,1},{1,2},{2,3},{3,4},{4,5},{5,6},{6,7},{7,0},{8,9},{9,10},{10,1... | collective-permute-start | bytes 393224 | tf_op jit(solution)/shard_map/ppermute | solution.py:446
  49.5 4.6 %collective-permute-start.10 = (f32[8,32,128]{2,1,0:T(8,128)S(1)}, f32[8,32,128]{2,1,0:T(8,128)S(1)}, u32[]{:S(2)}, u32[]{:S(2)}) collective-permute-start(f32[8,32,128]{2,1,0:T(8,128)S(1)} %get-tuple-element.49), channel_id=1, source_target_pairs={{0,7},{1,0},{2,1},{3,2},{4,3},{5,4},{6,5},{7,6},{8,15},{9,8},{10,9... | collective-permute-start | bytes 393224 | tf_op jit(solution)/shard_map/ppermute | solution.py:446
  51.5 4.4 %collective-permute-start.11 = (f32[2,12,8,128]{3,2,1,0:T(8,128)S(1)}, f32[2,12,8,128]{3,2,1,0:T(8,128)S(1)}, u32[]{:S(2)}, u32[]{:S(2)}) collective-permute-start(f32[2,12,8,128]{3,2,1,0:T(8,128)S(1)} %get-tuple-element.50), channel_id=1, source_target_pairs={{0,1},{1,2},{2,3},{3,4},{4,5},{5,6},{6,7},{7,0},{8,9},{9,10},{10,1... | collective-permute-start | bytes 294920 | tf_op jit(solution)/shard_map/ppermute | solution.py:446
  54.2 4.3 %collective-permute-start.12 = (f32[2,12,8,128]{3,2,1,0:T(8,128)S(1)}, f32[2,12,8,128]{3,2,1,0:T(8,128)S(1)}, u32[]{:S(2)}, u32[]{:S(2)}) collective-permute-start(f32[2,12,8,128]{3,2,1,0:T(8,128)S(1)} %get-tuple-element.51), channel_id=1, source_target_pairs={{0,7},{1,0},{2,1},{3,2},{4,3},{5,4},{6,5},{7,6},{8,15},{9,8},{10,9... | collective-permute-start | bytes 294920 | tf_op jit(solution)/shard_map/ppermute | solution.py:446
  61.8 2.0 %collective-permute-start.13 = (f32[17,16,128]{2,1,0:T(8,128)S(1)}, f32[17,16,128]{2,1,0:T(8,128)S(1)}, u32[]{:S(2)}, u32[]{:S(2)}) collective-permute-start(f32[17,16,128]{2,1,0:T(8,128)S(1)} %get-tuple-element.54.mine), channel_id=1, source_target_pairs={{0,1},{1,2},{2,3},{3,4},{4,5},{5,6},{6,7},{7,0},{8,9},{9,10},{10,1... | collective-permute-start | bytes 417800 | tf_op jit(solution)/shard_map/ppermute | solution.py:446
  63.9 12.2 %collective-permute-start.14 = (f32[2,8,16,128]{3,2,1,0:T(8,128)S(1)}, f32[2,8,16,128]{3,2,1,0:T(8,128)S(1)}, u32[]{:S(2)}, u32[]{:S(2)}) collective-permute-start(f32[2,8,16,128]{3,2,1,0:T(8,128)S(1)} %get-tuple-element.55), channel_id=1, source_target_pairs={{0,2},{1,3},{2,4},{3,5},{4,6},{5,7},{6,0},{7,1},{8,10},{9,11},{10,... | collective-permute-start | bytes 393224 | tf_op jit(solution)/shard_map/ppermute | solution.py:446
  66.9 9.2 %collective-permute-start.15 = (f32[2,8,16,128]{3,2,1,0:T(8,128)S(1)}, f32[2,8,16,128]{3,2,1,0:T(8,128)S(1)}, u32[]{:S(2)}, u32[]{:S(2)}) collective-permute-start(f32[2,8,16,128]{3,2,1,0:T(8,128)S(1)} %get-tuple-element.56), channel_id=1, source_target_pairs={{0,4},{1,5},{2,6},{3,7},{4,0},{5,1},{6,2},{7,3},{8,12},{9,13},{10,... | collective-permute-start | bytes 393224 | tf_op jit(solution)/shard_map/ppermute | solution.py:446
  72.1 6.6 %collective-permute-start.16 = (f32[2,8,16,128]{3,2,1,0:T(8,128)S(1)}, f32[2,8,16,128]{3,2,1,0:T(8,128)S(1)}, u32[]{:S(2)}, u32[]{:S(2)}) collective-permute-start(f32[2,8,16,128]{3,2,1,0:T(8,128)S(1)} %get-tuple-element.57), channel_id=1, source_target_pairs={{0,6},{1,7},{2,0},{3,1},{4,2},{5,3},{6,4},{7,5},{8,14},{9,15},{10,... | collective-permute-start | bytes 393224 | tf_op jit(solution)/shard_map/ppermute | solution.py:446

commit v3 on v2

v3 whole, which is shorter than its diff:
```python
import jax
import jax.numpy as jnp
from jax import lax
from jax.experimental import pallas as pl
from jax.experimental.pallas import tpu as pltpu
from jax.sharding import PartitionSpec as P

STEPS = 2
SWEEPS = 4
VEL = (
    (0, 0, 0), (1, 0, 0), (-1, 0, 0), (0, 1, 0), (0, -1, 0), (0, 0, 1), (0, 0, -1),
    (1, 1, 0), (-1, -1, 0), (1, -1, 0), (-1, 1, 0), (1, 0, 1), (-1, 0, -1), (1, 0, -1),
    (-1, 0, 1), (0, 1, 1), (0, -1, -1), (0, 1, -1), (0, -1, 1),
)
WEIGHT = (1.0 / 3.0,) + (1.0 / 18.0,) * 6 + (1.0 / 36.0,) * 12
OPP = (0, 2, 1, 4, 3, 6, 5, 8, 7, 10, 9, 12, 11, 14, 13, 16, 15, 18, 17)
TAU = 0.8
COUPLING = 0.05
DRIVE = 0.001
DIFF = (0.1, 0.15)
VALENCE = (1.0, -1.0)

CX, CY, NZ = 8, 16, 128
EX, EY = 20, 32
F32 = jnp.float32

X_IN_LO = tuple(i for i in range(19) if VEL[i][0] == 1)
X_IN_HI = tuple(i for i in range(19) if VEL[i][0] == -1)
Y_IN_LO = tuple(i for i in range(19) if VEL[i][1] == 1)
Y_IN_HI = tuple(i for i in range(19) if VEL[i][1] == -1)
LO_LO, HI_LO = VEL.index((1, 1, 0)), VEL.index((-1, 1, 0))
LO_HI, HI_HI = VEL.index((1, -1, 0)), VEL.index((-1, -1, 0))


def shape(*dims):
    return jax.ShapeDtypeStruct(dims, F32)


def turn(v, by, axis):
    return pltpu.roll(v, by % v.shape[axis], axis)


class Plan:
    def __init__(self, first):
        self.first = first
        rows = [("phi", 6)] + [("perm", 6)] * first + [("charge", 4), ("conc", 2)] + [("fluid", 1)] * first
        self.y = {}
        at = 0
        for name, n in rows + [("pop", 5), ("dm", 4), ("owner", 1)]:
            self.y[name] = at
            at += n
        self.y_rows = -(-at // 8) * 8
        self.skip = 0 if first else 2
        planes = [("phi", 6 - self.skip)] + [("perm", 6)] * first + [("charge", 4), ("conc", 2)]
        planes += [("fluid", 1)] * first + [("pop", 5), ("dm", 4), ("cphi", 3)]
        planes += [("cperm", 3)] * first + [("ccharge", 2), ("cmisc", 1)]
        self.x = {}
        at = 0
        for name, n in planes:
            self.x[name] = at
            at += n
        self.x_planes = at


ONE, TWO = Plan(True), Plan(False)
DEEP = ((1, 6, 6, 1), (2, 5, 5, 2), (3, 4, 4, 3))
CHARGE = ((1, 5, 4, 2), (2, 4, 3, 3))


def pack_y(plan, out, low, owner, phi, charge, conc, pop, dm, perm=None, fluid=None):
    y = plan.y
    six = slice(0, 6) if low else slice(10, 16)
    four = slice(1, 5) if low else slice(11, 15)
    row = slice(0, 1) if low else slice(15, 16)
    out[:, 0:6] = phi[:, six]
    if plan.first:
        out[:, y["perm"] : y["perm"] + 6] = perm[:, six]
        out[:, y["fluid"] : y["fluid"] + 1] = fluid[:, row]
    out[:, y["charge"] : y["charge"] + 4] = charge[:, four]
    for s in range(2):
        out[:, y["conc"] + s : y["conc"] + s + 1] = conc[s, :, row]
    for k, i in enumerate(Y_IN_HI if low else Y_IN_LO):
        out[:, y["pop"] + k : y["pop"] + k + 1] = pop[i, :, row]
    for k in range(4):
        out[:, y["dm"] + k : y["dm"] + k + 1] = dm[k, :, row]
    out[0, y["owner"] : y["owner"] + 1] = owner


def pack_x(plan, out, low, yl, yh, phi, charge, conc, pop, dm, perm=None, fluid=None):
    x, y = plan.x, plan.y

    def at(depth):
        return depth - 1 if low else CX - depth

    def spread(to, field, first, last):
        lo = min(at(first), at(last))
        out[to : to + last - first + 1] = field[lo : lo + last - first + 1]

    spread(0, phi, 1 + plan.skip, 6)
    spread(x["charge"], charge, 2, 5)
    edge = at(1)
    for s in range(2):
        out[x["conc"] + s] = conc[s, edge]
    if plan.first:
        spread(x["perm"], perm, 1, 6)
        out[x["fluid"]] = fluid[edge]
    for k, i in enumerate(X_IN_HI if low else X_IN_LO):
        out[x["pop"] + k] = pop[i, edge]
    for k in range(4):
        out[x["dm"] + k] = dm[k, edge]
    for name in ("phi", "perm")[: 1 + plan.first]:
        for k, (d, n, e, m) in enumerate(DEEP):
            c, r = x["c" + name] + k, y[name]
            out[c, 8 - n : 8] = yl[at(d), r + 6 - n : r + 6]
            out[c, 0:m] = yl[at(e), r + 6 - m : r + 6]
            out[c, 8 : 8 + n] = yh[at(d), r : r + n]
            out[c, 16 - m : 16] = yh[at(e), r : r + m]
    q, o = y["charge"], y["conc"]

    def near(msg, depth):
        return msg[at(depth), o : o + 1] - msg[at(depth), o + 1 : o + 2]

    for k, (d, n, e, m) in enumerate(CHARGE):
        c = x["ccharge"] + k
        out[c, 8 - n : 7] = yl[at(d), q + 5 - n : q + 4]
        out[c, 7:8] = near(yl, d)
        out[c, 0 : m - 1] = yl[at(e), q + 5 - m : q + 4]
        out[c, m - 1 : m] = near(yl, e)
        out[c, 8:9] = near(yh, d)
        out[c, 9 : 8 + n] = yh[at(d), q : q + n - 1]
        out[c, 16 - m : 17 - m] = near(yh, e)
        out[c, 17 - m : 16] = yh[at(e), q : q + m - 1]
    for r, msg, names, pick in ((0, yl, Y_IN_LO, HI_LO if low else LO_LO), (8, yh, Y_IN_HI, HI_HI if low else LO_HI)):
        take = [(1, y["pop"] + names.index(pick))] + [(2 + k, y["dm"] + k) for k in range(4)]
        if plan.first:
            take.append((0, y["fluid"]))
        for to, source in take:
            out[x["cmisc"], r + to : r + to + 1] = msg[edge, source : source + 1]
        out[x["cmisc"], r + 6 : r + 7] = near(msg, 5)


def lay(ext, own, name, depth, pairs, plan, xl, xh, yl, yh):
    x, y = plan.x, plan.y
    skip = plan.skip if name == "phi" else 0
    n = 6 - skip
    ext[6:14, 8:24] = own
    ext[0:n, 8:24] = xl[x[name] : x[name] + n]
    ext[14 + skip : 20, 8:24] = xh[x[name] : x[name] + n]
    ext[6:14, 2:8] = yl[:, y[name] : y[name] + 6]
    ext[6:14, 24:30] = yh[:, y[name] : y[name] + 6]
    corners(ext, x["c" + name], pairs, xl, xh)


def corners(ext, at, pairs, xl, xh):
    for k, (d, n, e, m) in enumerate(pairs):
        for msg, p, q in ((xl, 6 - d, 6 - e), (xh, 13 + d, 13 + e)):
            ext[p, 8 - n : 8] = msg[at + k, 8 - n : 8]
            ext[q, 8 - m : 8] = msg[at + k, 0:m]
            ext[p, 24 : 24 + n] = msg[at + k, 8 : 8 + n]
            ext[q, 24 : 24 + m] = msg[at + k, 16 - m : 16]


def moments(load):
    dens = load(0)
    mom = [None, None, None]
    for i in range(1, 19):
        v = load(i)
        dens = dens + v
        for c in range(3):
            if VEL[i][c]:
                t = v if VEL[i][c] > 0 else -v
                mom[c] = t if mom[c] is None else mom[c] + t
    return [dens] + mom


def first_kernel(owner, *refs):
    far, near, sems = refs[:5], refs[11:16], refs[16]
    pop, conc, phi, perm, mask = near
    y_hi, y_lo, dm, charge, fluid, owner_row = refs[5:11]
    copies = [pltpu.make_async_copy(a, b, sems.at[k]) for k, (a, b) in enumerate(zip(far, near))]
    for copy in copies:
        copy.start()
    owner_row[...] = jnp.full((8, NZ), owner[0, 0], jnp.int32).astype(F32)
    for copy in copies:
        copy.wait()
    charge[...] = conc[0] - conc[1]
    fluid[...] = mask[...].astype(F32)

    def plane(x, _):
        for k, v in enumerate(moments(lambda i: pop[i, x])):
            dm[k, x] = v
        return 0

    lax.fori_loop(0, CX, plane, 0, unroll=2)
    for low, yo in ((False, y_hi), (True, y_lo)):
        pack_y(ONE, yo, low, owner_row[0:1], phi, charge, conc, pop, dm, perm, fluid)


def x_one_kernel(phi, charge, conc, pop, dm, perm, fluid, yl, yh, x_hi, x_lo, owner):
    for low, xo in ((False, x_hi), (True, x_lo)):
        pack_x(ONE, xo, low, yl, yh, phi, charge, conc, pop, dm, perm, fluid)
    owner[...] = jnp.broadcast_to(yl[0, ONE.y["owner"] : ONE.y["owner"] + 1], (8, NZ))


def x_two_kernel(phi, charge, conc, pop, dm, yl, yh, x_hi, x_lo):
    for low, xo in ((False, x_hi), (True, x_lo)):
        pack_x(TWO, xo, low, yl, yh, phi, charge, conc, pop, dm)


def lay_all(plan, phi, conc, dm, charge, msgs, pa, ce, dn, mm, cc):
    xl, xh, yl, yh = msgs
    x, y = plan.x, plan.y
    lay(pa, phi[...], "phi", 6, DEEP, plan, xl, xh, yl, yh)
    ce[6:14, 8:24] = charge[...]
    q = x["charge"]
    ce[1:5, 8:24] = xl[q : q + 4]
    ce[15:19, 8:24] = xh[q : q + 4]
    c = x["conc"]
    ce[5, 8:24] = xl[c] - xl[c + 1]
    ce[14, 8:24] = xh[c] - xh[c + 1]
    q, c = y["charge"], y["conc"]
    ce[6:14, 3:7] = yl[:, q : q + 4]
    ce[6:14, 7:8] = yl[:, c : c + 1] - yl[:, c + 1 : c + 2]
    ce[6:14, 24:25] = yh[:, c : c + 1] - yh[:, c + 1 : c + 2]
    ce[6:14, 25:29] = yh[:, q : q + 4]
    corners(ce, x["ccharge"], CHARGE, xl, xh)
    m = x["cmisc"]
    for msg, p in ((xl, 1), (xh, 18)):
        ce[p, 7:8] = msg[m, 6:7]
        ce[p, 24:25] = msg[m, 14:15]
    for s in range(2):
        cc[s, 1:9, 8:24] = conc[s]
        cc[s, 0, 8:24] = xl[x["conc"] + s]
        cc[s, 9, 8:24] = xh[x["conc"] + s]
        cc[s, 1:9, 7:8] = yl[:, c + s : c + s + 1]
        cc[s, 1:9, 24:25] = yh[:, c + s : c + s + 1]
    for k, ext in enumerate((dn, mm.at[0], mm.at[1], mm.at[2])):
        ext[1:9, 8:24] = dm[k]
        for msg, p in ((xl, 0), (xh, 9)):
            ext[p, 8:24] = msg[x["dm"] + k]
            ext[p, 7:8] = msg[m, 2 + k : 3 + k]
            ext[p, 24:25] = msg[m, 10 + k : 11 + k]
        for msg, r in ((yl, 7), (yh, 24)):
            ext[1:9, r : r + 1] = msg[:, y["dm"] + k : y["dm"] + k + 1]


LO_T, MID_T, HI_T = slice(0, 8), slice(8, 24), slice(24, 32)


def sweeps(coef, inv, ce, src, dst):
    for sweep in range(SWEEPS):

        def relax(x, _, src=src, dst=dst):
            mid = src[x]
            acc = ce[x] * inv[x]
            acc += coef[0, x] * src[x - 1] + coef[1, x] * src[x + 1]
            acc += coef[2, x] * turn(mid, 1, 0) + coef[3, x] * turn(mid, -1, 0)
            acc += coef[4, x] * turn(mid, 1, 1) + coef[5, x] * turn(mid, -1, 1)
            dst[x] = acc
            return 0

        lax.fori_loop(1 + sweep, 19 - sweep, relax, 0, unroll=6)
        src, dst = dst, src
    return src


def motion(fin, ce, fl, dn, mm, vel, sh):
    def plane(p, _):
        mid = fin[p + 5]
        grad = [
            -0.5 * (fin[p + 6] - fin[p + 4]),
            -0.5 * (turn(mid, -1, 0) - turn(mid, 1, 0)),
            -0.5 * (turn(mid, -1, 1) - turn(mid, 1, 1)),
        ]
        f = fl[p]
        scale = COUPLING * ce[p + 5]
        force = [f * (scale * g + d) if d else f * (scale * g) for g, d in zip(grad, (DRIVE, 0, 0))]
        dens = dn[p]
        over = 1.0 / dens
        mom = [mm[c, p] for c in range(3)]
        for c in range(3):
            vel[c, p] = f * (mom[c] + 0.5 * force[c]) * over
        u = [(mom[c] + TAU * force[c]) * over for c in range(3)]
        for c in range(3):
            sh[c, p] = u[c]
        sh[3, p] = 1.0 - 1.5 * (u[0] * u[0] + u[1] * u[1] + u[2] * u[2])
        sh[4, p] = dens * (1.0 / TAU)
        return 0

    lax.fori_loop(0, 10, plane, 0, unroll=2)


def ions(fin, fl, cc, vel, store):
    def flux(s, ca, cb, pot_a, pot_b, ua, ub, wall):
        total = ca + cb
        speed = 0.25 * (ua + ub) - (0.5 * DIFF[s] * VALENCE[s]) * (pot_b - pot_a)
        return wall * (total * speed - DIFF[s] * (cb - ca))

    def x_face(s, p):
        wall = fl[p, MID_T] * fl[p + 1, MID_T]
        return flux(s, cc[s, p, MID_T], cc[s, p + 1, MID_T], fin[p + 5, MID_T], fin[p + 6, MID_T],
                    vel[0, p, MID_T], vel[0, p + 1, MID_T], wall)

    def plane(p, before):
        after = []
        f, pot, vy = fl[p], fin[p + 5], vel[1, p]
        for s in range(2):
            face = x_face(s, p)
            total = face - before[s]
            after.append(face)
            c = cc[s, p]
            face = flux(s, c, turn(c, -1, 0), pot, turn(pot, -1, 0), vy, turn(vy, -1, 0), f * turn(f, -1, 0))
            total = total + (face - turn(face, 1, 0))[MID_T]
            fm, cm, pm, vz = f[MID_T], c[MID_T], pot[MID_T], vel[2, p, MID_T]
            face = flux(s, cm, turn(cm, -1, 1), pm, turn(pm, -1, 1), vz, turn(vz, -1, 1), fm * turn(fm, -1, 1))
            total = total + face - turn(face, 1, 1)
            store(s, p - 1, cm - total)
        return tuple(after)

    lax.fori_loop(1, 9, plane, (x_face(0, 0), x_face(1, 0)), unroll=4)


def collide_and_stream(plan, pop, fl, sh, msgs, lv, pop_out, dm_out):
    xl, xh, yl, yh = msgs
    y_pop, x_pop, misc = plan.y["pop"], plan.x["pop"], plan.x["cmisc"]
    bad = float("nan")

    def load(p, rows):
        return [sh[c, p, rows] for c in range(5)] + [fl[p, rows] != 0.0]

    def relaxed_of(i, pop_i, part):
        pr = None
        for c in range(3):
            if VEL[i][c]:
                t = part[c] if VEL[i][c] > 0 else -part[c]
                pr = t if pr is None else pr + t
        poly = part[3]
        if pr is not None:
            poly = poly + pr * (3.0 + 4.5 * pr)
        return (1.0 - 1.0 / TAU) * pop_i + (WEIGHT[i] * part[4]) * poly

    def collide(p, _):
        x = p - 1
        part = load(p, MID_T)
        wet = part[5]
        for i in range(19):
            j = OPP[i]
            if i > j:
                continue
            pi = pop[i, x]
            ri = relaxed_of(i, pi, part)
            if i == j:
                pop_out[i, x] = jnp.where(wet, ri, pi)
                continue
            pj = pop[j, x]
            rj = relaxed_of(j, pj, part)
            lv[i, p, MID_T] = jnp.where(wet, ri, bad)
            lv[j, p, MID_T] = jnp.where(wet, rj, bad)
            pop_out[i, x] = jnp.where(wet, rj, pi)
            pop_out[j, x] = jnp.where(wet, ri, pj)
        for y, names, r in ((yl, Y_IN_LO, 7), (yh, Y_IN_HI, 24)):
            row = slice(r, r + 1)
            part = load(p, row)
            for k, i in enumerate(names):
                value = relaxed_of(i, y[x, y_pop + k : y_pop + k + 1], part)
                lv[i, p, row] = jnp.where(part[5], value, bad)
        return 0

    lax.fori_loop(1, 9, collide, 0)
    for p, x, names, low_pop, high_pop in (
        (0, xl, X_IN_LO, LO_LO, LO_HI),
        (9, xh, X_IN_HI, HI_LO, HI_HI),
    ):
        part = load(p, MID_T)
        for k, i in enumerate(names):
            lv[i, p, MID_T] = jnp.where(part[5], relaxed_of(i, x[x_pop + k], part), bad)
        for c, r, i in ((1, 7, low_pop), (9, 24, high_pop)):
            row = slice(r, r + 1)
            part = load(p, row)
            lv[i, p, row] = jnp.where(part[5], relaxed_of(i, x[misc, c : c + 1], part), bad)

    def stream(x, _):
        wet = fl[x + 1, MID_T] != 0.0
        for i in range(1, 19):
            ex, ey, ez = VEL[i]
            came = lv[i, x + 1 - ex, 8 - ey : 24 - ey]
            if ez:
                came = turn(came, ez, 1)
            pop_out[i, x] = jnp.where(wet & (came == came), came, pop_out[i, x])
        if dm_out is not None:
            for k, v in enumerate(moments(lambda i: pop_out[i, x])):
                dm_out[k, x] = v
        return 0

    lax.fori_loop(0, CX, stream, 0, unroll=2)


def step_one_kernel(pop, conc, phi, perm, dm, charge, fluid, owner_two, yl, yh, xl, xh,
                    pop_out, phi_out, conc_out, charge_out, y_hi, y_lo, dm_out, rim, coef, inv, fl,
                    pe, pa, pb, ce, dn, mm, cc, vel, sh, lv):
    msgs = (xl, xh, yl, yh)
    lay(pe, perm[...], "perm", 6, DEEP, ONE, xl, xh, yl, yh)

    def coefs(x, _):
        mid = pe[x]
        faces = [0.5 * (mid + other) for other in (
            pe[x - 1], pe[x + 1], turn(mid, 1, 0), turn(mid, -1, 0), turn(mid, 1, 1), turn(mid, -1, 1))]
        over = 1.0 / (faces[0] + faces[1] + faces[2] + faces[3] + faces[4] + faces[5])
        inv[x] = over
        for k in range(6):
            coef[k, x] = faces[k] * over
        return 0

    lax.fori_loop(1, 19, coefs, 0, unroll=6)
    fl[1:9, 8:24] = fluid[...]
    x, y = ONE.x, ONE.y
    for msg, p in ((xl, 0), (xh, 9)):
        fl[p, 8:24] = msg[x["fluid"]]
        fl[p, 7:8] = msg[x["cmisc"], 0:1]
        fl[p, 24:25] = msg[x["cmisc"], 8:9]
    fl[1:9, 7:8] = yl[:, y["fluid"] : y["fluid"] + 1]
    fl[1:9, 24:25] = yh[:, y["fluid"] : y["fluid"] + 1]
    lay_all(ONE, phi, conc, dm, charge, msgs, pa, ce, dn, mm, cc)
    fin = sweeps(coef, inv, ce, pa, pb)
    phi_out[...] = fin[6:14, MID_T]
    rim[0:2] = fin[4:6, MID_T]
    rim[2:4] = fin[14:16, MID_T]
    motion(fin, ce, fl, dn, mm, vel, sh)

    def store(s, x, values):
        conc_out[s, x] = values

    ions(fin, fl, cc, vel, store)
    collide_and_stream(ONE, pop, fl, sh, msgs, lv, pop_out, dm_out)
    charge_out[...] = conc_out[0] - conc_out[1]
    above = yh[0, y["owner"] : y["owner"] + 1]
    for low, yo, owner in ((False, y_hi, owner_two[0:1]), (True, y_lo, above)):
        pack_y(TWO, yo, low, owner, phi_out, charge_out, conc_out, pop_out, dm_out)


def ions_two_kernel(conc, phi, charge, dm, rim, coef, inv, fl, yl, yh, xl, xh,
                    phi_out, slab, sh, pa, pb, ce, dn, mm, cc, vel):
    lay_all(TWO, phi, conc, dm, charge, (xl, xh, yl, yh), pa, ce, dn, mm, cc)
    pa[4:6, MID_T] = rim[0:2]
    pa[14:16, MID_T] = rim[2:4]
    fin = sweeps(coef, inv, ce, pa, pb)
    phi_out[...] = fin[6:14, MID_T]
    motion(fin, ce, fl, dn, mm, vel, sh)

    def store(s, x, values):
        slab[s * CX + x] = values

    ions(fin, fl, cc, vel, store)
    slab[2 * CX, 0:8] = jnp.broadcast_to(yl[0, TWO.y["owner"] : TWO.y["owner"] + 1], (8, NZ))


def flow_two_kernel(pop, fl, sh, yl, yh, xl, xh, pop_out, lv):
    collide_and_stream(TWO, pop, fl, sh, (xl, xh, yl, yh), lv, pop_out, None)


def route_kernel(mine, other, yh, owner, owner_two, out, wanted):
    me = lax.axis_index("gy")
    wanted[0] = owner[...]
    wanted[1, 0:1] = yh[0, TWO.y["owner"] : TWO.y["owner"] + 1]
    wanted[2] = other[2 * CX, 0:8]
    wanted[3] = owner_two[...]
    row = jnp.full((1, NZ), me, jnp.int32).astype(F32)
    for k in range(4):
        pick = wanted[lax.rem(k - me // 2 + 4, 4), 0:1] == row
        for x in range(2 * CX):
            out[k, x] = jnp.where(pick, mine[x], other[x])


def arrive_kernel(owner, came, out):
    me = lax.axis_index("gy")
    away = lax.rem(me - owner[0, 0] + 8, 8)
    out[...] = came[lax.rem(me // 2 - away // 2 + 4, 4)]


VMEM, FAR, SMEM = (pl.BlockSpec(memory_space=m) for m in (pltpu.VMEM, pltpu.HBM, pltpu.SMEM))


def call(kernel, outs, args, scratch=(), specs=None, flops=0):
    return pl.pallas_call(
        kernel,
        out_shape=outs,
        in_specs=specs or [VMEM] * len(args),
        out_specs=[VMEM] * len(outs),
        scratch_shapes=[pltpu.VMEM(s, F32) if isinstance(s, tuple) else s for s in scratch],
        compiler_params=pltpu.CompilerParams(vmem_limit_bytes=24 * 1024 * 1024),
        cost_estimate=pl.CostEstimate(flops=flops, bytes_accessed=0, transcendentals=0) if flops else None,
    )(*args)


HALO = (EX, EY, NZ)
RIM = (10, EY, NZ)
FIELDS = (HALO, HALO, HALO, RIM, (3,) + RIM, (2,) + RIM, (3,) + RIM)


def shift(values, axis, by):
    n = lax.axis_size(axis)
    return lax.ppermute(values, axis, [(i, (i + by) % n) for i in range(n)])


def body(populations, concentration, potential, permittivity, fluid_mask, owners):
    block, row = shape(CX, CY, NZ), shape(8, NZ)
    pops, both, four = shape(19, CX, CY, NZ), shape(2, CX, CY, NZ), shape(4, CX, CY, NZ)
    y_one, y_two = (shape(CX, plan.y_rows, NZ) for plan in (ONE, TWO))
    x_one, x_two = (shape(plan.x_planes, CY, NZ) for plan in (ONE, TWO))
    y_hi, y_lo, dm, charge, fluid, owner = call(
        first_kernel, (y_one, y_one, four, block, block, row),
        (owners,) + tuple(pltpu.with_memory_space_constraint(v, pltpu.HBM) for v in (
            populations, concentration, potential, permittivity, fluid_mask)),
        (pops.shape, both.shape, block.shape, block.shape, pltpu.VMEM(block.shape, jnp.int32),
         pltpu.SemaphoreType.DMA((5,))),
        [SMEM] + [FAR] * 5)
    yl, yh = shift(y_hi, "gy", 1), shift(y_lo, "gy", -1)
    x_hi, x_lo, owner_one = call(
        x_one_kernel, (x_one, x_one, row),
        (potential, charge, concentration, populations, dm, permittivity, fluid, yl, yh))
    owner_two = shift(owner_one, "gy", 1)
    xl, xh = shift(x_hi, "gx", 1), shift(x_lo, "gx", -1)
    pop, phi, conc, charge, y_hi, y_lo, dm, rim, coef, inv, fl = call(
        step_one_kernel,
        (pops, block, both, block, y_two, y_two, four, shape(4, CY, NZ), shape(6, *HALO), shape(*HALO), shape(*RIM)),
        (populations, concentration, potential, permittivity, dm, charge, fluid, owner_two, yl, yh, xl, xh),
        (HALO,) + FIELDS + ((5,) + RIM, (19,) + RIM))
    yl, yh = shift(y_hi, "gy", 1), shift(y_lo, "gy", -1)
    x_hi, x_lo = call(x_two_kernel, (x_two, x_two), (phi, charge, conc, pop, dm, yl, yh))
    xl, xh = shift(x_hi, "gx", 1), shift(x_lo, "gx", -1)
    phi, mine, sh = call(
        ions_two_kernel, (block, shape(2 * CX + 1, CY, NZ), shape(5, *RIM)),
        (conc, phi, charge, dm, rim, coef, inv, fl, yl, yh, xl, xh), FIELDS)
    other = shift(mine, "gy", 1)
    (pop,) = call(flow_two_kernel, (pops,), (pop, fl, sh, yl, yh, xl, xh), ((19,) + RIM,), flops=40_000_000)
    (routed,) = call(
        route_kernel, (shape(4, 2 * CX, CY, NZ),), (mine, other, yh, owner, owner_two), ((4, 8, NZ),))
    came = lax.all_to_all(
        routed, "gy", 0, 0, axis_index_groups=[[0, 2, 4, 6], [1, 3, 5, 7]], tiled=True)
    (migrated,) = call(arrive_kernel, (shape(2 * CX, CY, NZ),), (owners, came), (), [SMEM, VMEM])
    return (pop, phi, migrated.reshape(2, CX, CY, NZ))


def solution(mesh):
    in_specs = (
        P(None, "gx", "gy", None),
        P(None, "gx", "gy", None),
        P("gx", "gy", None),
        P("gx", "gy", None),
        P("gx", "gy", None),
        P("gx", "gy"),
    )
    out_specs = (P(None, "gx", "gy", None), P("gx", "gy", None), P(None, "gx", "gy", None))
    return jax.shard_map(body, mesh=mesh, in_specs=in_specs, out_specs=out_specs, check_vma=False)
```

time: 81 us -> 79.7 us (0.984)
  the two profiles are of different devices: /device:TPU:1 before, /device:TPU:2 now
where the time goes in v3:
time: 79.7 us; the launch traced here: 79.4 us
  starting transfers between devices  41.8 us (52%)
  waiting for transfers between devices  23.3 us (29%)
  Pallas kernels  12.8 us (16%)
  between operations  1.52 us (2%)
    ppermute x10, starting transfers between devices, shift(): return lax.ppermute(values, axis, [(i, (i + by) % n) for i in range(n)])  34.8 us
    ppermute x10, waiting for transfers between devices, shift(): return lax.ppermute(values, axis, [(i, (i + by) % n) for i in range(n)])  18.7 us
    pallas_call x8, Pallas kernels, call(): pl.pallas_call(kernel, out_shape=outs, in_specs=specs or [VMEM] * len(arg...  12.8 us
    all_to_all x1, starting transfers between devices, body(): lax.all_to_all(routed, 'gy', 0, 0, axis_index_groups=[[0, 2, 4, 6], [1, 3...  6.96 us
    all_to_all x1, waiting for transfers between devices, body(): lax.all_to_all(routed, 'gy', 0, 0, axis_index_groups=[[0, 2, 4, 6], [1, 3...  4.57 us
  transfers between devices with their start and end apart: 11, of which 9 were waited for; matrix products, arithmetic and copies ran while one was open for 0% of the time, Pallas kernels for 3%

profile of v3, /device:TPU:2, one launch (start us, length us, event | category | flops | bytes accessed | tf_op | source)
XLA Modules:
  0.0 79.4 jit_solution(52970827234508979)
XLA Ops:
  0.6 0.0 copy-start.3
  0.6 0.0 copy-start.2
  0.7 0.0 copy-start.1
  0.7 0.0 copy-start
  1.4 1.6 %shard_map.85 = (f32[8,32,128]{2,1,0:T(8,128)S(1)}, f32[8,32,128]{2,1,0:T(8,128)S(1)}, f32[4,8,16,128]{3,2,1,0:T(8,128)S(1)}, f32[8,16,128]{2,1,0:T(8,128)S(1)},...) custom-call(s32[1,1]{1,0:T(1,128)S(6)} %copy.9.owner, f32[19,8,16,128]{3,2,1,0:T(8,128)} %pop.3, f32[2,8,16,128]{3,2,1,0:T(8,128)} %conc.3, ...), custom_call_target="tpu_custom_call" | custom-call | tf_op jit(solution)/shard_map/pallas_call | solution.py:484
  3.0 0.0 collective-permute-start
  3.0 1.7 %collective-permute-start.1 = (f32[8,32,128]{2,1,0:T(8,128)S(1)}, f32[8,32,128]{2,1,0:T(8,128)S(1)}, u32[]{:S(2)}, u32[]{:S(2)}) collective-permute-start(f32[8,32,128]{2,1,0:T(8,128)S(1)} %get-tuple-element.32), channel_id=1, source_target_pairs={{0,7},{1,0},{2,1},{3,2},{4,3},{5,4},{6,5},{7,6},{8,15},{9,8},{10,9... | collective-permute-start | bytes 393224 | tf_op jit(solution)/shard_map/ppermute | solution.py:502
  4.8 2.6 %collective-permute-done.yl = f32[8,32,128]{2,1,0:T(8,128)S(1)} collective-permute-done((f32[8,32,128]{2,1,0:T(8,128)S(1)}, f32[8,32,128]{2,1,0:T(8,128)S(1)}, u32[]{:S(2)}, u32[]{:S(2)}) %collective-permute-start) | collective-permute-done | bytes 131104 | tf_op jit(solution)/shard_map/ppermute | solution.py:502
  7.4 0.0 collective-permute-done.1.yh
  7.4 0.0 copy-done.3
  7.4 0.0 copy-done.2
  7.4 0.0 copy-done.1
  7.4 0.0 copy-done
  7.5 0.1 shard_map.86
  7.5 3.5 %collective-permute-start.3 = (f32[37,16,128]{2,1,0:T(8,128)S(1)}, f32[37,16,128]{2,1,0:T(8,128)S(1)}, u32[]{:S(2)}, u32[]{:S(2)}) collective-permute-start(f32[37,16,128]{2,1,0:T(8,128)S(1)} %get-tuple-element.34), channel_id=1, source_target_pairs={{0,8},{8,16},{16,24},{24,32},{32,40},{40,48},{48,56},{56,64},{64,7... | collective-permute-start | bytes 909320 | tf_op jit(solution)/shard_map/ppermute | solution.py:502
  11.0 15.9 %collective-permute-start.4 = (f32[37,16,128]{2,1,0:T(8,128)S(1)}, f32[37,16,128]{2,1,0:T(8,128)S(1)}, u32[]{:S(2)}, u32[]{:S(2)}) collective-permute-start(f32[37,16,128]{2,1,0:T(8,128)S(1)} %get-tuple-element.35), channel_id=1, source_target_pairs={{0,760},{8,0},{16,8},{24,16},{32,24},{40,32},{48,40},{56,48},{64,5... | collective-permute-start | bytes 909320 | tf_op jit(solution)/shard_map/ppermute | solution.py:502
  27.0 1.3 %collective-permute-start.2 = (f32[8,128]{1,0:T(8,128)S(1)}, f32[8,128]{1,0:T(8,128)S(1)}, u32[]{:S(2)}, u32[]{:S(2)}) collective-permute-start(f32[8,128]{1,0:T(8,128)S(1)} %get-tuple-element.33), channel_id=1, source_target_pairs={{0,1},{1,2},{2,3},{3,4},{4,5},{5,6},{6,7},{7,0},{8,9},{9,10},{10,1... | collective-permute-start | bytes 12296 | tf_op jit(solution)/shard_map/ppermute | solution.py:502
  28.3 1.7 %collective-permute-done.2.owner_two = f32[8,128]{1,0:T(8,128)S(1)} collective-permute-done((f32[8,128]{1,0:T(8,128)S(1)}, f32[8,128]{1,0:T(8,128)S(1)}, u32[]{:S(2)}, u32[]{:S(2)}) %collective-permute-start.2) | collective-permute-done | bytes 4128 | tf_op jit(solution)/shard_map/ppermute | solution.py:502
  30.0 2.2 %collective-permute-done.3.xl = f32[37,16,128]{2,1,0:T(8,128)S(1)} collective-permute-done((f32[37,16,128]{2,1,0:T(8,128)S(1)}, f32[37,16,128]{2,1,0:T(8,128)S(1)}, u32[]{:S(2)}, u32[]{:S(2)}) %collective-permute-start.3) | collective-permute-done | bytes 303136 | tf_op jit(solution)/shard_map/ppermute | solution.py:502
  32.2 1.8 %collective-permute-done.4.xh = f32[37,16,128]{2,1,0:T(8,128)S(1)} collective-permute-done((f32[37,16,128]{2,1,0:T(8,128)S(1)}, f32[37,16,128]{2,1,0:T(8,128)S(1)}, u32[]{:S(2)}, u32[]{:S(2)}) %collective-permute-start.4) | collective-permute-done | bytes 303136 | tf_op jit(solution)/shard_map/ppermute | solution.py:502
  33.9 4.3 %shard_map.87 = (f32[19,8,16,128]{3,2,1,0:T(8,128)S(1)}, f32[8,16,128]{2,1,0:T(8,128)S(1)}, f32[2,8,16,128]{3,2,1,0:T(8,128)S(1)}, f32[8,16,128]{2,1,0:T(8,128)S...) custom-call(f32[19,8,16,128]{3,2,1,0:T(8,128)S(1)} %copy-done, ...), custom_call_target="tpu_custom_call" | custom-call | tf_op jit(solution)/shard_map/pallas_call | solution.py:484
  38.2 0.7 collective-permute-start.5
  38.9 1.1 %collective-permute-start.6 = (f32[8,24,128]{2,1,0:T(8,128)S(1)}, f32[8,24,128]{2,1,0:T(8,128)S(1)}, u32[]{:S(2)}, u32[]{:S(2)}) collective-permute-start(f32[8,24,128]{2,1,0:T(8,128)S(1)} %get-tuple-element.46), channel_id=1, source_target_pairs={{0,7},{1,0},{2,1},{3,2},{4,3},{5,4},{6,5},{7,6},{8,15},{9,8},{10,9... | collective-permute-start | bytes 294920 | tf_op jit(solution)/shard_map/ppermute | solution.py:502
  40.0 2.3 %collective-permute-done.5.yl = f32[8,24,128]{2,1,0:T(8,128)S(1)} collective-permute-done((f32[8,24,128]{2,1,0:T(8,128)S(1)}, f32[8,24,128]{2,1,0:T(8,128)S(1)}, u32[]{:S(2)}, u32[]{:S(2)}) %collective-permute-start.5) | collective-permute-done | bytes 98336 | tf_op jit(solution)/shard_map/ppermute | solution.py:502
  42.3 0.0 collective-permute-done.6.yh
  42.3 1.9 %collective-permute-start.7 = (f32[25,16,128]{2,1,0:T(8,128)S(1)}, f32[25,16,128]{2,1,0:T(8,128)S(1)}, u32[]{:S(2)}, u32[]{:S(2)}) collective-permute-start(f32[25,16,128]{2,1,0:T(8,128)S(1)} %get-tuple-element.47), channel_id=1, source_target_pairs={{0,8},{8,16},{16,24},{24,32},{32,40},{40,48},{48,56},{56,64},{64,7... | collective-permute-start | bytes 614408 | tf_op jit(solution)/shard_map/ppermute | solution.py:502
  44.3 7.7 %collective-permute-start.8 = (f32[25,16,128]{2,1,0:T(8,128)S(1)}, f32[25,16,128]{2,1,0:T(8,128)S(1)}, u32[]{:S(2)}, u32[]{:S(2)}) collective-permute-start(f32[25,16,128]{2,1,0:T(8,128)S(1)} %get-tuple-element.48), channel_id=1, source_target_pairs={{0,760},{8,0},{16,8},{24,16},{32,24},{40,32},{48,40},{56,48},{64,5... | collective-permute-start | bytes 614408 | tf_op jit(solution)/shard_map/ppermute | solution.py:502
  52.0 2.8 %collective-permute-done.7.xl = f32[25,16,128]{2,1,0:T(8,128)S(1)} collective-permute-done((f32[25,16,128]{2,1,0:T(8,128)S(1)}, f32[25,16,128]{2,1,0:T(8,128)S(1)}, u32[]{:S(2)}, u32[]{:S(2)}) %collective-permute-start.7) | collective-permute-done | bytes 204832 | tf_op jit(solution)/shard_map/ppermute | solution.py:502
  54.8 1.8 %collective-permute-done.8.xh = f32[25,16,128]{2,1,0:T(8,128)S(1)} collective-permute-done((f32[25,16,128]{2,1,0:T(8,128)S(1)}, f32[25,16,128]{2,1,0:T(8,128)S(1)}, u32[]{:S(2)}, u32[]{:S(2)}) %collective-permute-start.8) | collective-permute-done | bytes 204832 | tf_op jit(solution)/shard_map/ppermute | solution.py:502
  56.6 3.3 %shard_map.89 = (f32[8,16,128]{2,1,0:T(8,128)}, f32[17,16,128]{2,1,0:T(8,128)S(1)}, f32[5,10,32,128]{3,2,1,0:T(8,128)S(1)}) custom-call(f32[2,8,16,128]{3,2,1,0:T(8,128)S(1)} %get-tuple-element.38.conc, f32[8,16,128]{2,1,0:T(8,128)S(1)} %get-tuple-element.39.phi, f32[8,16,128]{2,1,0:T(8,128)S(1)} %get-tuple-element.40.charge, ...), custom_call_target="tpu_custom_call" | custom-call | tf_op jit(solution)/shard_map/pallas_call | solution.py:484
  59.9 1.0 %collective-permute-start.9 = (f32[17,16,128]{2,1,0:T(8,128)S(1)}, f32[17,16,128]{2,1,0:T(8,128)S(1)}, u32[]{:S(2)}, u32[]{:S(2)}) collective-permute-start(f32[17,16,128]{2,1,0:T(8,128)S(1)} %get-tuple-element.51.mine), channel_id=1, source_target_pairs={{0,1},{1,2},{2,3},{3,4},{4,5},{5,6},{6,7},{7,0},{8,9},{9,10},{10,1... | collective-permute-start | bytes 417800 | tf_op jit(solution)/shard_map/ppermute | solution.py:502
  60.8 3.5 %collective-permute-done.9.other = f32[17,16,128]{2,1,0:T(8,128)S(1)} collective-permute-done((f32[17,16,128]{2,1,0:T(8,128)S(1)}, f32[17,16,128]{2,1,0:T(8,128)S(1)}, u32[]{:S(2)}, u32[]{:S(2)}) %collective-permute-start.9) | collective-permute-done | bytes 139296 | tf_op jit(solution)/shard_map/ppermute | solution.py:502
  64.3 0.8 %shard_map.91 = f32[4,16,16,128]{3,2,1,0:T(8,128)} custom-call(f32[17,16,128]{2,1,0:T(8,128)S(1)} %get-tuple-element.51.mine, f32[17,16,128]{2,1,0:T(8,128)S(1)} %collective-permute-done.9.other, f32[8,24,128]{2,1,0:T(8,128)S(1)} %collective-permute-done.6.yh, f32[8,128]{1,0:T(8,128)S(1)} %get-tuple-element.52.owner, ...), custom_call_target="tpu_custom_call" | custom-call | tf_op jit(solution)/shard_map/pallas_call | solution.py:484
  65.2 7.0 %all-to-all-start = ((f32[4,16,16,128]{3,2,1,0:T(8,128)}), f32[4,16,16,128]{3,2,1,0:T(8,128)S(1)}, u32[]{:S(2)}, u32[]{:S(2)}) async-start(f32[4,16,16,128]{3,2,1,0:T(8,128)} %shard_map.91), calls=%async_computation | async-start | bytes 1048576 | tf_op jit(solution)/shard_map/all_to_all | solution.py:538
  72.1 2.1 %shard_map.90 = f32[19,8,16,128]{3,2,1,0:T(8,128)} custom-call(f32[19,8,16,128]{3,2,1,0:T(8,128)S(1)} %get-tuple-element.36.pop, f32[10,32,128]{2,1,0:T(8,128)S(1)} %get-tuple-element.37.fl, f32[5,10,32,128]{3,2,1,0:T(8,128)S(1)} %get-tuple-element.49.sh, f32[8,24,128]{2,1,0:T(8,128)S(1)} %collective-permute-done.5.yl, ...), custom_call_target="tpu_custom_call" | custom-call | flops 40000000 | tf_op jit(solution)/shard_map/pallas_call | solution.py:484
  74.2 4.6 %all-to-all-done.came = f32[4,16,16,128]{3,2,1,0:T(8,128)S(1)} async-done(((f32[4,16,16,128]{3,2,1,0:T(8,128)}), f32[4,16,16,128]{3,2,1,0:T(8,128)S(1)}, u32[]{:S(2)}, u32[]{:S(2)}) %all-to-all-start) | async-done | bytes 524320 | tf_op jit(solution)/shard_map/all_to_all | solution.py:538
  78.8 0.7 shard_map.92
  (1 shorter events, 0.0 us)
Async XLA Ops:
  0.6 6.8 %copy-start.3 = (f32[8,16,128]{2,1,0:T(8,128)S(1)}, f32[8,16,128]{2,1,0:T(8,128)}, u32[]{:S(2)}) copy-start(f32[8,16,128]{2,1,0:T(8,128)} %perm.3) | copy-start | bytes 196612
  0.6 6.8 %copy-start.2 = (f32[8,16,128]{2,1,0:T(8,128)S(1)}, f32[8,16,128]{2,1,0:T(8,128)}, u32[]{:S(2)}) copy-start(f32[8,16,128]{2,1,0:T(8,128)} %phi.3) | copy-start | bytes 196612
  0.7 6.8 %copy-start.1 = (f32[2,8,16,128]{3,2,1,0:T(8,128)S(1)}, f32[2,8,16,128]{3,2,1,0:T(8,128)}, u32[]{:S(2)}) copy-start(f32[2,8,16,128]{3,2,1,0:T(8,128)} %conc.3) | copy-start | bytes 393220
  0.7 6.8 %copy-start = (f32[19,8,16,128]{3,2,1,0:T(8,128)S(1)}, f32[19,8,16,128]{3,2,1,0:T(8,128)}, u32[]{:S(2)}) copy-start(f32[19,8,16,128]{3,2,1,0:T(8,128)} %pop.3) | copy-start | bytes 3735556
  3.0 4.4 %collective-permute-start = (f32[8,32,128]{2,1,0:T(8,128)S(1)}, f32[8,32,128]{2,1,0:T(8,128)S(1)}, u32[]{:S(2)}, u32[]{:S(2)}) collective-permute-start(f32[8,32,128]{2,1,0:T(8,128)S(1)} %get-tuple-element.31), channel_id=1, source_target_pairs={{0,1},{1,2},{2,3},{3,4},{4,5},{5,6},{6,7},{7,0},{8,9},{9,10},{10,1... | collective-permute-start | bytes 393224 | tf_op jit(solution)/shard_map/ppermute | solution.py:502
  3.0 4.4 %collective-permute-start.1 = (f32[8,32,128]{2,1,0:T(8,128)S(1)}, f32[8,32,128]{2,1,0:T(8,128)S(1)}, u32[]{:S(2)}, u32[]{:S(2)}) collective-permute-start(f32[8,32,128]{2,1,0:T(8,128)S(1)} %get-tuple-element.32), channel_id=1, source_target_pairs={{0,7},{1,0},{2,1},{3,2},{4,3},{5,4},{6,5},{7,6},{8,15},{9,8},{10,9... | collective-permute-start | bytes 393224 | tf_op jit(solution)/shard_map/ppermute | solution.py:502
  7.5 24.6 %collective-permute-start.3 = (f32[37,16,128]{2,1,0:T(8,128)S(1)}, f32[37,16,128]{2,1,0:T(8,128)S(1)}, u32[]{:S(2)}, u32[]{:S(2)}) collective-permute-start(f32[37,16,128]{2,1,0:T(8,128)S(1)} %get-tuple-element.34), channel_id=1, source_target_pairs={{0,8},{8,16},{16,24},{24,32},{32,40},{40,48},{48,56},{56,64},{64,7... | collective-permute-start | bytes 909320 | tf_op jit(solution)/shard_map/ppermute | solution.py:502
  11.0 22.9 %collective-permute-start.4 = (f32[37,16,128]{2,1,0:T(8,128)S(1)}, f32[37,16,128]{2,1,0:T(8,128)S(1)}, u32[]{:S(2)}, u32[]{:S(2)}) collective-permute-start(f32[37,16,128]{2,1,0:T(8,128)S(1)} %get-tuple-element.35), channel_id=1, source_target_pairs={{0,760},{8,0},{16,8},{24,16},{32,24},{40,32},{48,40},{56,48},{64,5... | collective-permute-start | bytes 909320 | tf_op jit(solution)/shard_map/ppermute | solution.py:502
  27.0 3.0 %collective-permute-start.2 = (f32[8,128]{1,0:T(8,128)S(1)}, f32[8,128]{1,0:T(8,128)S(1)}, u32[]{:S(2)}, u32[]{:S(2)}) collective-permute-start(f32[8,128]{1,0:T(8,128)S(1)} %get-tuple-element.33), channel_id=1, source_target_pairs={{0,1},{1,2},{2,3},{3,4},{4,5},{5,6},{6,7},{7,0},{8,9},{9,10},{10,1... | collective-permute-start | bytes 12296 | tf_op jit(solution)/shard_map/ppermute | solution.py:502
  38.2 4.1 %collective-permute-start.5 = (f32[8,24,128]{2,1,0:T(8,128)S(1)}, f32[8,24,128]{2,1,0:T(8,128)S(1)}, u32[]{:S(2)}, u32[]{:S(2)}) collective-permute-start(f32[8,24,128]{2,1,0:T(8,128)S(1)} %get-tuple-element.45), channel_id=1, source_target_pairs={{0,1},{1,2},{2,3},{3,4},{4,5},{5,6},{6,7},{7,0},{8,9},{9,10},{10,1... | collective-permute-start | bytes 294920 | tf_op jit(solution)/shard_map/ppermute | solution.py:502
  38.9 3.4 %collective-permute-start.6 = (f32[8,24,128]{2,1,0:T(8,128)S(1)}, f32[8,24,128]{2,1,0:T(8,128)S(1)}, u32[]{:S(2)}, u32[]{:S(2)}) collective-permute-start(f32[8,24,128]{2,1,0:T(8,128)S(1)} %get-tuple-element.46), channel_id=1, source_target_pairs={{0,7},{1,0},{2,1},{3,2},{4,3},{5,4},{6,5},{7,6},{8,15},{9,8},{10,9... | collective-permute-start | bytes 294920 | tf_op jit(solution)/shard_map/ppermute | solution.py:502
  42.3 12.5 %collective-permute-start.7 = (f32[25,16,128]{2,1,0:T(8,128)S(1)}, f32[25,16,128]{2,1,0:T(8,128)S(1)}, u32[]{:S(2)}, u32[]{:S(2)}) collective-permute-start(f32[25,16,128]{2,1,0:T(8,128)S(1)} %get-tuple-element.47), channel_id=1, source_target_pairs={{0,8},{8,16},{16,24},{24,32},{32,40},{40,48},{48,56},{56,64},{64,7... | collective-permute-start | bytes 614408 | tf_op jit(solution)/shard_map/ppermute | solution.py:502
  44.3 12.3 %collective-permute-start.8 = (f32[25,16,128]{2,1,0:T(8,128)S(1)}, f32[25,16,128]{2,1,0:T(8,128)S(1)}, u32[]{:S(2)}, u32[]{:S(2)}) collective-permute-start(f32[25,16,128]{2,1,0:T(8,128)S(1)} %get-tuple-element.48), channel_id=1, source_target_pairs={{0,760},{8,0},{16,8},{24,16},{32,24},{40,32},{48,40},{56,48},{64,5... | collective-permute-start | bytes 614408 | tf_op jit(solution)/shard_map/ppermute | solution.py:502
  59.9 4.5 %collective-permute-start.9 = (f32[17,16,128]{2,1,0:T(8,128)S(1)}, f32[17,16,128]{2,1,0:T(8,128)S(1)}, u32[]{:S(2)}, u32[]{:S(2)}) collective-permute-start(f32[17,16,128]{2,1,0:T(8,128)S(1)} %get-tuple-element.51.mine), channel_id=1, source_target_pairs={{0,1},{1,2},{2,3},{3,4},{4,5},{5,6},{6,7},{7,0},{8,9},{9,10},{10,1... | collective-permute-start | bytes 417800 | tf_op jit(solution)/shard_map/ppermute | solution.py:502
  65.2 13.6 %all-to-all-start = ((f32[4,16,16,128]{3,2,1,0:T(8,128)}), f32[4,16,16,128]{3,2,1,0:T(8,128)S(1)}, u32[]{:S(2)}, u32[]{:S(2)}) async-start(f32[4,16,16,128]{3,2,1,0:T(8,128)} %shard_map.91), calls=%async_computation | async-start | bytes 1048576 | tf_op jit(solution)/shard_map/all_to_all | solution.py:538

commit v4 on v3

--- a/solution.py
+++ b/solution.py
@@ -46,20 +46,21 @@
         rows = [("phi", 6)] + [("perm", 6)] * first + [("charge", 4), ("conc", 2)] + [("fluid", 1)] * first
         self.y = {}
         at = 0
-        for name, n in rows + [("pop", 5), ("dm", 4), ("owner", 1)]:
+        for name, n in rows + [("pop", 5), ("dm", 4)] + [("owner", 1)] * (not first):
             self.y[name] = at
             at += n
         self.y_rows = -(-at // 8) * 8
         self.skip = 0 if first else 2
         planes = [("phi", 6 - self.skip)] + [("perm", 6)] * first + [("charge", 4), ("conc", 2)]
-        planes += [("fluid", 1)] * first + [("pop", 5), ("dm", 4), ("cphi", 3)]
-        planes += [("cperm", 3)] * first + [("ccharge", 2), ("cmisc", 1)]
+        planes += [("fluid", 1)] * first + [("pop", 5), ("dm", 4)]
         self.x = {}
         at = 0
         for name, n in planes:
             self.x[name] = at
             at += n
         self.x_planes = at
+        self.c = {"phi": 0, "perm": 3, "charge": 3 + 3 * first, "misc": 5 + 3 * first}
+        self.tiles = 6 + 3 * first
 
 
 ONE, TWO = Plan(True), Plan(False)
@@ -83,22 +84,20 @@
         out[:, y["pop"] + k : y["pop"] + k + 1] = pop[i, :, row]
     for k in range(4):
         out[:, y["dm"] + k : y["dm"] + k + 1] = dm[k, :, row]
-    out[0, y["owner"] : y["owner"] + 1] = owner
-
-
-def pack_x(plan, out, low, yl, yh, phi, charge, conc, pop, dm, perm=None, fluid=None):
-    x, y = plan.x, plan.y
-
-    def at(depth):
-        return depth - 1 if low else CX - depth
+    if not plan.first:
+        out[0, y["owner"] : y["owner"] + 1] = owner
+
+
+def pack_x(plan, out, low, phi, charge, conc, pop, dm, perm=None, fluid=None):
+    x = plan.x
 
     def spread(to, field, first, last):
-        lo = min(at(first), at(last))
+        lo = first - 1 if low else CX - last
         out[to : to + last - first + 1] = field[lo : lo + last - first + 1]
 
     spread(0, phi, 1 + plan.skip, 6)
     spread(x["charge"], charge, 2, 5)
-    edge = at(1)
+    edge = 0 if low else CX - 1
     for s in range(2):
         out[x["conc"] + s] = conc[s, edge]
     if plan.first:
@@ -108,38 +107,52 @@
         out[x["pop"] + k] = pop[i, edge]
     for k in range(4):
         out[x["dm"] + k] = dm[k, edge]
-    for name in ("phi", "perm")[: 1 + plan.first]:
-        for k, (d, n, e, m) in enumerate(DEEP):
-            c, r = x["c" + name] + k, y[name]
-            out[c, 8 - n : 8] = yl[at(d), r + 6 - n : r + 6]
-            out[c, 0:m] = yl[at(e), r + 6 - m : r + 6]
-            out[c, 8 : 8 + n] = yh[at(d), r : r + n]
-            out[c, 16 - m : 16] = yh[at(e), r : r + m]
-    q, o = y["charge"], y["conc"]
-
-    def near(msg, depth):
-        return msg[at(depth), o : o + 1] - msg[at(depth), o + 1 : o + 2]
-
-    for k, (d, n, e, m) in enumerate(CHARGE):
-        c = x["ccharge"] + k
-        out[c, 8 - n : 7] = yl[at(d), q + 5 - n : q + 4]
-        out[c, 7:8] = near(yl, d)
-        out[c, 0 : m - 1] = yl[at(e), q + 5 - m : q + 4]
-        out[c, m - 1 : m] = near(yl, e)
-        out[c, 8:9] = near(yh, d)
-        out[c, 9 : 8 + n] = yh[at(d), q : q + n - 1]
-        out[c, 16 - m : 17 - m] = near(yh, e)
-        out[c, 17 - m : 16] = yh[at(e), q : q + m - 1]
-    for r, msg, names, pick in ((0, yl, Y_IN_LO, HI_LO if low else LO_LO), (8, yh, Y_IN_HI, HI_HI if low else LO_HI)):
-        take = [(1, y["pop"] + names.index(pick))] + [(2 + k, y["dm"] + k) for k in range(4)]
+
+
+def pack_corners(plan, out, low, xl, xh, rim=None):
+    x = plan.x
+
+    def rows(n):
+        return slice(0, n) if low else slice(16 - n, 16)
+
+    for side, msg, names in ((0, xl, X_IN_LO), (1, xh, X_IN_HI)):
+        base = side * plan.tiles
+
+        def phi(d, r):
+            if d <= plan.skip:
+                return rim[1 + d if side else 2 - d, r]
+            return msg[x["phi"] + (d - 1 - plan.skip if side else 6 - d), r]
+
+        def perm(d, r):
+            return msg[x["perm"] + (d - 1 if side else 6 - d), r]
+
+        def charge(d, r):
+            if d == 1:
+                return msg[x["conc"], r] - msg[x["conc"] + 1, r]
+            return msg[x["charge"] + (d - 2 if side else 5 - d), r]
+
+        fields = [("phi", phi, DEEP), ("charge", charge, CHARGE)] + [("perm", perm, DEEP)] * plan.first
+        for name, load, pairs in fields:
+            for k, (d, n, e, m) in enumerate(pairs):
+                tile = base + plan.c[name] + k
+                if low:
+                    out[tile, 0:n] = load(d, rows(n))
+                    out[tile, 8 - m : 8] = load(e, rows(m))
+                else:
+                    out[tile, 8 - n : 8] = load(d, rows(n))
+                    out[tile, 0:m] = load(e, rows(m))
+        pick = (LO_HI, HI_HI)[side] if low else (LO_LO, HI_LO)[side]
+        misc = base + plan.c["misc"]
         if plan.first:
-            take.append((0, y["fluid"]))
-        for to, source in take:
-            out[x["cmisc"], r + to : r + to + 1] = msg[edge, source : source + 1]
-        out[x["cmisc"], r + 6 : r + 7] = near(msg, 5)
-
-
-def lay(ext, own, name, depth, pairs, plan, xl, xh, yl, yh):
+            out[misc, 0:1] = msg[x["fluid"], rows(1)]
+        out[misc, 1:2] = msg[x["pop"] + names.index(pick), rows(1)]
+        for k in range(4):
+            out[misc, 2 + k : 3 + k] = msg[x["dm"] + k, rows(1)]
+        out[misc, 6:7] = charge(5, rows(1))
+
+
+def lay(ext, own, name, plan, msgs):
+    xl, xh, yl, yh, cl, ch = msgs
     x, y = plan.x, plan.y
     skip = plan.skip if name == "phi" else 0
     n = 6 - skip
@@ -148,16 +161,17 @@
     ext[14 + skip : 20, 8:24] = xh[x[name] : x[name] + n]
     ext[6:14, 2:8] = yl[:, y[name] : y[name] + 6]
     ext[6:14, 24:30] = yh[:, y[name] : y[name] + 6]
-    corners(ext, x["c" + name], pairs, xl, xh)
-
-
-def corners(ext, at, pairs, xl, xh):
+    corners(ext, plan, name, DEEP, cl, ch)
+
+
+def corners(ext, plan, name, pairs, cl, ch):
     for k, (d, n, e, m) in enumerate(pairs):
-        for msg, p, q in ((xl, 6 - d, 6 - e), (xh, 13 + d, 13 + e)):
-            ext[p, 8 - n : 8] = msg[at + k, 8 - n : 8]
-            ext[q, 8 - m : 8] = msg[at + k, 0:m]
-            ext[p, 24 : 24 + n] = msg[at + k, 8 : 8 + n]
-            ext[q, 24 : 24 + m] = msg[at + k, 16 - m : 16]
+        for side, p, q in ((0, 6 - d, 6 - e), (1, 13 + d, 13 + e)):
+            tile = side * plan.tiles + plan.c[name] + k
+            ext[p, 8 - n : 8] = cl[tile, 8 - n : 8]
+            ext[q, 8 - m : 8] = cl[tile, 0:m]
+            ext[p, 24 : 24 + n] = ch[tile, 0:n]
+            ext[q, 24 : 24 + m] = ch[tile, 8 - m : 8]
 
 
 def moments(load):
@@ -173,14 +187,13 @@
     return [dens] + mom
 
 
-def first_kernel(owner, *refs):
-    far, near, sems = refs[:5], refs[11:16], refs[16]
+def first_kernel(*refs):
+    far, near, sems = refs[:5], refs[12:17], refs[17]
     pop, conc, phi, perm, mask = near
-    y_hi, y_lo, dm, charge, fluid, owner_row = refs[5:11]
+    x_hi, x_lo, y_hi, y_lo, dm, charge, fluid = refs[5:12]
     copies = [pltpu.make_async_copy(a, b, sems.at[k]) for k, (a, b) in enumerate(zip(far, near))]
     for copy in copies:
         copy.start()
-    owner_row[...] = jnp.full((8, NZ), owner[0, 0], jnp.int32).astype(F32)
     for copy in copies:
         copy.wait()
     charge[...] = conc[0] - conc[1]
@@ -192,25 +205,25 @@
         return 0
 
     lax.fori_loop(0, CX, plane, 0, unroll=2)
-    for low, yo in ((False, y_hi), (True, y_lo)):
-        pack_y(ONE, yo, low, owner_row[0:1], phi, charge, conc, pop, dm, perm, fluid)
-
-
-def x_one_kernel(phi, charge, conc, pop, dm, perm, fluid, yl, yh, x_hi, x_lo, owner):
-    for low, xo in ((False, x_hi), (True, x_lo)):
-        pack_x(ONE, xo, low, yl, yh, phi, charge, conc, pop, dm, perm, fluid)
-    owner[...] = jnp.broadcast_to(yl[0, ONE.y["owner"] : ONE.y["owner"] + 1], (8, NZ))
-
-
-def x_two_kernel(phi, charge, conc, pop, dm, yl, yh, x_hi, x_lo):
-    for low, xo in ((False, x_hi), (True, x_lo)):
-        pack_x(TWO, xo, low, yl, yh, phi, charge, conc, pop, dm)
+    for low, xo, yo in ((False, x_hi, y_hi), (True, x_lo, y_lo)):
+        pack_x(ONE, xo, low, phi, charge, conc, pop, dm, perm, fluid)
+        pack_y(ONE, yo, low, None, phi, charge, conc, pop, dm, perm, fluid)
+
+
+def corner_one_kernel(xl, xh, c_hi, c_lo):
+    pack_corners(ONE, c_hi, False, xl, xh)
+    pack_corners(ONE, c_lo, True, xl, xh)
+
+
+def corner_two_kernel(xl, xh, rim, c_hi, c_lo):
+    pack_corners(TWO, c_hi, False, xl, xh, rim)
+    pack_corners(TWO, c_lo, True, xl, xh, rim)
 
 
 def lay_all(plan, phi, conc, dm, charge, msgs, pa, ce, dn, mm, cc):
-    xl, xh, yl, yh = msgs
+    xl, xh, yl, yh, cl, ch = msgs
     x, y = plan.x, plan.y
-    lay(pa, phi[...], "phi", 6, DEEP, plan, xl, xh, yl, yh)
+    lay(pa, phi[...], "phi", plan, msgs)
     ce[6:14, 8:24] = charge[...]
     q = x["charge"]
     ce[1:5, 8:24] = xl[q : q + 4]
@@ -223,11 +236,11 @@
     ce[6:14, 7:8] = yl[:, c : c + 1] - yl[:, c + 1 : c + 2]
     ce[6:14, 24:25] = yh[:, c : c + 1] - yh[:, c + 1 : c + 2]
     ce[6:14, 25:29] = yh[:, q : q + 4]
-    corners(ce, x["ccharge"], CHARGE, xl, xh)
-    m = x["cmisc"]
-    for msg, p in ((xl, 1), (xh, 18)):
-        ce[p, 7:8] = msg[m, 6:7]
-        ce[p, 24:25] = msg[m, 14:15]
+    corners(ce, plan, "charge", CHARGE, cl, ch)
+    misc = plan.c["misc"], plan.tiles + plan.c["misc"]
+    for m, p in zip(misc, (1, 18)):
+        ce[p, 7:8] = cl[m, 6:7]
+        ce[p, 24:25] = ch[m, 6:7]
     for s in range(2):
         cc[s, 1:9, 8:24] = conc[s]
         cc[s, 0, 8:24] = xl[x["conc"] + s]
@@ -236,10 +249,10 @@
         cc[s, 1:9, 24:25] = yh[:, c + s : c + s + 1]
     for k, ext in enumerate((dn, mm.at[0], mm.at[1], mm.at[2])):
         ext[1:9, 8:24] = dm[k]
-        for msg, p in ((xl, 0), (xh, 9)):
+        for msg, m, p in ((xl, misc[0], 0), (xh, misc[1], 9)):
             ext[p, 8:24] = msg[x["dm"] + k]
-            ext[p, 7:8] = msg[m, 2 + k : 3 + k]
-            ext[p, 24:25] = msg[m, 10 + k : 11 + k]
+            ext[p, 7:8] = cl[m, 2 + k : 3 + k]
+            ext[p, 24:25] = ch[m, 2 + k : 3 + k]
         for msg, r in ((yl, 7), (yh, 24)):
             ext[1:9, r : r + 1] = msg[:, y["dm"] + k : y["dm"] + k + 1]
 
@@ -321,8 +334,8 @@
 
 
 def collide_and_stream(plan, pop, fl, sh, msgs, lv, pop_out, dm_out):
-    xl, xh, yl, yh = msgs
-    y_pop, x_pop, misc = plan.y["pop"], plan.x["pop"], plan.x["cmisc"]
+    xl, xh, yl, yh, cl, ch = msgs
+    y_pop, x_pop = plan.y["pop"], plan.x["pop"]
     bad = float("nan")
 
     def load(p, rows):
@@ -367,17 +380,18 @@
         return 0
 
     lax.fori_loop(1, 9, collide, 0)
-    for p, x, names, low_pop, high_pop in (
-        (0, xl, X_IN_LO, LO_LO, LO_HI),
-        (9, xh, X_IN_HI, HI_LO, HI_HI),
+    for p, side, x, names, low_pop, high_pop in (
+        (0, 0, xl, X_IN_LO, LO_LO, LO_HI),
+        (9, 1, xh, X_IN_HI, HI_LO, HI_HI),
     ):
+        misc = side * plan.tiles + plan.c["misc"]
         part = load(p, MID_T)
         for k, i in enumerate(names):
             lv[i, p, MID_T] = jnp.where(part[5], relaxed_of(i, x[x_pop + k], part), bad)
-        for c, r, i in ((1, 7, low_pop), (9, 24, high_pop)):
+        for c, r, i in ((cl, 7, low_pop), (ch, 24, high_pop)):
             row = slice(r, r + 1)
             part = load(p, row)
-            lv[i, p, row] = jnp.where(part[5], relaxed_of(i, x[misc, c : c + 1], part), bad)
+            lv[i, p, row] = jnp.where(part[5], relaxed_of(i, c[misc, 1:2], part), bad)
 
     def stream(x, _):
         wet = fl[x + 1, MID_T] != 0.0
@@ -395,11 +409,12 @@
     lax.fori_loop(0, CX, stream, 0, unroll=2)
 
 
-def step_one_kernel(pop, conc, phi, perm, dm, charge, fluid, owner_two, yl, yh, xl, xh,
-                    pop_out, phi_out, conc_out, charge_out, y_hi, y_lo, dm_out, rim, coef, inv, fl,
+def step_one_kernel(owner, pop, conc, phi, perm, dm, charge, fluid, xl, xh, yl, yh, cl, ch,
+                    pop_out, phi_out, conc_out, charge_out, x_hi, x_lo, y_hi, y_lo, dm_out, rim, coef, inv, fl, owner_row,
                     pe, pa, pb, ce, dn, mm, cc, vel, sh, lv):
-    msgs = (xl, xh, yl, yh)
-    lay(pe, perm[...], "perm", 6, DEEP, ONE, xl, xh, yl, yh)
+    msgs = (xl, xh, yl, yh, cl, ch)
+    owner_row[...] = jnp.full((8, NZ), owner[0, 0], jnp.int32).astype(F32)
+    lay(pe, perm[...], "perm", ONE, msgs)
 
     def coefs(x, _):
         mid = pe[x]
@@ -414,10 +429,11 @@
     lax.fori_loop(1, 19, coefs, 0, unroll=6)
     fl[1:9, 8:24] = fluid[...]
     x, y = ONE.x, ONE.y
-    for msg, p in ((xl, 0), (xh, 9)):
+    for side, msg, p in ((0, xl, 0), (1, xh, 9)):
+        m = side * ONE.tiles + ONE.c["misc"]
         fl[p, 8:24] = msg[x["fluid"]]
-        fl[p, 7:8] = msg[x["cmisc"], 0:1]
-        fl[p, 24:25] = msg[x["cmisc"], 8:9]
+        fl[p, 7:8] = cl[m, 0:1]
+        fl[p, 24:25] = ch[m, 0:1]
     fl[1:9, 7:8] = yl[:, y["fluid"] : y["fluid"] + 1]
     fl[1:9, 24:25] = yh[:, y["fluid"] : y["fluid"] + 1]
     lay_all(ONE, phi, conc, dm, charge, msgs, pa, ce, dn, mm, cc)
@@ -433,14 +449,14 @@
     ions(fin, fl, cc, vel, store)
     collide_and_stream(ONE, pop, fl, sh, msgs, lv, pop_out, dm_out)
     charge_out[...] = conc_out[0] - conc_out[1]
-    above = yh[0, y["owner"] : y["owner"] + 1]
-    for low, yo, owner in ((False, y_hi, owner_two[0:1]), (True, y_lo, above)):
-        pack_y(TWO, yo, low, owner, phi_out, charge_out, conc_out, pop_out, dm_out)
-
-
-def ions_two_kernel(conc, phi, charge, dm, rim, coef, inv, fl, yl, yh, xl, xh,
+    for low, xo, yo in ((False, x_hi, y_hi), (True, x_lo, y_lo)):
+        pack_x(TWO, xo, low, phi_out, charge_out, conc_out, pop_out, dm_out)
+        pack_y(TWO, yo, low, owner_row[0:1], phi_out, charge_out, conc_out, pop_out, dm_out)
+
+
+def ions_two_kernel(conc, phi, charge, dm, rim, coef, inv, fl, xl, xh, yl, yh, cl, ch,
                     phi_out, slab, sh, pa, pb, ce, dn, mm, cc, vel):
-    lay_all(TWO, phi, conc, dm, charge, (xl, xh, yl, yh), pa, ce, dn, mm, cc)
+    lay_all(TWO, phi, conc, dm, charge, (xl, xh, yl, yh, cl, ch), pa, ce, dn, mm, cc)
     pa[4:6, MID_T] = rim[0:2]
     pa[14:16, MID_T] = rim[2:4]
     fin = sweeps(coef, inv, ce, pa, pb)
@@ -448,33 +464,40 @@
     motion(fin, ce, fl, dn, mm, vel, sh)
 
     def store(s, x, values):
-        slab[s * CX + x] = values
+        for k in range(4):
+            slab[k, s * CX + x] = values
 
     ions(fin, fl, cc, vel, store)
-    slab[2 * CX, 0:8] = jnp.broadcast_to(yl[0, TWO.y["owner"] : TWO.y["owner"] + 1], (8, NZ))
-
-
-def flow_two_kernel(pop, fl, sh, yl, yh, xl, xh, pop_out, lv):
-    collide_and_stream(TWO, pop, fl, sh, (xl, xh, yl, yh), lv, pop_out, None)
-
-
-def route_kernel(mine, other, yh, owner, owner_two, out, wanted):
-    me = lax.axis_index("gy")
-    wanted[0] = owner[...]
-    wanted[1, 0:1] = yh[0, TWO.y["owner"] : TWO.y["owner"] + 1]
-    wanted[2] = other[2 * CX, 0:8]
-    wanted[3] = owner_two[...]
-    row = jnp.full((1, NZ), me, jnp.int32).astype(F32)
-    for k in range(4):
-        pick = wanted[lax.rem(k - me // 2 + 4, 4), 0:1] == row
-        for x in range(2 * CX):
-            out[k, x] = jnp.where(pick, mine[x], other[x])
-
-
-def arrive_kernel(owner, came, out):
-    me = lax.axis_index("gy")
-    away = lax.rem(me - owner[0, 0] + 8, 8)
-    out[...] = came[lax.rem(me // 2 - away // 2 + 4, 4)]
+
+
+def flow_two_kernel(pop, fl, sh, xl, xh, yl, yh, cl, ch, pop_out, lv):
+    collide_and_stream(TWO, pop, fl, sh, (xl, xh, yl, yh, cl, ch), lv, pop_out, None)
+
+
+def chip_of(slab):
+    return jnp.floor(slab * 0.5)
+
+
+def choose(came, chip, x):
+    v = came[0, x]
+    for k in range(1, 4):
+        v = jnp.where(chip == float(k), came[k, x], v)
+    return v
+
+
+def route_kernel(came, yl, yh, out):
+    o = TWO.y["owner"]
+    mate = jnp.where(lax.rem(lax.axis_index("gy"), 2) == 0, yh[0, o : o + 1], yl[0, o : o + 1])
+    for x in range(2 * CX):
+        out[x] = choose(came, chip_of(mate), x)
+
+
+def arrive_kernel(came, crossed, owner, out):
+    slab = owner[0:1]
+    core = jnp.full((1, NZ), lax.rem(lax.axis_index("gy"), 2), jnp.int32).astype(F32)
+    here = slab - 2.0 * chip_of(slab) == core
+    for x in range(2 * CX):
+        out[x] = jnp.where(here, choose(came, chip_of(slab), x), crossed[x])
 
 
 VMEM, FAR, SMEM = (pl.BlockSpec(memory_space=m) for m in (pltpu.VMEM, pltpu.HBM, pltpu.SMEM))
@@ -502,42 +525,53 @@
     return lax.ppermute(values, axis, [(i, (i + by) % n) for i in range(n)])
 
 
+def exchange(x_hi, x_lo, y_hi, y_lo):
+    yl, yh = shift(y_hi, "gy", 1), shift(y_lo, "gy", -1)
+    xl, xh = shift(x_hi, "gx", 1), shift(x_lo, "gx", -1)
+    return xl, xh, yl, yh
+
+
 def body(populations, concentration, potential, permittivity, fluid_mask, owners):
     block, row = shape(CX, CY, NZ), shape(8, NZ)
     pops, both, four = shape(19, CX, CY, NZ), shape(2, CX, CY, NZ), shape(4, CX, CY, NZ)
-    y_one, y_two = (shape(CX, plan.y_rows, NZ) for plan in (ONE, TWO))
-    x_one, x_two = (shape(plan.x_planes, CY, NZ) for plan in (ONE, TWO))
-    y_hi, y_lo, dm, charge, fluid, owner = call(
-        first_kernel, (y_one, y_one, four, block, block, row),
-        (owners,) + tuple(pltpu.with_memory_space_constraint(v, pltpu.HBM) for v in (
+
+    def messages(plan):
+        x, y = shape(plan.x_planes, CY, NZ), shape(CX, plan.y_rows, NZ)
+        return (x, x, y, y)
+
+    def tiles(plan):
+        return (shape(2 * plan.tiles, 8, NZ),) * 2
+
+    *sent, dm, charge, fluid = call(
+        first_kernel, messages(ONE) + (four, block, block),
+        tuple(pltpu.with_memory_space_constraint(v, pltpu.HBM) for v in (
             populations, concentration, potential, permittivity, fluid_mask)),
         (pops.shape, both.shape, block.shape, block.shape, pltpu.VMEM(block.shape, jnp.int32),
          pltpu.SemaphoreType.DMA((5,))),
-        [SMEM] + [FAR] * 5)
-    yl, yh = shift(y_hi, "gy", 1), shift(y_lo, "gy", -1)
-    x_hi, x_lo, owner_one = call(
-        x_one_kernel, (x_one, x_one, row),
-        (potential, charge, concentration, populations, dm, permittivity, fluid, yl, yh))
-    owner_two = shift(owner_one, "gy", 1)
-    xl, xh = shift(x_hi, "gx", 1), shift(x_lo, "gx", -1)
-    pop, phi, conc, charge, y_hi, y_lo, dm, rim, coef, inv, fl = call(
+        [FAR] * 5)
+    got = exchange(*sent)
+    c_hi, c_lo = call(corner_one_kernel, tiles(ONE), got[:2])
+    got += (shift(c_hi, "gy", 1), shift(c_lo, "gy", -1))
+    pop, phi, conc, charge, *rest = call(
         step_one_kernel,
-        (pops, block, both, block, y_two, y_two, four, shape(4, CY, NZ), shape(6, *HALO), shape(*HALO), shape(*RIM)),
-        (populations, concentration, potential, permittivity, dm, charge, fluid, owner_two, yl, yh, xl, xh),
-        (HALO,) + FIELDS + ((5,) + RIM, (19,) + RIM))
-    yl, yh = shift(y_hi, "gy", 1), shift(y_lo, "gy", -1)
-    x_hi, x_lo = call(x_two_kernel, (x_two, x_two), (phi, charge, conc, pop, dm, yl, yh))
-    xl, xh = shift(x_hi, "gx", 1), shift(x_lo, "gx", -1)
+        (pops, block, both, block) + messages(TWO)
+        + (four, shape(4, CY, NZ), shape(6, *HALO), shape(*HALO), shape(*RIM), row),
+        (owners, populations, concentration, potential, permittivity, dm, charge, fluid) + got,
+        (HALO,) + FIELDS + ((5,) + RIM, (19,) + RIM), [SMEM] + [VMEM] * 13)
+    sent, (dm, rim, coef, inv, fl, owner) = rest[:4], rest[4:]
+    got = exchange(*sent)
+    c_hi, c_lo = call(corner_two_kernel, tiles(TWO), got[:2] + (rim,))
+    got += (shift(c_hi, "gy", 1), shift(c_lo, "gy", -1))
+    slab = shape(2 * CX, CY, NZ)
     phi, mine, sh = call(
-        ions_two_kernel, (block, shape(2 * CX + 1, CY, NZ), shape(5, *RIM)),
-        (conc, phi, charge, dm, rim, coef, inv, fl, yl, yh, xl, xh), FIELDS)
-    other = shift(mine, "gy", 1)
-    (pop,) = call(flow_two_kernel, (pops,), (pop, fl, sh, yl, yh, xl, xh), ((19,) + RIM,), flops=40_000_000)
-    (routed,) = call(
-        route_kernel, (shape(4, 2 * CX, CY, NZ),), (mine, other, yh, owner, owner_two), ((4, 8, NZ),))
+        ions_two_kernel, (block, shape(4, *slab.shape), shape(5, *RIM)),
+        (conc, phi, charge, dm, rim, coef, inv, fl) + got, FIELDS)
+    (pop,) = call(flow_two_kernel, (pops,), (pop, fl, sh) + got, ((19,) + RIM,), flops=40_000_000)
     came = lax.all_to_all(
-        routed, "gy", 0, 0, axis_index_groups=[[0, 2, 4, 6], [1, 3, 5, 7]], tiled=True)
-    (migrated,) = call(arrive_kernel, (shape(2 * CX, CY, NZ),), (owners, came), (), [SMEM, VMEM])
+        mine, "gy", 0, 0, axis_index_groups=[[0, 2, 4, 6], [1, 3, 5, 7]], tiled=True)
+    (cross,) = call(route_kernel, (slab,), (came, got[2], got[3]))
+    crossed = lax.ppermute(cross, "gy", [(i, i ^ 1) for i in range(8)])
+    (migrated,) = call(arrive_kernel, (slab,), (came, crossed, owner))
     return (pop, phi, migrated.reshape(2, CX, CY, NZ))
 
 

time: 79.7 us -> 76.4 us (0.959)
  the two profiles are of different devices: /device:TPU:2 before, /device:TPU:1 now
where the time goes in v4:
time: 76.4 us; the launch traced here: 76.1 us
  starting transfers between devices  37.5 us (49%)
  blocking collectives  13.9 us (18%)
  Pallas kernels  11.8 us (15%)
  waiting for transfers between devices  11.4 us (15%)
  between operations  1.42 us (2%)
    ppermute x12, starting transfers between devices, shift(): return lax.ppermute(values, axis, [(i, (i + by) % n) for i in range(n)])  35.5 us
    all_to_all x1, blocking collectives, body(): lax.all_to_all(mine, 'gy', 0, 0, axis_index_groups=[[0, 2, 4, 6], [1, 3,...  13.9 us
    pallas_call x8, Pallas kernels, call(): pl.pallas_call(kernel, out_shape=outs, in_specs=specs or [VMEM] * len(arg...  11.8 us
    ppermute x12, waiting for transfers between devices, shift(): return lax.ppermute(values, axis, [(i, (i + by) % n) for i in range(n)])  11.4 us
    ppermute x1, starting transfers between devices, body(): crossed = lax.ppermute(cross, 'gy', [(i, i ^ 1) for i in range(8)])  1.92 us
  transfers between devices with their start and end apart: 13, of which 9 were waited for; matrix products, arithmetic and copies ran while one was open for 0% of the time, Pallas kernels for 3%

profile of v4, /device:TPU:1, one launch (start us, length us, event | category | flops | bytes accessed | tf_op | source)
XLA Modules:
  0.0 76.1 jit_solution(5747329453938894594)
XLA Ops:
  0.6 0.0 copy-start.3
  0.6 0.0 copy-start.2
  0.7 0.0 copy-start.1
  0.7 0.0 copy-start
  0.7 1.7 %shard_map.85 = (f32[28,16,128]{2,1,0:T(8,128)S(1)}, f32[28,16,128]{2,1,0:T(8,128)S(1)}, f32[8,32,128]{2,1,0:T(8,128)S(1)}, f32[8,32,128]{2,1,0:T(8,128)S(1)}, f...) custom-call(f32[19,8,16,128]{3,2,1,0:T(8,128)} %pop.1, f32[2,8,16,128]{3,2,1,0:T(8,128)} %conc.1, ...), custom_call_target="tpu_custom_call" | custom-call | tf_op jit(solution)/shard_map/pallas_call | solution.py:507
  2.4 4.0 %collective-permute-start = (f32[28,16,128]{2,1,0:T(8,128)S(1)}, f32[28,16,128]{2,1,0:T(8,128)S(1)}, u32[]{:S(2)}, u32[]{:S(2)}) collective-permute-start(f32[28,16,128]{2,1,0:T(8,128)S(1)} %get-tuple-element.34), channel_id=1, source_target_pairs={{0,8},{8,16},{16,24},{24,32},{32,40},{40,48},{48,56},{56,64},{64,7... | collective-permute-start | bytes 688136 | tf_op jit(solution)/shard_map/ppermute | solution.py:525
  6.4 15.9 %collective-permute-start.1 = (f32[28,16,128]{2,1,0:T(8,128)S(1)}, f32[28,16,128]{2,1,0:T(8,128)S(1)}, u32[]{:S(2)}, u32[]{:S(2)}) collective-permute-start(f32[28,16,128]{2,1,0:T(8,128)S(1)} %get-tuple-element.35), channel_id=1, source_target_pairs={{0,760},{8,0},{16,8},{24,16},{32,24},{40,32},{48,40},{56,48},{64,5... | collective-permute-start | bytes 688136 | tf_op jit(solution)/shard_map/ppermute | solution.py:525
  22.4 2.1 %collective-permute-start.2 = (f32[8,32,128]{2,1,0:T(8,128)S(1)}, f32[8,32,128]{2,1,0:T(8,128)S(1)}, u32[]{:S(2)}, u32[]{:S(2)}) collective-permute-start(f32[8,32,128]{2,1,0:T(8,128)S(1)} %get-tuple-element.36), channel_id=1, source_target_pairs={{0,1},{1,2},{2,3},{3,4},{4,5},{5,6},{6,7},{7,0},{8,9},{9,10},{10,1... | collective-permute-start | bytes 393224 | tf_op jit(solution)/shard_map/ppermute | solution.py:525
  24.4 0.0 collective-permute-start.3
  24.4 1.3 %collective-permute-done.xl = f32[28,16,128]{2,1,0:T(8,128)S(1)} collective-permute-done((f32[28,16,128]{2,1,0:T(8,128)S(1)}, f32[28,16,128]{2,1,0:T(8,128)S(1)}, u32[]{:S(2)}, u32[]{:S(2)}) %collective-permute-start) | collective-permute-done | bytes 229408 | tf_op jit(solution)/shard_map/ppermute | solution.py:525
  25.8 0.9 %collective-permute-done.1.xh = f32[28,16,128]{2,1,0:T(8,128)S(1)} collective-permute-done((f32[28,16,128]{2,1,0:T(8,128)S(1)}, f32[28,16,128]{2,1,0:T(8,128)S(1)}, u32[]{:S(2)}, u32[]{:S(2)}) %collective-permute-start.1) | collective-permute-done | bytes 229408 | tf_op jit(solution)/shard_map/ppermute | solution.py:525
  26.7 2.7 %collective-permute-start.4 = (f32[18,8,128]{2,1,0:T(8,128)S(1)}, f32[18,8,128]{2,1,0:T(8,128)S(1)}, u32[]{:S(2)}, u32[]{:S(2)}) collective-permute-start(f32[18,8,128]{2,1,0:T(8,128)S(1)} %get-tuple-element.38), channel_id=1, source_target_pairs={{0,1},{1,2},{2,3},{3,4},{4,5},{5,6},{6,7},{7,0},{8,9},{9,10},{10,1... | collective-permute-start | bytes 221192 | tf_op jit(solution)/shard_map/ppermute | solution.py:525
  29.3 0.0 collective-permute-start.5
  30.0 0.0 collective-permute-done.2.yl
  30.0 0.0 collective-permute-done.3.yh
  30.0 0.7 collective-permute-done.4.cl
  30.7 2.4 %collective-permute-done.5.ch = f32[18,8,128]{2,1,0:T(8,128)S(1)} collective-permute-done((f32[18,8,128]{2,1,0:T(8,128)S(1)}, f32[18,8,128]{2,1,0:T(8,128)S(1)}, u32[]{:S(2)}, u32[]{:S(2)}) %collective-permute-start.5) | collective-permute-done | bytes 73760 | tf_op jit(solution)/shard_map/ppermute | solution.py:525
  33.1 0.0 copy-done.3
  33.1 0.0 copy-done.2
  33.1 0.0 copy-done.1
  33.1 0.0 copy-done
  33.1 4.2 %shard_map.87 = (f32[19,8,16,128]{3,2,1,0:T(8,128)S(1)}, f32[8,16,128]{2,1,0:T(8,128)S(1)}, f32[2,8,16,128]{3,2,1,0:T(8,128)S(1)}, f32[8,16,128]{2,1,0:T(8,128)S...) custom-call(s32[1,1]{1,0:T(1,128)S(6)} %copy.9.owner, ...), custom_call_target="tpu_custom_call" | custom-call | tf_op jit(solution)/shard_map/pallas_call | solution.py:507
  37.4 1.9 %collective-permute-start.6 = (f32[19,16,128]{2,1,0:T(8,128)S(1)}, f32[19,16,128]{2,1,0:T(8,128)S(1)}, u32[]{:S(2)}, u32[]{:S(2)}) collective-permute-start(f32[19,16,128]{2,1,0:T(8,128)S(1)} %get-tuple-element.49), channel_id=1, source_target_pairs={{0,8},{8,16},{16,24},{24,32},{32,40},{40,48},{48,56},{56,64},{64,7... | collective-permute-start | bytes 466952 | tf_op jit(solution)/shard_map/ppermute | solution.py:525
  39.3 7.4 %collective-permute-start.7 = (f32[19,16,128]{2,1,0:T(8,128)S(1)}, f32[19,16,128]{2,1,0:T(8,128)S(1)}, u32[]{:S(2)}, u32[]{:S(2)}) collective-permute-start(f32[19,16,128]{2,1,0:T(8,128)S(1)} %get-tuple-element.50), channel_id=1, source_target_pairs={{0,760},{8,0},{16,8},{24,16},{32,24},{40,32},{48,40},{56,48},{64,5... | collective-permute-start | bytes 466952 | tf_op jit(solution)/shard_map/ppermute | solution.py:525
  46.7 0.3 collective-permute-start.8
  47.0 0.2 collective-permute-start.9
  47.3 1.8 %collective-permute-done.6.xl = f32[19,16,128]{2,1,0:T(8,128)S(1)} collective-permute-done((f32[19,16,128]{2,1,0:T(8,128)S(1)}, f32[19,16,128]{2,1,0:T(8,128)S(1)}, u32[]{:S(2)}, u32[]{:S(2)}) %collective-permute-start.6) | collective-permute-done | bytes 155680 | tf_op jit(solution)/shard_map/ppermute | solution.py:525
  49.1 0.9 %collective-permute-done.7.xh = f32[19,16,128]{2,1,0:T(8,128)S(1)} collective-permute-done((f32[19,16,128]{2,1,0:T(8,128)S(1)}, f32[19,16,128]{2,1,0:T(8,128)S(1)}, u32[]{:S(2)}, u32[]{:S(2)}) %collective-permute-start.7) | collective-permute-done | bytes 155680 | tf_op jit(solution)/shard_map/ppermute | solution.py:525
  50.0 0.9 %collective-permute-start.10 = (f32[12,8,128]{2,1,0:T(8,128)S(1)}, f32[12,8,128]{2,1,0:T(8,128)S(1)}, u32[]{:S(2)}, u32[]{:S(2)}) collective-permute-start(f32[12,8,128]{2,1,0:T(8,128)S(1)} %get-tuple-element.53), channel_id=1, source_target_pairs={{0,1},{1,2},{2,3},{3,4},{4,5},{5,6},{6,7},{7,0},{8,9},{9,10},{10,1... | collective-permute-start | bytes 147464 | tf_op jit(solution)/shard_map/ppermute | solution.py:525
  50.9 0.1 collective-permute-start.11
  51.0 0.0 collective-permute-done.8.yl
  51.0 0.4 collective-permute-done.9.yh
  51.4 0.7 collective-permute-done.10.cl
  52.1 2.3 %collective-permute-done.11.ch = f32[12,8,128]{2,1,0:T(8,128)S(1)} collective-permute-done((f32[12,8,128]{2,1,0:T(8,128)S(1)}, f32[12,8,128]{2,1,0:T(8,128)S(1)}, u32[]{:S(2)}, u32[]{:S(2)}) %collective-permute-start.11) | collective-permute-done | bytes 49184 | tf_op jit(solution)/shard_map/ppermute | solution.py:525
  54.4 3.0 %shard_map.89 = (f32[8,16,128]{2,1,0:T(8,128)}, f32[4,16,16,128]{3,2,1,0:T(8,128)S(1)}, f32[5,10,32,128]{3,2,1,0:T(8,128)S(1)}) custom-call(f32[2,8,16,128]{3,2,1,0:T(8,128)S(1)} %get-tuple-element.42.conc, f32[8,16,128]{2,1,0:T(8,128)S(1)} %get-tuple-element.43.phi, f32[8,16,128]{2,1,0:T(8,128)S(1)} %get-tuple-element.44.charge, ...), custom_call_target="tpu_custom_call" | custom-call | tf_op jit(solution)/shard_map/pallas_call | solution.py:507
  57.4 13.9 %all_to_all.5.came = f32[4,16,16,128]{3,2,1,0:T(8,128)S(1)} all-to-all(f32[4,16,16,128]{3,2,1,0:T(8,128)S(1)} %get-tuple-element.57), channel_id=1, replica_groups={{0,2,4,6},{1,3,5,7},{8,10,12,14},{9,11,13,15},{16,18,20,22},{17,19,21,2..., dimensions={0} | all-to-all | bytes 1048576 | tf_op jit(solution)/shard_map/all_to_all | solution.py:570
  71.4 1.9 %collective-permute-start.12 = (f32[16,16,128]{2,1,0:T(8,128)S(1)}, f32[16,16,128]{2,1,0:T(8,128)S(1)}, u32[]{:S(2)}, u32[]{:S(2)}) collective-permute-start(f32[16,16,128]{2,1,0:T(8,128)S(1)} %shard_map.91), channel_id=1, source_target_pairs={{0,1},{1,0},{2,3},{3,2},{4,5},{5,4},{6,7},{7,6},{8,9},{9,8},{10,11... | collective-permute-start | bytes 393224 | tf_op jit(solution)/shard_map/ppermute | solution.py:573
  73.3 2.1 %shard_map.90 = f32[19,8,16,128]{3,2,1,0:T(8,128)} custom-call(f32[19,8,16,128]{3,2,1,0:T(8,128)S(1)} %get-tuple-element.40.pop, f32[10,32,128]{2,1,0:T(8,128)S(1)} %get-tuple-element.41.fl, f32[5,10,32,128]{3,2,1,0:T(8,128)S(1)} %get-tuple-element.55.sh, f32[19,16,128]{2,1,0:T(8,128)S(1)} %collective-permute-done.6.xl, ...), custom_call_target="tpu_custom_call" | custom-call | flops 40000000 | tf_op jit(solution)/shard_map/pallas_call | solution.py:507
  75.4 0.0 collective-permute-done.12.crossed
  75.4 0.7 shard_map.92
  (3 shorter events, 0.1 us)
Async XLA Ops:
  0.6 32.5 %copy-start.3 = (f32[8,16,128]{2,1,0:T(8,128)S(1)}, f32[8,16,128]{2,1,0:T(8,128)}, u32[]{:S(2)}) copy-start(f32[8,16,128]{2,1,0:T(8,128)} %perm.1) | copy-start | bytes 196612
  0.6 32.5 %copy-start.2 = (f32[8,16,128]{2,1,0:T(8,128)S(1)}, f32[8,16,128]{2,1,0:T(8,128)}, u32[]{:S(2)}) copy-start(f32[8,16,128]{2,1,0:T(8,128)} %phi.1) | copy-start | bytes 196612
  0.7 32.5 %copy-start.1 = (f32[2,8,16,128]{3,2,1,0:T(8,128)S(1)}, f32[2,8,16,128]{3,2,1,0:T(8,128)}, u32[]{:S(2)}) copy-start(f32[2,8,16,128]{3,2,1,0:T(8,128)} %conc.1) | copy-start | bytes 393220
  0.7 32.5 %copy-start = (f32[19,8,16,128]{3,2,1,0:T(8,128)S(1)}, f32[19,8,16,128]{3,2,1,0:T(8,128)}, u32[]{:S(2)}) copy-start(f32[19,8,16,128]{3,2,1,0:T(8,128)} %pop.1) | copy-start | bytes 3735556
  2.4 23.4 %collective-permute-start = (f32[28,16,128]{2,1,0:T(8,128)S(1)}, f32[28,16,128]{2,1,0:T(8,128)S(1)}, u32[]{:S(2)}, u32[]{:S(2)}) collective-permute-start(f32[28,16,128]{2,1,0:T(8,128)S(1)} %get-tuple-element.34), channel_id=1, source_target_pairs={{0,8},{8,16},{16,24},{24,32},{32,40},{40,48},{48,56},{56,64},{64,7... | collective-permute-start | bytes 688136 | tf_op jit(solution)/shard_map/ppermute | solution.py:525
  6.4 20.2 %collective-permute-start.1 = (f32[28,16,128]{2,1,0:T(8,128)S(1)}, f32[28,16,128]{2,1,0:T(8,128)S(1)}, u32[]{:S(2)}, u32[]{:S(2)}) collective-permute-start(f32[28,16,128]{2,1,0:T(8,128)S(1)} %get-tuple-element.35), channel_id=1, source_target_pairs={{0,760},{8,0},{16,8},{24,16},{32,24},{40,32},{48,40},{56,48},{64,5... | collective-permute-start | bytes 688136 | tf_op jit(solution)/shard_map/ppermute | solution.py:525
  22.4 7.6 %collective-permute-start.2 = (f32[8,32,128]{2,1,0:T(8,128)S(1)}, f32[8,32,128]{2,1,0:T(8,128)S(1)}, u32[]{:S(2)}, u32[]{:S(2)}) collective-permute-start(f32[8,32,128]{2,1,0:T(8,128)S(1)} %get-tuple-element.36), channel_id=1, source_target_pairs={{0,1},{1,2},{2,3},{3,4},{4,5},{5,6},{6,7},{7,0},{8,9},{9,10},{10,1... | collective-permute-start | bytes 393224 | tf_op jit(solution)/shard_map/ppermute | solution.py:525
  24.4 5.5 %collective-permute-start.3 = (f32[8,32,128]{2,1,0:T(8,128)S(1)}, f32[8,32,128]{2,1,0:T(8,128)S(1)}, u32[]{:S(2)}, u32[]{:S(2)}) collective-permute-start(f32[8,32,128]{2,1,0:T(8,128)S(1)} %get-tuple-element.37), channel_id=1, source_target_pairs={{0,7},{1,0},{2,1},{3,2},{4,3},{5,4},{6,5},{7,6},{8,15},{9,8},{10,9... | collective-permute-start | bytes 393224 | tf_op jit(solution)/shard_map/ppermute | solution.py:525
  26.7 4.1 %collective-permute-start.4 = (f32[18,8,128]{2,1,0:T(8,128)S(1)}, f32[18,8,128]{2,1,0:T(8,128)S(1)}, u32[]{:S(2)}, u32[]{:S(2)}) collective-permute-start(f32[18,8,128]{2,1,0:T(8,128)S(1)} %get-tuple-element.38), channel_id=1, source_target_pairs={{0,1},{1,2},{2,3},{3,4},{4,5},{5,6},{6,7},{7,0},{8,9},{9,10},{10,1... | collective-permute-start | bytes 221192 | tf_op jit(solution)/shard_map/ppermute | solution.py:525
  29.3 3.8 %collective-permute-start.5 = (f32[18,8,128]{2,1,0:T(8,128)S(1)}, f32[18,8,128]{2,1,0:T(8,128)S(1)}, u32[]{:S(2)}, u32[]{:S(2)}) collective-permute-start(f32[18,8,128]{2,1,0:T(8,128)S(1)} %get-tuple-element.39), channel_id=1, source_target_pairs={{0,7},{1,0},{2,1},{3,2},{4,3},{5,4},{6,5},{7,6},{8,15},{9,8},{10,9... | collective-permute-start | bytes 221192 | tf_op jit(solution)/shard_map/ppermute | solution.py:525
  37.4 11.7 %collective-permute-start.6 = (f32[19,16,128]{2,1,0:T(8,128)S(1)}, f32[19,16,128]{2,1,0:T(8,128)S(1)}, u32[]{:S(2)}, u32[]{:S(2)}) collective-permute-start(f32[19,16,128]{2,1,0:T(8,128)S(1)} %get-tuple-element.49), channel_id=1, source_target_pairs={{0,8},{8,16},{16,24},{24,32},{32,40},{40,48},{48,56},{56,64},{64,7... | collective-permute-start | bytes 466952 | tf_op jit(solution)/shard_map/ppermute | solution.py:525
  39.3 10.7 %collective-permute-start.7 = (f32[19,16,128]{2,1,0:T(8,128)S(1)}, f32[19,16,128]{2,1,0:T(8,128)S(1)}, u32[]{:S(2)}, u32[]{:S(2)}) collective-permute-start(f32[19,16,128]{2,1,0:T(8,128)S(1)} %get-tuple-element.50), channel_id=1, source_target_pairs={{0,760},{8,0},{16,8},{24,16},{32,24},{40,32},{48,40},{56,48},{64,5... | collective-permute-start | bytes 466952 | tf_op jit(solution)/shard_map/ppermute | solution.py:525
  46.7 4.3 %collective-permute-start.8 = (f32[8,24,128]{2,1,0:T(8,128)S(1)}, f32[8,24,128]{2,1,0:T(8,128)S(1)}, u32[]{:S(2)}, u32[]{:S(2)}) collective-permute-start(f32[8,24,128]{2,1,0:T(8,128)S(1)} %get-tuple-element.51), channel_id=1, source_target_pairs={{0,1},{1,2},{2,3},{3,4},{4,5},{5,6},{6,7},{7,0},{8,9},{9,10},{10,1... | collective-permute-start | bytes 294920 | tf_op jit(solution)/shard_map/ppermute | solution.py:525
  47.0 4.3 %collective-permute-start.9 = (f32[8,24,128]{2,1,0:T(8,128)S(1)}, f32[8,24,128]{2,1,0:T(8,128)S(1)}, u32[]{:S(2)}, u32[]{:S(2)}) collective-permute-start(f32[8,24,128]{2,1,0:T(8,128)S(1)} %get-tuple-element.52), channel_id=1, source_target_pairs={{0,7},{1,0},{2,1},{3,2},{4,3},{5,4},{6,5},{7,6},{8,15},{9,8},{10,9... | collective-permute-start | bytes 294920 | tf_op jit(solution)/shard_map/ppermute | solution.py:525
  50.0 2.0 %collective-permute-start.10 = (f32[12,8,128]{2,1,0:T(8,128)S(1)}, f32[12,8,128]{2,1,0:T(8,128)S(1)}, u32[]{:S(2)}, u32[]{:S(2)}) collective-permute-start(f32[12,8,128]{2,1,0:T(8,128)S(1)} %get-tuple-element.53), channel_id=1, source_target_pairs={{0,1},{1,2},{2,3},{3,4},{4,5},{5,6},{6,7},{7,0},{8,9},{9,10},{10,1... | collective-permute-start | bytes 147464 | tf_op jit(solution)/shard_map/ppermute | solution.py:525
  50.9 3.5 %collective-permute-start.11 = (f32[12,8,128]{2,1,0:T(8,128)S(1)}, f32[12,8,128]{2,1,0:T(8,128)S(1)}, u32[]{:S(2)}, u32[]{:S(2)}) collective-permute-start(f32[12,8,128]{2,1,0:T(8,128)S(1)} %get-tuple-element.54), channel_id=1, source_target_pairs={{0,7},{1,0},{2,1},{3,2},{4,3},{5,4},{6,5},{7,6},{8,15},{9,8},{10,9... | collective-permute-start | bytes 147464 | tf_op jit(solution)/shard_map/ppermute | solution.py:525
  71.4 4.0 %collective-permute-start.12 = (f32[16,16,128]{2,1,0:T(8,128)S(1)}, f32[16,16,128]{2,1,0:T(8,128)S(1)}, u32[]{:S(2)}, u32[]{:S(2)}) collective-permute-start(f32[16,16,128]{2,1,0:T(8,128)S(1)} %shard_map.91), channel_id=1, source_target_pairs={{0,1},{1,0},{2,3},{3,2},{4,5},{5,4},{6,7},{7,6},{8,9},{9,8},{10,11... | collective-permute-start | bytes 393224 | tf_op jit(solution)/shard_map/ppermute | solution.py:573

commit v5 on v4

--- a/solution.py
+++ b/solution.py
@@ -272,7 +272,7 @@
             dst[x] = acc
             return 0
 
-        lax.fori_loop(1 + sweep, 19 - sweep, relax, 0, unroll=6)
+        lax.fori_loop(1 + sweep, 19 - sweep, relax, 0, unroll=True)
         src, dst = dst, src
     return src
 
@@ -300,7 +300,7 @@
         sh[4, p] = dens * (1.0 / TAU)
         return 0
 
-    lax.fori_loop(0, 10, plane, 0, unroll=2)
+    lax.fori_loop(0, 10, plane, 0, unroll=5)
 
 
 def ions(fin, fl, cc, vel, store):
@@ -330,7 +330,7 @@
             store(s, p - 1, cm - total)
         return tuple(after)
 
-    lax.fori_loop(1, 9, plane, (x_face(0, 0), x_face(1, 0)), unroll=4)
+    lax.fori_loop(1, 9, plane, (x_face(0, 0), x_face(1, 0)), unroll=8)
 
 
 def collide_and_stream(plan, pop, fl, sh, msgs, lv, pop_out, dm_out):
@@ -406,7 +406,7 @@
                 dm_out[k, x] = v
         return 0
 
-    lax.fori_loop(0, CX, stream, 0, unroll=2)
+    lax.fori_loop(0, CX, stream, 0, unroll=4)
 
 
 def step_one_kernel(owner, pop, conc, phi, perm, dm, charge, fluid, xl, xh, yl, yh, cl, ch,
@@ -426,7 +426,7 @@
             coef[k, x] = faces[k] * over
         return 0
 
-    lax.fori_loop(1, 19, coefs, 0, unroll=6)
+    lax.fori_loop(1, 19, coefs, 0, unroll=9)
     fl[1:9, 8:24] = fluid[...]
     x, y = ONE.x, ONE.y
     for side, msg, p in ((0, xl, 0), (1, xh, 9)):
@@ -470,7 +470,8 @@
     ions(fin, fl, cc, vel, store)
 
 
-def flow_two_kernel(pop, fl, sh, xl, xh, yl, yh, cl, ch, pop_out, lv):
+def flow_two_kernel(pop, fl, sh, xl, xh, yl, yh, cl, ch, pop_out, mark, lv):
+    mark[...] = fl[0, 8:16]
     collide_and_stream(TWO, pop, fl, sh, (xl, xh, yl, yh, cl, ch), lv, pop_out, None)
 
 
@@ -485,7 +486,7 @@
     return v
 
 
-def route_kernel(came, yl, yh, out):
+def route_kernel(came, yl, yh, mark, out):
     o = TWO.y["owner"]
     mate = jnp.where(lax.rem(lax.axis_index("gy"), 2) == 0, yh[0, o : o + 1], yl[0, o : o + 1])
     for x in range(2 * CX):
@@ -566,10 +567,10 @@
     phi, mine, sh = call(
         ions_two_kernel, (block, shape(4, *slab.shape), shape(5, *RIM)),
         (conc, phi, charge, dm, rim, coef, inv, fl) + got, FIELDS)
-    (pop,) = call(flow_two_kernel, (pops,), (pop, fl, sh) + got, ((19,) + RIM,), flops=40_000_000)
+    pop, mark = call(flow_two_kernel, (pops, row), (pop, fl, sh) + got, ((19,) + RIM,), flops=40_000_000)
     came = lax.all_to_all(
         mine, "gy", 0, 0, axis_index_groups=[[0, 2, 4, 6], [1, 3, 5, 7]], tiled=True)
-    (cross,) = call(route_kernel, (slab,), (came, got[2], got[3]))
+    (cross,) = call(route_kernel, (slab,), (came, got[2], got[3], mark))
     crossed = lax.ppermute(cross, "gy", [(i, i ^ 1) for i in range(8)])
     (migrated,) = call(arrive_kernel, (slab,), (came, crossed, owner))
     return (pop, phi, migrated.reshape(2, CX, CY, NZ))

time: 76.4 us -> 75.1 us (0.983)
  blocking collectives: 13.9 us -> 0 us
  waiting for transfers between devices: 11.4 us -> 20.4 us
  starting transfers between devices: 37.5 us -> 43.1 us
  Pallas kernels: 11.8 us -> 9.03 us
  local copies, waits for them, and re-layouts: 0.02 us -> 0.82 us
    all_to_all x1 -> x0, blocking collectives: 13.9 us -> none  [body(): lax.all_to_all(mine, 'gy', 0, 0, axis_index_groups=[[0, 2, 4, 6], [1, 3,...]
    all_to_all x0 -> x1, waiting for transfers between devices: none -> 8.04 us  [body(): lax.all_to_all(mine, 'gy', 0, 0, axis_index_groups=[[0, 2, 4, 6], [1, 3,...]
    all_to_all x0 -> x1, starting transfers between devices: none -> 5.15 us  [body(): lax.all_to_all(mine, 'gy', 0, 0, axis_index_groups=[[0, 2, 4, 6], [1, 3,...]
    pallas_call x8, Pallas kernels: 11.8 us -> 9.03 us  [call(): pl.pallas_call(kernel, out_shape=outs, in_specs=specs or [VMEM] * len(arg...]
    ppermute x1, waiting for transfers between devices: 0.01 us -> 0.96 us  [body(): crossed = lax.ppermute(cross, 'gy', [(i, i ^ 1) for i in range(8)])]
    unnamed x8 -> x10, local copies, waits for them, and re-layouts: 0.02 us -> 0.82 us
  transfers between devices with their start and end apart: 13 -> 14, of which waited for: 9 -> 11; matrix products, arithmetic and copies ran while one was open for 0% -> 0% of each run, Pallas kernels for 3% -> 3%
where the time goes in v5:
time: 75.1 us; the launch traced here: 74.8 us
  starting transfers between devices  43.1 us (57%)
  waiting for transfers between devices  20.4 us (27%)
  Pallas kernels  9.03 us (12%)
  between operations  1.42 us (2%)
  local copies, waits for them, and re-layouts  0.82 us (1%)
    ppermute x12, starting transfers between devices, shift(): return lax.ppermute(values, axis, [(i, (i + by) % n) for i in range(n)])  35.5 us
    ppermute x12, waiting for transfers between devices, shift(): return lax.ppermute(values, axis, [(i, (i + by) % n) for i in range(n)])  11.4 us
    pallas_call x8, Pallas kernels, call(): pl.pallas_call(kernel, out_shape=outs, in_specs=specs or [VMEM] * len(arg...  9.03 us
    all_to_all x1, waiting for transfers between devices, body(): lax.all_to_all(mine, 'gy', 0, 0, axis_index_groups=[[0, 2, 4, 6], [1, 3,...  8.04 us
    all_to_all x1, starting transfers between devices, body(): lax.all_to_all(mine, 'gy', 0, 0, axis_index_groups=[[0, 2, 4, 6], [1, 3,...  5.15 us
    ppermute x1, starting transfers between devices, body(): crossed = lax.ppermute(cross, 'gy', [(i, i ^ 1) for i in range(8)])  2.38 us
  transfers between devices with their start and end apart: 14, of which 11 were waited for; matrix products, arithmetic and copies ran while one was open for 0% of the time, Pallas kernels for 3%

profile of v5, /device:TPU:1, one launch (start us, length us, event | category | flops | bytes accessed | tf_op | source)
XLA Modules:
  0.0 74.8 jit_solution(9526987365749742748)
XLA Ops:
  0.6 0.0 copy-start.4
  0.6 0.0 copy-start.3
  0.7 0.0 copy-start.1
  0.7 0.0 copy-start
  0.7 1.7 %shard_map.85 = (f32[28,16,128]{2,1,0:T(8,128)S(1)}, f32[28,16,128]{2,1,0:T(8,128)S(1)}, f32[8,32,128]{2,1,0:T(8,128)S(1)}, f32[8,32,128]{2,1,0:T(8,128)S(1)}, f...) custom-call(f32[19,8,16,128]{3,2,1,0:T(8,128)} %pop.1, f32[2,8,16,128]{3,2,1,0:T(8,128)} %conc.1, ...), custom_call_target="tpu_custom_call" | custom-call | tf_op jit(solution)/shard_map/pallas_call | solution.py:508
  2.4 4.0 %collective-permute-start = (f32[28,16,128]{2,1,0:T(8,128)S(1)}, f32[28,16,128]{2,1,0:T(8,128)S(1)}, u32[]{:S(2)}, u32[]{:S(2)}) collective-permute-start(f32[28,16,128]{2,1,0:T(8,128)S(1)} %get-tuple-element.36), channel_id=1, source_target_pairs={{0,8},{8,16},{16,24},{24,32},{32,40},{40,48},{48,56},{56,64},{64,7... | collective-permute-start | bytes 688136 | tf_op jit(solution)/shard_map/ppermute | solution.py:526
  6.4 15.9 %collective-permute-start.1 = (f32[28,16,128]{2,1,0:T(8,128)S(1)}, f32[28,16,128]{2,1,0:T(8,128)S(1)}, u32[]{:S(2)}, u32[]{:S(2)}) collective-permute-start(f32[28,16,128]{2,1,0:T(8,128)S(1)} %get-tuple-element.37), channel_id=1, source_target_pairs={{0,760},{8,0},{16,8},{24,16},{32,24},{40,32},{48,40},{56,48},{64,5... | collective-permute-start | bytes 688136 | tf_op jit(solution)/shard_map/ppermute | solution.py:526
  22.4 2.1 %collective-permute-start.2 = (f32[8,32,128]{2,1,0:T(8,128)S(1)}, f32[8,32,128]{2,1,0:T(8,128)S(1)}, u32[]{:S(2)}, u32[]{:S(2)}) collective-permute-start(f32[8,32,128]{2,1,0:T(8,128)S(1)} %get-tuple-element.38), channel_id=1, source_target_pairs={{0,1},{1,2},{2,3},{3,4},{4,5},{5,6},{6,7},{7,0},{8,9},{9,10},{10,1... | collective-permute-start | bytes 393224 | tf_op jit(solution)/shard_map/ppermute | solution.py:526
  24.4 0.0 collective-permute-start.3
  24.4 1.3 %collective-permute-done.xl = f32[28,16,128]{2,1,0:T(8,128)S(1)} collective-permute-done((f32[28,16,128]{2,1,0:T(8,128)S(1)}, f32[28,16,128]{2,1,0:T(8,128)S(1)}, u32[]{:S(2)}, u32[]{:S(2)}) %collective-permute-start) | collective-permute-done | bytes 229408 | tf_op jit(solution)/shard_map/ppermute | solution.py:526
  25.8 0.9 %collective-permute-done.1.xh = f32[28,16,128]{2,1,0:T(8,128)S(1)} collective-permute-done((f32[28,16,128]{2,1,0:T(8,128)S(1)}, f32[28,16,128]{2,1,0:T(8,128)S(1)}, u32[]{:S(2)}, u32[]{:S(2)}) %collective-permute-start.1) | collective-permute-done | bytes 229408 | tf_op jit(solution)/shard_map/ppermute | solution.py:526
  26.7 2.7 %collective-permute-start.4 = (f32[18,8,128]{2,1,0:T(8,128)S(1)}, f32[18,8,128]{2,1,0:T(8,128)S(1)}, u32[]{:S(2)}, u32[]{:S(2)}) collective-permute-start(f32[18,8,128]{2,1,0:T(8,128)S(1)} %get-tuple-element.40), channel_id=1, source_target_pairs={{0,1},{1,2},{2,3},{3,4},{4,5},{5,6},{6,7},{7,0},{8,9},{9,10},{10,1... | collective-permute-start | bytes 221192 | tf_op jit(solution)/shard_map/ppermute | solution.py:526
  29.3 0.0 collective-permute-start.5
  30.0 0.0 collective-permute-done.2.yl
  30.0 0.0 collective-permute-done.3.yh
  30.0 0.7 collective-permute-done.4.cl
  30.7 2.4 %collective-permute-done.5.ch = f32[18,8,128]{2,1,0:T(8,128)S(1)} collective-permute-done((f32[18,8,128]{2,1,0:T(8,128)S(1)}, f32[18,8,128]{2,1,0:T(8,128)S(1)}, u32[]{:S(2)}, u32[]{:S(2)}) %collective-permute-start.5) | collective-permute-done | bytes 73760 | tf_op jit(solution)/shard_map/ppermute | solution.py:526
  33.1 0.0 copy-done.4
  33.1 0.0 copy-done.3
  33.1 0.0 copy-done.1
  33.1 0.0 copy-done
  33.1 2.7 %shard_map.87 = (f32[19,8,16,128]{3,2,1,0:T(8,128)S(1)}, f32[8,16,128]{2,1,0:T(8,128)S(1)}, f32[2,8,16,128]{3,2,1,0:T(8,128)S(1)}, f32[8,16,128]{2,1,0:T(8,128)S...) custom-call(s32[1,1]{1,0:T(1,128)S(6)} %copy.9.owner, ...), custom_call_target="tpu_custom_call" | custom-call | tf_op jit(solution)/shard_map/pallas_call | solution.py:508
  35.9 1.9 %collective-permute-start.6 = (f32[19,16,128]{2,1,0:T(8,128)S(1)}, f32[19,16,128]{2,1,0:T(8,128)S(1)}, u32[]{:S(2)}, u32[]{:S(2)}) collective-permute-start(f32[19,16,128]{2,1,0:T(8,128)S(1)} %get-tuple-element.51), channel_id=1, source_target_pairs={{0,8},{8,16},{16,24},{24,32},{32,40},{40,48},{48,56},{56,64},{64,7... | collective-permute-start | bytes 466952 | tf_op jit(solution)/shard_map/ppermute | solution.py:526
  37.8 7.4 %collective-permute-start.7 = (f32[19,16,128]{2,1,0:T(8,128)S(1)}, f32[19,16,128]{2,1,0:T(8,128)S(1)}, u32[]{:S(2)}, u32[]{:S(2)}) collective-permute-start(f32[19,16,128]{2,1,0:T(8,128)S(1)} %get-tuple-element.52), channel_id=1, source_target_pairs={{0,760},{8,0},{16,8},{24,16},{32,24},{40,32},{48,40},{56,48},{64,5... | collective-permute-start | bytes 466952 | tf_op jit(solution)/shard_map/ppermute | solution.py:526
  45.2 0.3 collective-permute-start.8
  45.5 0.2 collective-permute-start.9
  45.7 1.8 %collective-permute-done.6.xl = f32[19,16,128]{2,1,0:T(8,128)S(1)} collective-permute-done((f32[19,16,128]{2,1,0:T(8,128)S(1)}, f32[19,16,128]{2,1,0:T(8,128)S(1)}, u32[]{:S(2)}, u32[]{:S(2)}) %collective-permute-start.6) | collective-permute-done | bytes 155680 | tf_op jit(solution)/shard_map/ppermute | solution.py:526
  47.6 0.9 %collective-permute-done.7.xh = f32[19,16,128]{2,1,0:T(8,128)S(1)} collective-permute-done((f32[19,16,128]{2,1,0:T(8,128)S(1)}, f32[19,16,128]{2,1,0:T(8,128)S(1)}, u32[]{:S(2)}, u32[]{:S(2)}) %collective-permute-start.7) | collective-permute-done | bytes 155680 | tf_op jit(solution)/shard_map/ppermute | solution.py:526
  48.5 0.9 %collective-permute-start.10 = (f32[12,8,128]{2,1,0:T(8,128)S(1)}, f32[12,8,128]{2,1,0:T(8,128)S(1)}, u32[]{:S(2)}, u32[]{:S(2)}) collective-permute-start(f32[12,8,128]{2,1,0:T(8,128)S(1)} %get-tuple-element.55), channel_id=1, source_target_pairs={{0,1},{1,2},{2,3},{3,4},{4,5},{5,6},{6,7},{7,0},{8,9},{9,10},{10,1... | collective-permute-start | bytes 147464 | tf_op jit(solution)/shard_map/ppermute | solution.py:526
  49.4 0.1 collective-permute-start.11
  49.5 0.0 collective-permute-done.8.yl
  49.5 0.4 collective-permute-done.9.yh
  49.9 0.7 collective-permute-done.10.cl
  50.5 2.3 %collective-permute-done.11.ch = f32[12,8,128]{2,1,0:T(8,128)S(1)} collective-permute-done((f32[12,8,128]{2,1,0:T(8,128)S(1)}, f32[12,8,128]{2,1,0:T(8,128)S(1)}, u32[]{:S(2)}, u32[]{:S(2)}) %collective-permute-start.11) | collective-permute-done | bytes 49184 | tf_op jit(solution)/shard_map/ppermute | solution.py:526
  52.9 1.9 %shard_map.89 = (f32[8,16,128]{2,1,0:T(8,128)}, f32[4,16,16,128]{3,2,1,0:T(8,128)S(1)}, f32[5,10,32,128]{3,2,1,0:T(8,128)S(1)}) custom-call(f32[2,8,16,128]{3,2,1,0:T(8,128)S(1)} %get-tuple-element.44.conc, f32[8,16,128]{2,1,0:T(8,128)S(1)} %get-tuple-element.45.phi, f32[8,16,128]{2,1,0:T(8,128)S(1)} %get-tuple-element.46.charge, ...), custom_call_target="tpu_custom_call" | custom-call | tf_op jit(solution)/shard_map/pallas_call | solution.py:508
  54.8 0.0 copy-start.2
  54.8 0.8 %copy-done.2 = f32[4,16,16,128]{3,2,1,0:T(8,128)} copy-done((f32[4,16,16,128]{3,2,1,0:T(8,128)}, f32[4,16,16,128]{3,2,1,0:T(8,128)S(1)}, u32[]{:S(2)}) %copy-start.2) | copy-done | bytes 524312
  55.6 5.1 %all-to-all-start = ((f32[4,16,16,128]{3,2,1,0:T(8,128)}), f32[4,16,16,128]{3,2,1,0:T(8,128)S(1)}, u32[]{:S(2)}, u32[]{:S(2)}) async-start(f32[4,16,16,128]{3,2,1,0:T(8,128)} %copy-done.2), calls=%async_computation | async-start | bytes 1048576 | tf_op jit(solution)/shard_map/all_to_all | solution.py:571
  60.7 1.9 %shard_map.90 = (f32[19,8,16,128]{3,2,1,0:T(8,128)}, f32[8,128]{1,0:T(8,128)S(1)}) custom-call(f32[19,8,16,128]{3,2,1,0:T(8,128)S(1)} %get-tuple-element.42.pop, f32[10,32,128]{2,1,0:T(8,128)S(1)} %get-tuple-element.43.fl, f32[5,10,32,128]{3,2,1,0:T(8,128)S(1)} %get-tuple-element.57.sh, f32[19,16,128]{2,1,0:T(8,128)S(1)} %collective-permute-done.6.xl, ...), custom_call_target="tpu_custom_call" | custom-call | flops 40000000 | tf_op jit(solution)/shard_map/pallas_call | solution.py:508
  62.6 8.0 %all-to-all-done.came = f32[4,16,16,128]{3,2,1,0:T(8,128)S(1)} async-done(((f32[4,16,16,128]{3,2,1,0:T(8,128)}), f32[4,16,16,128]{3,2,1,0:T(8,128)S(1)}, u32[]{:S(2)}, u32[]{:S(2)}) %all-to-all-start) | async-done | bytes 524320 | tf_op jit(solution)/shard_map/all_to_all | solution.py:571
  70.7 2.4 %collective-permute-start.12 = (f32[16,16,128]{2,1,0:T(8,128)S(1)}, f32[16,16,128]{2,1,0:T(8,128)S(1)}, u32[]{:S(2)}, u32[]{:S(2)}) collective-permute-start(f32[16,16,128]{2,1,0:T(8,128)S(1)} %shard_map.91), channel_id=1, source_target_pairs={{0,1},{1,0},{2,3},{3,2},{4,5},{5,4},{6,7},{7,6},{8,9},{9,8},{10,11... | collective-permute-start | bytes 393224 | tf_op jit(solution)/shard_map/ppermute | solution.py:574
  73.1 1.0 %collective-permute-done.12.crossed = f32[16,16,128]{2,1,0:T(8,128)S(1)} collective-permute-done((f32[16,16,128]{2,1,0:T(8,128)S(1)}, f32[16,16,128]{2,1,0:T(8,128)S(1)}, u32[]{:S(2)}, u32[]{:S(2)}) %collective-permute-start.12) | collective-permute-done | bytes 131104 | tf_op jit(solution)/shard_map/ppermute | solution.py:574
  74.1 0.7 shard_map.92
  (3 shorter events, 0.1 us)
Async XLA Ops:
  0.6 32.5 %copy-start.4 = (f32[8,16,128]{2,1,0:T(8,128)S(1)}, f32[8,16,128]{2,1,0:T(8,128)}, u32[]{:S(2)}) copy-start(f32[8,16,128]{2,1,0:T(8,128)} %perm.1) | copy-start | bytes 196612
  0.6 32.5 %copy-start.3 = (f32[8,16,128]{2,1,0:T(8,128)S(1)}, f32[8,16,128]{2,1,0:T(8,128)}, u32[]{:S(2)}) copy-start(f32[8,16,128]{2,1,0:T(8,128)} %phi.1) | copy-start | bytes 196612
  0.7 32.5 %copy-start.1 = (f32[2,8,16,128]{3,2,1,0:T(8,128)S(1)}, f32[2,8,16,128]{3,2,1,0:T(8,128)}, u32[]{:S(2)}) copy-start(f32[2,8,16,128]{3,2,1,0:T(8,128)} %conc.1) | copy-start | bytes 393220
  0.7 32.5 %copy-start = (f32[19,8,16,128]{3,2,1,0:T(8,128)S(1)}, f32[19,8,16,128]{3,2,1,0:T(8,128)}, u32[]{:S(2)}) copy-start(f32[19,8,16,128]{3,2,1,0:T(8,128)} %pop.1) | copy-start | bytes 3735556
  2.4 23.4 %collective-permute-start = (f32[28,16,128]{2,1,0:T(8,128)S(1)}, f32[28,16,128]{2,1,0:T(8,128)S(1)}, u32[]{:S(2)}, u32[]{:S(2)}) collective-permute-start(f32[28,16,128]{2,1,0:T(8,128)S(1)} %get-tuple-element.36), channel_id=1, source_target_pairs={{0,8},{8,16},{16,24},{24,32},{32,40},{40,48},{48,56},{56,64},{64,7... | collective-permute-start | bytes 688136 | tf_op jit(solution)/shard_map/ppermute | solution.py:526
  6.4 20.2 %collective-permute-start.1 = (f32[28,16,128]{2,1,0:T(8,128)S(1)}, f32[28,16,128]{2,1,0:T(8,128)S(1)}, u32[]{:S(2)}, u32[]{:S(2)}) collective-permute-start(f32[28,16,128]{2,1,0:T(8,128)S(1)} %get-tuple-element.37), channel_id=1, source_target_pairs={{0,760},{8,0},{16,8},{24,16},{32,24},{40,32},{48,40},{56,48},{64,5... | collective-permute-start | bytes 688136 | tf_op jit(solution)/shard_map/ppermute | solution.py:526
  22.4 7.6 %collective-permute-start.2 = (f32[8,32,128]{2,1,0:T(8,128)S(1)}, f32[8,32,128]{2,1,0:T(8,128)S(1)}, u32[]{:S(2)}, u32[]{:S(2)}) collective-permute-start(f32[8,32,128]{2,1,0:T(8,128)S(1)} %get-tuple-element.38), channel_id=1, source_target_pairs={{0,1},{1,2},{2,3},{3,4},{4,5},{5,6},{6,7},{7,0},{8,9},{9,10},{10,1... | collective-permute-start | bytes 393224 | tf_op jit(solution)/shard_map/ppermute | solution.py:526
  24.4 5.5 %collective-permute-start.3 = (f32[8,32,128]{2,1,0:T(8,128)S(1)}, f32[8,32,128]{2,1,0:T(8,128)S(1)}, u32[]{:S(2)}, u32[]{:S(2)}) collective-permute-start(f32[8,32,128]{2,1,0:T(8,128)S(1)} %get-tuple-element.39), channel_id=1, source_target_pairs={{0,7},{1,0},{2,1},{3,2},{4,3},{5,4},{6,5},{7,6},{8,15},{9,8},{10,9... | collective-permute-start | bytes 393224 | tf_op jit(solution)/shard_map/ppermute | solution.py:526
  26.7 4.1 %collective-permute-start.4 = (f32[18,8,128]{2,1,0:T(8,128)S(1)}, f32[18,8,128]{2,1,0:T(8,128)S(1)}, u32[]{:S(2)}, u32[]{:S(2)}) collective-permute-start(f32[18,8,128]{2,1,0:T(8,128)S(1)} %get-tuple-element.40), channel_id=1, source_target_pairs={{0,1},{1,2},{2,3},{3,4},{4,5},{5,6},{6,7},{7,0},{8,9},{9,10},{10,1... | collective-permute-start | bytes 221192 | tf_op jit(solution)/shard_map/ppermute | solution.py:526
  29.3 3.8 %collective-permute-start.5 = (f32[18,8,128]{2,1,0:T(8,128)S(1)}, f32[18,8,128]{2,1,0:T(8,128)S(1)}, u32[]{:S(2)}, u32[]{:S(2)}) collective-permute-start(f32[18,8,128]{2,1,0:T(8,128)S(1)} %get-tuple-element.41), channel_id=1, source_target_pairs={{0,7},{1,0},{2,1},{3,2},{4,3},{5,4},{6,5},{7,6},{8,15},{9,8},{10,9... | collective-permute-start | bytes 221192 | tf_op jit(solution)/shard_map/ppermute | solution.py:526
  35.9 11.7 %collective-permute-start.6 = (f32[19,16,128]{2,1,0:T(8,128)S(1)}, f32[19,16,128]{2,1,0:T(8,128)S(1)}, u32[]{:S(2)}, u32[]{:S(2)}) collective-permute-start(f32[19,16,128]{2,1,0:T(8,128)S(1)} %get-tuple-element.51), channel_id=1, source_target_pairs={{0,8},{8,16},{16,24},{24,32},{32,40},{40,48},{48,56},{56,64},{64,7... | collective-permute-start | bytes 466952 | tf_op jit(solution)/shard_map/ppermute | solution.py:526
  37.8 10.7 %collective-permute-start.7 = (f32[19,16,128]{2,1,0:T(8,128)S(1)}, f32[19,16,128]{2,1,0:T(8,128)S(1)}, u32[]{:S(2)}, u32[]{:S(2)}) collective-permute-start(f32[19,16,128]{2,1,0:T(8,128)S(1)} %get-tuple-element.52), channel_id=1, source_target_pairs={{0,760},{8,0},{16,8},{24,16},{32,24},{40,32},{48,40},{56,48},{64,5... | collective-permute-start | bytes 466952 | tf_op jit(solution)/shard_map/ppermute | solution.py:526
  45.2 4.3 %collective-permute-start.8 = (f32[8,24,128]{2,1,0:T(8,128)S(1)}, f32[8,24,128]{2,1,0:T(8,128)S(1)}, u32[]{:S(2)}, u32[]{:S(2)}) collective-permute-start(f32[8,24,128]{2,1,0:T(8,128)S(1)} %get-tuple-element.53), channel_id=1, source_target_pairs={{0,1},{1,2},{2,3},{3,4},{4,5},{5,6},{6,7},{7,0},{8,9},{9,10},{10,1... | collective-permute-start | bytes 294920 | tf_op jit(solution)/shard_map/ppermute | solution.py:526
  45.5 4.3 %collective-permute-start.9 = (f32[8,24,128]{2,1,0:T(8,128)S(1)}, f32[8,24,128]{2,1,0:T(8,128)S(1)}, u32[]{:S(2)}, u32[]{:S(2)}) collective-permute-start(f32[8,24,128]{2,1,0:T(8,128)S(1)} %get-tuple-element.54), channel_id=1, source_target_pairs={{0,7},{1,0},{2,1},{3,2},{4,3},{5,4},{6,5},{7,6},{8,15},{9,8},{10,9... | collective-permute-start | bytes 294920 | tf_op jit(solution)/shard_map/ppermute | solution.py:526
  48.5 2.0 %collective-permute-start.10 = (f32[12,8,128]{2,1,0:T(8,128)S(1)}, f32[12,8,128]{2,1,0:T(8,128)S(1)}, u32[]{:S(2)}, u32[]{:S(2)}) collective-permute-start(f32[12,8,128]{2,1,0:T(8,128)S(1)} %get-tuple-element.55), channel_id=1, source_target_pairs={{0,1},{1,2},{2,3},{3,4},{4,5},{5,6},{6,7},{7,0},{8,9},{9,10},{10,1... | collective-permute-start | bytes 147464 | tf_op jit(solution)/shard_map/ppermute | solution.py:526
  49.4 3.5 %collective-permute-start.11 = (f32[12,8,128]{2,1,0:T(8,128)S(1)}, f32[12,8,128]{2,1,0:T(8,128)S(1)}, u32[]{:S(2)}, u32[]{:S(2)}) collective-permute-start(f32[12,8,128]{2,1,0:T(8,128)S(1)} %get-tuple-element.56), channel_id=1, source_target_pairs={{0,7},{1,0},{2,1},{3,2},{4,3},{5,4},{6,5},{7,6},{8,15},{9,8},{10,9... | collective-permute-start | bytes 147464 | tf_op jit(solution)/shard_map/ppermute | solution.py:526
  54.8 0.8 %copy-start.2 = (f32[4,16,16,128]{3,2,1,0:T(8,128)}, f32[4,16,16,128]{3,2,1,0:T(8,128)S(1)}, u32[]{:S(2)}) copy-start(f32[4,16,16,128]{3,2,1,0:T(8,128)S(1)} %get-tuple-element.60) | copy-start | bytes 1572868
  55.6 15.1 %all-to-all-start = ((f32[4,16,16,128]{3,2,1,0:T(8,128)}), f32[4,16,16,128]{3,2,1,0:T(8,128)S(1)}, u32[]{:S(2)}, u32[]{:S(2)}) async-start(f32[4,16,16,128]{3,2,1,0:T(8,128)} %copy-done.2), calls=%async_computation | async-start | bytes 1048576 | tf_op jit(solution)/shard_map/all_to_all | solution.py:571
  70.7 3.4 %collective-permute-start.12 = (f32[16,16,128]{2,1,0:T(8,128)S(1)}, f32[16,16,128]{2,1,0:T(8,128)S(1)}, u32[]{:S(2)}, u32[]{:S(2)}) collective-permute-start(f32[16,16,128]{2,1,0:T(8,128)S(1)} %shard_map.91), channel_id=1, source_target_pairs={{0,1},{1,0},{2,3},{3,2},{4,5},{5,4},{6,7},{7,6},{8,9},{9,8},{10,11... | collective-permute-start | bytes 393224 | tf_op jit(solution)/shard_map/ppermute | solution.py:574

commit v6 on v5

--- a/solution.py
+++ b/solution.py
@@ -215,9 +215,14 @@
     pack_corners(ONE, c_lo, True, xl, xh)
 
 
-def corner_two_kernel(xl, xh, rim, c_hi, c_lo):
+def owner_kernel(owner, out):
+    out[...] = jnp.full((8, NZ), owner[0, 0], jnp.int32).astype(F32)
+
+
+def corner_two_kernel(xl, xh, rim, yl, c_hi, c_lo):
     pack_corners(TWO, c_hi, False, xl, xh, rim)
     pack_corners(TWO, c_lo, True, xl, xh, rim)
+    c_hi[TWO.c["misc"], 7:8] = yl[0, TWO.y["owner"] : TWO.y["owner"] + 1]
 
 
 def lay_all(plan, phi, conc, dm, charge, msgs, pa, ce, dn, mm, cc):
@@ -409,11 +414,10 @@
     lax.fori_loop(0, CX, stream, 0, unroll=4)
 
 
-def step_one_kernel(owner, pop, conc, phi, perm, dm, charge, fluid, xl, xh, yl, yh, cl, ch,
-                    pop_out, phi_out, conc_out, charge_out, x_hi, x_lo, y_hi, y_lo, dm_out, rim, coef, inv, fl, owner_row,
+def step_one_kernel(below, pop, conc, phi, perm, dm, charge, fluid, xl, xh, yl, yh, cl, ch,
+                    pop_out, phi_out, conc_out, charge_out, x_hi, x_lo, y_hi, y_lo, dm_out, rim, coef, inv, fl,
                     pe, pa, pb, ce, dn, mm, cc, vel, sh, lv):
     msgs = (xl, xh, yl, yh, cl, ch)
-    owner_row[...] = jnp.full((8, NZ), owner[0, 0], jnp.int32).astype(F32)
     lay(pe, perm[...], "perm", ONE, msgs)
 
     def coefs(x, _):
@@ -451,7 +455,7 @@
     charge_out[...] = conc_out[0] - conc_out[1]
     for low, xo, yo in ((False, x_hi, y_hi), (True, x_lo, y_lo)):
         pack_x(TWO, xo, low, phi_out, charge_out, conc_out, pop_out, dm_out)
-        pack_y(TWO, yo, low, owner_row[0:1], phi_out, charge_out, conc_out, pop_out, dm_out)
+        pack_y(TWO, yo, low, below[0:1], phi_out, charge_out, conc_out, pop_out, dm_out)
 
 
 def ions_two_kernel(conc, phi, charge, dm, rim, coef, inv, fl, xl, xh, yl, yh, cl, ch,
@@ -464,41 +468,35 @@
     motion(fin, ce, fl, dn, mm, vel, sh)
 
     def store(s, x, values):
-        for k in range(4):
-            slab[k, s * CX + x] = values
+        slab[s * CX + x] = values
 
     ions(fin, fl, cc, vel, store)
-
-
-def flow_two_kernel(pop, fl, sh, xl, xh, yl, yh, cl, ch, pop_out, mark, lv):
-    mark[...] = fl[0, 8:16]
+    slab[2 * CX, 0:8] = jnp.broadcast_to(cl[TWO.c["misc"], 7:8], (8, NZ))
+
+
+def flow_two_kernel(pop, fl, sh, xl, xh, yl, yh, cl, ch, pop_out, lv):
     collide_and_stream(TWO, pop, fl, sh, (xl, xh, yl, yh, cl, ch), lv, pop_out, None)
 
 
-def chip_of(slab):
-    return jnp.floor(slab * 0.5)
-
-
-def choose(came, chip, x):
-    v = came[0, x]
-    for k in range(1, 4):
-        v = jnp.where(chip == float(k), came[k, x], v)
-    return v
-
-
-def route_kernel(came, yl, yh, mark, out):
-    o = TWO.y["owner"]
-    mate = jnp.where(lax.rem(lax.axis_index("gy"), 2) == 0, yh[0, o : o + 1], yl[0, o : o + 1])
+def place(up):
+    me = lax.rem(lax.axis_index("gy") + up, 8)
+    return jnp.full((1, NZ), me, jnp.int32).astype(F32)
+
+
+def route_kernel(mine, below, above, out):
+    want = below[2 * CX, 0:1]
     for x in range(2 * CX):
-        out[x] = choose(came, chip_of(mate), x)
-
-
-def arrive_kernel(came, crossed, owner, out):
+        out[x] = jnp.where(want == place(0), mine[x], jnp.where(want == place(1), above[x], below[x]))
+
+
+def arrive_kernel(mine, below, above, below_two, above_two, far, owner, out):
     slab = owner[0:1]
-    core = jnp.full((1, NZ), lax.rem(lax.axis_index("gy"), 2), jnp.int32).astype(F32)
-    here = slab - 2.0 * chip_of(slab) == core
+    near = ((0, mine), (7, below), (1, above), (6, below_two), (2, above_two))
     for x in range(2 * CX):
-        out[x] = jnp.where(here, choose(came, chip_of(slab), x), crossed[x])
+        v = far[x]
+        for up, values in near:
+            v = jnp.where(slab == place(up), values[x], v)
+        out[x] = v
 
 
 VMEM, FAR, SMEM = (pl.BlockSpec(memory_space=m) for m in (pltpu.VMEM, pltpu.HBM, pltpu.SMEM))
@@ -553,26 +551,28 @@
     got = exchange(*sent)
     c_hi, c_lo = call(corner_one_kernel, tiles(ONE), got[:2])
     got += (shift(c_hi, "gy", 1), shift(c_lo, "gy", -1))
+    (owner,) = call(owner_kernel, (row,), (owners,), (), [SMEM])
+    below = shift(owner, "gy", 1)
     pop, phi, conc, charge, *rest = call(
         step_one_kernel,
         (pops, block, both, block) + messages(TWO)
-        + (four, shape(4, CY, NZ), shape(6, *HALO), shape(*HALO), shape(*RIM), row),
-        (owners, populations, concentration, potential, permittivity, dm, charge, fluid) + got,
-        (HALO,) + FIELDS + ((5,) + RIM, (19,) + RIM), [SMEM] + [VMEM] * 13)
-    sent, (dm, rim, coef, inv, fl, owner) = rest[:4], rest[4:]
+        + (four, shape(4, CY, NZ), shape(6, *HALO), shape(*HALO), shape(*RIM)),
+        (below, populations, concentration, potential, permittivity, dm, charge, fluid) + got,
+        (HALO,) + FIELDS + ((5,) + RIM, (19,) + RIM))
+    sent, (dm, rim, coef, inv, fl) = rest[:4], rest[4:]
     got = exchange(*sent)
-    c_hi, c_lo = call(corner_two_kernel, tiles(TWO), got[:2] + (rim,))
+    c_hi, c_lo = call(corner_two_kernel, tiles(TWO), got[:2] + (rim, got[2]))
     got += (shift(c_hi, "gy", 1), shift(c_lo, "gy", -1))
     slab = shape(2 * CX, CY, NZ)
     phi, mine, sh = call(
-        ions_two_kernel, (block, shape(4, *slab.shape), shape(5, *RIM)),
+        ions_two_kernel, (block, shape(2 * CX + 1, CY, NZ), shape(5, *RIM)),
         (conc, phi, charge, dm, rim, coef, inv, fl) + got, FIELDS)
-    pop, mark = call(flow_two_kernel, (pops, row), (pop, fl, sh) + got, ((19,) + RIM,), flops=40_000_000)
-    came = lax.all_to_all(
-        mine, "gy", 0, 0, axis_index_groups=[[0, 2, 4, 6], [1, 3, 5, 7]], tiled=True)
-    (cross,) = call(route_kernel, (slab,), (came, got[2], got[3], mark))
-    crossed = lax.ppermute(cross, "gy", [(i, i ^ 1) for i in range(8)])
-    (migrated,) = call(arrive_kernel, (slab,), (came, crossed, owner))
+    below, above = shift(mine, "gy", 1), shift(mine, "gy", -1)
+    (pop,) = call(flow_two_kernel, (pops,), (pop, fl, sh) + got, ((19,) + RIM,), flops=40_000_000)
+    (routed,) = call(route_kernel, (slab,), (mine, below, above))
+    far = shift(routed, "gy", 4)
+    below_two, above_two = shift(below, "gy", 1), shift(above, "gy", -1)
+    (migrated,) = call(arrive_kernel, (slab,), (mine, below, above, below_two, above_two, far, owner))
     return (pop, phi, migrated.reshape(2, CX, CY, NZ))
 
 

time: 75.1 us -> 77.1 us (1.027)
  the two profiles are of different devices: /device:TPU:1 before, /device:TPU:7 now
where the time goes in v6:
time: 77.1 us; the launch traced here: 76.8 us
  starting transfers between devices  48.8 us (63%)
  waiting for transfers between devices  17 us (22%)
  Pallas kernels  9.56 us (12%)
  between operations  1.42 us (2%)
    ppermute x18, starting transfers between devices, shift(): return lax.ppermute(values, axis, [(i, (i + by) % n) for i in range(n)])  48.8 us
    ppermute x18, waiting for transfers between devices, shift(): return lax.ppermute(values, axis, [(i, (i + by) % n) for i in range(n)])  17 us
    pallas_call x9, Pallas kernels, call(): pl.pallas_call(kernel, out_shape=outs, in_specs=specs or [VMEM] * len(arg...  9.56 us
  transfers between devices with their start and end apart: 18, of which 9 were waited for; matrix products, arithmetic and copies ran while one was open for 0% of the time, Pallas kernels for 3%

profile of v6, /device:TPU:7, one launch (start us, length us, event | category | flops | bytes accessed | tf_op | source)
XLA Modules:
  0.0 76.8 jit_solution(7679536770913706455)
XLA Ops:
  0.6 0.0 copy-start.3
  0.6 0.0 copy-start.2
  0.7 0.0 copy-start.1
  0.7 0.0 copy-start
  0.7 1.7 %shard_map.86 = (f32[28,16,128]{2,1,0:T(8,128)S(1)}, f32[28,16,128]{2,1,0:T(8,128)S(1)}, f32[8,32,128]{2,1,0:T(8,128)S(1)}, f32[8,32,128]{2,1,0:T(8,128)S(1)}, f...) custom-call(f32[19,8,16,128]{3,2,1,0:T(8,128)} %pop.1, f32[2,8,16,128]{3,2,1,0:T(8,128)} %conc.1, ...), custom_call_target="tpu_custom_call" | custom-call | tf_op jit(solution)/shard_map/pallas_call | solution.py:506
  2.4 3.2 %collective-permute-start.1 = (f32[28,16,128]{2,1,0:T(8,128)S(1)}, f32[28,16,128]{2,1,0:T(8,128)S(1)}, u32[]{:S(2)}, u32[]{:S(2)}) collective-permute-start(f32[28,16,128]{2,1,0:T(8,128)S(1)} %get-tuple-element.33), channel_id=1, source_target_pairs={{0,8},{8,16},{16,24},{24,32},{32,40},{40,48},{48,56},{56,64},{64,7... | collective-permute-start | bytes 688136 | tf_op jit(solution)/shard_map/ppermute | solution.py:524
  5.6 15.9 %collective-permute-start.2 = (f32[28,16,128]{2,1,0:T(8,128)S(1)}, f32[28,16,128]{2,1,0:T(8,128)S(1)}, u32[]{:S(2)}, u32[]{:S(2)}) collective-permute-start(f32[28,16,128]{2,1,0:T(8,128)S(1)} %get-tuple-element.34), channel_id=1, source_target_pairs={{0,760},{8,0},{16,8},{24,16},{32,24},{40,32},{48,40},{56,48},{64,5... | collective-permute-start | bytes 688136 | tf_op jit(solution)/shard_map/ppermute | solution.py:524
  21.6 1.0 %collective-permute-start.3 = (f32[8,32,128]{2,1,0:T(8,128)S(1)}, f32[8,32,128]{2,1,0:T(8,128)S(1)}, u32[]{:S(2)}, u32[]{:S(2)}) collective-permute-start(f32[8,32,128]{2,1,0:T(8,128)S(1)} %get-tuple-element.35), channel_id=1, source_target_pairs={{0,1},{1,2},{2,3},{3,4},{4,5},{5,6},{6,7},{7,0},{8,9},{9,10},{10,1... | collective-permute-start | bytes 393224 | tf_op jit(solution)/shard_map/ppermute | solution.py:524
  22.6 0.0 collective-permute-start.4
  22.6 2.3 %collective-permute-done.1.xl = f32[28,16,128]{2,1,0:T(8,128)S(1)} collective-permute-done((f32[28,16,128]{2,1,0:T(8,128)S(1)}, f32[28,16,128]{2,1,0:T(8,128)S(1)}, u32[]{:S(2)}, u32[]{:S(2)}) %collective-permute-start.1) | collective-permute-done | bytes 229408 | tf_op jit(solution)/shard_map/ppermute | solution.py:524
  24.9 0.9 %collective-permute-done.2.xh = f32[28,16,128]{2,1,0:T(8,128)S(1)} collective-permute-done((f32[28,16,128]{2,1,0:T(8,128)S(1)}, f32[28,16,128]{2,1,0:T(8,128)S(1)}, u32[]{:S(2)}, u32[]{:S(2)}) %collective-permute-start.2) | collective-permute-done | bytes 229408 | tf_op jit(solution)/shard_map/ppermute | solution.py:524
  25.8 1.6 %collective-permute-start.5 = (f32[18,8,128]{2,1,0:T(8,128)S(1)}, f32[18,8,128]{2,1,0:T(8,128)S(1)}, u32[]{:S(2)}, u32[]{:S(2)}) collective-permute-start(f32[18,8,128]{2,1,0:T(8,128)S(1)} %get-tuple-element.37), channel_id=1, source_target_pairs={{0,1},{1,2},{2,3},{3,4},{4,5},{5,6},{6,7},{7,0},{8,9},{9,10},{10,1... | collective-permute-start | bytes 221192 | tf_op jit(solution)/shard_map/ppermute | solution.py:524
  27.5 0.0 collective-permute-start.6
  28.1 3.0 %collective-permute-start = (f32[8,128]{1,0:T(8,128)S(1)}, f32[8,128]{1,0:T(8,128)S(1)}, u32[]{:S(2)}, u32[]{:S(2)}) collective-permute-start(f32[8,128]{1,0:T(8,128)S(1)} %shard_map.85.owner), channel_id=1, source_target_pairs={{0,1},{1,2},{2,3},{3,4},{4,5},{5,6},{6,7},{7,0},{8,9},{9,10},{10,1... | collective-permute-start | bytes 12296 | tf_op jit(solution)/shard_map/ppermute | solution.py:524
  31.1 0.8 collective-permute-done.below
  31.9 0.0 collective-permute-done.3.yl
  31.9 0.0 collective-permute-done.4.yh
  31.9 0.0 collective-permute-done.5.cl
  31.9 0.6 collective-permute-done.6.ch
  32.5 0.0 copy-done.3
  32.5 0.0 copy-done.2
  32.5 0.0 copy-done.1
  32.5 3.0 %shard_map.88 = (f32[19,8,16,128]{3,2,1,0:T(8,128)S(1)}, f32[8,16,128]{2,1,0:T(8,128)S(1)}, f32[2,8,16,128]{3,2,1,0:T(8,128)S(1)}, f32[8,16,128]{2,1,0:T(8,128)S...) custom-call(f32[8,128]{1,0:T(8,128)S(1)} %collective-permute-done.be, ...), custom_call_target="tpu_custom_call" | custom-call | tf_op jit(solution)/shard_map/pallas_call | solution.py:506
  35.5 1.9 %collective-permute-start.7 = (f32[19,16,128]{2,1,0:T(8,128)S(1)}, f32[19,16,128]{2,1,0:T(8,128)S(1)}, u32[]{:S(2)}, u32[]{:S(2)}) collective-permute-start(f32[19,16,128]{2,1,0:T(8,128)S(1)} %get-tuple-element.48), channel_id=1, source_target_pairs={{0,8},{8,16},{16,24},{24,32},{32,40},{40,48},{48,56},{56,64},{64,7... | collective-permute-start | bytes 466952 | tf_op jit(solution)/shard_map/ppermute | solution.py:524
  37.4 7.4 %collective-permute-start.8 = (f32[19,16,128]{2,1,0:T(8,128)S(1)}, f32[19,16,128]{2,1,0:T(8,128)S(1)}, u32[]{:S(2)}, u32[]{:S(2)}) collective-permute-start(f32[19,16,128]{2,1,0:T(8,128)S(1)} %get-tuple-element.49), channel_id=1, source_target_pairs={{0,760},{8,0},{16,8},{24,16},{32,24},{40,32},{48,40},{56,48},{64,5... | collective-permute-start | bytes 466952 | tf_op jit(solution)/shard_map/ppermute | solution.py:524
  44.8 3.2 %collective-permute-start.9 = (f32[8,24,128]{2,1,0:T(8,128)S(1)}, f32[8,24,128]{2,1,0:T(8,128)S(1)}, u32[]{:S(2)}, u32[]{:S(2)}) collective-permute-start(f32[8,24,128]{2,1,0:T(8,128)S(1)} %get-tuple-element.50), channel_id=1, source_target_pairs={{0,1},{1,2},{2,3},{3,4},{4,5},{5,6},{6,7},{7,0},{8,9},{9,10},{10,1... | collective-permute-start | bytes 294920 | tf_op jit(solution)/shard_map/ppermute | solution.py:524
  48.1 0.0 collective-permute-start.10
  48.1 1.6 %collective-permute-done.9.yl = f32[8,24,128]{2,1,0:T(8,128)S(1)} collective-permute-done((f32[8,24,128]{2,1,0:T(8,128)S(1)}, f32[8,24,128]{2,1,0:T(8,128)S(1)}, u32[]{:S(2)}, u32[]{:S(2)}) %collective-permute-start.9) | collective-permute-done | bytes 98336 | tf_op jit(solution)/shard_map/ppermute | solution.py:524
  49.7 0.0 collective-permute-done.7.xl
  49.7 0.0 collective-permute-done.8.xh
  49.7 3.6 %collective-permute-start.11 = (f32[12,8,128]{2,1,0:T(8,128)S(1)}, f32[12,8,128]{2,1,0:T(8,128)S(1)}, u32[]{:S(2)}, u32[]{:S(2)}) collective-permute-start(f32[12,8,128]{2,1,0:T(8,128)S(1)} %get-tuple-element.52), channel_id=1, source_target_pairs={{0,1},{1,2},{2,3},{3,4},{4,5},{5,6},{6,7},{7,0},{8,9},{9,10},{10,1... | collective-permute-start | bytes 147464 | tf_op jit(solution)/shard_map/ppermute | solution.py:524
  53.4 0.0 collective-permute-start.12
  53.4 0.0 collective-permute-done.10.yh
  53.4 1.2 %collective-permute-done.11.cl = f32[12,8,128]{2,1,0:T(8,128)S(1)} collective-permute-done((f32[12,8,128]{2,1,0:T(8,128)S(1)}, f32[12,8,128]{2,1,0:T(8,128)S(1)}, u32[]{:S(2)}, u32[]{:S(2)}) %collective-permute-start.11) | collective-permute-done | bytes 49184 | tf_op jit(solution)/shard_map/ppermute | solution.py:524
  54.5 3.5 %collective-permute-done.12.ch = f32[12,8,128]{2,1,0:T(8,128)S(1)} collective-permute-done((f32[12,8,128]{2,1,0:T(8,128)S(1)}, f32[12,8,128]{2,1,0:T(8,128)S(1)}, u32[]{:S(2)}, u32[]{:S(2)}) %collective-permute-start.12) | collective-permute-done | bytes 49184 | tf_op jit(solution)/shard_map/ppermute | solution.py:524
  58.1 2.1 %shard_map.90 = (f32[8,16,128]{2,1,0:T(8,128)}, f32[17,16,128]{2,1,0:T(8,128)S(1)}, f32[5,10,32,128]{3,2,1,0:T(8,128)S(1)}) custom-call(f32[2,8,16,128]{3,2,1,0:T(8,128)S(1)} %get-tuple-element.41.conc, f32[8,16,128]{2,1,0:T(8,128)S(1)} %get-tuple-element.42.phi, f32[8,16,128]{2,1,0:T(8,128)S(1)} %get-tuple-element.43.charge, ...), custom_call_target="tpu_custom_call" | custom-call | tf_op jit(solution)/shard_map/pallas_call | solution.py:506
  60.2 0.0 collective-permute-start.14
  60.2 3.0 %collective-permute-start.13 = (f32[17,16,128]{2,1,0:T(8,128)S(1)}, f32[17,16,128]{2,1,0:T(8,128)S(1)}, u32[]{:S(2)}, u32[]{:S(2)}) collective-permute-start(f32[17,16,128]{2,1,0:T(8,128)S(1)} %get-tuple-element.56.mine), channel_id=1, source_target_pairs={{0,1},{1,2},{2,3},{3,4},{4,5},{5,6},{6,7},{7,0},{8,9},{9,10},{10,1... | collective-permute-start | bytes 417800 | tf_op jit(solution)/shard_map/ppermute | solution.py:524
  63.2 2.7 %collective-permute-done.14.above = f32[17,16,128]{2,1,0:T(8,128)S(1)} collective-permute-done((f32[17,16,128]{2,1,0:T(8,128)S(1)}, f32[17,16,128]{2,1,0:T(8,128)S(1)}, u32[]{:S(2)}, u32[]{:S(2)}) %collective-permute-start.14) | collective-permute-done | bytes 139296 | tf_op jit(solution)/shard_map/ppermute | solution.py:524
  65.9 0.0 collective-permute-start.16
  65.9 0.0 collective-permute-done.13.below
  65.9 3.0 %collective-permute-start.15 = (f32[17,16,128]{2,1,0:T(8,128)S(1)}, f32[17,16,128]{2,1,0:T(8,128)S(1)}, u32[]{:S(2)}, u32[]{:S(2)}) collective-permute-start(f32[17,16,128]{2,1,0:T(8,128)S(1)} %collective-permute-done.13.below), channel_id=1, source_target_pairs={{0,1},{1,2},{2,3},{3,4},{4,5},{5,6},{6,7},{7,0},{8,9},{9,10},{10,1... | collective-permute-start | bytes 417800 | tf_op jit(solution)/shard_map/ppermute | solution.py:524
  68.9 1.9 %collective-permute-start.17 = (f32[16,16,128]{2,1,0:T(8,128)S(1)}, f32[16,16,128]{2,1,0:T(8,128)S(1)}, u32[]{:S(2)}, u32[]{:S(2)}) collective-permute-start(f32[16,16,128]{2,1,0:T(8,128)S(1)} %shard_map.92), channel_id=1, source_target_pairs={{0,4},{1,5},{2,6},{3,7},{4,0},{5,1},{6,2},{7,3},{8,12},{9,13},{10,... | collective-permute-start | bytes 393224 | tf_op jit(solution)/shard_map/ppermute | solution.py:524
  70.8 1.9 %shard_map.91 = f32[19,8,16,128]{3,2,1,0:T(8,128)} custom-call(f32[19,8,16,128]{3,2,1,0:T(8,128)S(1)} %get-tuple-element.39.pop, f32[10,32,128]{2,1,0:T(8,128)S(1)} %get-tuple-element.40.fl, f32[5,10,32,128]{3,2,1,0:T(8,128)S(1)} %get-tuple-element.54.sh, f32[19,16,128]{2,1,0:T(8,128)S(1)} %collective-permute-done.7.xl, ...), custom_call_target="tpu_custom_call" | custom-call | flops 40000000 | tf_op jit(solution)/shard_map/pallas_call | solution.py:506
  72.7 3.4 %collective-permute-done.17.far = f32[16,16,128]{2,1,0:T(8,128)S(1)} collective-permute-done((f32[16,16,128]{2,1,0:T(8,128)S(1)}, f32[16,16,128]{2,1,0:T(8,128)S(1)}, u32[]{:S(2)}, u32[]{:S(2)}) %collective-permute-start.17) | collective-permute-done | bytes 131104 | tf_op jit(solution)/shard_map/ppermute | solution.py:524
  76.1 0.0 collective-permute-done.16.above_two
  76.1 0.0 collective-permute-done.15.below_two
  76.1 0.7 shard_map.93
  (5 shorter events, 0.1 us)
Async XLA Ops:
  0.6 31.8 %copy-start.3 = (f32[8,16,128]{2,1,0:T(8,128)S(1)}, f32[8,16,128]{2,1,0:T(8,128)}, u32[]{:S(2)}) copy-start(f32[8,16,128]{2,1,0:T(8,128)} %perm.1) | copy-start | bytes 196612
  0.6 31.8 %copy-start.2 = (f32[8,16,128]{2,1,0:T(8,128)S(1)}, f32[8,16,128]{2,1,0:T(8,128)}, u32[]{:S(2)}) copy-start(f32[8,16,128]{2,1,0:T(8,128)} %phi.1) | copy-start | bytes 196612
  0.7 31.8 %copy-start.1 = (f32[2,8,16,128]{3,2,1,0:T(8,128)S(1)}, f32[2,8,16,128]{3,2,1,0:T(8,128)}, u32[]{:S(2)}) copy-start(f32[2,8,16,128]{3,2,1,0:T(8,128)} %conc.1) | copy-start | bytes 393220
  0.7 31.8 %copy-start = (f32[19,8,16,128]{3,2,1,0:T(8,128)S(1)}, f32[19,8,16,128]{3,2,1,0:T(8,128)}, u32[]{:S(2)}) copy-start(f32[19,8,16,128]{3,2,1,0:T(8,128)} %pop.1) | copy-start | bytes 3735556
  2.4 22.5 %collective-permute-start.1 = (f32[28,16,128]{2,1,0:T(8,128)S(1)}, f32[28,16,128]{2,1,0:T(8,128)S(1)}, u32[]{:S(2)}, u32[]{:S(2)}) collective-permute-start(f32[28,16,128]{2,1,0:T(8,128)S(1)} %get-tuple-element.33), channel_id=1, source_target_pairs={{0,8},{8,16},{16,24},{24,32},{32,40},{40,48},{48,56},{56,64},{64,7... | collective-permute-start | bytes 688136 | tf_op jit(solution)/shard_map/ppermute | solution.py:524
  5.6 20.2 %collective-permute-start.2 = (f32[28,16,128]{2,1,0:T(8,128)S(1)}, f32[28,16,128]{2,1,0:T(8,128)S(1)}, u32[]{:S(2)}, u32[]{:S(2)}) collective-permute-start(f32[28,16,128]{2,1,0:T(8,128)S(1)} %get-tuple-element.34), channel_id=1, source_target_pairs={{0,760},{8,0},{16,8},{24,16},{32,24},{40,32},{48,40},{56,48},{64,5... | collective-permute-start | bytes 688136 | tf_op jit(solution)/shard_map/ppermute | solution.py:524
  21.6 10.3 %collective-permute-start.3 = (f32[8,32,128]{2,1,0:T(8,128)S(1)}, f32[8,32,128]{2,1,0:T(8,128)S(1)}, u32[]{:S(2)}, u32[]{:S(2)}) collective-permute-start(f32[8,32,128]{2,1,0:T(8,128)S(1)} %get-tuple-element.35), channel_id=1, source_target_pairs={{0,1},{1,2},{2,3},{3,4},{4,5},{5,6},{6,7},{7,0},{8,9},{9,10},{10,1... | collective-permute-start | bytes 393224 | tf_op jit(solution)/shard_map/ppermute | solution.py:524
  22.6 9.3 %collective-permute-start.4 = (f32[8,32,128]{2,1,0:T(8,128)S(1)}, f32[8,32,128]{2,1,0:T(8,128)S(1)}, u32[]{:S(2)}, u32[]{:S(2)}) collective-permute-start(f32[8,32,128]{2,1,0:T(8,128)S(1)} %get-tuple-element.36), channel_id=1, source_target_pairs={{0,7},{1,0},{2,1},{3,2},{4,3},{5,4},{6,5},{7,6},{8,15},{9,8},{10,9... | collective-permute-start | bytes 393224 | tf_op jit(solution)/shard_map/ppermute | solution.py:524
  25.8 6.0 %collective-permute-start.5 = (f32[18,8,128]{2,1,0:T(8,128)S(1)}, f32[18,8,128]{2,1,0:T(8,128)S(1)}, u32[]{:S(2)}, u32[]{:S(2)}) collective-permute-start(f32[18,8,128]{2,1,0:T(8,128)S(1)} %get-tuple-element.37), channel_id=1, source_target_pairs={{0,1},{1,2},{2,3},{3,4},{4,5},{5,6},{6,7},{7,0},{8,9},{9,10},{10,1... | collective-permute-start | bytes 221192 | tf_op jit(solution)/shard_map/ppermute | solution.py:524
  27.5 5.0 %collective-permute-start.6 = (f32[18,8,128]{2,1,0:T(8,128)S(1)}, f32[18,8,128]{2,1,0:T(8,128)S(1)}, u32[]{:S(2)}, u32[]{:S(2)}) collective-permute-start(f32[18,8,128]{2,1,0:T(8,128)S(1)} %get-tuple-element.38), channel_id=1, source_target_pairs={{0,7},{1,0},{2,1},{3,2},{4,3},{5,4},{6,5},{7,6},{8,15},{9,8},{10,9... | collective-permute-start | bytes 221192 | tf_op jit(solution)/shard_map/ppermute | solution.py:524
  28.1 3.7 %collective-permute-start = (f32[8,128]{1,0:T(8,128)S(1)}, f32[8,128]{1,0:T(8,128)S(1)}, u32[]{:S(2)}, u32[]{:S(2)}) collective-permute-start(f32[8,128]{1,0:T(8,128)S(1)} %shard_map.85.owner), channel_id=1, source_target_pairs={{0,1},{1,2},{2,3},{3,4},{4,5},{5,6},{6,7},{7,0},{8,9},{9,10},{10,1... | collective-permute-start | bytes 12296 | tf_op jit(solution)/shard_map/ppermute | solution.py:524
  35.5 14.2 %collective-permute-start.7 = (f32[19,16,128]{2,1,0:T(8,128)S(1)}, f32[19,16,128]{2,1,0:T(8,128)S(1)}, u32[]{:S(2)}, u32[]{:S(2)}) collective-permute-start(f32[19,16,128]{2,1,0:T(8,128)S(1)} %get-tuple-element.48), channel_id=1, source_target_pairs={{0,8},{8,16},{16,24},{24,32},{32,40},{40,48},{48,56},{56,64},{64,7... | collective-permute-start | bytes 466952 | tf_op jit(solution)/shard_map/ppermute | solution.py:524
  37.4 12.3 %collective-permute-start.8 = (f32[19,16,128]{2,1,0:T(8,128)S(1)}, f32[19,16,128]{2,1,0:T(8,128)S(1)}, u32[]{:S(2)}, u32[]{:S(2)}) collective-permute-start(f32[19,16,128]{2,1,0:T(8,128)S(1)} %get-tuple-element.49), channel_id=1, source_target_pairs={{0,760},{8,0},{16,8},{24,16},{32,24},{40,32},{48,40},{56,48},{64,5... | collective-permute-start | bytes 466952 | tf_op jit(solution)/shard_map/ppermute | solution.py:524
  44.8 4.9 %collective-permute-start.9 = (f32[8,24,128]{2,1,0:T(8,128)S(1)}, f32[8,24,128]{2,1,0:T(8,128)S(1)}, u32[]{:S(2)}, u32[]{:S(2)}) collective-permute-start(f32[8,24,128]{2,1,0:T(8,128)S(1)} %get-tuple-element.50), channel_id=1, source_target_pairs={{0,1},{1,2},{2,3},{3,4},{4,5},{5,6},{6,7},{7,0},{8,9},{9,10},{10,1... | collective-permute-start | bytes 294920 | tf_op jit(solution)/shard_map/ppermute | solution.py:524
  48.1 5.3 %collective-permute-start.10 = (f32[8,24,128]{2,1,0:T(8,128)S(1)}, f32[8,24,128]{2,1,0:T(8,128)S(1)}, u32[]{:S(2)}, u32[]{:S(2)}) collective-permute-start(f32[8,24,128]{2,1,0:T(8,128)S(1)} %get-tuple-element.51), channel_id=1, source_target_pairs={{0,7},{1,0},{2,1},{3,2},{4,3},{5,4},{6,5},{7,6},{8,15},{9,8},{10,9... | collective-permute-start | bytes 294920 | tf_op jit(solution)/shard_map/ppermute | solution.py:524
  49.7 4.8 %collective-permute-start.11 = (f32[12,8,128]{2,1,0:T(8,128)S(1)}, f32[12,8,128]{2,1,0:T(8,128)S(1)}, u32[]{:S(2)}, u32[]{:S(2)}) collective-permute-start(f32[12,8,128]{2,1,0:T(8,128)S(1)} %get-tuple-element.52), channel_id=1, source_target_pairs={{0,1},{1,2},{2,3},{3,4},{4,5},{5,6},{6,7},{7,0},{8,9},{9,10},{10,1... | collective-permute-start | bytes 147464 | tf_op jit(solution)/shard_map/ppermute | solution.py:524
  53.4 4.7 %collective-permute-start.12 = (f32[12,8,128]{2,1,0:T(8,128)S(1)}, f32[12,8,128]{2,1,0:T(8,128)S(1)}, u32[]{:S(2)}, u32[]{:S(2)}) collective-permute-start(f32[12,8,128]{2,1,0:T(8,128)S(1)} %get-tuple-element.53), channel_id=1, source_target_pairs={{0,7},{1,0},{2,1},{3,2},{4,3},{5,4},{6,5},{7,6},{8,15},{9,8},{10,9... | collective-permute-start | bytes 147464 | tf_op jit(solution)/shard_map/ppermute | solution.py:524
  60.2 5.7 %collective-permute-start.14 = (f32[17,16,128]{2,1,0:T(8,128)S(1)}, f32[17,16,128]{2,1,0:T(8,128)S(1)}, u32[]{:S(2)}, u32[]{:S(2)}) collective-permute-start(f32[17,16,128]{2,1,0:T(8,128)S(1)} %get-tuple-element.56.mine), channel_id=1, source_target_pairs={{0,7},{1,0},{2,1},{3,2},{4,3},{5,4},{6,5},{7,6},{8,15},{9,8},{10,9... | collective-permute-start | bytes 417800 | tf_op jit(solution)/shard_map/ppermute | solution.py:524
  60.2 5.7 %collective-permute-start.13 = (f32[17,16,128]{2,1,0:T(8,128)S(1)}, f32[17,16,128]{2,1,0:T(8,128)S(1)}, u32[]{:S(2)}, u32[]{:S(2)}) collective-permute-start(f32[17,16,128]{2,1,0:T(8,128)S(1)} %get-tuple-element.56.mine), channel_id=1, source_target_pairs={{0,1},{1,2},{2,3},{3,4},{4,5},{5,6},{6,7},{7,0},{8,9},{9,10},{10,1... | collective-permute-start | bytes 417800 | tf_op jit(solution)/shard_map/ppermute | solution.py:524
  65.9 10.2 %collective-permute-start.16 = (f32[17,16,128]{2,1,0:T(8,128)S(1)}, f32[17,16,128]{2,1,0:T(8,128)S(1)}, u32[]{:S(2)}, u32[]{:S(2)}) collective-permute-start(f32[17,16,128]{2,1,0:T(8,128)S(1)} %collective-permute-done.14.above), channel_id=1, source_target_pairs={{0,7},{1,0},{2,1},{3,2},{4,3},{5,4},{6,5},{7,6},{8,15},{9,8},{10,9... | collective-permute-start | bytes 417800 | tf_op jit(solution)/shard_map/ppermute | solution.py:524
  65.9 10.2 %collective-permute-start.15 = (f32[17,16,128]{2,1,0:T(8,128)S(1)}, f32[17,16,128]{2,1,0:T(8,128)S(1)}, u32[]{:S(2)}, u32[]{:S(2)}) collective-permute-start(f32[17,16,128]{2,1,0:T(8,128)S(1)} %collective-permute-done.13.below), channel_id=1, source_target_pairs={{0,1},{1,2},{2,3},{3,4},{4,5},{5,6},{6,7},{7,0},{8,9},{9,10},{10,1... | collective-permute-start | bytes 417800 | tf_op jit(solution)/shard_map/ppermute | solution.py:524
  68.9 7.2 %collective-permute-start.17 = (f32[16,16,128]{2,1,0:T(8,128)S(1)}, f32[16,16,128]{2,1,0:T(8,128)S(1)}, u32[]{:S(2)}, u32[]{:S(2)}) collective-permute-start(f32[16,16,128]{2,1,0:T(8,128)S(1)} %shard_map.92), channel_id=1, source_target_pairs={{0,4},{1,5},{2,6},{3,7},{4,0},{5,1},{6,2},{7,3},{8,12},{9,13},{10,... | collective-permute-start | bytes 393224 | tf_op jit(solution)/shard_map/ppermute | solution.py:524

commit v7 on v6

--- a/solution.py
+++ b/solution.py
@@ -46,7 +46,7 @@
         rows = [("phi", 6)] + [("perm", 6)] * first + [("charge", 4), ("conc", 2)] + [("fluid", 1)] * first
         self.y = {}
         at = 0
-        for name, n in rows + [("pop", 5), ("dm", 4)] + [("owner", 1)] * (not first):
+        for name, n in rows + [("pop", 5), ("dm", 4)]:
             self.y[name] = at
             at += n
         self.y_rows = -(-at // 8) * 8
@@ -68,7 +68,7 @@
 CHARGE = ((1, 5, 4, 2), (2, 4, 3, 3))
 
 
-def pack_y(plan, out, low, owner, phi, charge, conc, pop, dm, perm=None, fluid=None):
+def pack_y(plan, out, low, phi, charge, conc, pop, dm, perm=None, fluid=None):
     y = plan.y
     six = slice(0, 6) if low else slice(10, 16)
     four = slice(1, 5) if low else slice(11, 15)
@@ -84,8 +84,6 @@
         out[:, y["pop"] + k : y["pop"] + k + 1] = pop[i, :, row]
     for k in range(4):
         out[:, y["dm"] + k : y["dm"] + k + 1] = dm[k, :, row]
-    if not plan.first:
-        out[0, y["owner"] : y["owner"] + 1] = owner
 
 
 def pack_x(plan, out, low, phi, charge, conc, pop, dm, perm=None, fluid=None):
@@ -207,7 +205,7 @@
     lax.fori_loop(0, CX, plane, 0, unroll=2)
     for low, xo, yo in ((False, x_hi, y_hi), (True, x_lo, y_lo)):
         pack_x(ONE, xo, low, phi, charge, conc, pop, dm, perm, fluid)
-        pack_y(ONE, yo, low, None, phi, charge, conc, pop, dm, perm, fluid)
+        pack_y(ONE, yo, low, phi, charge, conc, pop, dm, perm, fluid)
 
 
 def corner_one_kernel(xl, xh, c_hi, c_lo):
@@ -215,14 +213,9 @@
     pack_corners(ONE, c_lo, True, xl, xh)
 
 
-def owner_kernel(owner, out):
-    out[...] = jnp.full((8, NZ), owner[0, 0], jnp.int32).astype(F32)
-
-
-def corner_two_kernel(xl, xh, rim, yl, c_hi, c_lo):
+def corner_two_kernel(xl, xh, rim, c_hi, c_lo):
     pack_corners(TWO, c_hi, False, xl, xh, rim)
     pack_corners(TWO, c_lo, True, xl, xh, rim)
-    c_hi[TWO.c["misc"], 7:8] = yl[0, TWO.y["owner"] : TWO.y["owner"] + 1]
 
 
 def lay_all(plan, phi, conc, dm, charge, msgs, pa, ce, dn, mm, cc):
@@ -414,10 +407,11 @@
     lax.fori_loop(0, CX, stream, 0, unroll=4)
 
 
-def step_one_kernel(below, pop, conc, phi, perm, dm, charge, fluid, xl, xh, yl, yh, cl, ch,
-                    pop_out, phi_out, conc_out, charge_out, x_hi, x_lo, y_hi, y_lo, dm_out, rim, coef, inv, fl,
+def step_one_kernel(owner, pop, conc, phi, perm, dm, charge, fluid, xl, xh, yl, yh, cl, ch,
+                    pop_out, phi_out, conc_out, charge_out, x_hi, x_lo, y_hi, y_lo, dm_out, rim, coef, inv, fl, owner_row,
                     pe, pa, pb, ce, dn, mm, cc, vel, sh, lv):
     msgs = (xl, xh, yl, yh, cl, ch)
+    owner_row[...] = jnp.full((8, NZ), owner[0, 0], jnp.int32).astype(F32)
     lay(pe, perm[...], "perm", ONE, msgs)
 
     def coefs(x, _):
@@ -455,7 +449,7 @@
     charge_out[...] = conc_out[0] - conc_out[1]
     for low, xo, yo in ((False, x_hi, y_hi), (True, x_lo, y_lo)):
         pack_x(TWO, xo, low, phi_out, charge_out, conc_out, pop_out, dm_out)
-        pack_y(TWO, yo, low, below[0:1], phi_out, charge_out, conc_out, pop_out, dm_out)
+        pack_y(TWO, yo, low, phi_out, charge_out, conc_out, pop_out, dm_out)
 
 
 def ions_two_kernel(conc, phi, charge, dm, rim, coef, inv, fl, xl, xh, yl, yh, cl, ch,
@@ -471,7 +465,6 @@
         slab[s * CX + x] = values
 
     ions(fin, fl, cc, vel, store)
-    slab[2 * CX, 0:8] = jnp.broadcast_to(cl[TWO.c["misc"], 7:8], (8, NZ))
 
 
 def flow_two_kernel(pop, fl, sh, xl, xh, yl, yh, cl, ch, pop_out, lv):
@@ -483,8 +476,8 @@
     return jnp.full((1, NZ), me, jnp.int32).astype(F32)
 
 
-def route_kernel(mine, below, above, out):
-    want = below[2 * CX, 0:1]
+def route_kernel(mine, below, above, wanted, out):
+    want = wanted[0:1]
     for x in range(2 * CX):
         out[x] = jnp.where(want == place(0), mine[x], jnp.where(want == place(1), above[x], below[x]))
 
@@ -551,25 +544,24 @@
     got = exchange(*sent)
     c_hi, c_lo = call(corner_one_kernel, tiles(ONE), got[:2])
     got += (shift(c_hi, "gy", 1), shift(c_lo, "gy", -1))
-    (owner,) = call(owner_kernel, (row,), (owners,), (), [SMEM])
-    below = shift(owner, "gy", 1)
     pop, phi, conc, charge, *rest = call(
         step_one_kernel,
         (pops, block, both, block) + messages(TWO)
-        + (four, shape(4, CY, NZ), shape(6, *HALO), shape(*HALO), shape(*RIM)),
-        (below, populations, concentration, potential, permittivity, dm, charge, fluid) + got,
-        (HALO,) + FIELDS + ((5,) + RIM, (19,) + RIM))
-    sent, (dm, rim, coef, inv, fl) = rest[:4], rest[4:]
+        + (four, shape(4, CY, NZ), shape(6, *HALO), shape(*HALO), shape(*RIM), row),
+        (owners, populations, concentration, potential, permittivity, dm, charge, fluid) + got,
+        (HALO,) + FIELDS + ((5,) + RIM, (19,) + RIM), [SMEM] + [VMEM] * 13)
+    sent, (dm, rim, coef, inv, fl, owner) = rest[:4], rest[4:]
     got = exchange(*sent)
-    c_hi, c_lo = call(corner_two_kernel, tiles(TWO), got[:2] + (rim, got[2]))
+    c_hi, c_lo = call(corner_two_kernel, tiles(TWO), got[:2] + (rim,))
     got += (shift(c_hi, "gy", 1), shift(c_lo, "gy", -1))
     slab = shape(2 * CX, CY, NZ)
     phi, mine, sh = call(
-        ions_two_kernel, (block, shape(2 * CX + 1, CY, NZ), shape(5, *RIM)),
+        ions_two_kernel, (block, slab, shape(5, *RIM)),
         (conc, phi, charge, dm, rim, coef, inv, fl) + got, FIELDS)
     below, above = shift(mine, "gy", 1), shift(mine, "gy", -1)
     (pop,) = call(flow_two_kernel, (pops,), (pop, fl, sh) + got, ((19,) + RIM,), flops=40_000_000)
-    (routed,) = call(route_kernel, (slab,), (mine, below, above))
+    wanted = shift(owner, "gy", 4)
+    (routed,) = call(route_kernel, (slab,), (mine, below, above, wanted))
     far = shift(routed, "gy", 4)
     below_two, above_two = shift(below, "gy", 1), shift(above, "gy", -1)
     (migrated,) = call(arrive_kernel, (slab,), (mine, below, above, below_two, above_two, far, owner))

time: 77.1 us -> 73 us (0.947)
  the two profiles are of different devices: /device:TPU:7 before, /device:TPU:1 now
where the time goes in v7:
time: 73 us; the launch traced here: 72.5 us
  starting transfers between devices  48.8 us (67%)
  waiting for transfers between devices  13.4 us (18%)
  Pallas kernels  8.83 us (12%)
  between operations  1.44 us (2%)
    ppermute x18, starting transfers between devices, shift(): return lax.ppermute(values, axis, [(i, (i + by) % n) for i in range(n)])  48.8 us
    ppermute x18, waiting for transfers between devices, shift(): return lax.ppermute(values, axis, [(i, (i + by) % n) for i in range(n)])  13.4 us
    pallas_call x8, Pallas kernels, call(): pl.pallas_call(kernel, out_shape=outs, in_specs=specs or [VMEM] * len(arg...  8.83 us
  transfers between devices with their start and end apart: 18, of which 11 were waited for; matrix products, arithmetic and copies ran while one was open for 0% of the time, Pallas kernels for 3%

profile of v7, /device:TPU:1, one launch (start us, length us, event | category | flops | bytes accessed | tf_op | source)
XLA Modules:
  0.0 72.5 jit_solution(9998800922338735674)
XLA Ops:
  0.6 0.0 copy-start.3
  0.6 0.0 copy-start.2
  0.7 0.0 copy-start.1
  0.7 0.0 copy-start
  0.7 1.7 %shard_map.85 = (f32[28,16,128]{2,1,0:T(8,128)S(1)}, f32[28,16,128]{2,1,0:T(8,128)S(1)}, f32[8,32,128]{2,1,0:T(8,128)S(1)}, f32[8,32,128]{2,1,0:T(8,128)S(1)}, f...) custom-call(f32[19,8,16,128]{3,2,1,0:T(8,128)} %pop.1, f32[2,8,16,128]{3,2,1,0:T(8,128)} %conc.1, ...), custom_call_target="tpu_custom_call" | custom-call | tf_op jit(solution)/shard_map/pallas_call | solution.py:499
  2.4 4.0 %collective-permute-start = (f32[28,16,128]{2,1,0:T(8,128)S(1)}, f32[28,16,128]{2,1,0:T(8,128)S(1)}, u32[]{:S(2)}, u32[]{:S(2)}) collective-permute-start(f32[28,16,128]{2,1,0:T(8,128)S(1)} %get-tuple-element.34), channel_id=1, source_target_pairs={{0,8},{8,16},{16,24},{24,32},{32,40},{40,48},{48,56},{56,64},{64,7... | collective-permute-start | bytes 688136 | tf_op jit(solution)/shard_map/ppermute | solution.py:517
  6.4 15.9 %collective-permute-start.1 = (f32[28,16,128]{2,1,0:T(8,128)S(1)}, f32[28,16,128]{2,1,0:T(8,128)S(1)}, u32[]{:S(2)}, u32[]{:S(2)}) collective-permute-start(f32[28,16,128]{2,1,0:T(8,128)S(1)} %get-tuple-element.35), channel_id=1, source_target_pairs={{0,760},{8,0},{16,8},{24,16},{32,24},{40,32},{48,40},{56,48},{64,5... | collective-permute-start | bytes 688136 | tf_op jit(solution)/shard_map/ppermute | solution.py:517
  22.4 2.1 %collective-permute-start.2 = (f32[8,32,128]{2,1,0:T(8,128)S(1)}, f32[8,32,128]{2,1,0:T(8,128)S(1)}, u32[]{:S(2)}, u32[]{:S(2)}) collective-permute-start(f32[8,32,128]{2,1,0:T(8,128)S(1)} %get-tuple-element.36), channel_id=1, source_target_pairs={{0,1},{1,2},{2,3},{3,4},{4,5},{5,6},{6,7},{7,0},{8,9},{9,10},{10,1... | collective-permute-start | bytes 393224 | tf_op jit(solution)/shard_map/ppermute | solution.py:517
  24.4 0.0 collective-permute-start.3
  24.4 1.3 %collective-permute-done.xl = f32[28,16,128]{2,1,0:T(8,128)S(1)} collective-permute-done((f32[28,16,128]{2,1,0:T(8,128)S(1)}, f32[28,16,128]{2,1,0:T(8,128)S(1)}, u32[]{:S(2)}, u32[]{:S(2)}) %collective-permute-start) | collective-permute-done | bytes 229408 | tf_op jit(solution)/shard_map/ppermute | solution.py:517
  25.8 0.9 %collective-permute-done.1.xh = f32[28,16,128]{2,1,0:T(8,128)S(1)} collective-permute-done((f32[28,16,128]{2,1,0:T(8,128)S(1)}, f32[28,16,128]{2,1,0:T(8,128)S(1)}, u32[]{:S(2)}, u32[]{:S(2)}) %collective-permute-start.1) | collective-permute-done | bytes 229408 | tf_op jit(solution)/shard_map/ppermute | solution.py:517
  26.7 2.7 %collective-permute-start.4 = (f32[18,8,128]{2,1,0:T(8,128)S(1)}, f32[18,8,128]{2,1,0:T(8,128)S(1)}, u32[]{:S(2)}, u32[]{:S(2)}) collective-permute-start(f32[18,8,128]{2,1,0:T(8,128)S(1)} %get-tuple-element.38), channel_id=1, source_target_pairs={{0,1},{1,2},{2,3},{3,4},{4,5},{5,6},{6,7},{7,0},{8,9},{9,10},{10,1... | collective-permute-start | bytes 221192 | tf_op jit(solution)/shard_map/ppermute | solution.py:517
  29.3 0.0 collective-permute-start.5
  30.0 0.0 collective-permute-done.2.yl
  30.0 0.0 collective-permute-done.3.yh
  30.0 0.7 %collective-permute-done.4.cl = f32[18,8,128]{2,1,0:T(8,128)S(1)} collective-permute-done((f32[18,8,128]{2,1,0:T(8,128)S(1)}, f32[18,8,128]{2,1,0:T(8,128)S(1)}, u32[]{:S(2)}, u32[]{:S(2)}) %collective-permute-start.4) | collective-permute-done | bytes 73760 | tf_op jit(solution)/shard_map/ppermute | solution.py:517
  30.7 2.4 %collective-permute-done.5.ch = f32[18,8,128]{2,1,0:T(8,128)S(1)} collective-permute-done((f32[18,8,128]{2,1,0:T(8,128)S(1)}, f32[18,8,128]{2,1,0:T(8,128)S(1)}, u32[]{:S(2)}, u32[]{:S(2)}) %collective-permute-start.5) | collective-permute-done | bytes 73760 | tf_op jit(solution)/shard_map/ppermute | solution.py:517
  33.1 0.0 copy-done.3
  33.1 0.0 copy-done.2
  33.1 0.0 copy-done.1
  33.1 2.7 %shard_map.87 = (f32[19,8,16,128]{3,2,1,0:T(8,128)S(1)}, f32[8,16,128]{2,1,0:T(8,128)S(1)}, f32[2,8,16,128]{3,2,1,0:T(8,128)S(1)}, f32[8,16,128]{2,1,0:T(8,128)S...) custom-call(s32[1,1]{1,0:T(1,128)S(6)} %copy.9.owner, ...), custom_call_target="tpu_custom_call" | custom-call | tf_op jit(solution)/shard_map/pallas_call | solution.py:499
  35.9 1.9 %collective-permute-start.6 = (f32[19,16,128]{2,1,0:T(8,128)S(1)}, f32[19,16,128]{2,1,0:T(8,128)S(1)}, u32[]{:S(2)}, u32[]{:S(2)}) collective-permute-start(f32[19,16,128]{2,1,0:T(8,128)S(1)} %get-tuple-element.49), channel_id=1, source_target_pairs={{0,8},{8,16},{16,24},{24,32},{32,40},{40,48},{48,56},{56,64},{64,7... | collective-permute-start | bytes 466952 | tf_op jit(solution)/shard_map/ppermute | solution.py:517
  37.8 7.4 %collective-permute-start.7 = (f32[19,16,128]{2,1,0:T(8,128)S(1)}, f32[19,16,128]{2,1,0:T(8,128)S(1)}, u32[]{:S(2)}, u32[]{:S(2)}) collective-permute-start(f32[19,16,128]{2,1,0:T(8,128)S(1)} %get-tuple-element.50), channel_id=1, source_target_pairs={{0,760},{8,0},{16,8},{24,16},{32,24},{40,32},{48,40},{56,48},{64,5... | collective-permute-start | bytes 466952 | tf_op jit(solution)/shard_map/ppermute | solution.py:517
  45.2 0.3 collective-permute-start.8
  45.5 0.2 collective-permute-start.9
  45.8 1.8 %collective-permute-done.6.xl = f32[19,16,128]{2,1,0:T(8,128)S(1)} collective-permute-done((f32[19,16,128]{2,1,0:T(8,128)S(1)}, f32[19,16,128]{2,1,0:T(8,128)S(1)}, u32[]{:S(2)}, u32[]{:S(2)}) %collective-permute-start.6) | collective-permute-done | bytes 155680 | tf_op jit(solution)/shard_map/ppermute | solution.py:517
  47.6 0.9 %collective-permute-done.7.xh = f32[19,16,128]{2,1,0:T(8,128)S(1)} collective-permute-done((f32[19,16,128]{2,1,0:T(8,128)S(1)}, f32[19,16,128]{2,1,0:T(8,128)S(1)}, u32[]{:S(2)}, u32[]{:S(2)}) %collective-permute-start.7) | collective-permute-done | bytes 155680 | tf_op jit(solution)/shard_map/ppermute | solution.py:517
  48.5 0.9 %collective-permute-start.10 = (f32[12,8,128]{2,1,0:T(8,128)S(1)}, f32[12,8,128]{2,1,0:T(8,128)S(1)}, u32[]{:S(2)}, u32[]{:S(2)}) collective-permute-start(f32[12,8,128]{2,1,0:T(8,128)S(1)} %get-tuple-element.53), channel_id=1, source_target_pairs={{0,1},{1,2},{2,3},{3,4},{4,5},{5,6},{6,7},{7,0},{8,9},{9,10},{10,1... | collective-permute-start | bytes 147464 | tf_op jit(solution)/shard_map/ppermute | solution.py:517
  49.4 0.1 collective-permute-start.11
  49.5 0.0 collective-permute-done.8.yl
  49.5 0.4 collective-permute-done.9.yh
  49.9 0.7 collective-permute-done.10.cl
  50.6 2.3 %collective-permute-done.11.ch = f32[12,8,128]{2,1,0:T(8,128)S(1)} collective-permute-done((f32[12,8,128]{2,1,0:T(8,128)S(1)}, f32[12,8,128]{2,1,0:T(8,128)S(1)}, u32[]{:S(2)}, u32[]{:S(2)}) %collective-permute-start.11) | collective-permute-done | bytes 49184 | tf_op jit(solution)/shard_map/ppermute | solution.py:517
  52.9 1.6 %shard_map.89 = (f32[8,16,128]{2,1,0:T(8,128)}, f32[16,16,128]{2,1,0:T(8,128)S(1)}, f32[5,10,32,128]{3,2,1,0:T(8,128)S(1)}) custom-call(f32[2,8,16,128]{3,2,1,0:T(8,128)S(1)} %get-tuple-element.42.conc, f32[8,16,128]{2,1,0:T(8,128)S(1)} %get-tuple-element.43.phi, f32[8,16,128]{2,1,0:T(8,128)S(1)} %get-tuple-element.44.charge, ...), custom_call_target="tpu_custom_call" | custom-call | tf_op jit(solution)/shard_map/pallas_call | solution.py:499
  54.5 1.3 %collective-permute-start.13 = (f32[16,16,128]{2,1,0:T(8,128)S(1)}, f32[16,16,128]{2,1,0:T(8,128)S(1)}, u32[]{:S(2)}, u32[]{:S(2)}) collective-permute-start(f32[16,16,128]{2,1,0:T(8,128)S(1)} %get-tuple-element.57.mine), channel_id=1, source_target_pairs={{0,7},{1,0},{2,1},{3,2},{4,3},{5,4},{6,5},{7,6},{8,15},{9,8},{10,9... | collective-permute-start | bytes 393224 | tf_op jit(solution)/shard_map/ppermute | solution.py:517
  55.9 0.4 collective-permute-start.12
  56.3 4.1 %collective-permute-start.16 = (f32[8,128]{1,0:T(8,128)S(1)}, f32[8,128]{1,0:T(8,128)S(1)}, u32[]{:S(2)}, u32[]{:S(2)}) collective-permute-start(f32[8,128]{1,0:T(8,128)S(1)} %get-tuple-element.58.owner), channel_id=1, source_target_pairs={{0,4},{1,5},{2,6},{3,7},{4,0},{5,1},{6,2},{7,3},{8,12},{9,13},{10,... | collective-permute-start | bytes 12296 | tf_op jit(solution)/shard_map/ppermute | solution.py:517
  60.4 0.0 collective-permute-done.13.above
  60.4 0.9 %collective-permute-start.15 = (f32[16,16,128]{2,1,0:T(8,128)S(1)}, f32[16,16,128]{2,1,0:T(8,128)S(1)}, u32[]{:S(2)}, u32[]{:S(2)}) collective-permute-start(f32[16,16,128]{2,1,0:T(8,128)S(1)} %collective-permute-done.13.above), channel_id=1, source_target_pairs={{0,7},{1,0},{2,1},{3,2},{4,3},{5,4},{6,5},{7,6},{8,15},{9,8},{10,9... | collective-permute-start | bytes 393224 | tf_op jit(solution)/shard_map/ppermute | solution.py:517
  61.3 0.8 %collective-permute-done.16.wanted = f32[8,128]{1,0:T(8,128)S(1)} collective-permute-done((f32[8,128]{1,0:T(8,128)S(1)}, f32[8,128]{1,0:T(8,128)S(1)}, u32[]{:S(2)}, u32[]{:S(2)}) %collective-permute-start.16) | collective-permute-done | bytes 4128 | tf_op jit(solution)/shard_map/ppermute | solution.py:517
  62.1 0.0 collective-permute-done.12.below
  62.2 4.1 %collective-permute-start.17 = (f32[16,16,128]{2,1,0:T(8,128)S(1)}, f32[16,16,128]{2,1,0:T(8,128)S(1)}, u32[]{:S(2)}, u32[]{:S(2)}) collective-permute-start(f32[16,16,128]{2,1,0:T(8,128)S(1)} %shard_map.91), channel_id=1, source_target_pairs={{0,4},{1,5},{2,6},{3,7},{4,0},{5,1},{6,2},{7,3},{8,12},{9,13},{10,... | collective-permute-start | bytes 393224 | tf_op jit(solution)/shard_map/ppermute | solution.py:517
  66.3 2.3 %collective-permute-start.14 = (f32[16,16,128]{2,1,0:T(8,128)S(1)}, f32[16,16,128]{2,1,0:T(8,128)S(1)}, u32[]{:S(2)}, u32[]{:S(2)}) collective-permute-start(f32[16,16,128]{2,1,0:T(8,128)S(1)} %collective-permute-done.12.below), channel_id=1, source_target_pairs={{0,1},{1,2},{2,3},{3,4},{4,5},{5,6},{6,7},{7,0},{8,9},{9,10},{10,1... | collective-permute-start | bytes 393224 | tf_op jit(solution)/shard_map/ppermute | solution.py:517
  68.6 1.9 %shard_map.90 = f32[19,8,16,128]{3,2,1,0:T(8,128)} custom-call(f32[19,8,16,128]{3,2,1,0:T(8,128)S(1)} %get-tuple-element.40.pop, f32[10,32,128]{2,1,0:T(8,128)S(1)} %get-tuple-element.41.fl, f32[5,10,32,128]{3,2,1,0:T(8,128)S(1)} %get-tuple-element.55.sh, f32[19,16,128]{2,1,0:T(8,128)S(1)} %collective-permute-done.6.xl, ...), custom_call_target="tpu_custom_call" | custom-call | flops 40000000 | tf_op jit(solution)/shard_map/pallas_call | solution.py:499
  70.6 0.0 collective-permute-done.15.above_two
  70.6 0.0 collective-permute-done.17.far
  70.6 1.2 %collective-permute-done.14.below_two = f32[16,16,128]{2,1,0:T(8,128)S(1)} collective-permute-done((f32[16,16,128]{2,1,0:T(8,128)S(1)}, f32[16,16,128]{2,1,0:T(8,128)S(1)}, u32[]{:S(2)}, u32[]{:S(2)}) %collective-permute-start.14) | collective-permute-done | bytes 131104 | tf_op jit(solution)/shard_map/ppermute | solution.py:517
  71.8 0.7 shard_map.92
  (4 shorter events, 0.1 us)
Async XLA Ops:
  0.6 32.5 %copy-start.3 = (f32[8,16,128]{2,1,0:T(8,128)S(1)}, f32[8,16,128]{2,1,0:T(8,128)}, u32[]{:S(2)}) copy-start(f32[8,16,128]{2,1,0:T(8,128)} %perm.1) | copy-start | bytes 196612
  0.6 32.5 %copy-start.2 = (f32[8,16,128]{2,1,0:T(8,128)S(1)}, f32[8,16,128]{2,1,0:T(8,128)}, u32[]{:S(2)}) copy-start(f32[8,16,128]{2,1,0:T(8,128)} %phi.1) | copy-start | bytes 196612
  0.7 32.5 %copy-start.1 = (f32[2,8,16,128]{3,2,1,0:T(8,128)S(1)}, f32[2,8,16,128]{3,2,1,0:T(8,128)}, u32[]{:S(2)}) copy-start(f32[2,8,16,128]{3,2,1,0:T(8,128)} %conc.1) | copy-start | bytes 393220
  0.7 32.5 %copy-start = (f32[19,8,16,128]{3,2,1,0:T(8,128)S(1)}, f32[19,8,16,128]{3,2,1,0:T(8,128)}, u32[]{:S(2)}) copy-start(f32[19,8,16,128]{3,2,1,0:T(8,128)} %pop.1) | copy-start | bytes 3735556
  2.4 23.4 %collective-permute-start = (f32[28,16,128]{2,1,0:T(8,128)S(1)}, f32[28,16,128]{2,1,0:T(8,128)S(1)}, u32[]{:S(2)}, u32[]{:S(2)}) collective-permute-start(f32[28,16,128]{2,1,0:T(8,128)S(1)} %get-tuple-element.34), channel_id=1, source_target_pairs={{0,8},{8,16},{16,24},{24,32},{32,40},{40,48},{48,56},{56,64},{64,7... | collective-permute-start | bytes 688136 | tf_op jit(solution)/shard_map/ppermute | solution.py:517
  6.4 20.2 %collective-permute-start.1 = (f32[28,16,128]{2,1,0:T(8,128)S(1)}, f32[28,16,128]{2,1,0:T(8,128)S(1)}, u32[]{:S(2)}, u32[]{:S(2)}) collective-permute-start(f32[28,16,128]{2,1,0:T(8,128)S(1)} %get-tuple-element.35), channel_id=1, source_target_pairs={{0,760},{8,0},{16,8},{24,16},{32,24},{40,32},{48,40},{56,48},{64,5... | collective-permute-start | bytes 688136 | tf_op jit(solution)/shard_map/ppermute | solution.py:517
  22.4 7.6 %collective-permute-start.2 = (f32[8,32,128]{2,1,0:T(8,128)S(1)}, f32[8,32,128]{2,1,0:T(8,128)S(1)}, u32[]{:S(2)}, u32[]{:S(2)}) collective-permute-start(f32[8,32,128]{2,1,0:T(8,128)S(1)} %get-tuple-element.36), channel_id=1, source_target_pairs={{0,1},{1,2},{2,3},{3,4},{4,5},{5,6},{6,7},{7,0},{8,9},{9,10},{10,1... | collective-permute-start | bytes 393224 | tf_op jit(solution)/shard_map/ppermute | solution.py:517
  24.4 5.5 %collective-permute-start.3 = (f32[8,32,128]{2,1,0:T(8,128)S(1)}, f32[8,32,128]{2,1,0:T(8,128)S(1)}, u32[]{:S(2)}, u32[]{:S(2)}) collective-permute-start(f32[8,32,128]{2,1,0:T(8,128)S(1)} %get-tuple-element.37), channel_id=1, source_target_pairs={{0,7},{1,0},{2,1},{3,2},{4,3},{5,4},{6,5},{7,6},{8,15},{9,8},{10,9... | collective-permute-start | bytes 393224 | tf_op jit(solution)/shard_map/ppermute | solution.py:517
  26.7 4.1 %collective-permute-start.4 = (f32[18,8,128]{2,1,0:T(8,128)S(1)}, f32[18,8,128]{2,1,0:T(8,128)S(1)}, u32[]{:S(2)}, u32[]{:S(2)}) collective-permute-start(f32[18,8,128]{2,1,0:T(8,128)S(1)} %get-tuple-element.38), channel_id=1, source_target_pairs={{0,1},{1,2},{2,3},{3,4},{4,5},{5,6},{6,7},{7,0},{8,9},{9,10},{10,1... | collective-permute-start | bytes 221192 | tf_op jit(solution)/shard_map/ppermute | solution.py:517
  29.3 3.8 %collective-permute-start.5 = (f32[18,8,128]{2,1,0:T(8,128)S(1)}, f32[18,8,128]{2,1,0:T(8,128)S(1)}, u32[]{:S(2)}, u32[]{:S(2)}) collective-permute-start(f32[18,8,128]{2,1,0:T(8,128)S(1)} %get-tuple-element.39), channel_id=1, source_target_pairs={{0,7},{1,0},{2,1},{3,2},{4,3},{5,4},{6,5},{7,6},{8,15},{9,8},{10,9... | collective-permute-start | bytes 221192 | tf_op jit(solution)/shard_map/ppermute | solution.py:517
  35.9 11.7 %collective-permute-start.6 = (f32[19,16,128]{2,1,0:T(8,128)S(1)}, f32[19,16,128]{2,1,0:T(8,128)S(1)}, u32[]{:S(2)}, u32[]{:S(2)}) collective-permute-start(f32[19,16,128]{2,1,0:T(8,128)S(1)} %get-tuple-element.49), channel_id=1, source_target_pairs={{0,8},{8,16},{16,24},{24,32},{32,40},{40,48},{48,56},{56,64},{64,7... | collective-permute-start | bytes 466952 | tf_op jit(solution)/shard_map/ppermute | solution.py:517
  37.8 10.7 %collective-permute-start.7 = (f32[19,16,128]{2,1,0:T(8,128)S(1)}, f32[19,16,128]{2,1,0:T(8,128)S(1)}, u32[]{:S(2)}, u32[]{:S(2)}) collective-permute-start(f32[19,16,128]{2,1,0:T(8,128)S(1)} %get-tuple-element.50), channel_id=1, source_target_pairs={{0,760},{8,0},{16,8},{24,16},{32,24},{40,32},{48,40},{56,48},{64,5... | collective-permute-start | bytes 466952 | tf_op jit(solution)/shard_map/ppermute | solution.py:517
  45.2 4.3 %collective-permute-start.8 = (f32[8,24,128]{2,1,0:T(8,128)S(1)}, f32[8,24,128]{2,1,0:T(8,128)S(1)}, u32[]{:S(2)}, u32[]{:S(2)}) collective-permute-start(f32[8,24,128]{2,1,0:T(8,128)S(1)} %get-tuple-element.51), channel_id=1, source_target_pairs={{0,1},{1,2},{2,3},{3,4},{4,5},{5,6},{6,7},{7,0},{8,9},{9,10},{10,1... | collective-permute-start | bytes 294920 | tf_op jit(solution)/shard_map/ppermute | solution.py:517
  45.5 4.3 %collective-permute-start.9 = (f32[8,24,128]{2,1,0:T(8,128)S(1)}, f32[8,24,128]{2,1,0:T(8,128)S(1)}, u32[]{:S(2)}, u32[]{:S(2)}) collective-permute-start(f32[8,24,128]{2,1,0:T(8,128)S(1)} %get-tuple-element.52), channel_id=1, source_target_pairs={{0,7},{1,0},{2,1},{3,2},{4,3},{5,4},{6,5},{7,6},{8,15},{9,8},{10,9... | collective-permute-start | bytes 294920 | tf_op jit(solution)/shard_map/ppermute | solution.py:517
  48.5 2.0 %collective-permute-start.10 = (f32[12,8,128]{2,1,0:T(8,128)S(1)}, f32[12,8,128]{2,1,0:T(8,128)S(1)}, u32[]{:S(2)}, u32[]{:S(2)}) collective-permute-start(f32[12,8,128]{2,1,0:T(8,128)S(1)} %get-tuple-element.53), channel_id=1, source_target_pairs={{0,1},{1,2},{2,3},{3,4},{4,5},{5,6},{6,7},{7,0},{8,9},{9,10},{10,1... | collective-permute-start | bytes 147464 | tf_op jit(solution)/shard_map/ppermute | solution.py:517
  49.4 3.5 %collective-permute-start.11 = (f32[12,8,128]{2,1,0:T(8,128)S(1)}, f32[12,8,128]{2,1,0:T(8,128)S(1)}, u32[]{:S(2)}, u32[]{:S(2)}) collective-permute-start(f32[12,8,128]{2,1,0:T(8,128)S(1)} %get-tuple-element.54), channel_id=1, source_target_pairs={{0,7},{1,0},{2,1},{3,2},{4,3},{5,4},{6,5},{7,6},{8,15},{9,8},{10,9... | collective-permute-start | bytes 147464 | tf_op jit(solution)/shard_map/ppermute | solution.py:517
  54.5 5.9 %collective-permute-start.13 = (f32[16,16,128]{2,1,0:T(8,128)S(1)}, f32[16,16,128]{2,1,0:T(8,128)S(1)}, u32[]{:S(2)}, u32[]{:S(2)}) collective-permute-start(f32[16,16,128]{2,1,0:T(8,128)S(1)} %get-tuple-element.57.mine), channel_id=1, source_target_pairs={{0,7},{1,0},{2,1},{3,2},{4,3},{5,4},{6,5},{7,6},{8,15},{9,8},{10,9... | collective-permute-start | bytes 393224 | tf_op jit(solution)/shard_map/ppermute | solution.py:517
  55.9 6.3 %collective-permute-start.12 = (f32[16,16,128]{2,1,0:T(8,128)S(1)}, f32[16,16,128]{2,1,0:T(8,128)S(1)}, u32[]{:S(2)}, u32[]{:S(2)}) collective-permute-start(f32[16,16,128]{2,1,0:T(8,128)S(1)} %get-tuple-element.57.mine), channel_id=1, source_target_pairs={{0,1},{1,2},{2,3},{3,4},{4,5},{5,6},{6,7},{7,0},{8,9},{9,10},{10,1... | collective-permute-start | bytes 393224 | tf_op jit(solution)/shard_map/ppermute | solution.py:517
  56.3 5.8 %collective-permute-start.16 = (f32[8,128]{1,0:T(8,128)S(1)}, f32[8,128]{1,0:T(8,128)S(1)}, u32[]{:S(2)}, u32[]{:S(2)}) collective-permute-start(f32[8,128]{1,0:T(8,128)S(1)} %get-tuple-element.58.owner), channel_id=1, source_target_pairs={{0,4},{1,5},{2,6},{3,7},{4,0},{5,1},{6,2},{7,3},{8,12},{9,13},{10,... | collective-permute-start | bytes 12296 | tf_op jit(solution)/shard_map/ppermute | solution.py:517
  60.4 10.1 %collective-permute-start.15 = (f32[16,16,128]{2,1,0:T(8,128)S(1)}, f32[16,16,128]{2,1,0:T(8,128)S(1)}, u32[]{:S(2)}, u32[]{:S(2)}) collective-permute-start(f32[16,16,128]{2,1,0:T(8,128)S(1)} %collective-permute-done.13.above), channel_id=1, source_target_pairs={{0,7},{1,0},{2,1},{3,2},{4,3},{5,4},{6,5},{7,6},{8,15},{9,8},{10,9... | collective-permute-start | bytes 393224 | tf_op jit(solution)/shard_map/ppermute | solution.py:517
  62.2 8.4 %collective-permute-start.17 = (f32[16,16,128]{2,1,0:T(8,128)S(1)}, f32[16,16,128]{2,1,0:T(8,128)S(1)}, u32[]{:S(2)}, u32[]{:S(2)}) collective-permute-start(f32[16,16,128]{2,1,0:T(8,128)S(1)} %shard_map.91), channel_id=1, source_target_pairs={{0,4},{1,5},{2,6},{3,7},{4,0},{5,1},{6,2},{7,3},{8,12},{9,13},{10,... | collective-permute-start | bytes 393224 | tf_op jit(solution)/shard_map/ppermute | solution.py:517
  66.3 5.5 %collective-permute-start.14 = (f32[16,16,128]{2,1,0:T(8,128)S(1)}, f32[16,16,128]{2,1,0:T(8,128)S(1)}, u32[]{:S(2)}, u32[]{:S(2)}) collective-permute-start(f32[16,16,128]{2,1,0:T(8,128)S(1)} %collective-permute-done.12.below), channel_id=1, source_target_pairs={{0,1},{1,2},{2,3},{3,4},{4,5},{5,6},{6,7},{7,0},{8,9},{9,10},{10,1... | collective-permute-start | bytes 393224 | tf_op jit(solution)/shard_map/ppermute | solution.py:517

commit v8 on v6

--- a/solution.py
+++ b/solution.py
@@ -210,19 +210,16 @@
         pack_y(ONE, yo, low, None, phi, charge, conc, pop, dm, perm, fluid)
 
 
-def corner_one_kernel(xl, xh, c_hi, c_lo):
+def corner_one_kernel(owner, xl, xh, c_hi, c_lo, owner_row):
+    owner_row[...] = jnp.full((8, NZ), owner[0, 0], jnp.int32).astype(F32)
     pack_corners(ONE, c_hi, False, xl, xh)
+    c_hi[ONE.c["misc"], 7:8] = owner_row[0:1]
     pack_corners(ONE, c_lo, True, xl, xh)
 
 
-def owner_kernel(owner, out):
-    out[...] = jnp.full((8, NZ), owner[0, 0], jnp.int32).astype(F32)
-
-
-def corner_two_kernel(xl, xh, rim, yl, c_hi, c_lo):
+def corner_two_kernel(xl, xh, rim, c_hi, c_lo):
     pack_corners(TWO, c_hi, False, xl, xh, rim)
     pack_corners(TWO, c_lo, True, xl, xh, rim)
-    c_hi[TWO.c["misc"], 7:8] = yl[0, TWO.y["owner"] : TWO.y["owner"] + 1]
 
 
 def lay_all(plan, phi, conc, dm, charge, msgs, pa, ce, dn, mm, cc):
@@ -414,7 +411,7 @@
     lax.fori_loop(0, CX, stream, 0, unroll=4)
 
 
-def step_one_kernel(below, pop, conc, phi, perm, dm, charge, fluid, xl, xh, yl, yh, cl, ch,
+def step_one_kernel(pop, conc, phi, perm, dm, charge, fluid, xl, xh, yl, yh, cl, ch,
                     pop_out, phi_out, conc_out, charge_out, x_hi, x_lo, y_hi, y_lo, dm_out, rim, coef, inv, fl,
                     pe, pa, pb, ce, dn, mm, cc, vel, sh, lv):
     msgs = (xl, xh, yl, yh, cl, ch)
@@ -455,7 +452,7 @@
     charge_out[...] = conc_out[0] - conc_out[1]
     for low, xo, yo in ((False, x_hi, y_hi), (True, x_lo, y_lo)):
         pack_x(TWO, xo, low, phi_out, charge_out, conc_out, pop_out, dm_out)
-        pack_y(TWO, yo, low, below[0:1], phi_out, charge_out, conc_out, pop_out, dm_out)
+        pack_y(TWO, yo, low, cl[ONE.c["misc"], 7:8], phi_out, charge_out, conc_out, pop_out, dm_out)
 
 
 def ions_two_kernel(conc, phi, charge, dm, rim, coef, inv, fl, xl, xh, yl, yh, cl, ch,
@@ -471,7 +468,7 @@
         slab[s * CX + x] = values
 
     ions(fin, fl, cc, vel, store)
-    slab[2 * CX, 0:8] = jnp.broadcast_to(cl[TWO.c["misc"], 7:8], (8, NZ))
+    slab[2 * CX, 0:8] = jnp.broadcast_to(yl[0, TWO.y["owner"] : TWO.y["owner"] + 1], (8, NZ))
 
 
 def flow_two_kernel(pop, fl, sh, xl, xh, yl, yh, cl, ch, pop_out, lv):
@@ -483,15 +480,16 @@
     return jnp.full((1, NZ), me, jnp.int32).astype(F32)
 
 
-def route_kernel(mine, below, above, out):
+def route_kernel(mine, below, above, out, on):
     want = below[2 * CX, 0:1]
     for x in range(2 * CX):
-        out[x] = jnp.where(want == place(0), mine[x], jnp.where(want == place(1), above[x], below[x]))
-
-
-def arrive_kernel(mine, below, above, below_two, above_two, far, owner, out):
+        out[x] = jnp.where(want == place(0), mine[x], above[x])
+        on[x] = below[x]
+
+
+def arrive_kernel(mine, below, above, below_two, above_two, below_three, far, owner, out):
     slab = owner[0:1]
-    near = ((0, mine), (7, below), (1, above), (6, below_two), (2, above_two))
+    near = ((0, mine), (7, below), (1, above), (6, below_two), (2, above_two), (5, below_three))
     for x in range(2 * CX):
         v = far[x]
         for up, values in near:
@@ -549,19 +547,17 @@
          pltpu.SemaphoreType.DMA((5,))),
         [FAR] * 5)
     got = exchange(*sent)
-    c_hi, c_lo = call(corner_one_kernel, tiles(ONE), got[:2])
+    c_hi, c_lo, owner = call(corner_one_kernel, tiles(ONE) + (row,), (owners,) + got[:2], (), [SMEM, VMEM, VMEM])
     got += (shift(c_hi, "gy", 1), shift(c_lo, "gy", -1))
-    (owner,) = call(owner_kernel, (row,), (owners,), (), [SMEM])
-    below = shift(owner, "gy", 1)
     pop, phi, conc, charge, *rest = call(
         step_one_kernel,
         (pops, block, both, block) + messages(TWO)
         + (four, shape(4, CY, NZ), shape(6, *HALO), shape(*HALO), shape(*RIM)),
-        (below, populations, concentration, potential, permittivity, dm, charge, fluid) + got,
+        (populations, concentration, potential, permittivity, dm, charge, fluid) + got,
         (HALO,) + FIELDS + ((5,) + RIM, (19,) + RIM))
     sent, (dm, rim, coef, inv, fl) = rest[:4], rest[4:]
     got = exchange(*sent)
-    c_hi, c_lo = call(corner_two_kernel, tiles(TWO), got[:2] + (rim, got[2]))
+    c_hi, c_lo = call(corner_two_kernel, tiles(TWO), got[:2] + (rim,))
     got += (shift(c_hi, "gy", 1), shift(c_lo, "gy", -1))
     slab = shape(2 * CX, CY, NZ)
     phi, mine, sh = call(
@@ -569,10 +565,12 @@
         (conc, phi, charge, dm, rim, coef, inv, fl) + got, FIELDS)
     below, above = shift(mine, "gy", 1), shift(mine, "gy", -1)
     (pop,) = call(flow_two_kernel, (pops,), (pop, fl, sh) + got, ((19,) + RIM,), flops=40_000_000)
-    (routed,) = call(route_kernel, (slab,), (mine, below, above))
-    far = shift(routed, "gy", 4)
-    below_two, above_two = shift(below, "gy", 1), shift(above, "gy", -1)
-    (migrated,) = call(arrive_kernel, (slab,), (mine, below, above, below_two, above_two, far, owner))
+    routed, on = call(route_kernel, (slab, slab), (mine, below, above))
+    far = shift(routed, "gy", 5)
+    below_two, above_two = shift(on, "gy", 1), shift(above, "gy", -1)
+    below_three = shift(below_two, "gy", 1)
+    (migrated,) = call(
+        arrive_kernel, (slab,), (mine, below, above, below_two, above_two, below_three, far, owner))
     return (pop, phi, migrated.reshape(2, CX, CY, NZ))
 
 

time: 77.1 us -> 74.1 us (0.961)
  the two profiles are of different devices: /device:TPU:7 before, /device:TPU:1 now
where the time goes in v8:
time: 74.1 us; the launch traced here: 73.9 us
  starting transfers between devices  47.5 us (64%)
  waiting for transfers between devices  15.9 us (21%)
  Pallas kernels  9.07 us (12%)
  between operations  1.42 us (2%)
    ppermute x18, starting transfers between devices, shift(): return lax.ppermute(values, axis, [(i, (i + by) % n) for i in range(n)])  47.5 us
    ppermute x18, waiting for transfers between devices, shift(): return lax.ppermute(values, axis, [(i, (i + by) % n) for i in range(n)])  15.9 us
    pallas_call x8, Pallas kernels, call(): pl.pallas_call(kernel, out_shape=outs, in_specs=specs or [VMEM] * len(arg...  9.07 us
  transfers between devices with their start and end apart: 18, of which 13 were waited for; matrix products, arithmetic and copies ran while one was open for 0% of the time, Pallas kernels for 3%

profile of v8, /device:TPU:1, one launch (start us, length us, event | category | flops | bytes accessed | tf_op | source)
XLA Modules:
  0.0 73.9 jit_solution(13644817502691901908)
XLA Ops:
  0.6 0.0 copy-start.3
  0.6 0.0 copy-start.2
  0.7 0.0 copy-start.1
  0.7 0.0 copy-start
  0.7 1.7 %shard_map.85 = (f32[28,16,128]{2,1,0:T(8,128)S(1)}, f32[28,16,128]{2,1,0:T(8,128)S(1)}, f32[8,32,128]{2,1,0:T(8,128)S(1)}, f32[8,32,128]{2,1,0:T(8,128)S(1)}, f...) custom-call(f32[19,8,16,128]{3,2,1,0:T(8,128)} %pop.1, f32[2,8,16,128]{3,2,1,0:T(8,128)} %conc.1, ...), custom_call_target="tpu_custom_call" | custom-call | tf_op jit(solution)/shard_map/pallas_call | solution.py:504
  2.4 4.0 %collective-permute-start = (f32[28,16,128]{2,1,0:T(8,128)S(1)}, f32[28,16,128]{2,1,0:T(8,128)S(1)}, u32[]{:S(2)}, u32[]{:S(2)}) collective-permute-start(f32[28,16,128]{2,1,0:T(8,128)S(1)} %get-tuple-element.36), channel_id=1, source_target_pairs={{0,8},{8,16},{16,24},{24,32},{32,40},{40,48},{48,56},{56,64},{64,7... | collective-permute-start | bytes 688136 | tf_op jit(solution)/shard_map/ppermute | solution.py:522
  6.4 15.9 %collective-permute-start.1 = (f32[28,16,128]{2,1,0:T(8,128)S(1)}, f32[28,16,128]{2,1,0:T(8,128)S(1)}, u32[]{:S(2)}, u32[]{:S(2)}) collective-permute-start(f32[28,16,128]{2,1,0:T(8,128)S(1)} %get-tuple-element.37), channel_id=1, source_target_pairs={{0,760},{8,0},{16,8},{24,16},{32,24},{40,32},{48,40},{56,48},{64,5... | collective-permute-start | bytes 688136 | tf_op jit(solution)/shard_map/ppermute | solution.py:522
  22.4 2.1 %collective-permute-start.2 = (f32[8,32,128]{2,1,0:T(8,128)S(1)}, f32[8,32,128]{2,1,0:T(8,128)S(1)}, u32[]{:S(2)}, u32[]{:S(2)}) collective-permute-start(f32[8,32,128]{2,1,0:T(8,128)S(1)} %get-tuple-element.38), channel_id=1, source_target_pairs={{0,1},{1,2},{2,3},{3,4},{4,5},{5,6},{6,7},{7,0},{8,9},{9,10},{10,1... | collective-permute-start | bytes 393224 | tf_op jit(solution)/shard_map/ppermute | solution.py:522
  24.4 0.0 collective-permute-start.3
  25.1 0.7 collective-permute-done.xl
  25.8 0.9 %collective-permute-done.1.xh = f32[28,16,128]{2,1,0:T(8,128)S(1)} collective-permute-done((f32[28,16,128]{2,1,0:T(8,128)S(1)}, f32[28,16,128]{2,1,0:T(8,128)S(1)}, u32[]{:S(2)}, u32[]{:S(2)}) %collective-permute-start.1) | collective-permute-done | bytes 229408 | tf_op jit(solution)/shard_map/ppermute | solution.py:522
  26.7 2.7 %collective-permute-start.4 = (f32[18,8,128]{2,1,0:T(8,128)S(1)}, f32[18,8,128]{2,1,0:T(8,128)S(1)}, u32[]{:S(2)}, u32[]{:S(2)}) collective-permute-start(f32[18,8,128]{2,1,0:T(8,128)S(1)} %get-tuple-element.40), channel_id=1, source_target_pairs={{0,1},{1,2},{2,3},{3,4},{4,5},{5,6},{6,7},{7,0},{8,9},{9,10},{10,1... | collective-permute-start | bytes 221192 | tf_op jit(solution)/shard_map/ppermute | solution.py:522
  29.3 0.0 collective-permute-start.5
  29.3 0.0 collective-permute-done.2.yl
  29.3 0.0 collective-permute-done.3.yh
  29.3 1.4 %collective-permute-done.4.cl = f32[18,8,128]{2,1,0:T(8,128)S(1)} collective-permute-done((f32[18,8,128]{2,1,0:T(8,128)S(1)}, f32[18,8,128]{2,1,0:T(8,128)S(1)}, u32[]{:S(2)}, u32[]{:S(2)}) %collective-permute-start.4) | collective-permute-done | bytes 73760 | tf_op jit(solution)/shard_map/ppermute | solution.py:522
  30.7 2.4 %collective-permute-done.5.ch = f32[18,8,128]{2,1,0:T(8,128)S(1)} collective-permute-done((f32[18,8,128]{2,1,0:T(8,128)S(1)}, f32[18,8,128]{2,1,0:T(8,128)S(1)}, u32[]{:S(2)}, u32[]{:S(2)}) %collective-permute-start.5) | collective-permute-done | bytes 73760 | tf_op jit(solution)/shard_map/ppermute | solution.py:522
  33.1 0.0 copy-done.3
  33.1 0.0 copy-done.2
  33.1 0.0 copy-done
  33.1 2.7 %shard_map.87 = (f32[19,8,16,128]{3,2,1,0:T(8,128)S(1)}, f32[8,16,128]{2,1,0:T(8,128)S(1)}, f32[2,8,16,128]{3,2,1,0:T(8,128)S(1)}, f32[8,16,128]{2,1,0:T(8,128)S...) custom-call(f32[19,8,16,128]{3,2,1,0:T(8,128)S(1)} %copy-done, ...), custom_call_target="tpu_custom_call" | custom-call | tf_op jit(solution)/shard_map/pallas_call | solution.py:504
  35.9 1.9 %collective-permute-start.6 = (f32[19,16,128]{2,1,0:T(8,128)S(1)}, f32[19,16,128]{2,1,0:T(8,128)S(1)}, u32[]{:S(2)}, u32[]{:S(2)}) collective-permute-start(f32[19,16,128]{2,1,0:T(8,128)S(1)} %get-tuple-element.51), channel_id=1, source_target_pairs={{0,8},{8,16},{16,24},{24,32},{32,40},{40,48},{48,56},{56,64},{64,7... | collective-permute-start | bytes 466952 | tf_op jit(solution)/shard_map/ppermute | solution.py:522
  37.8 7.4 %collective-permute-start.7 = (f32[19,16,128]{2,1,0:T(8,128)S(1)}, f32[19,16,128]{2,1,0:T(8,128)S(1)}, u32[]{:S(2)}, u32[]{:S(2)}) collective-permute-start(f32[19,16,128]{2,1,0:T(8,128)S(1)} %get-tuple-element.52), channel_id=1, source_target_pairs={{0,760},{8,0},{16,8},{24,16},{32,24},{40,32},{48,40},{56,48},{64,5... | collective-permute-start | bytes 466952 | tf_op jit(solution)/shard_map/ppermute | solution.py:522
  45.2 0.3 collective-permute-start.8
  45.5 0.2 collective-permute-start.9
  45.7 1.8 %collective-permute-done.6.xl = f32[19,16,128]{2,1,0:T(8,128)S(1)} collective-permute-done((f32[19,16,128]{2,1,0:T(8,128)S(1)}, f32[19,16,128]{2,1,0:T(8,128)S(1)}, u32[]{:S(2)}, u32[]{:S(2)}) %collective-permute-start.6) | collective-permute-done | bytes 155680 | tf_op jit(solution)/shard_map/ppermute | solution.py:522
  47.5 0.9 %collective-permute-done.7.xh = f32[19,16,128]{2,1,0:T(8,128)S(1)} collective-permute-done((f32[19,16,128]{2,1,0:T(8,128)S(1)}, f32[19,16,128]{2,1,0:T(8,128)S(1)}, u32[]{:S(2)}, u32[]{:S(2)}) %collective-permute-start.7) | collective-permute-done | bytes 155680 | tf_op jit(solution)/shard_map/ppermute | solution.py:522
  48.5 0.9 %collective-permute-start.10 = (f32[12,8,128]{2,1,0:T(8,128)S(1)}, f32[12,8,128]{2,1,0:T(8,128)S(1)}, u32[]{:S(2)}, u32[]{:S(2)}) collective-permute-start(f32[12,8,128]{2,1,0:T(8,128)S(1)} %get-tuple-element.55), channel_id=1, source_target_pairs={{0,1},{1,2},{2,3},{3,4},{4,5},{5,6},{6,7},{7,0},{8,9},{9,10},{10,1... | collective-permute-start | bytes 147464 | tf_op jit(solution)/shard_map/ppermute | solution.py:522
  49.4 0.1 collective-permute-start.11
  49.5 0.0 collective-permute-done.8.yl
  49.5 0.4 collective-permute-done.9.yh
  49.9 0.7 collective-permute-done.10.cl
  50.5 2.3 %collective-permute-done.11.ch = f32[12,8,128]{2,1,0:T(8,128)S(1)} collective-permute-done((f32[12,8,128]{2,1,0:T(8,128)S(1)}, f32[12,8,128]{2,1,0:T(8,128)S(1)}, u32[]{:S(2)}, u32[]{:S(2)}) %collective-permute-start.11) | collective-permute-done | bytes 49184 | tf_op jit(solution)/shard_map/ppermute | solution.py:522
  52.9 1.9 %shard_map.89 = (f32[8,16,128]{2,1,0:T(8,128)}, f32[17,16,128]{2,1,0:T(8,128)S(1)}, f32[5,10,32,128]{3,2,1,0:T(8,128)S(1)}) custom-call(f32[2,8,16,128]{3,2,1,0:T(8,128)S(1)} %get-tuple-element.44.conc, f32[8,16,128]{2,1,0:T(8,128)S(1)} %get-tuple-element.45.phi, f32[8,16,128]{2,1,0:T(8,128)S(1)} %get-tuple-element.46.charge, ...), custom_call_target="tpu_custom_call" | custom-call | tf_op jit(solution)/shard_map/pallas_call | solution.py:504
  54.8 1.3 %collective-permute-start.13 = (f32[17,16,128]{2,1,0:T(8,128)S(1)}, f32[17,16,128]{2,1,0:T(8,128)S(1)}, u32[]{:S(2)}, u32[]{:S(2)}) collective-permute-start(f32[17,16,128]{2,1,0:T(8,128)S(1)} %get-tuple-element.59.mine), channel_id=1, source_target_pairs={{0,7},{1,0},{2,1},{3,2},{4,3},{5,4},{6,5},{7,6},{8,15},{9,8},{10,9... | collective-permute-start | bytes 417800 | tf_op jit(solution)/shard_map/ppermute | solution.py:522
  56.1 0.4 collective-permute-start.12
  56.5 2.7 %collective-permute-done.13.above = f32[17,16,128]{2,1,0:T(8,128)S(1)} collective-permute-done((f32[17,16,128]{2,1,0:T(8,128)S(1)}, f32[17,16,128]{2,1,0:T(8,128)S(1)}, u32[]{:S(2)}, u32[]{:S(2)}) %collective-permute-start.13) | collective-permute-done | bytes 139296 | tf_op jit(solution)/shard_map/ppermute | solution.py:522
  59.2 0.6 collective-permute-done.12.below
  59.9 1.1 %collective-permute-start.14 = (f32[16,16,128]{2,1,0:T(8,128)S(1)}, f32[16,16,128]{2,1,0:T(8,128)S(1)}, u32[]{:S(2)}, u32[]{:S(2)}) collective-permute-start(f32[16,16,128]{2,1,0:T(8,128)S(1)} %get-tuple-element.60), channel_id=1, source_target_pairs={{0,1},{1,2},{2,3},{3,4},{4,5},{5,6},{6,7},{7,0},{8,9},{9,10},{10,1... | collective-permute-start | bytes 393224 | tf_op jit(solution)/shard_map/ppermute | solution.py:522
  61.0 3.8 %collective-permute-start.15 = (f32[17,16,128]{2,1,0:T(8,128)S(1)}, f32[17,16,128]{2,1,0:T(8,128)S(1)}, u32[]{:S(2)}, u32[]{:S(2)}) collective-permute-start(f32[17,16,128]{2,1,0:T(8,128)S(1)} %collective-permute-done.13.above), channel_id=1, source_target_pairs={{0,7},{1,0},{2,1},{3,2},{4,3},{5,4},{6,5},{7,6},{8,15},{9,8},{10,9... | collective-permute-start | bytes 417800 | tf_op jit(solution)/shard_map/ppermute | solution.py:522
  64.8 1.9 %collective-permute-start.17 = (f32[16,16,128]{2,1,0:T(8,128)S(1)}, f32[16,16,128]{2,1,0:T(8,128)S(1)}, u32[]{:S(2)}, u32[]{:S(2)}) collective-permute-start(f32[16,16,128]{2,1,0:T(8,128)S(1)} %get-tuple-element.61), channel_id=1, source_target_pairs={{0,5},{1,6},{2,7},{3,0},{4,1},{5,2},{6,3},{7,4},{8,13},{9,14},{10,... | collective-permute-start | bytes 393224 | tf_op jit(solution)/shard_map/ppermute | solution.py:522
  66.7 0.0 collective-permute-done.14.below_two
  66.7 3.4 %collective-permute-start.16 = (f32[16,16,128]{2,1,0:T(8,128)S(1)}, f32[16,16,128]{2,1,0:T(8,128)S(1)}, u32[]{:S(2)}, u32[]{:S(2)}) collective-permute-start(f32[16,16,128]{2,1,0:T(8,128)S(1)} %collective-permute-done.14.below_two), channel_id=1, source_target_pairs={{0,1},{1,2},{2,3},{3,4},{4,5},{5,6},{6,7},{7,0},{8,9},{9,10},{10,1... | collective-permute-start | bytes 393224 | tf_op jit(solution)/shard_map/ppermute | solution.py:522
  70.1 1.9 %shard_map.90 = f32[19,8,16,128]{3,2,1,0:T(8,128)} custom-call(f32[19,8,16,128]{3,2,1,0:T(8,128)S(1)} %get-tuple-element.42.pop, f32[10,32,128]{2,1,0:T(8,128)S(1)} %get-tuple-element.43.fl, f32[5,10,32,128]{3,2,1,0:T(8,128)S(1)} %get-tuple-element.57.sh, f32[19,16,128]{2,1,0:T(8,128)S(1)} %collective-permute-done.6.xl, ...), custom_call_target="tpu_custom_call" | custom-call | flops 40000000 | tf_op jit(solution)/shard_map/pallas_call | solution.py:504
  72.0 0.5 collective-permute-done.17.far
  72.6 0.0 collective-permute-done.15.above_two
  72.6 0.5 collective-permute-done.16.below_three
  73.1 0.7 shard_map.92
  (4 shorter events, 0.1 us)
Async XLA Ops:
  0.6 32.5 %copy-start.3 = (f32[8,16,128]{2,1,0:T(8,128)S(1)}, f32[8,16,128]{2,1,0:T(8,128)}, u32[]{:S(2)}) copy-start(f32[8,16,128]{2,1,0:T(8,128)} %perm.1) | copy-start | bytes 196612
  0.6 32.5 %copy-start.2 = (f32[8,16,128]{2,1,0:T(8,128)S(1)}, f32[8,16,128]{2,1,0:T(8,128)}, u32[]{:S(2)}) copy-start(f32[8,16,128]{2,1,0:T(8,128)} %phi.1) | copy-start | bytes 196612
  0.7 32.5 %copy-start.1 = (f32[2,8,16,128]{3,2,1,0:T(8,128)S(1)}, f32[2,8,16,128]{3,2,1,0:T(8,128)}, u32[]{:S(2)}) copy-start(f32[2,8,16,128]{3,2,1,0:T(8,128)} %conc.1) | copy-start | bytes 393220
  0.7 32.5 %copy-start = (f32[19,8,16,128]{3,2,1,0:T(8,128)S(1)}, f32[19,8,16,128]{3,2,1,0:T(8,128)}, u32[]{:S(2)}) copy-start(f32[19,8,16,128]{3,2,1,0:T(8,128)} %pop.1) | copy-start | bytes 3735556
  2.4 23.4 %collective-permute-start = (f32[28,16,128]{2,1,0:T(8,128)S(1)}, f32[28,16,128]{2,1,0:T(8,128)S(1)}, u32[]{:S(2)}, u32[]{:S(2)}) collective-permute-start(f32[28,16,128]{2,1,0:T(8,128)S(1)} %get-tuple-element.36), channel_id=1, source_target_pairs={{0,8},{8,16},{16,24},{24,32},{32,40},{40,48},{48,56},{56,64},{64,7... | collective-permute-start | bytes 688136 | tf_op jit(solution)/shard_map/ppermute | solution.py:522
  6.4 20.2 %collective-permute-start.1 = (f32[28,16,128]{2,1,0:T(8,128)S(1)}, f32[28,16,128]{2,1,0:T(8,128)S(1)}, u32[]{:S(2)}, u32[]{:S(2)}) collective-permute-start(f32[28,16,128]{2,1,0:T(8,128)S(1)} %get-tuple-element.37), channel_id=1, source_target_pairs={{0,760},{8,0},{16,8},{24,16},{32,24},{40,32},{48,40},{56,48},{64,5... | collective-permute-start | bytes 688136 | tf_op jit(solution)/shard_map/ppermute | solution.py:522
  22.4 6.9 %collective-permute-start.2 = (f32[8,32,128]{2,1,0:T(8,128)S(1)}, f32[8,32,128]{2,1,0:T(8,128)S(1)}, u32[]{:S(2)}, u32[]{:S(2)}) collective-permute-start(f32[8,32,128]{2,1,0:T(8,128)S(1)} %get-tuple-element.38), channel_id=1, source_target_pairs={{0,1},{1,2},{2,3},{3,4},{4,5},{5,6},{6,7},{7,0},{8,9},{9,10},{10,1... | collective-permute-start | bytes 393224 | tf_op jit(solution)/shard_map/ppermute | solution.py:522
  24.4 4.9 %collective-permute-start.3 = (f32[8,32,128]{2,1,0:T(8,128)S(1)}, f32[8,32,128]{2,1,0:T(8,128)S(1)}, u32[]{:S(2)}, u32[]{:S(2)}) collective-permute-start(f32[8,32,128]{2,1,0:T(8,128)S(1)} %get-tuple-element.39), channel_id=1, source_target_pairs={{0,7},{1,0},{2,1},{3,2},{4,3},{5,4},{6,5},{7,6},{8,15},{9,8},{10,9... | collective-permute-start | bytes 393224 | tf_op jit(solution)/shard_map/ppermute | solution.py:522
  26.7 4.1 %collective-permute-start.4 = (f32[18,8,128]{2,1,0:T(8,128)S(1)}, f32[18,8,128]{2,1,0:T(8,128)S(1)}, u32[]{:S(2)}, u32[]{:S(2)}) collective-permute-start(f32[18,8,128]{2,1,0:T(8,128)S(1)} %get-tuple-element.40), channel_id=1, source_target_pairs={{0,1},{1,2},{2,3},{3,4},{4,5},{5,6},{6,7},{7,0},{8,9},{9,10},{10,1... | collective-permute-start | bytes 221192 | tf_op jit(solution)/shard_map/ppermute | solution.py:522
  29.3 3.8 %collective-permute-start.5 = (f32[18,8,128]{2,1,0:T(8,128)S(1)}, f32[18,8,128]{2,1,0:T(8,128)S(1)}, u32[]{:S(2)}, u32[]{:S(2)}) collective-permute-start(f32[18,8,128]{2,1,0:T(8,128)S(1)} %get-tuple-element.41), channel_id=1, source_target_pairs={{0,7},{1,0},{2,1},{3,2},{4,3},{5,4},{6,5},{7,6},{8,15},{9,8},{10,9... | collective-permute-start | bytes 221192 | tf_op jit(solution)/shard_map/ppermute | solution.py:522
  35.9 11.7 %collective-permute-start.6 = (f32[19,16,128]{2,1,0:T(8,128)S(1)}, f32[19,16,128]{2,1,0:T(8,128)S(1)}, u32[]{:S(2)}, u32[]{:S(2)}) collective-permute-start(f32[19,16,128]{2,1,0:T(8,128)S(1)} %get-tuple-element.51), channel_id=1, source_target_pairs={{0,8},{8,16},{16,24},{24,32},{32,40},{40,48},{48,56},{56,64},{64,7... | collective-permute-start | bytes 466952 | tf_op jit(solution)/shard_map/ppermute | solution.py:522
  37.8 10.7 %collective-permute-start.7 = (f32[19,16,128]{2,1,0:T(8,128)S(1)}, f32[19,16,128]{2,1,0:T(8,128)S(1)}, u32[]{:S(2)}, u32[]{:S(2)}) collective-permute-start(f32[19,16,128]{2,1,0:T(8,128)S(1)} %get-tuple-element.52), channel_id=1, source_target_pairs={{0,760},{8,0},{16,8},{24,16},{32,24},{40,32},{48,40},{56,48},{64,5... | collective-permute-start | bytes 466952 | tf_op jit(solution)/shard_map/ppermute | solution.py:522
  45.2 4.3 %collective-permute-start.8 = (f32[8,24,128]{2,1,0:T(8,128)S(1)}, f32[8,24,128]{2,1,0:T(8,128)S(1)}, u32[]{:S(2)}, u32[]{:S(2)}) collective-permute-start(f32[8,24,128]{2,1,0:T(8,128)S(1)} %get-tuple-element.53), channel_id=1, source_target_pairs={{0,1},{1,2},{2,3},{3,4},{4,5},{5,6},{6,7},{7,0},{8,9},{9,10},{10,1... | collective-permute-start | bytes 294920 | tf_op jit(solution)/shard_map/ppermute | solution.py:522
  45.5 4.3 %collective-permute-start.9 = (f32[8,24,128]{2,1,0:T(8,128)S(1)}, f32[8,24,128]{2,1,0:T(8,128)S(1)}, u32[]{:S(2)}, u32[]{:S(2)}) collective-permute-start(f32[8,24,128]{2,1,0:T(8,128)S(1)} %get-tuple-element.54), channel_id=1, source_target_pairs={{0,7},{1,0},{2,1},{3,2},{4,3},{5,4},{6,5},{7,6},{8,15},{9,8},{10,9... | collective-permute-start | bytes 294920 | tf_op jit(solution)/shard_map/ppermute | solution.py:522
  48.5 2.0 %collective-permute-start.10 = (f32[12,8,128]{2,1,0:T(8,128)S(1)}, f32[12,8,128]{2,1,0:T(8,128)S(1)}, u32[]{:S(2)}, u32[]{:S(2)}) collective-permute-start(f32[12,8,128]{2,1,0:T(8,128)S(1)} %get-tuple-element.55), channel_id=1, source_target_pairs={{0,1},{1,2},{2,3},{3,4},{4,5},{5,6},{6,7},{7,0},{8,9},{9,10},{10,1... | collective-permute-start | bytes 147464 | tf_op jit(solution)/shard_map/ppermute | solution.py:522
  49.4 3.5 %collective-permute-start.11 = (f32[12,8,128]{2,1,0:T(8,128)S(1)}, f32[12,8,128]{2,1,0:T(8,128)S(1)}, u32[]{:S(2)}, u32[]{:S(2)}) collective-permute-start(f32[12,8,128]{2,1,0:T(8,128)S(1)} %get-tuple-element.56), channel_id=1, source_target_pairs={{0,7},{1,0},{2,1},{3,2},{4,3},{5,4},{6,5},{7,6},{8,15},{9,8},{10,9... | collective-permute-start | bytes 147464 | tf_op jit(solution)/shard_map/ppermute | solution.py:522
  54.8 4.5 %collective-permute-start.13 = (f32[17,16,128]{2,1,0:T(8,128)S(1)}, f32[17,16,128]{2,1,0:T(8,128)S(1)}, u32[]{:S(2)}, u32[]{:S(2)}) collective-permute-start(f32[17,16,128]{2,1,0:T(8,128)S(1)} %get-tuple-element.59.mine), channel_id=1, source_target_pairs={{0,7},{1,0},{2,1},{3,2},{4,3},{5,4},{6,5},{7,6},{8,15},{9,8},{10,9... | collective-permute-start | bytes 417800 | tf_op jit(solution)/shard_map/ppermute | solution.py:522
  56.1 3.8 %collective-permute-start.12 = (f32[17,16,128]{2,1,0:T(8,128)S(1)}, f32[17,16,128]{2,1,0:T(8,128)S(1)}, u32[]{:S(2)}, u32[]{:S(2)}) collective-permute-start(f32[17,16,128]{2,1,0:T(8,128)S(1)} %get-tuple-element.59.mine), channel_id=1, source_target_pairs={{0,1},{1,2},{2,3},{3,4},{4,5},{5,6},{6,7},{7,0},{8,9},{9,10},{10,1... | collective-permute-start | bytes 417800 | tf_op jit(solution)/shard_map/ppermute | solution.py:522
  59.9 6.8 %collective-permute-start.14 = (f32[16,16,128]{2,1,0:T(8,128)S(1)}, f32[16,16,128]{2,1,0:T(8,128)S(1)}, u32[]{:S(2)}, u32[]{:S(2)}) collective-permute-start(f32[16,16,128]{2,1,0:T(8,128)S(1)} %get-tuple-element.60), channel_id=1, source_target_pairs={{0,1},{1,2},{2,3},{3,4},{4,5},{5,6},{6,7},{7,0},{8,9},{9,10},{10,1... | collective-permute-start | bytes 393224 | tf_op jit(solution)/shard_map/ppermute | solution.py:522
  61.0 11.5 %collective-permute-start.15 = (f32[17,16,128]{2,1,0:T(8,128)S(1)}, f32[17,16,128]{2,1,0:T(8,128)S(1)}, u32[]{:S(2)}, u32[]{:S(2)}) collective-permute-start(f32[17,16,128]{2,1,0:T(8,128)S(1)} %collective-permute-done.13.above), channel_id=1, source_target_pairs={{0,7},{1,0},{2,1},{3,2},{4,3},{5,4},{6,5},{7,6},{8,15},{9,8},{10,9... | collective-permute-start | bytes 417800 | tf_op jit(solution)/shard_map/ppermute | solution.py:522
  64.8 7.8 %collective-permute-start.17 = (f32[16,16,128]{2,1,0:T(8,128)S(1)}, f32[16,16,128]{2,1,0:T(8,128)S(1)}, u32[]{:S(2)}, u32[]{:S(2)}) collective-permute-start(f32[16,16,128]{2,1,0:T(8,128)S(1)} %get-tuple-element.61), channel_id=1, source_target_pairs={{0,5},{1,6},{2,7},{3,0},{4,1},{5,2},{6,3},{7,4},{8,13},{9,14},{10,... | collective-permute-start | bytes 393224 | tf_op jit(solution)/shard_map/ppermute | solution.py:522
  66.7 6.4 %collective-permute-start.16 = (f32[16,16,128]{2,1,0:T(8,128)S(1)}, f32[16,16,128]{2,1,0:T(8,128)S(1)}, u32[]{:S(2)}, u32[]{:S(2)}) collective-permute-start(f32[16,16,128]{2,1,0:T(8,128)S(1)} %collective-permute-done.14.below_two), channel_id=1, source_target_pairs={{0,1},{1,2},{2,3},{3,4},{4,5},{5,6},{6,7},{7,0},{8,9},{9,10},{10,1... | collective-permute-start | bytes 393224 | tf_op jit(solution)/shard_map/ppermute | solution.py:522

commit v9 on v8

--- a/solution.py
+++ b/solution.py
@@ -215,6 +215,7 @@
     pack_corners(ONE, c_hi, False, xl, xh)
     c_hi[ONE.c["misc"], 7:8] = owner_row[0:1]
     pack_corners(ONE, c_lo, True, xl, xh)
+    c_lo[ONE.c["misc"], 7:8] = owner_row[0:1]
 
 
 def corner_two_kernel(xl, xh, rim, c_hi, c_lo):
@@ -452,7 +453,7 @@
     charge_out[...] = conc_out[0] - conc_out[1]
     for low, xo, yo in ((False, x_hi, y_hi), (True, x_lo, y_lo)):
         pack_x(TWO, xo, low, phi_out, charge_out, conc_out, pop_out, dm_out)
-        pack_y(TWO, yo, low, cl[ONE.c["misc"], 7:8], phi_out, charge_out, conc_out, pop_out, dm_out)
+        pack_y(TWO, yo, low, (ch if low else cl)[ONE.c["misc"], 7:8], phi_out, charge_out, conc_out, pop_out, dm_out)
 
 
 def ions_two_kernel(conc, phi, charge, dm, rim, coef, inv, fl, xl, xh, yl, yh, cl, ch,
@@ -468,7 +469,8 @@
         slab[s * CX + x] = values
 
     ions(fin, fl, cc, vel, store)
-    slab[2 * CX, 0:8] = jnp.broadcast_to(yl[0, TWO.y["owner"] : TWO.y["owner"] + 1], (8, NZ))
+    for msg, rows in ((yl, LO_T), (yh, slice(8, 16))):
+        slab[2 * CX, rows] = jnp.broadcast_to(msg[0, TWO.y["owner"] : TWO.y["owner"] + 1], (8, NZ))
 
 
 def flow_two_kernel(pop, fl, sh, xl, xh, yl, yh, cl, ch, pop_out, lv):
@@ -480,18 +482,18 @@
     return jnp.full((1, NZ), me, jnp.int32).astype(F32)
 
 
-def route_kernel(mine, below, above, out, on):
-    want = below[2 * CX, 0:1]
+def route_kernel(mine, below, above, up, down):
+    want_up, want_down = above[2 * CX, 8:9], below[2 * CX, 0:1]
     for x in range(2 * CX):
-        out[x] = jnp.where(want == place(0), mine[x], above[x])
-        on[x] = below[x]
-
-
-def arrive_kernel(mine, below, above, below_two, above_two, below_three, far, owner, out):
+        up[x] = jnp.where(want_up == place(0), mine[x], jnp.where(want_up == place(1), above[x], below[x]))
+        down[x] = jnp.where(want_down == place(0), mine[x], below[x])
+
+
+def arrive_kernel(mine, below, above, from_low, from_high, owner, out):
     slab = owner[0:1]
-    near = ((0, mine), (7, below), (1, above), (6, below_two), (2, above_two), (5, below_three))
+    near = ((0, mine), (7, below), (1, above), (2, from_high), (3, from_high))
     for x in range(2 * CX):
-        v = far[x]
+        v = from_low[x]
         for up, values in near:
             v = jnp.where(slab == place(up), values[x], v)
         out[x] = v
@@ -565,12 +567,9 @@
         (conc, phi, charge, dm, rim, coef, inv, fl) + got, FIELDS)
     below, above = shift(mine, "gy", 1), shift(mine, "gy", -1)
     (pop,) = call(flow_two_kernel, (pops,), (pop, fl, sh) + got, ((19,) + RIM,), flops=40_000_000)
-    routed, on = call(route_kernel, (slab, slab), (mine, below, above))
-    far = shift(routed, "gy", 5)
-    below_two, above_two = shift(on, "gy", 1), shift(above, "gy", -1)
-    below_three = shift(below_two, "gy", 1)
-    (migrated,) = call(
-        arrive_kernel, (slab,), (mine, below, above, below_two, above_two, below_three, far, owner))
+    up, down = call(route_kernel, (slab, slab), (mine, below, above))
+    from_low, from_high = shift(up, "gy", 3), shift(down, "gy", -3)
+    (migrated,) = call(arrive_kernel, (slab,), (mine, below, above, from_low, from_high, owner))
     return (pop, phi, migrated.reshape(2, CX, CY, NZ))
 
 

time: 74.1 us -> 74.4 us (level)
  waiting for transfers between devices: 15.9 us -> 19.4 us
  starting transfers between devices: 47.5 us -> 44.1 us
    ppermute x18 -> x16, waiting for transfers between devices: 15.9 us -> 19.4 us  [shift(): return lax.ppermute(values, axis, [(i, (i + by) % n) for i in range(n)])]
    ppermute x18 -> x16, starting transfers between devices: 47.5 us -> 44.1 us  [shift(): return lax.ppermute(values, axis, [(i, (i + by) % n) for i in range(n)])]
  transfers between devices with their start and end apart: 18 -> 16, of which waited for: 13 -> 12; matrix products, arithmetic and copies ran while one was open for 0% -> 0% of each run, Pallas kernels for 3% -> 3%
where the time goes in v9:
time: 74.4 us; the launch traced here: 73.6 us
  starting transfers between devices  44.1 us (59%)
  waiting for transfers between devices  19.4 us (26%)
  Pallas kernels  8.68 us (12%)
  between operations  1.41 us (2%)
    ppermute x16, starting transfers between devices, shift(): return lax.ppermute(values, axis, [(i, (i + by) % n) for i in range(n)])  44.1 us
    ppermute x16, waiting for transfers between devices, shift(): return lax.ppermute(values, axis, [(i, (i + by) % n) for i in range(n)])  19.4 us
    pallas_call x8, Pallas kernels, call(): pl.pallas_call(kernel, out_shape=outs, in_specs=specs or [VMEM] * len(arg...  8.68 us
  transfers between devices with their start and end apart: 16, of which 12 were waited for; matrix products, arithmetic and copies ran while one was open for 0% of the time, Pallas kernels for 3%

profile of v9, /device:TPU:1, one launch (start us, length us, event | category | flops | bytes accessed | tf_op | source)
XLA Modules:
  0.0 73.6 jit_solution(15420564566012088168)
XLA Ops:
  0.6 0.0 copy-start.3
  0.6 0.0 copy-start.2
  0.7 0.0 copy-start.1
  0.7 0.0 copy-start
  0.7 1.7 %shard_map.85 = (f32[28,16,128]{2,1,0:T(8,128)S(1)}, f32[28,16,128]{2,1,0:T(8,128)S(1)}, f32[8,32,128]{2,1,0:T(8,128)S(1)}, f32[8,32,128]{2,1,0:T(8,128)S(1)}, f...) custom-call(f32[19,8,16,128]{3,2,1,0:T(8,128)} %pop.1, f32[2,8,16,128]{3,2,1,0:T(8,128)} %conc.1, ...), custom_call_target="tpu_custom_call" | custom-call | tf_op jit(solution)/shard_map/pallas_call | solution.py:506
  2.4 4.0 %collective-permute-start = (f32[28,16,128]{2,1,0:T(8,128)S(1)}, f32[28,16,128]{2,1,0:T(8,128)S(1)}, u32[]{:S(2)}, u32[]{:S(2)}) collective-permute-start(f32[28,16,128]{2,1,0:T(8,128)S(1)} %get-tuple-element.36), channel_id=1, source_target_pairs={{0,8},{8,16},{16,24},{24,32},{32,40},{40,48},{48,56},{56,64},{64,7... | collective-permute-start | bytes 688136 | tf_op jit(solution)/shard_map/ppermute | solution.py:524
  6.4 15.9 %collective-permute-start.1 = (f32[28,16,128]{2,1,0:T(8,128)S(1)}, f32[28,16,128]{2,1,0:T(8,128)S(1)}, u32[]{:S(2)}, u32[]{:S(2)}) collective-permute-start(f32[28,16,128]{2,1,0:T(8,128)S(1)} %get-tuple-element.37), channel_id=1, source_target_pairs={{0,760},{8,0},{16,8},{24,16},{32,24},{40,32},{48,40},{56,48},{64,5... | collective-permute-start | bytes 688136 | tf_op jit(solution)/shard_map/ppermute | solution.py:524
  22.4 2.1 %collective-permute-start.2 = (f32[8,32,128]{2,1,0:T(8,128)S(1)}, f32[8,32,128]{2,1,0:T(8,128)S(1)}, u32[]{:S(2)}, u32[]{:S(2)}) collective-permute-start(f32[8,32,128]{2,1,0:T(8,128)S(1)} %get-tuple-element.38), channel_id=1, source_target_pairs={{0,1},{1,2},{2,3},{3,4},{4,5},{5,6},{6,7},{7,0},{8,9},{9,10},{10,1... | collective-permute-start | bytes 393224 | tf_op jit(solution)/shard_map/ppermute | solution.py:524
  24.4 0.0 collective-permute-start.3
  25.1 0.7 collective-permute-done.xl
  25.8 0.9 %collective-permute-done.1.xh = f32[28,16,128]{2,1,0:T(8,128)S(1)} collective-permute-done((f32[28,16,128]{2,1,0:T(8,128)S(1)}, f32[28,16,128]{2,1,0:T(8,128)S(1)}, u32[]{:S(2)}, u32[]{:S(2)}) %collective-permute-start.1) | collective-permute-done | bytes 229408 | tf_op jit(solution)/shard_map/ppermute | solution.py:524
  26.7 2.7 %collective-permute-start.4 = (f32[18,8,128]{2,1,0:T(8,128)S(1)}, f32[18,8,128]{2,1,0:T(8,128)S(1)}, u32[]{:S(2)}, u32[]{:S(2)}) collective-permute-start(f32[18,8,128]{2,1,0:T(8,128)S(1)} %get-tuple-element.40), channel_id=1, source_target_pairs={{0,1},{1,2},{2,3},{3,4},{4,5},{5,6},{6,7},{7,0},{8,9},{9,10},{10,1... | collective-permute-start | bytes 221192 | tf_op jit(solution)/shard_map/ppermute | solution.py:524
  29.3 0.0 collective-permute-start.5
  29.3 0.0 collective-permute-done.2.yl
  29.3 0.0 collective-permute-done.3.yh
  29.3 1.4 %collective-permute-done.4.cl = f32[18,8,128]{2,1,0:T(8,128)S(1)} collective-permute-done((f32[18,8,128]{2,1,0:T(8,128)S(1)}, f32[18,8,128]{2,1,0:T(8,128)S(1)}, u32[]{:S(2)}, u32[]{:S(2)}) %collective-permute-start.4) | collective-permute-done | bytes 73760 | tf_op jit(solution)/shard_map/ppermute | solution.py:524
  30.7 2.4 %collective-permute-done.5.ch = f32[18,8,128]{2,1,0:T(8,128)S(1)} collective-permute-done((f32[18,8,128]{2,1,0:T(8,128)S(1)}, f32[18,8,128]{2,1,0:T(8,128)S(1)}, u32[]{:S(2)}, u32[]{:S(2)}) %collective-permute-start.5) | collective-permute-done | bytes 73760 | tf_op jit(solution)/shard_map/ppermute | solution.py:524
  33.1 0.0 copy-done.3
  33.1 0.0 copy-done.2
  33.1 0.0 copy-done.1
  33.1 0.0 copy-done
  33.1 2.7 %shard_map.87 = (f32[19,8,16,128]{3,2,1,0:T(8,128)S(1)}, f32[8,16,128]{2,1,0:T(8,128)S(1)}, f32[2,8,16,128]{3,2,1,0:T(8,128)S(1)}, f32[8,16,128]{2,1,0:T(8,128)S...) custom-call(f32[19,8,16,128]{3,2,1,0:T(8,128)S(1)} %copy-done, ...), custom_call_target="tpu_custom_call" | custom-call | tf_op jit(solution)/shard_map/pallas_call | solution.py:506
  35.9 1.9 %collective-permute-start.6 = (f32[19,16,128]{2,1,0:T(8,128)S(1)}, f32[19,16,128]{2,1,0:T(8,128)S(1)}, u32[]{:S(2)}, u32[]{:S(2)}) collective-permute-start(f32[19,16,128]{2,1,0:T(8,128)S(1)} %get-tuple-element.51), channel_id=1, source_target_pairs={{0,8},{8,16},{16,24},{24,32},{32,40},{40,48},{48,56},{56,64},{64,7... | collective-permute-start | bytes 466952 | tf_op jit(solution)/shard_map/ppermute | solution.py:524
  37.8 7.4 %collective-permute-start.7 = (f32[19,16,128]{2,1,0:T(8,128)S(1)}, f32[19,16,128]{2,1,0:T(8,128)S(1)}, u32[]{:S(2)}, u32[]{:S(2)}) collective-permute-start(f32[19,16,128]{2,1,0:T(8,128)S(1)} %get-tuple-element.52), channel_id=1, source_target_pairs={{0,760},{8,0},{16,8},{24,16},{32,24},{40,32},{48,40},{56,48},{64,5... | collective-permute-start | bytes 466952 | tf_op jit(solution)/shard_map/ppermute | solution.py:524
  45.2 0.3 collective-permute-start.8
  45.5 0.2 collective-permute-start.9
  45.7 1.8 %collective-permute-done.6.xl = f32[19,16,128]{2,1,0:T(8,128)S(1)} collective-permute-done((f32[19,16,128]{2,1,0:T(8,128)S(1)}, f32[19,16,128]{2,1,0:T(8,128)S(1)}, u32[]{:S(2)}, u32[]{:S(2)}) %collective-permute-start.6) | collective-permute-done | bytes 155680 | tf_op jit(solution)/shard_map/ppermute | solution.py:524
  47.6 0.9 %collective-permute-done.7.xh = f32[19,16,128]{2,1,0:T(8,128)S(1)} collective-permute-done((f32[19,16,128]{2,1,0:T(8,128)S(1)}, f32[19,16,128]{2,1,0:T(8,128)S(1)}, u32[]{:S(2)}, u32[]{:S(2)}) %collective-permute-start.7) | collective-permute-done | bytes 155680 | tf_op jit(solution)/shard_map/ppermute | solution.py:524
  48.5 0.9 %collective-permute-start.10 = (f32[12,8,128]{2,1,0:T(8,128)S(1)}, f32[12,8,128]{2,1,0:T(8,128)S(1)}, u32[]{:S(2)}, u32[]{:S(2)}) collective-permute-start(f32[12,8,128]{2,1,0:T(8,128)S(1)} %get-tuple-element.55), channel_id=1, source_target_pairs={{0,1},{1,2},{2,3},{3,4},{4,5},{5,6},{6,7},{7,0},{8,9},{9,10},{10,1... | collective-permute-start | bytes 147464 | tf_op jit(solution)/shard_map/ppermute | solution.py:524
  49.4 0.1 collective-permute-start.11
  49.5 0.0 collective-permute-done.8.yl
  49.5 0.4 collective-permute-done.9.yh
  49.9 0.7 collective-permute-done.10.cl
  50.5 2.3 %collective-permute-done.11.ch = f32[12,8,128]{2,1,0:T(8,128)S(1)} collective-permute-done((f32[12,8,128]{2,1,0:T(8,128)S(1)}, f32[12,8,128]{2,1,0:T(8,128)S(1)}, u32[]{:S(2)}, u32[]{:S(2)}) %collective-permute-start.11) | collective-permute-done | bytes 49184 | tf_op jit(solution)/shard_map/ppermute | solution.py:524
  52.9 1.5 %shard_map.89 = (f32[8,16,128]{2,1,0:T(8,128)}, f32[17,16,128]{2,1,0:T(8,128)S(1)}, f32[5,10,32,128]{3,2,1,0:T(8,128)S(1)}) custom-call(f32[2,8,16,128]{3,2,1,0:T(8,128)S(1)} %get-tuple-element.44.conc, f32[8,16,128]{2,1,0:T(8,128)S(1)} %get-tuple-element.45.phi, f32[8,16,128]{2,1,0:T(8,128)S(1)} %get-tuple-element.46.charge, ...), custom_call_target="tpu_custom_call" | custom-call | tf_op jit(solution)/shard_map/pallas_call | solution.py:506
  54.4 1.3 %collective-permute-start.13 = (f32[17,16,128]{2,1,0:T(8,128)S(1)}, f32[17,16,128]{2,1,0:T(8,128)S(1)}, u32[]{:S(2)}, u32[]{:S(2)}) collective-permute-start(f32[17,16,128]{2,1,0:T(8,128)S(1)} %get-tuple-element.59.mine), channel_id=1, source_target_pairs={{0,7},{1,0},{2,1},{3,2},{4,3},{5,4},{6,5},{7,6},{8,15},{9,8},{10,9... | collective-permute-start | bytes 417800 | tf_op jit(solution)/shard_map/ppermute | solution.py:524
  55.7 0.4 collective-permute-start.12
  56.1 2.7 %collective-permute-done.13.above = f32[17,16,128]{2,1,0:T(8,128)S(1)} collective-permute-done((f32[17,16,128]{2,1,0:T(8,128)S(1)}, f32[17,16,128]{2,1,0:T(8,128)S(1)}, u32[]{:S(2)}, u32[]{:S(2)}) %collective-permute-start.13) | collective-permute-done | bytes 139296 | tf_op jit(solution)/shard_map/ppermute | solution.py:524
  58.9 0.6 collective-permute-done.12.below
  59.6 4.8 %collective-permute-start.14 = (f32[16,16,128]{2,1,0:T(8,128)S(1)}, f32[16,16,128]{2,1,0:T(8,128)S(1)}, u32[]{:S(2)}, u32[]{:S(2)}) collective-permute-start(f32[16,16,128]{2,1,0:T(8,128)S(1)} %get-tuple-element.60), channel_id=1, source_target_pairs={{0,3},{1,4},{2,5},{3,6},{4,7},{5,0},{6,1},{7,2},{8,11},{9,12},{10,... | collective-permute-start | bytes 393224 | tf_op jit(solution)/shard_map/ppermute | solution.py:524
  64.3 2.0 %collective-permute-start.15 = (f32[16,16,128]{2,1,0:T(8,128)S(1)}, f32[16,16,128]{2,1,0:T(8,128)S(1)}, u32[]{:S(2)}, u32[]{:S(2)}) collective-permute-start(f32[16,16,128]{2,1,0:T(8,128)S(1)} %get-tuple-element.61), channel_id=1, source_target_pairs={{0,5},{1,6},{2,7},{3,0},{4,1},{5,2},{6,3},{7,4},{8,13},{9,14},{10,... | collective-permute-start | bytes 393224 | tf_op jit(solution)/shard_map/ppermute | solution.py:524
  66.3 1.9 %shard_map.90 = f32[19,8,16,128]{3,2,1,0:T(8,128)} custom-call(f32[19,8,16,128]{3,2,1,0:T(8,128)S(1)} %get-tuple-element.42.pop, f32[10,32,128]{2,1,0:T(8,128)S(1)} %get-tuple-element.43.fl, f32[5,10,32,128]{3,2,1,0:T(8,128)S(1)} %get-tuple-element.57.sh, f32[19,16,128]{2,1,0:T(8,128)S(1)} %collective-permute-done.6.xl, ...), custom_call_target="tpu_custom_call" | custom-call | flops 40000000 | tf_op jit(solution)/shard_map/pallas_call | solution.py:506
  68.3 0.0 collective-permute-done.14.from_low
  68.3 4.6 %collective-permute-done.15.from_high = f32[16,16,128]{2,1,0:T(8,128)S(1)} collective-permute-done((f32[16,16,128]{2,1,0:T(8,128)S(1)}, f32[16,16,128]{2,1,0:T(8,128)S(1)}, u32[]{:S(2)}, u32[]{:S(2)}) %collective-permute-start.15) | collective-permute-done | bytes 131104 | tf_op jit(solution)/shard_map/ppermute | solution.py:524
  72.9 0.7 shard_map.92
  (3 shorter events, 0.1 us)
Async XLA Ops:
  0.6 32.5 %copy-start.3 = (f32[8,16,128]{2,1,0:T(8,128)S(1)}, f32[8,16,128]{2,1,0:T(8,128)}, u32[]{:S(2)}) copy-start(f32[8,16,128]{2,1,0:T(8,128)} %perm.1) | copy-start | bytes 196612
  0.6 32.5 %copy-start.2 = (f32[8,16,128]{2,1,0:T(8,128)S(1)}, f32[8,16,128]{2,1,0:T(8,128)}, u32[]{:S(2)}) copy-start(f32[8,16,128]{2,1,0:T(8,128)} %phi.1) | copy-start | bytes 196612
  0.7 32.5 %copy-start.1 = (f32[2,8,16,128]{3,2,1,0:T(8,128)S(1)}, f32[2,8,16,128]{3,2,1,0:T(8,128)}, u32[]{:S(2)}) copy-start(f32[2,8,16,128]{3,2,1,0:T(8,128)} %conc.1) | copy-start | bytes 393220
  0.7 32.5 %copy-start = (f32[19,8,16,128]{3,2,1,0:T(8,128)S(1)}, f32[19,8,16,128]{3,2,1,0:T(8,128)}, u32[]{:S(2)}) copy-start(f32[19,8,16,128]{3,2,1,0:T(8,128)} %pop.1) | copy-start | bytes 3735556
  2.4 23.4 %collective-permute-start = (f32[28,16,128]{2,1,0:T(8,128)S(1)}, f32[28,16,128]{2,1,0:T(8,128)S(1)}, u32[]{:S(2)}, u32[]{:S(2)}) collective-permute-start(f32[28,16,128]{2,1,0:T(8,128)S(1)} %get-tuple-element.36), channel_id=1, source_target_pairs={{0,8},{8,16},{16,24},{24,32},{32,40},{40,48},{48,56},{56,64},{64,7... | collective-permute-start | bytes 688136 | tf_op jit(solution)/shard_map/ppermute | solution.py:524
  6.4 20.2 %collective-permute-start.1 = (f32[28,16,128]{2,1,0:T(8,128)S(1)}, f32[28,16,128]{2,1,0:T(8,128)S(1)}, u32[]{:S(2)}, u32[]{:S(2)}) collective-permute-start(f32[28,16,128]{2,1,0:T(8,128)S(1)} %get-tuple-element.37), channel_id=1, source_target_pairs={{0,760},{8,0},{16,8},{24,16},{32,24},{40,32},{48,40},{56,48},{64,5... | collective-permute-start | bytes 688136 | tf_op jit(solution)/shard_map/ppermute | solution.py:524
  22.4 6.9 %collective-permute-start.2 = (f32[8,32,128]{2,1,0:T(8,128)S(1)}, f32[8,32,128]{2,1,0:T(8,128)S(1)}, u32[]{:S(2)}, u32[]{:S(2)}) collective-permute-start(f32[8,32,128]{2,1,0:T(8,128)S(1)} %get-tuple-element.38), channel_id=1, source_target_pairs={{0,1},{1,2},{2,3},{3,4},{4,5},{5,6},{6,7},{7,0},{8,9},{9,10},{10,1... | collective-permute-start | bytes 393224 | tf_op jit(solution)/shard_map/ppermute | solution.py:524
  24.4 4.9 %collective-permute-start.3 = (f32[8,32,128]{2,1,0:T(8,128)S(1)}, f32[8,32,128]{2,1,0:T(8,128)S(1)}, u32[]{:S(2)}, u32[]{:S(2)}) collective-permute-start(f32[8,32,128]{2,1,0:T(8,128)S(1)} %get-tuple-element.39), channel_id=1, source_target_pairs={{0,7},{1,0},{2,1},{3,2},{4,3},{5,4},{6,5},{7,6},{8,15},{9,8},{10,9... | collective-permute-start | bytes 393224 | tf_op jit(solution)/shard_map/ppermute | solution.py:524
  26.7 4.1 %collective-permute-start.4 = (f32[18,8,128]{2,1,0:T(8,128)S(1)}, f32[18,8,128]{2,1,0:T(8,128)S(1)}, u32[]{:S(2)}, u32[]{:S(2)}) collective-permute-start(f32[18,8,128]{2,1,0:T(8,128)S(1)} %get-tuple-element.40), channel_id=1, source_target_pairs={{0,1},{1,2},{2,3},{3,4},{4,5},{5,6},{6,7},{7,0},{8,9},{9,10},{10,1... | collective-permute-start | bytes 221192 | tf_op jit(solution)/shard_map/ppermute | solution.py:524
  29.3 3.8 %collective-permute-start.5 = (f32[18,8,128]{2,1,0:T(8,128)S(1)}, f32[18,8,128]{2,1,0:T(8,128)S(1)}, u32[]{:S(2)}, u32[]{:S(2)}) collective-permute-start(f32[18,8,128]{2,1,0:T(8,128)S(1)} %get-tuple-element.41), channel_id=1, source_target_pairs={{0,7},{1,0},{2,1},{3,2},{4,3},{5,4},{6,5},{7,6},{8,15},{9,8},{10,9... | collective-permute-start | bytes 221192 | tf_op jit(solution)/shard_map/ppermute | solution.py:524
  35.9 11.7 %collective-permute-start.6 = (f32[19,16,128]{2,1,0:T(8,128)S(1)}, f32[19,16,128]{2,1,0:T(8,128)S(1)}, u32[]{:S(2)}, u32[]{:S(2)}) collective-permute-start(f32[19,16,128]{2,1,0:T(8,128)S(1)} %get-tuple-element.51), channel_id=1, source_target_pairs={{0,8},{8,16},{16,24},{24,32},{32,40},{40,48},{48,56},{56,64},{64,7... | collective-permute-start | bytes 466952 | tf_op jit(solution)/shard_map/ppermute | solution.py:524
  37.8 10.7 %collective-permute-start.7 = (f32[19,16,128]{2,1,0:T(8,128)S(1)}, f32[19,16,128]{2,1,0:T(8,128)S(1)}, u32[]{:S(2)}, u32[]{:S(2)}) collective-permute-start(f32[19,16,128]{2,1,0:T(8,128)S(1)} %get-tuple-element.52), channel_id=1, source_target_pairs={{0,760},{8,0},{16,8},{24,16},{32,24},{40,32},{48,40},{56,48},{64,5... | collective-permute-start | bytes 466952 | tf_op jit(solution)/shard_map/ppermute | solution.py:524
  45.2 4.3 %collective-permute-start.8 = (f32[8,24,128]{2,1,0:T(8,128)S(1)}, f32[8,24,128]{2,1,0:T(8,128)S(1)}, u32[]{:S(2)}, u32[]{:S(2)}) collective-permute-start(f32[8,24,128]{2,1,0:T(8,128)S(1)} %get-tuple-element.53), channel_id=1, source_target_pairs={{0,1},{1,2},{2,3},{3,4},{4,5},{5,6},{6,7},{7,0},{8,9},{9,10},{10,1... | collective-permute-start | bytes 294920 | tf_op jit(solution)/shard_map/ppermute | solution.py:524
  45.5 4.3 %collective-permute-start.9 = (f32[8,24,128]{2,1,0:T(8,128)S(1)}, f32[8,24,128]{2,1,0:T(8,128)S(1)}, u32[]{:S(2)}, u32[]{:S(2)}) collective-permute-start(f32[8,24,128]{2,1,0:T(8,128)S(1)} %get-tuple-element.54), channel_id=1, source_target_pairs={{0,7},{1,0},{2,1},{3,2},{4,3},{5,4},{6,5},{7,6},{8,15},{9,8},{10,9... | collective-permute-start | bytes 294920 | tf_op jit(solution)/shard_map/ppermute | solution.py:524
  48.5 2.0 %collective-permute-start.10 = (f32[12,8,128]{2,1,0:T(8,128)S(1)}, f32[12,8,128]{2,1,0:T(8,128)S(1)}, u32[]{:S(2)}, u32[]{:S(2)}) collective-permute-start(f32[12,8,128]{2,1,0:T(8,128)S(1)} %get-tuple-element.55), channel_id=1, source_target_pairs={{0,1},{1,2},{2,3},{3,4},{4,5},{5,6},{6,7},{7,0},{8,9},{9,10},{10,1... | collective-permute-start | bytes 147464 | tf_op jit(solution)/shard_map/ppermute | solution.py:524
  49.4 3.5 %collective-permute-start.11 = (f32[12,8,128]{2,1,0:T(8,128)S(1)}, f32[12,8,128]{2,1,0:T(8,128)S(1)}, u32[]{:S(2)}, u32[]{:S(2)}) collective-permute-start(f32[12,8,128]{2,1,0:T(8,128)S(1)} %get-tuple-element.56), channel_id=1, source_target_pairs={{0,7},{1,0},{2,1},{3,2},{4,3},{5,4},{6,5},{7,6},{8,15},{9,8},{10,9... | collective-permute-start | bytes 147464 | tf_op jit(solution)/shard_map/ppermute | solution.py:524
  54.4 4.5 %collective-permute-start.13 = (f32[17,16,128]{2,1,0:T(8,128)S(1)}, f32[17,16,128]{2,1,0:T(8,128)S(1)}, u32[]{:S(2)}, u32[]{:S(2)}) collective-permute-start(f32[17,16,128]{2,1,0:T(8,128)S(1)} %get-tuple-element.59.mine), channel_id=1, source_target_pairs={{0,7},{1,0},{2,1},{3,2},{4,3},{5,4},{6,5},{7,6},{8,15},{9,8},{10,9... | collective-permute-start | bytes 417800 | tf_op jit(solution)/shard_map/ppermute | solution.py:524
  55.7 3.8 %collective-permute-start.12 = (f32[17,16,128]{2,1,0:T(8,128)S(1)}, f32[17,16,128]{2,1,0:T(8,128)S(1)}, u32[]{:S(2)}, u32[]{:S(2)}) collective-permute-start(f32[17,16,128]{2,1,0:T(8,128)S(1)} %get-tuple-element.59.mine), channel_id=1, source_target_pairs={{0,1},{1,2},{2,3},{3,4},{4,5},{5,6},{6,7},{7,0},{8,9},{9,10},{10,1... | collective-permute-start | bytes 417800 | tf_op jit(solution)/shard_map/ppermute | solution.py:524
  59.6 8.7 %collective-permute-start.14 = (f32[16,16,128]{2,1,0:T(8,128)S(1)}, f32[16,16,128]{2,1,0:T(8,128)S(1)}, u32[]{:S(2)}, u32[]{:S(2)}) collective-permute-start(f32[16,16,128]{2,1,0:T(8,128)S(1)} %get-tuple-element.60), channel_id=1, source_target_pairs={{0,3},{1,4},{2,5},{3,6},{4,7},{5,0},{6,1},{7,2},{8,11},{9,12},{10,... | collective-permute-start | bytes 393224 | tf_op jit(solution)/shard_map/ppermute | solution.py:524
  64.3 8.6 %collective-permute-start.15 = (f32[16,16,128]{2,1,0:T(8,128)S(1)}, f32[16,16,128]{2,1,0:T(8,128)S(1)}, u32[]{:S(2)}, u32[]{:S(2)}) collective-permute-start(f32[16,16,128]{2,1,0:T(8,128)S(1)} %get-tuple-element.61), channel_id=1, source_target_pairs={{0,5},{1,6},{2,7},{3,0},{4,1},{5,2},{6,3},{7,4},{8,13},{9,14},{10,... | collective-permute-start | bytes 393224 | tf_op jit(solution)/shard_map/ppermute | solution.py:524
